TPU v7x, 32 devices: a whole 2x2x4 slice. The times are simulated.
32 devices in a mesh: slab: 2 (over y), vox: 8 (over z, x), ray: 2 (over core).
Axes of the slice: x: 2, y: 2, z: 4, core: 2. Of those that a mesh axis runs over, the one named last changes fastest.
Arguments:
- volume: float32 [256, 4, 128], P(('slab', 'vox', 'ray')), parts along dimension 0, may hold values from 0 to 1
- tiles: bfloat16 [16, 2, 48, 128, 128], P(('slab', 'vox'), 'ray'), parts along dimension 0, may hold values from 0 to 0.015625
- tile_row: int32 [16, 2, 48], P(('slab', 'vox'), 'ray'), parts along dimension 0, may hold values from 0 to 7
- tile_col: int32 [16, 2, 48], P(('slab', 'vox'), 'ray'), parts along dimension 0, may hold values from 0 to 15
- tile_count: int32 [16, 2], P(('slab', 'vox'), 'ray'), parts along dimension 0, may hold values from 12 to 48, as said below
- measured: float32 [2, 16, 4, 128], P('ray', ('slab', 'vox')), parts along dimension 1, may hold values from 0 to 48, as said below
Outputs:
- new_volume: float32 [256, 4, 128], P(('slab', 'vox', 'ray')), parts along dimension 0
- residual: bfloat16 [2, 16, 4, 128], P('ray', ('slab', 'vox')), parts along dimension 1
There are 2 independent parts, one for each index of `slab`. A program takes and returns all parts, laid end to end along the dimension named above; each array names one. Nothing has to cross between parts.
Inputs may be any that keep to these rules, and one draw needn't show every extreme that they name: Each device uses its first tile_count slots; the most, 48, is reached by some device of every part. `measured`: recorded intensities are nonnegative.
All inputs are finite; a program needn't handle non-finite values.
Results may differ from a plain program's by a relative error of at most 0.0025.
Values may be sent and summed in bfloat16 or wider, within the bound.
No kernel may reach another device: no remote copies, remote signals or barrier semaphores. Data moves between devices by JAX's collectives and lax.ppermute only.
A program may use at most 64 MiB of HBM per device.

v0:
```python
import jax
import jax.numpy as jnp
from jax import lax
from jax.sharding import PartitionSpec as P


def on_device(volume, tiles, tile_row, tile_col, tile_count, measured):
    block = tiles[0, 0]
    rows = tile_row[0, 0]
    cols = tile_col[0, 0]
    used = tile_count[0, 0]
    inst = volume.shape[1]
    width = volume.shape[2]
    slots = block.shape[0]
    own = measured.shape[1]
    highest = lax.Precision.HIGHEST
    valid = jnp.arange(slots, dtype=jnp.int32) < used
    ones = jnp.ones((slots, 1, width), jnp.bfloat16)
    panel = lax.all_gather(volume.astype(jnp.bfloat16), "ray", axis=0, tiled=True)
    picked = jnp.concatenate([panel[cols], ones], axis=1)
    prod = jnp.einsum("nrv,ncv->ncr", block, picked, preferred_element_type=jnp.float32)
    blocks = jnp.arange(own * lax.axis_size("vox"), dtype=jnp.int32)
    onehot = ((rows[:, None] == blocks[None, :]) & valid[:, None]).astype(jnp.float32)
    sums = lax.psum_scatter(
        jnp.einsum("nb,ncr->bcr", onehot, prod, precision=highest),
        "vox",
        scatter_dimension=0,
        tiled=True,
    )
    mine = ((measured[0] - sums[:, :inst]) / (sums[:, inst:] + 1.0)).astype(jnp.bfloat16)
    whole_res = lax.all_gather(mine, "vox", axis=0, tiled=True)
    gathered = jnp.concatenate([whole_res[rows], ones], axis=1)
    back = jnp.einsum("nrv,ncr->ncv", block, gathered, preferred_element_type=jnp.float32)
    blocks = jnp.arange(lax.axis_size("ray") * volume.shape[0], dtype=jnp.int32)
    onehot = ((cols[:, None] == blocks[None, :]) & valid[:, None]).astype(jnp.float32)
    bsum = lax.psum_scatter(
        jnp.einsum("nb,ncv->bcv", onehot, back, precision=highest).astype(jnp.bfloat16),
        "ray",
        scatter_dimension=0,
        tiled=True,
    ).astype(jnp.float32)
    new_volume = jnp.maximum(volume + bsum[:, :inst] / (bsum[:, inst:] + 1.0), 0.0)
    return (new_volume, mine[None])


def solution(mesh):
    in_specs = (
        P(("slab", "vox", "ray"), None, None),
        P(("slab", "vox"), "ray", None, None, None),
        P(("slab", "vox"), "ray", None),
        P(("slab", "vox"), "ray", None),
        P(("slab", "vox"), "ray"),
        P("ray", ("slab", "vox"), None, None),
    )
    out_specs = (P(("slab", "vox", "ray"), None, None), P("ray", ("slab", "vox"), None, None))
    return jax.shard_map(
        on_device, mesh=mesh, in_specs=in_specs, out_specs=out_specs, check_vma=False
    )
```

profile of v0, /device:TPU:0, one launch (start us, length us, event | category | flops | bytes accessed | tf_op | source)
XLA Modules:
  0.0 70.7 jit_solution(10105855342322695486)
XLA Ops:
  0.6 0.0 copy-start
  0.6 0.0 copy-start.6
  0.7 0.0 copy-start.3
  0.7 0.0 copy-start.2
  1.5 0.7 %convert_element_type.14 = bf16[8,4,128]{2,1,0:T(4,128)(2,1)S(1)} convert(f32[8,4,128]{2,1,0:T(4,128)} %param.6) | non-fusion elementwise | flops 4096 | bytes 24576 | tf_op jit(solution)/shard_map/convert_element_type | solution.py:19
  2.2 1.9 %all_gather.6 = bf16[16,4,128]{2,1,0:T(4,128)(2,1)S(1)} all-gather(bf16[8,4,128]{2,1,0:T(4,128)(2,1)S(1)} %convert_element_type.14), channel_id=1, replica_groups=mesh['slab'=2,'vox'=8,'ray'=2] {'ray'}, dimensions={0}, use_global_device_ids=true | all-gather | bytes 24576 | tf_op jit(solution)/shard_map/all_gather | solution.py:19
  4.1 0.7 fusion.26
  4.8 0.6 gather_fusion
  5.4 0.0 copy-done
  5.4 0.0 copy-start.4
  5.4 0.9 %fusion.2 = f32[48,5,128]{2,1,0:T(8,128)S(1)} fusion(bf16[1,1,48,128,128]{4,3,2,1,0:T(8,128)(2,1)S(1)} %copy-done, bf16[48,4,128]{2,1,0:T(4,128)(2,1)S(1)} %gather_fusion), kind=kOutput, calls=%fused_computation.4 | convolution fusion | flops 7864320 | bytes 1744896 | tf_op jit(solution)/shard_map/nrv,ncv->ncr/dot_general | solution.py:21
  6.3 0.0 copy-start.5
  6.3 0.0 copy-start.1
  6.3 0.0 copy-done.3
  6.3 0.2 fusion.5
  6.5 38.7 %all-reduce.2 = f32[8,5,128]{2,0,1:T(8,128)S(1)} all-reduce(f32[8,5,128]{2,0,1:T(8,128)S(1)} %fusion.5), channel_id=2, replica_groups=mesh['slab'=2,'vox'=8,'ray'=2] {'vox'}, use_global_device_ids=true, to_apply=%region_0.0.clone | all-reduce | flops 5120 | bytes 40960
  45.2 0.0 copy-done.6
  45.2 0.6 dynamic-slice
  45.8 0.7 fusion.25
  46.5 0.0 copy-done.2
  46.5 0.7 fusion.22
  47.1 16.3 %all_gather.7 = bf16[8,4,128]{2,1,0:T(4,128)(2,1)S(1)} all-gather(bf16[1,4,128]{2,1,0:T(4,128)(2,1)S(1)} %copy.14), channel_id=1, replica_groups=mesh['slab'=2,'vox'=8,'ray'=2] {'vox'}, dimensions={0}, use_global_device_ids=true | all-gather | bytes 9216 | tf_op jit(solution)/shard_map/all_gather | solution.py:31
  63.4 0.6 gather_fusion.1
  64.1 0.5 fusion
  64.6 0.0 copy-done.4
  64.6 0.2 convolution_convert_fusion
  64.8 3.4 %all-reduce.3 = bf16[16,5,128]{2,0,1:T(8,128)(2,1)S(1)} all-reduce(bf16[16,5,128]{2,0,1:T(8,128)(2,1)S(1)} %convolution_convert_fusion), channel_id=3, replica_groups=mesh['slab'=2,'vox'=8,'ray'=2] {'ray'}, use_global_device_ids=true, to_apply=%region_1.0.clone | all-reduce | flops 10240 | bytes 40960
  68.2 0.0 copy-done.5
  68.2 0.6 dynamic-slice.2
  69.5 0.0 copy-done.1
  69.5 0.6 copy.17
  70.1 0.6 copy.29
  (8 shorter events, 0.1 us)
Async XLA Ops:
  0.6 4.8 %copy-start = (bf16[1,1,48,128,128]{4,3,2,1,0:T(8,128)(2,1)S(1)}, bf16[1,1,48,128,128]{4,3,2,1,0:T(8,128)(2,1)}, u32[]{:S(2)}) copy-start(bf16[1,1,48,128,128]{4,3,2,1,0:T(8,128)(2,1)} %param.7) | copy-start | bytes 4718596
  0.6 44.6 %copy-start.6 = (u32[32]{0:T(128)S(1)}, u32[32]{0:T(128)}, u32[]{:S(2)}) copy-start(u32[32]{0:T(128)} %constant.25) | copy-start | bytes 388
  0.7 5.7 %copy-start.3 = (s32[1,1,48]{2,1,0:T(1,128)S(1)}, s32[1,1,48]{2,1,0:T(1,128)}, u32[]{:S(2)}) copy-start(s32[1,1,48]{2,1,0:T(1,128)} %param.8) | copy-start | bytes 580
  0.7 45.8 %copy-start.2 = (f32[1,1,4,128]{3,2,1,0:T(4,128)S(1)}, f32[1,1,4,128]{3,2,1,0:T(4,128)}, u32[]{:S(2)}) copy-start(f32[1,1,4,128]{3,2,1,0:T(4,128)} %param.11) | copy-start | bytes 6148
  5.4 59.2 %copy-start.4 = (s32[1,1,48]{2,1,0:T(1,128)S(1)}, s32[1,1,48]{2,1,0:T(1,128)}, u32[]{:S(2)}) copy-start(s32[1,1,48]{2,1,0:T(1,128)} %param.9) | copy-start | bytes 580
  6.3 61.9 %copy-start.5 = (u32[32]{0:T(128)S(1)}, u32[32]{0:T(128)}, u32[]{:S(2)}) copy-start(u32[32]{0:T(128)} %constant.29) | copy-start | bytes 388
  6.3 63.1 %copy-start.1 = (f32[8,4,128]{2,1,0:T(4,128)S(1)}, f32[8,4,128]{2,1,0:T(4,128)}, u32[]{:S(2)}) copy-start(f32[8,4,128]{2,1,0:T(4,128)} %param.6) | copy-start | bytes 49156
where the time goes:
time: 71 us; the launch traced here: 70.7 us
  blocking collectives  60.3 us (85%)
  local copies, waits for them, and re-layouts  3.65 us (5%)
  other arithmetic  2.74 us (4%)
  between operations  2.19 us (3%)
  matrix products  1.78 us (3%)
    unnamed x2, blocking collectives  42.1 us
    all_gather x1, blocking collectives, on_device(): whole_res = lax.all_gather(mine, 'vox', axis=0, tiled=True)  16.3 us
    all_gather x1, blocking collectives, on_device(): lax.all_gather(volume.astype(jnp.bfloat16), 'ray', axis=0, tiled=True)  1.93 us
    unnamed x17, local copies, waits for them, and re-layouts  1.82 us

commit v1 on v0

v1 whole, which is shorter than its diff:
```python
import jax
import jax.numpy as jnp
from jax import lax
from jax.sharding import PartitionSpec as P


def exchange(value, axis, mask):
    size = lax.axis_size(axis)
    return lax.ppermute(value, axis, [(i, i ^ mask) for i in range(size)])


def radices_of(size, most):
    out = []
    while size > 1:
        radix = min(size, most)
        out.append(radix)
        size //= radix
    return out


def all_sum(value, axis, most):
    stride = 1
    for radix in radices_of(lax.axis_size(axis), most):
        terms = [value] + [exchange(value, axis, stride * k) for k in range(1, radix)]
        while len(terms) > 1:
            terms = [a + b for a, b in zip(terms[::2], terms[1::2])]
        value = terms[0]
        stride *= radix
    return value


def on_device(volume, tiles, tile_row, tile_col, tile_count, measured):
    block = tiles[0, 0]
    rows = tile_row[0, 0]
    cols = tile_col[0, 0]
    used = tile_count[0, 0]
    inst = volume.shape[1]
    width = volume.shape[2]
    half = volume.shape[0]
    slots = block.shape[0]
    highest = lax.Precision.HIGHEST
    ray = lax.axis_index("ray")
    vox = lax.axis_index("vox")
    valid = jnp.arange(slots, dtype=jnp.int32) < used
    ones = jnp.ones((slots, 1, width), jnp.bfloat16)

    own = volume.astype(jnp.bfloat16)
    other = exchange(own, "ray", 1)
    place = jnp.where(ray == 0, cols, lax.rem(cols + half, 2 * half))
    panel = jnp.concatenate([own, other], axis=0)
    picked = jnp.concatenate([panel[place], ones], axis=1)
    prod = jnp.einsum("nrv,ncv->ncr", block, picked, preferred_element_type=jnp.float32)
    blocks = jnp.arange(lax.axis_size("vox"), dtype=jnp.int32)
    onehot = ((rows[:, None] == blocks[None, :]) & valid[:, None]).astype(jnp.float32)
    sums = jnp.einsum("nb,ncr->bcr", onehot, prod, precision=highest)
    mine = (blocks == vox)[:, None, None]
    part = jnp.concatenate([jnp.where(mine, measured[0], 0.0) - sums[:, :inst], sums[:, inst:]], axis=1)
    total = all_sum(part, "vox", 8)
    residual = (total[:, :inst] / (total[:, inst:] + 1.0)).astype(jnp.bfloat16)
    own_res = lax.dynamic_slice_in_dim(residual, vox, 1, 0)
    gathered = jnp.concatenate([residual[rows], ones], axis=1)
    back = jnp.einsum("nrv,ncr->ncv", block, gathered, preferred_element_type=jnp.float32)
    blocks = jnp.arange(2 * half, dtype=jnp.int32)
    onehot = ((place[:, None] == blocks[None, :]) & valid[:, None]).astype(jnp.float32)
    bsum = jnp.einsum("nb,ncv->bcv", onehot, back, precision=highest)
    there = exchange(bsum[half:].astype(jnp.bfloat16), "ray", 1)
    bsum = bsum[:half] + there.astype(jnp.float32)
    new_volume = jnp.maximum(volume + bsum[:, :inst] / (bsum[:, inst:] + 1.0), 0.0)
    return (new_volume, own_res[None])


def solution(mesh):
    in_specs = (
        P(("slab", "vox", "ray"), None, None),
        P(("slab", "vox"), "ray", None, None, None),
        P(("slab", "vox"), "ray", None),
        P(("slab", "vox"), "ray", None),
        P(("slab", "vox"), "ray"),
        P("ray", ("slab", "vox"), None, None),
    )
    out_specs = (P(("slab", "vox", "ray"), None, None), P("ray", ("slab", "vox"), None, None))
    return jax.shard_map(
        on_device, mesh=mesh, in_specs=in_specs, out_specs=out_specs, check_vma=False
    )
```

time: 71 us -> 26.4 us (0.37)
  blocking collectives: 60.3 us -> 0 us
  starting transfers between devices: 0 us -> 12.6 us
  waiting for transfers between devices: 0 us -> 5.49 us
  local copies, waits for them, and re-layouts: 3.65 us -> 2.49 us
  between operations: 2.19 us -> 1.45 us
    unnamed x2 -> x0, blocking collectives: 42.1 us -> none
    all_gather x2 -> x0, blocking collectives: 18.2 us -> none  [the longest x1 16.3 us: on_device(): whole_res = lax.all_gather(mine, 'vox', axis=0, tiled=True)]
    ppermute x0 -> x9, starting transfers between devices: none -> 12.6 us  [exchange(): return lax.ppermute(value, axis, [(i, i ^ mask) for i in range(size)])]
    ppermute x0 -> x9, waiting for transfers between devices: none -> 5.49 us  [exchange(): return lax.ppermute(value, axis, [(i, i ^ mask) for i in range(size)])]
    unnamed x17 -> x12, local copies, waits for them, and re-layouts: 1.82 us -> 1.21 us
  transfers between devices with their start and end apart: 0 -> 9, of which waited for: 0 -> 3; matrix products, arithmetic and copies ran while one was open for 0% -> 7% of each run, Pallas kernels for 0% -> 0%
where the time goes in v1:
time: 26.4 us; the launch traced here: 26.2 us
  starting transfers between devices  12.6 us (48%)
  waiting for transfers between devices  5.49 us (21%)
  local copies, waits for them, and re-layouts  2.49 us (9%)
  other arithmetic  2.34 us (9%)
  matrix products  1.78 us (7%)
  between operations  1.45 us (5%)
    ppermute x9, starting transfers between devices, exchange(): return lax.ppermute(value, axis, [(i, i ^ mask) for i in range(size)])  12.6 us
    ppermute x9, waiting for transfers between devices, exchange(): return lax.ppermute(value, axis, [(i, i ^ mask) for i in range(size)])  5.49 us
    unnamed x12, local copies, waits for them, and re-layouts  1.21 us
    dot_general x1, matrix products, on_device(): jnp.einsum('nrv,ncv->ncr', block, picked, preferred_element_type=jnp.floa...  0.91 us
    convert_element_type x1, other arithmetic, on_device(): own = volume.astype(jnp.bfloat16)  0.84 us
    select_n x1, other arithmetic, on_device(): picked = jnp.concatenate([panel[place], ones], axis=1)  0.66 us
    select_n x1, other arithmetic, on_device(): gathered = jnp.concatenate([residual[rows], ones], axis=1)  0.66 us
    gather x1, local copies, waits for them, and re-layouts, on_device(): picked = jnp.concatenate([panel[place], ones], axis=1)  0.63 us
  transfers between devices with their start and end apart: 9, of which 3 were waited for; matrix products, arithmetic and copies ran while one was open for 7% of the time, Pallas kernels for 0%

profile of v1, /device:TPU:0, one launch (start us, length us, event | category | flops | bytes accessed | tf_op | source)
XLA Modules:
  0.0 26.2 jit_solution(6956415339053221836)
XLA Ops:
  0.6 0.0 copy-start
  0.6 0.0 copy-start.3
  0.7 0.0 copy-start.4
  0.7 0.0 copy-start.2
  0.7 0.8 %convert_element_type.12 = bf16[8,4,128]{2,1,0:T(4,128)(2,1)S(1)} convert(f32[8,4,128]{2,1,0:T(4,128)} %param.6) | non-fusion elementwise | flops 4096 | bytes 24576 | tf_op jit(solution)/shard_map/convert_element_type | solution.py:47
  1.5 0.5 %collective-permute-start = (bf16[8,4,128]{2,1,0:T(4,128)(2,1)S(1)}, bf16[8,4,128]{2,1,0:T(4,128)(2,1)S(1)}, u32[]{:S(2)}, u32[]{:S(2)}) collective-permute-start(bf16[8,4,128]{2,1,0:T(4,128)(2,1)S(1)} %convert_element_type.12), channel_id=1, source_target_pairs={{0,1},{1,0},{2,3},{3,2},{4,5},{5,4},{6,7},{7,6},{8,9},{9,8},{10,11... | collective-permute-start | bytes 24584 | tf_op jit(solution)/shard_map/ppermute | solution.py:9
  2.6 0.7 %fusion.27 = s32[48]{0:T(128)S(1)} fusion(s32[1,1,48]{2,1,0:T(1,128)} %param.8), kind=kLoop, calls=%fused_computation.50 | loop fusion | flops 144 | bytes 384 | tf_op jit(solution)/shard_map/select_n | solution.py:61
  3.3 0.7 %fusion.28 = s32[48]{0:T(128)S(1)} fusion(s32[1,1,48]{2,1,0:T(1,128)} %param.9, pred[]{:T(512)S(6)} %eq.41), kind=kLoop, calls=%fused_computation.55 | loop fusion | flops 528 | bytes 385 | tf_op jit(solution)/shard_map/select_n | solution.py:51
  4.0 0.0 collective-permute-done
  4.0 0.6 %gather_fusion = bf16[48,4,128]{2,1,0:T(4,128)(2,1)S(1)} fusion(bf16[16,4,128]{2,1,0:T(4,128)(2,1)S(1)} %pad_maximum_fusion.1, s32[1024]{0:T(1024)S(1)} %pad_clamp_fusion.1), kind=kCustom, calls=%fused_computation | custom fusion | bytes 98496 | tf_op jit(solution)/shard_map/gather | solution.py:51
  4.7 0.0 copy-done
  4.7 0.9 %fusion.2 = f32[48,5,128]{2,1,0:T(8,128)S(1)} fusion(bf16[1,1,48,128,128]{4,3,2,1,0:T(8,128)(2,1)S(1)} %copy-done, bf16[48,4,128]{2,1,0:T(4,128)(2,1)S(1)} %gather_fusion), kind=kOutput, calls=%fused_computation.4 | convolution fusion | flops 7864320 | bytes 1744896 | tf_op jit(solution)/shard_map/nrv,ncv->ncr/dot_general | solution.py:52
  5.6 0.0 copy-start.1
  5.6 0.0 copy-done.3
  5.6 0.2 fusion.6
  5.8 0.0 copy-done.2
  5.8 0.1 slice_subtract_fusion
  5.9 4.6 %collective-permute-start.6 = (f32[8,5,128]{2,0,1:T(8,128)S(1)}, f32[8,5,128]{2,0,1:T(8,128)S(1)}, u32[]{:S(2)}, u32[]{:S(2)}) collective-permute-start(f32[8,5,128]{2,0,1:T(8,128)S(1)} %pad_maximum_fusion), channel_id=1, source_target_pairs={{0,12},{2,14},{4,8},{6,10},{8,4},{10,6},{12,0},{14,2},{1,13},{3,15... | collective-permute-start | bytes 61448 | tf_op jit(solution)/shard_map/ppermute | solution.py:9
  10.5 0.4 %collective-permute-start.5 = (f32[8,5,128]{2,0,1:T(8,128)S(1)}, f32[8,5,128]{2,0,1:T(8,128)S(1)}, u32[]{:S(2)}, u32[]{:S(2)}) collective-permute-start(f32[8,5,128]{2,0,1:T(8,128)S(1)} %pad_maximum_fusion), channel_id=1, source_target_pairs={{0,10},{2,8},{4,14},{6,12},{8,2},{10,0},{12,6},{14,4},{1,11},{3,9}... | collective-permute-start | bytes 61448 | tf_op jit(solution)/shard_map/ppermute | solution.py:9
  10.8 0.0 copy-done.4
  10.8 3.6 %collective-permute-start.4 = (f32[8,5,128]{2,0,1:T(8,128)S(1)}, f32[8,5,128]{2,0,1:T(8,128)S(1)}, u32[]{:S(2)}, u32[]{:S(2)}) collective-permute-start(f32[8,5,128]{2,0,1:T(8,128)S(1)} %pad_maximum_fusion), channel_id=1, source_target_pairs={{0,8},{2,10},{4,12},{6,14},{8,0},{10,2},{12,4},{14,6},{1,9},{3,11}... | collective-permute-start | bytes 61448 | tf_op jit(solution)/shard_map/ppermute | solution.py:9
  14.4 0.0 collective-permute-start.3
  14.4 2.0 %collective-permute-start.2 = (f32[8,5,128]{2,0,1:T(8,128)S(1)}, f32[8,5,128]{2,0,1:T(8,128)S(1)}, u32[]{:S(2)}, u32[]{:S(2)}) collective-permute-start(f32[8,5,128]{2,0,1:T(8,128)S(1)} %pad_maximum_fusion), channel_id=1, source_target_pairs={{0,4},{2,6},{4,0},{6,2},{8,12},{10,14},{12,8},{14,10},{1,5},{3,7},... | collective-permute-start | bytes 61448 | tf_op jit(solution)/shard_map/ppermute | solution.py:9
  16.4 0.0 collective-permute-done.6
  16.4 1.2 %collective-permute-start.7 = (f32[8,5,128]{2,0,1:T(8,128)S(1)}, f32[8,5,128]{2,0,1:T(8,128)S(1)}, u32[]{:S(2)}, u32[]{:S(2)}) collective-permute-start(f32[8,5,128]{2,0,1:T(8,128)S(1)} %pad_maximum_fusion), channel_id=1, source_target_pairs={{0,14},{2,12},{4,10},{6,8},{8,6},{10,4},{12,2},{14,0},{1,15},{3,13... | collective-permute-start | bytes 61448 | tf_op jit(solution)/shard_map/ppermute | solution.py:9
  17.6 0.0 collective-permute-done.5
  17.6 0.4 %collective-permute-start.1 = (f32[8,5,128]{2,0,1:T(8,128)S(1)}, f32[8,5,128]{2,0,1:T(8,128)S(1)}, u32[]{:S(2)}, u32[]{:S(2)}) collective-permute-start(f32[8,5,128]{2,0,1:T(8,128)S(1)} %pad_maximum_fusion), channel_id=1, source_target_pairs={{0,2},{2,0},{4,6},{6,4},{8,10},{10,8},{12,14},{14,12},{1,3},{3,1},... | collective-permute-start | bytes 61448 | tf_op jit(solution)/shard_map/ppermute | solution.py:9
  18.0 0.0 collective-permute-done.4
  18.0 1.1 %collective-permute-done.3 = f32[8,5,128]{2,0,1:T(8,128)S(1)} collective-permute-done((f32[8,5,128]{2,0,1:T(8,128)S(1)}, f32[8,5,128]{2,0,1:T(8,128)S(1)}, u32[]{:S(2)}, u32[]{:S(2)}) %collective-permute-start.3) | collective-permute-done | bytes 20512 | tf_op jit(solution)/shard_map/ppermute | solution.py:9
  19.1 0.0 collective-permute-done.2
  19.1 3.8 %collective-permute-done.7 = f32[8,5,128]{2,0,1:T(8,128)S(1)} collective-permute-done((f32[8,5,128]{2,0,1:T(8,128)S(1)}, f32[8,5,128]{2,0,1:T(8,128)S(1)}, u32[]{:S(2)}, u32[]{:S(2)}) %collective-permute-start.7) | collective-permute-done | bytes 20512 | tf_op jit(solution)/shard_map/ppermute | solution.py:9
  22.9 0.0 collective-permute-done.1
  22.9 0.6 %gather_fusion.1 = bf16[48,4,128]{2,1,0:T(4,128)(2,1)S(1)} fusion(bf16[8,4,128]{2,1,0:T(4,128)(2,1)S(1)} %copy.10, s32[1024]{0:T(1024)S(1)} %pad_clamp_fusion), kind=kCustom, calls=%fused_computation.1 | custom fusion | bytes 98496 | tf_op jit(solution)/shard_map/gather | solution.py:61
  23.6 0.5 %fusion = f32[48,5,128]{2,1,0:T(8,128)S(1)} fusion(bf16[1,1,48,128,128]{4,3,2,1,0:T(8,128)(2,1)S(1)} %copy-done, bf16[48,4,128]{2,1,0:T(4,128)(2,1)S(1)} %gather_fusion.1), kind=kOutput, calls=%fused_computation.2 | convolution fusion | flops 7864320 | bytes 1744896 | tf_op jit(solution)/shard_map/nrv,ncr->ncv/dot_general | solution.py:62
  24.1 0.2 fusion.4
  24.3 0.1 collective-permute-start.8
  24.4 0.6 %copy.22 = bf16[1,4,128]{2,1,0:T(4,128)(2,1)} copy(bf16[1,4,128]{2,0,1:T(2,128)(2,1)S(1)} %constant_dynamic-slice_fusion) | data formatting | bytes 2048
  24.9 0.6 %collective-permute-done.8 = bf16[8,5,128]{2,0,1:T(8,128)(2,1)S(1)} collective-permute-done((bf16[8,5,128]{2,0,1:T(8,128)(2,1)S(1)}, bf16[8,5,128]{2,0,1:T(8,128)(2,1)S(1)}, u32[]{:S(2)}, u32[]{:S(2)}) %collective-permute-start.8) | collective-permute-done | bytes 10272 | tf_op jit(solution)/shard_map/ppermute | solution.py:9
  25.5 0.0 copy-done.1
  25.6 0.6 %copy.12 = f32[8,4,128]{2,1,0:T(4,128)} copy(f32[8,4,128]{2,0,1:T(8,128)S(1)} %fusion.11) | data formatting | bytes 32768
  (17 shorter events, 0.1 us)
Async XLA Ops:
  0.6 4.0 %copy-start = (bf16[1,1,48,128,128]{4,3,2,1,0:T(8,128)(2,1)S(1)}, bf16[1,1,48,128,128]{4,3,2,1,0:T(8,128)(2,1)}, u32[]{:S(2)}) copy-start(bf16[1,1,48,128,128]{4,3,2,1,0:T(8,128)(2,1)} %param.7) | copy-start | bytes 4718596
  0.6 4.9 %copy-start.3 = (s32[1,1,48]{2,1,0:T(1,128)S(1)}, s32[1,1,48]{2,1,0:T(1,128)}, u32[]{:S(2)}) copy-start(s32[1,1,48]{2,1,0:T(1,128)} %param.8) | copy-start | bytes 580
  0.7 10.2 %copy-start.4 = (s32[1,1,48]{2,1,0:T(1,128)S(1)}, s32[1,1,48]{2,1,0:T(1,128)}, u32[]{:S(2)}) copy-start(s32[1,1,48]{2,1,0:T(1,128)} %param.9) | copy-start | bytes 580
  0.7 5.1 %copy-start.2 = (f32[1,1,4,128]{3,2,1,0:T(4,128)S(1)}, f32[1,1,4,128]{3,2,1,0:T(4,128)}, u32[]{:S(2)}) copy-start(f32[1,1,4,128]{3,2,1,0:T(4,128)} %param.11) | copy-start | bytes 6148
  1.5 2.5 %collective-permute-start = (bf16[8,4,128]{2,1,0:T(4,128)(2,1)S(1)}, bf16[8,4,128]{2,1,0:T(4,128)(2,1)S(1)}, u32[]{:S(2)}, u32[]{:S(2)}) collective-permute-start(bf16[8,4,128]{2,1,0:T(4,128)(2,1)S(1)} %convert_element_type.12), channel_id=1, source_target_pairs={{0,1},{1,0},{2,3},{3,2},{4,5},{5,4},{6,7},{7,6},{8,9},{9,8},{10,11... | collective-permute-start | bytes 24584 | tf_op jit(solution)/shard_map/ppermute | solution.py:9
  5.6 20.0 %copy-start.1 = (f32[8,4,128]{2,1,0:T(4,128)S(1)}, f32[8,4,128]{2,1,0:T(4,128)}, u32[]{:S(2)}) copy-start(f32[8,4,128]{2,1,0:T(4,128)} %param.6) | copy-start | bytes 49156
  5.9 10.5 %collective-permute-start.6 = (f32[8,5,128]{2,0,1:T(8,128)S(1)}, f32[8,5,128]{2,0,1:T(8,128)S(1)}, u32[]{:S(2)}, u32[]{:S(2)}) collective-permute-start(f32[8,5,128]{2,0,1:T(8,128)S(1)} %pad_maximum_fusion), channel_id=1, source_target_pairs={{0,12},{2,14},{4,8},{6,10},{8,4},{10,6},{12,0},{14,2},{1,13},{3,15... | collective-permute-start | bytes 61448 | tf_op jit(solution)/shard_map/ppermute | solution.py:9
  10.5 7.1 %collective-permute-start.5 = (f32[8,5,128]{2,0,1:T(8,128)S(1)}, f32[8,5,128]{2,0,1:T(8,128)S(1)}, u32[]{:S(2)}, u32[]{:S(2)}) collective-permute-start(f32[8,5,128]{2,0,1:T(8,128)S(1)} %pad_maximum_fusion), channel_id=1, source_target_pairs={{0,10},{2,8},{4,14},{6,12},{8,2},{10,0},{12,6},{14,4},{1,11},{3,9}... | collective-permute-start | bytes 61448 | tf_op jit(solution)/shard_map/ppermute | solution.py:9
  10.8 7.1 %collective-permute-start.4 = (f32[8,5,128]{2,0,1:T(8,128)S(1)}, f32[8,5,128]{2,0,1:T(8,128)S(1)}, u32[]{:S(2)}, u32[]{:S(2)}) collective-permute-start(f32[8,5,128]{2,0,1:T(8,128)S(1)} %pad_maximum_fusion), channel_id=1, source_target_pairs={{0,8},{2,10},{4,12},{6,14},{8,0},{10,2},{12,4},{14,6},{1,9},{3,11}... | collective-permute-start | bytes 61448 | tf_op jit(solution)/shard_map/ppermute | solution.py:9
  14.4 4.7 %collective-permute-start.3 = (f32[8,5,128]{2,0,1:T(8,128)S(1)}, f32[8,5,128]{2,0,1:T(8,128)S(1)}, u32[]{:S(2)}, u32[]{:S(2)}) collective-permute-start(f32[8,5,128]{2,0,1:T(8,128)S(1)} %pad_maximum_fusion), channel_id=1, source_target_pairs={{0,6},{2,4},{4,2},{6,0},{8,14},{10,12},{12,10},{14,8},{1,7},{3,5},... | collective-permute-start | bytes 61448 | tf_op jit(solution)/shard_map/ppermute | solution.py:9
  14.4 4.7 %collective-permute-start.2 = (f32[8,5,128]{2,0,1:T(8,128)S(1)}, f32[8,5,128]{2,0,1:T(8,128)S(1)}, u32[]{:S(2)}, u32[]{:S(2)}) collective-permute-start(f32[8,5,128]{2,0,1:T(8,128)S(1)} %pad_maximum_fusion), channel_id=1, source_target_pairs={{0,4},{2,6},{4,0},{6,2},{8,12},{10,14},{12,8},{14,10},{1,5},{3,7},... | collective-permute-start | bytes 61448 | tf_op jit(solution)/shard_map/ppermute | solution.py:9
  16.4 6.5 %collective-permute-start.7 = (f32[8,5,128]{2,0,1:T(8,128)S(1)}, f32[8,5,128]{2,0,1:T(8,128)S(1)}, u32[]{:S(2)}, u32[]{:S(2)}) collective-permute-start(f32[8,5,128]{2,0,1:T(8,128)S(1)} %pad_maximum_fusion), channel_id=1, source_target_pairs={{0,14},{2,12},{4,10},{6,8},{8,6},{10,4},{12,2},{14,0},{1,15},{3,13... | collective-permute-start | bytes 61448 | tf_op jit(solution)/shard_map/ppermute | solution.py:9
  17.6 5.3 %collective-permute-start.1 = (f32[8,5,128]{2,0,1:T(8,128)S(1)}, f32[8,5,128]{2,0,1:T(8,128)S(1)}, u32[]{:S(2)}, u32[]{:S(2)}) collective-permute-start(f32[8,5,128]{2,0,1:T(8,128)S(1)} %pad_maximum_fusion), channel_id=1, source_target_pairs={{0,2},{2,0},{4,6},{6,4},{8,10},{10,8},{12,14},{14,12},{1,3},{3,1},... | collective-permute-start | bytes 61448 | tf_op jit(solution)/shard_map/ppermute | solution.py:9
  24.3 1.2 %collective-permute-start.8 = (bf16[8,5,128]{2,0,1:T(8,128)(2,1)S(1)}, bf16[8,5,128]{2,0,1:T(8,128)(2,1)S(1)}, u32[]{:S(2)}, u32[]{:S(2)}) collective-permute-start(bf16[8,5,128]{2,0,1:T(8,128)(2,1)S(1)} %slice.62), channel_id=1, source_target_pairs={{0,1},{1,0},{2,3},{3,2},{4,5},{5,4},{6,7},{7,6},{8,9},{9,8},{10,11... | collective-permute-start | bytes 30728 | tf_op jit(solution)/shard_map/ppermute | solution.py:9

commit v2 on v1

--- a/solution.py
+++ b/solution.py
@@ -7,26 +7,6 @@
 def exchange(value, axis, mask):
     size = lax.axis_size(axis)
     return lax.ppermute(value, axis, [(i, i ^ mask) for i in range(size)])
-
-
-def radices_of(size, most):
-    out = []
-    while size > 1:
-        radix = min(size, most)
-        out.append(radix)
-        size //= radix
-    return out
-
-
-def all_sum(value, axis, most):
-    stride = 1
-    for radix in radices_of(lax.axis_size(axis), most):
-        terms = [value] + [exchange(value, axis, stride * k) for k in range(1, radix)]
-        while len(terms) > 1:
-            terms = [a + b for a, b in zip(terms[::2], terms[1::2])]
-        value = terms[0]
-        stride *= radix
-    return value
 
 
 def on_device(volume, tiles, tile_row, tile_col, tile_count, measured):
@@ -40,7 +20,6 @@
     slots = block.shape[0]
     highest = lax.Precision.HIGHEST
     ray = lax.axis_index("ray")
-    vox = lax.axis_index("vox")
     valid = jnp.arange(slots, dtype=jnp.int32) < used
     ones = jnp.ones((slots, 1, width), jnp.bfloat16)
 
@@ -53,11 +32,10 @@
     blocks = jnp.arange(lax.axis_size("vox"), dtype=jnp.int32)
     onehot = ((rows[:, None] == blocks[None, :]) & valid[:, None]).astype(jnp.float32)
     sums = jnp.einsum("nb,ncr->bcr", onehot, prod, precision=highest)
-    mine = (blocks == vox)[:, None, None]
-    part = jnp.concatenate([jnp.where(mine, measured[0], 0.0) - sums[:, :inst], sums[:, inst:]], axis=1)
-    total = all_sum(part, "vox", 8)
-    residual = (total[:, :inst] / (total[:, inst:] + 1.0)).astype(jnp.bfloat16)
-    own_res = lax.dynamic_slice_in_dim(residual, vox, 1, 0)
+    sums = jnp.sum(lax.all_to_all(sums, "vox", 0, 0, tiled=True), axis=0, keepdims=True)
+    own_res = ((measured[0] - sums[:, :inst]) / (sums[:, inst:] + 1.0)).astype(jnp.bfloat16)
+    copies = jnp.broadcast_to(own_res, (blocks.shape[0],) + own_res.shape[1:])
+    residual = lax.all_to_all(copies, "vox", 0, 0, tiled=True)
     gathered = jnp.concatenate([residual[rows], ones], axis=1)
     back = jnp.einsum("nrv,ncr->ncv", block, gathered, preferred_element_type=jnp.float32)
     blocks = jnp.arange(2 * half, dtype=jnp.int32)

time: 26.4 us -> 33.9 us (1.28)
  waiting for transfers between devices: 5.49 us -> 13.7 us
  starting transfers between devices: 12.6 us -> 10.7 us
  local copies, waits for them, and re-layouts: 2.49 us -> 3.13 us
  other arithmetic: 2.34 us -> 2.83 us
    all_to_all x0 -> x2, waiting for transfers between devices: none -> 13.1 us  [the longest x1 6.67 us: on_device(): lax.all_to_all(sums, 'vox', 0, 0, tiled=True)]
    ppermute x9 -> x2, starting transfers between devices: 12.6 us -> 0.52 us  [exchange(): return lax.ppermute(value, axis, [(i, i ^ mask) for i in range(size)])]
    all_to_all x0 -> x2, starting transfers between devices: none -> 10.1 us  [the longest x1 6.8 us: on_device(): lax.all_to_all(sums, 'vox', 0, 0, tiled=True)]
    ppermute x9 -> x2, waiting for transfers between devices: 5.49 us -> 0.59 us  [exchange(): return lax.ppermute(value, axis, [(i, i ^ mask) for i in range(size)])]
    dot_general x0 -> x1, local copies, waits for them, and re-layouts: none -> 0.62 us  [on_device(): sums = jnp.einsum('nb,ncr->bcr', onehot, prod, precision=highest)]
    broadcast_in_dim x0 -> x1, local copies, waits for them, and re-layouts: none -> 0.6 us  [on_device(): copies = jnp.broadcast_to(own_res, (blocks.shape[0],) + own_res.shape[1:])]
    broadcast_in_dim x0 -> x2, other arithmetic: none -> 0.58 us  [the longest x1 0.57 us: on_device(): return (new_volume, own_res[None])]
    unnamed x12 -> x11, local copies, waits for them, and re-layouts: 1.21 us -> 0.64 us
  transfers between devices with their start and end apart: 9 -> 4, of which waited for: 3 -> 3; matrix products, arithmetic and copies ran while one was open for 7% -> 6% of each run, Pallas kernels for 0% -> 0%
where the time goes in v2:
time: 33.9 us; the launch traced here: 33.5 us
  waiting for transfers between devices  13.7 us (40%)
  starting transfers between devices  10.7 us (32%)
  local copies, waits for them, and re-layouts  3.13 us (9%)
  other arithmetic  2.83 us (8%)
  matrix products  1.78 us (5%)
  between operations  1.43 us (4%)
    all_to_all x1, starting transfers between devices, on_device(): lax.all_to_all(sums, 'vox', 0, 0, tiled=True)  6.8 us
    all_to_all x1, waiting for transfers between devices, on_device(): lax.all_to_all(sums, 'vox', 0, 0, tiled=True)  6.67 us
    all_to_all x1, waiting for transfers between devices, on_device(): residual = lax.all_to_all(copies, 'vox', 0, 0, tiled=True)  6.44 us
    all_to_all x1, starting transfers between devices, on_device(): residual = lax.all_to_all(copies, 'vox', 0, 0, tiled=True)  3.33 us
    dot_general x1, matrix products, on_device(): jnp.einsum('nrv,ncv->ncr', block, picked, preferred_element_type=jnp.floa...  0.91 us
    convert_element_type x1, other arithmetic, on_device(): own = volume.astype(jnp.bfloat16)  0.83 us
  transfers between devices with their start and end apart: 4, of which 3 were waited for; matrix products, arithmetic and copies ran while one was open for 6% of the time, Pallas kernels for 0%

profile of v2, /device:TPU:0, one launch (start us, length us, event | category | flops | bytes accessed | tf_op | source)
XLA Modules:
  0.0 33.5 jit_solution(15086381380801937593)
XLA Ops:
  0.6 0.0 copy-start
  0.6 0.0 copy-start.3
  0.7 0.0 copy-start.4
  0.7 0.0 copy-start.2
  0.7 0.8 %convert_element_type.12 = bf16[8,4,128]{2,1,0:T(4,128)(2,1)S(1)} convert(f32[8,4,128]{2,1,0:T(4,128)} %param.6) | non-fusion elementwise | flops 4096 | bytes 24576 | tf_op jit(solution)/shard_map/convert_element_type | solution.py:26
  1.5 0.5 %collective-permute-start = (bf16[8,4,128]{2,1,0:T(4,128)(2,1)S(1)}, bf16[8,4,128]{2,1,0:T(4,128)(2,1)S(1)}, u32[]{:S(2)}, u32[]{:S(2)}) collective-permute-start(bf16[8,4,128]{2,1,0:T(4,128)(2,1)S(1)} %convert_element_type.12), channel_id=1, source_target_pairs={{0,1},{1,0},{2,3},{3,2},{4,5},{5,4},{6,7},{7,6},{8,9},{9,8},{10,11... | collective-permute-start | bytes 24584 | tf_op jit(solution)/shard_map/ppermute | solution.py:9
  2.6 0.7 %fusion.27 = s32[48]{0:T(128)S(1)} fusion(s32[1,1,48]{2,1,0:T(1,128)} %param.8), kind=kLoop, calls=%fused_computation.45 | loop fusion | flops 144 | bytes 384 | tf_op jit(solution)/shard_map/select_n | solution.py:39
  3.3 0.7 %fusion.28 = s32[48]{0:T(128)S(1)} fusion(s32[1,1,48]{2,1,0:T(1,128)} %param.9, pred[]{:T(512)S(6)} %eq.31), kind=kLoop, calls=%fused_computation.50 | loop fusion | flops 528 | bytes 385 | tf_op jit(solution)/shard_map/select_n | solution.py:30
  4.0 0.0 collective-permute-done
  4.0 0.6 %gather_fusion = bf16[48,4,128]{2,1,0:T(4,128)(2,1)S(1)} fusion(bf16[16,4,128]{2,1,0:T(4,128)(2,1)S(1)} %pad_maximum_fusion, s32[1024]{0:T(1024)S(1)} %pad_clamp_fusion.1), kind=kCustom, calls=%fused_computation | custom fusion | bytes 98496 | tf_op jit(solution)/shard_map/gather | solution.py:30
  4.6 0.0 copy-done
  4.6 0.9 %fusion.2 = f32[48,5,128]{2,1,0:T(8,128)S(1)} fusion(bf16[1,1,48,128,128]{4,3,2,1,0:T(8,128)(2,1)S(1)} %copy-done, bf16[48,4,128]{2,1,0:T(4,128)(2,1)S(1)} %gather_fusion), kind=kOutput, calls=%fused_computation.4 | convolution fusion | flops 7864320 | bytes 1744896 | tf_op jit(solution)/shard_map/nrv,ncv->ncr/dot_general | solution.py:31
  5.5 0.0 copy-start.1
  5.5 0.0 copy-done.3
  5.5 0.2 fusion.6
  5.7 0.6 %copy.10 = f32[8,5,128]{2,1,0:T(8,128)} copy(f32[8,5,128]{2,0,1:T(8,128)S(1)} %fusion.6) | data formatting | bytes 40960 | tf_op jit(solution)/shard_map/nb,ncr->bcr/dot_general | solution.py:34
  6.4 6.8 %all-to-all-start = ((f32[8,5,128]{2,1,0:T(8,128)}), f32[8,5,128]{2,1,0:T(8,128)S(1)}, u32[]{:S(2)}, u32[]{:S(2)}) async-start(f32[8,5,128]{2,1,0:T(8,128)} %copy.10), calls=%async_computation | async-start | bytes 65536 | tf_op jit(solution)/shard_map/all_to_all | solution.py:35
  13.2 0.0 copy-done.4
  13.2 6.7 %all-to-all-done = f32[8,5,128]{2,1,0:T(8,128)S(1)} async-done(((f32[8,5,128]{2,1,0:T(8,128)}), f32[8,5,128]{2,1,0:T(8,128)S(1)}, u32[]{:S(2)}, u32[]{:S(2)}) %all-to-all-start) | async-done | bytes 20512 | tf_op jit(solution)/shard_map/all_to_all | solution.py:35
  19.9 0.0 copy-done.2
  19.9 0.6 %broadcast_in_dim.10 = bf16[8,4,128]{2,1,0:T(4,128)(2,1)} broadcast(bf16[4,128]{1,0:T(4,128)(2,1)S(1)} %fusion.32), dimensions={1,2} | broadcast | bytes 9216 | tf_op jit(solution)/shard_map/broadcast_in_dim | solution.py:37
  20.5 3.3 %all-to-all-start.1 = ((bf16[8,4,128]{2,1,0:T(4,128)(2,1)}), bf16[8,4,128]{2,1,0:T(4,128)(2,1)S(1)}, u32[]{:S(2)}, u32[]{:S(2)}) async-start(bf16[8,4,128]{2,1,0:T(4,128)(2,1)} %broadcast_in_dim.10), calls=%async_computation.1 | async-start | bytes 16384 | tf_op jit(solution)/shard_map/all_to_all | solution.py:38
  23.9 6.4 %all-to-all-done.1 = bf16[8,4,128]{2,1,0:T(4,128)(2,1)S(1)} async-done(((bf16[8,4,128]{2,1,0:T(4,128)(2,1)}), bf16[8,4,128]{2,1,0:T(4,128)(2,1)S(1)}, u32[]{:S(2)}, u32[]{:S(2)}) %all-to-all-start.1) | async-done | bytes 8224 | tf_op jit(solution)/shard_map/all_to_all | solution.py:38
  30.3 0.6 %gather_fusion.1 = bf16[48,4,128]{2,1,0:T(4,128)(2,1)S(1)} fusion(bf16[8,4,128]{2,1,0:T(4,128)(2,1)S(1)} %all-to-all-done.1, s32[1024]{0:T(1024)S(1)} %pad_clamp_fusion), kind=kCustom, calls=%fused_computation.1 | custom fusion | bytes 98496 | tf_op jit(solution)/shard_map/gather | solution.py:39
  30.9 0.5 %fusion = f32[48,5,128]{2,1,0:T(8,128)S(1)} fusion(bf16[1,1,48,128,128]{4,3,2,1,0:T(8,128)(2,1)S(1)} %copy-done, bf16[48,4,128]{2,1,0:T(4,128)(2,1)S(1)} %gather_fusion.1), kind=kOutput, calls=%fused_computation.2 | convolution fusion | flops 7864320 | bytes 1744896 | tf_op jit(solution)/shard_map/nrv,ncr->ncv/dot_general | solution.py:40
  31.4 0.2 fusion.4
  31.6 0.1 collective-permute-start.1
  31.7 0.6 %fusion.31 = bf16[1,1,4,128]{3,2,1,0:T(4,128)(2,1)} fusion(f32[128]{0:T(128)S(1)} %add_bitcast_fusion, f32[1,5,128]{2,1,0:T(8,128)S(1)} %bitcast.53, f32[1,1,4,128]{3,2,1,0:T(4,128)S(1)} %copy-done.2), kind=kLoop, calls=%fused_computation.53 | loop fusion | flops 1536 | bytes 5632 | tf_op jit(solution)/shard_map/broadcast_in_dim | solution.py:47
  32.3 0.6 %collective-permute-done.1 = bf16[8,5,128]{2,0,1:T(8,128)(2,1)S(1)} collective-permute-done((bf16[8,5,128]{2,0,1:T(8,128)(2,1)S(1)}, bf16[8,5,128]{2,0,1:T(8,128)(2,1)S(1)}, u32[]{:S(2)}, u32[]{:S(2)}) %collective-permute-start.1) | collective-permute-done | bytes 10272 | tf_op jit(solution)/shard_map/ppermute | solution.py:9
  32.9 0.0 copy-done.1
  32.9 0.6 %copy.12 = f32[8,4,128]{2,1,0:T(4,128)} copy(f32[8,4,128]{2,0,1:T(8,128)S(1)} %fusion.11) | data formatting | bytes 32768
  (12 shorter events, 0.1 us)
Async XLA Ops:
  0.6 4.0 %copy-start = (bf16[1,1,48,128,128]{4,3,2,1,0:T(8,128)(2,1)S(1)}, bf16[1,1,48,128,128]{4,3,2,1,0:T(8,128)(2,1)}, u32[]{:S(2)}) copy-start(bf16[1,1,48,128,128]{4,3,2,1,0:T(8,128)(2,1)} %param.7) | copy-start | bytes 4718596
  0.6 4.9 %copy-start.3 = (s32[1,1,48]{2,1,0:T(1,128)S(1)}, s32[1,1,48]{2,1,0:T(1,128)}, u32[]{:S(2)}) copy-start(s32[1,1,48]{2,1,0:T(1,128)} %param.8) | copy-start | bytes 580
  0.7 12.5 %copy-start.4 = (s32[1,1,48]{2,1,0:T(1,128)S(1)}, s32[1,1,48]{2,1,0:T(1,128)}, u32[]{:S(2)}) copy-start(s32[1,1,48]{2,1,0:T(1,128)} %param.9) | copy-start | bytes 580
  0.7 19.2 %copy-start.2 = (f32[1,1,4,128]{3,2,1,0:T(4,128)S(1)}, f32[1,1,4,128]{3,2,1,0:T(4,128)}, u32[]{:S(2)}) copy-start(f32[1,1,4,128]{3,2,1,0:T(4,128)} %param.11) | copy-start | bytes 6148
  1.5 2.5 %collective-permute-start = (bf16[8,4,128]{2,1,0:T(4,128)(2,1)S(1)}, bf16[8,4,128]{2,1,0:T(4,128)(2,1)S(1)}, u32[]{:S(2)}, u32[]{:S(2)}) collective-permute-start(bf16[8,4,128]{2,1,0:T(4,128)(2,1)S(1)} %convert_element_type.12), channel_id=1, source_target_pairs={{0,1},{1,0},{2,3},{3,2},{4,5},{5,4},{6,7},{7,6},{8,9},{9,8},{10,11... | collective-permute-start | bytes 24584 | tf_op jit(solution)/shard_map/ppermute | solution.py:9
  5.5 27.3 %copy-start.1 = (f32[8,4,128]{2,1,0:T(4,128)S(1)}, f32[8,4,128]{2,1,0:T(4,128)}, u32[]{:S(2)}) copy-start(f32[8,4,128]{2,1,0:T(4,128)} %param.6) | copy-start | bytes 49156
  6.4 13.5 %all-to-all-start = ((f32[8,5,128]{2,1,0:T(8,128)}), f32[8,5,128]{2,1,0:T(8,128)S(1)}, u32[]{:S(2)}, u32[]{:S(2)}) async-start(f32[8,5,128]{2,1,0:T(8,128)} %copy.10), calls=%async_computation | async-start | bytes 65536 | tf_op jit(solution)/shard_map/all_to_all | solution.py:35
  20.5 9.8 %all-to-all-start.1 = ((bf16[8,4,128]{2,1,0:T(4,128)(2,1)}), bf16[8,4,128]{2,1,0:T(4,128)(2,1)S(1)}, u32[]{:S(2)}, u32[]{:S(2)}) async-start(bf16[8,4,128]{2,1,0:T(4,128)(2,1)} %broadcast_in_dim.10), calls=%async_computation.1 | async-start | bytes 16384 | tf_op jit(solution)/shard_map/all_to_all | solution.py:38
  31.6 1.2 %collective-permute-start.1 = (bf16[8,5,128]{2,0,1:T(8,128)(2,1)S(1)}, bf16[8,5,128]{2,0,1:T(8,128)(2,1)S(1)}, u32[]{:S(2)}, u32[]{:S(2)}) collective-permute-start(bf16[8,5,128]{2,0,1:T(8,128)(2,1)S(1)} %slice.47), channel_id=1, source_target_pairs={{0,1},{1,0},{2,3},{3,2},{4,5},{5,4},{6,7},{7,6},{8,9},{9,8},{10,11... | collective-permute-start | bytes 30728 | tf_op jit(solution)/shard_map/ppermute | solution.py:9

commit v3 on v1

--- a/solution.py
+++ b/solution.py
@@ -55,7 +55,7 @@
     sums = jnp.einsum("nb,ncr->bcr", onehot, prod, precision=highest)
     mine = (blocks == vox)[:, None, None]
     part = jnp.concatenate([jnp.where(mine, measured[0], 0.0) - sums[:, :inst], sums[:, inst:]], axis=1)
-    total = all_sum(part, "vox", 8)
+    total = all_sum(part, "vox", 2)
     residual = (total[:, :inst] / (total[:, inst:] + 1.0)).astype(jnp.bfloat16)
     own_res = lax.dynamic_slice_in_dim(residual, vox, 1, 0)
     gathered = jnp.concatenate([residual[rows], ones], axis=1)

time: 26.4 us -> 21.7 us (0.82)
  starting transfers between devices: 12.6 us -> 8.13 us
  other arithmetic: 2.34 us -> 1.69 us
  waiting for transfers between devices: 5.49 us -> 5.87 us
    ppermute x9 -> x5, starting transfers between devices: 12.6 us -> 8.13 us  [exchange(): return lax.ppermute(value, axis, [(i, i ^ mask) for i in range(size)])]
    select_n x1, other arithmetic: 0.66 us -> 0.01 us  [on_device(): gathered = jnp.concatenate([residual[rows], ones], axis=1)]
    ppermute x9 -> x5, waiting for transfers between devices: 5.49 us -> 5.87 us  [exchange(): return lax.ppermute(value, axis, [(i, i ^ mask) for i in range(size)])]
  transfers between devices with their start and end apart: 9 -> 5, of which waited for: 3 -> 4; matrix products, arithmetic and copies ran while one was open for 7% -> 6% of each run, Pallas kernels for 0% -> 0%
where the time goes in v3:
time: 21.7 us; the launch traced here: 21.4 us
  starting transfers between devices  8.13 us (37%)
  waiting for transfers between devices  5.87 us (27%)
  local copies, waits for them, and re-layouts  2.5 us (12%)
  matrix products  1.78 us (8%)
  other arithmetic  1.69 us (8%)
  between operations  1.43 us (7%)
    ppermute x5, starting transfers between devices, exchange(): return lax.ppermute(value, axis, [(i, i ^ mask) for i in range(size)])  8.13 us
    ppermute x5, waiting for transfers between devices, exchange(): return lax.ppermute(value, axis, [(i, i ^ mask) for i in range(size)])  5.87 us
    unnamed x12, local copies, waits for them, and re-layouts  1.2 us
    dot_general x1, matrix products, on_device(): jnp.einsum('nrv,ncv->ncr', block, picked, preferred_element_type=jnp.floa...  0.91 us
    convert_element_type x1, other arithmetic, on_device(): own = volume.astype(jnp.bfloat16)  0.84 us
    select_n x1, other arithmetic, on_device(): picked = jnp.concatenate([panel[place], ones], axis=1)  0.67 us
    gather x1, local copies, waits for them, and re-layouts, on_device(): gathered = jnp.concatenate([residual[rows], ones], axis=1)  0.63 us
    gather x1, local copies, waits for them, and re-layouts, on_device(): picked = jnp.concatenate([panel[place], ones], axis=1)  0.63 us
  transfers between devices with their start and end apart: 5, of which 4 were waited for; matrix products, arithmetic and copies ran while one was open for 6% of the time, Pallas kernels for 0%

profile of v3, /device:TPU:0, one launch (start us, length us, event | category | flops | bytes accessed | tf_op | source)
XLA Modules:
  0.0 21.4 jit_solution(4154786493666330342)
XLA Ops:
  0.6 0.0 copy-start
  0.6 0.0 copy-start.4
  0.7 0.0 copy-start.3
  0.7 0.0 copy-start.2
  0.7 0.8 %convert_element_type.12 = bf16[8,4,128]{2,1,0:T(4,128)(2,1)S(1)} convert(f32[8,4,128]{2,1,0:T(4,128)} %param.6) | non-fusion elementwise | flops 4096 | bytes 24576 | tf_op jit(solution)/shard_map/convert_element_type | solution.py:47
  1.5 0.5 %collective-permute-start = (bf16[8,4,128]{2,1,0:T(4,128)(2,1)S(1)}, bf16[8,4,128]{2,1,0:T(4,128)(2,1)S(1)}, u32[]{:S(2)}, u32[]{:S(2)}) collective-permute-start(bf16[8,4,128]{2,1,0:T(4,128)(2,1)S(1)} %convert_element_type.12), channel_id=1, source_target_pairs={{0,1},{1,0},{2,3},{3,2},{4,5},{5,4},{6,7},{7,6},{8,9},{9,8},{10,11... | collective-permute-start | bytes 24584 | tf_op jit(solution)/shard_map/ppermute | solution.py:9
  2.6 0.7 %fusion.28 = s32[48]{0:T(128)S(1)} fusion(s32[1,1,48]{2,1,0:T(1,128)} %param.9, pred[]{:T(512)S(6)} %eq.41), kind=kLoop, calls=%fused_computation.54 | loop fusion | flops 528 | bytes 385 | tf_op jit(solution)/shard_map/select_n | solution.py:51
  3.3 0.0 collective-permute-done
  3.4 0.6 %gather_fusion = bf16[48,4,128]{2,1,0:T(4,128)(2,1)S(1)} fusion(bf16[16,4,128]{2,1,0:T(4,128)(2,1)S(1)} %pad_maximum_fusion.1, s32[1024]{0:T(1024)S(1)} %pad_clamp_fusion.1), kind=kCustom, calls=%fused_computation | custom fusion | bytes 98496 | tf_op jit(solution)/shard_map/gather | solution.py:51
  4.0 0.0 copy-done
  4.0 0.9 %fusion.2 = f32[48,5,128]{2,1,0:T(8,128)S(1)} fusion(bf16[1,1,48,128,128]{4,3,2,1,0:T(8,128)(2,1)S(1)} %copy-done, bf16[48,4,128]{2,1,0:T(4,128)(2,1)S(1)} %gather_fusion), kind=kOutput, calls=%fused_computation.4 | convolution fusion | flops 7864320 | bytes 1744896 | tf_op jit(solution)/shard_map/nrv,ncv->ncr/dot_general | solution.py:52
  4.9 0.0 copy-start.1
  4.9 0.0 copy-done.3
  4.9 0.2 fusion.6
  5.1 0.0 copy-done.2
  5.1 0.1 slice_subtract_fusion
  5.2 2.5 %collective-permute-start.1 = (f32[8,5,128]{2,0,1:T(8,128)S(1)}, f32[8,5,128]{2,0,1:T(8,128)S(1)}, u32[]{:S(2)}, u32[]{:S(2)}) collective-permute-start(f32[8,5,128]{2,0,1:T(8,128)S(1)} %pad_maximum_fusion), channel_id=1, source_target_pairs={{0,2},{2,0},{4,6},{6,4},{8,10},{10,8},{12,14},{14,12},{1,3},{3,1},... | collective-permute-start | bytes 61448 | tf_op jit(solution)/shard_map/ppermute | solution.py:9
  7.7 1.8 %collective-permute-done.1 = f32[8,5,128]{2,0,1:T(8,128)S(1)} collective-permute-done((f32[8,5,128]{2,0,1:T(8,128)S(1)}, f32[8,5,128]{2,0,1:T(8,128)S(1)}, u32[]{:S(2)}, u32[]{:S(2)}) %collective-permute-start.1) | collective-permute-done | bytes 20512 | tf_op jit(solution)/shard_map/ppermute | solution.py:9
  9.5 2.1 %collective-permute-start.2 = (f32[8,5,128]{2,0,1:T(8,128)S(1)}, f32[8,5,128]{2,0,1:T(8,128)S(1)}, u32[]{:S(2)}, u32[]{:S(2)}) collective-permute-start(f32[8,5,128]{2,0,1:T(8,128)S(1)} %fusion.31), channel_id=1, source_target_pairs={{0,4},{2,6},{4,0},{6,2},{8,12},{10,14},{12,8},{14,10},{1,5},{3,7},... | collective-permute-start | bytes 61448 | tf_op jit(solution)/shard_map/ppermute | solution.py:9
  11.6 0.0 copy-done.4
  11.6 1.7 %collective-permute-done.2 = f32[8,5,128]{2,0,1:T(8,128)S(1)} collective-permute-done((f32[8,5,128]{2,0,1:T(8,128)S(1)}, f32[8,5,128]{2,0,1:T(8,128)S(1)}, u32[]{:S(2)}, u32[]{:S(2)}) %collective-permute-start.2) | collective-permute-done | bytes 20512 | tf_op jit(solution)/shard_map/ppermute | solution.py:9
  13.3 3.0 %collective-permute-start.3 = (f32[8,5,128]{2,0,1:T(8,128)S(1)}, f32[8,5,128]{2,0,1:T(8,128)S(1)}, u32[]{:S(2)}, u32[]{:S(2)}) collective-permute-start(f32[8,5,128]{2,0,1:T(8,128)S(1)} %add.67), channel_id=1, source_target_pairs={{0,8},{2,10},{4,12},{6,14},{8,0},{10,2},{12,4},{14,6},{1,9},{3,11}... | collective-permute-start | bytes 61448 | tf_op jit(solution)/shard_map/ppermute | solution.py:9
  16.4 1.8 %collective-permute-done.3 = f32[8,5,128]{2,0,1:T(8,128)S(1)} collective-permute-done((f32[8,5,128]{2,0,1:T(8,128)S(1)}, f32[8,5,128]{2,0,1:T(8,128)S(1)}, u32[]{:S(2)}, u32[]{:S(2)}) %collective-permute-start.3) | collective-permute-done | bytes 20512 | tf_op jit(solution)/shard_map/ppermute | solution.py:9
  18.2 0.6 %gather_fusion.1 = bf16[48,4,128]{2,1,0:T(4,128)(2,1)S(1)} fusion(bf16[8,4,128]{2,1,0:T(4,128)(2,1)S(1)} %copy.10, s32[1024]{0:T(1024)S(1)} %pad_clamp_fusion), kind=kCustom, calls=%fused_computation.1 | custom fusion | bytes 98496 | tf_op jit(solution)/shard_map/gather | solution.py:61
  18.8 0.5 %fusion = f32[48,5,128]{2,1,0:T(8,128)S(1)} fusion(bf16[1,1,48,128,128]{4,3,2,1,0:T(8,128)(2,1)S(1)} %copy-done, bf16[48,4,128]{2,1,0:T(4,128)(2,1)S(1)} %gather_fusion.1), kind=kOutput, calls=%fused_computation.2 | convolution fusion | flops 7864320 | bytes 1744896 | tf_op jit(solution)/shard_map/nrv,ncr->ncv/dot_general | solution.py:62
  19.3 0.2 fusion.4
  19.5 0.1 collective-permute-start.4
  19.6 0.6 %copy.22 = bf16[1,4,128]{2,1,0:T(4,128)(2,1)} copy(bf16[1,4,128]{2,0,1:T(2,128)(2,1)S(1)} %constant_dynamic-slice_fusion) | data formatting | bytes 2048
  20.2 0.6 %collective-permute-done.4 = bf16[8,5,128]{2,0,1:T(8,128)(2,1)S(1)} collective-permute-done((bf16[8,5,128]{2,0,1:T(8,128)(2,1)S(1)}, bf16[8,5,128]{2,0,1:T(8,128)(2,1)S(1)}, u32[]{:S(2)}, u32[]{:S(2)}) %collective-permute-start.4) | collective-permute-done | bytes 10272 | tf_op jit(solution)/shard_map/ppermute | solution.py:9
  20.8 0.0 copy-done.1
  20.8 0.6 %copy.12 = f32[8,4,128]{2,1,0:T(4,128)} copy(f32[8,4,128]{2,0,1:T(8,128)S(1)} %fusion.11) | data formatting | bytes 32768
  (20 shorter events, 0.1 us)
Async XLA Ops:
  0.6 3.4 %copy-start = (bf16[1,1,48,128,128]{4,3,2,1,0:T(8,128)(2,1)S(1)}, bf16[1,1,48,128,128]{4,3,2,1,0:T(8,128)(2,1)}, u32[]{:S(2)}) copy-start(bf16[1,1,48,128,128]{4,3,2,1,0:T(8,128)(2,1)} %param.7) | copy-start | bytes 4718596
  0.6 10.9 %copy-start.4 = (s32[1,1,48]{2,1,0:T(1,128)S(1)}, s32[1,1,48]{2,1,0:T(1,128)}, u32[]{:S(2)}) copy-start(s32[1,1,48]{2,1,0:T(1,128)} %param.9) | copy-start | bytes 580
  0.7 4.3 %copy-start.3 = (s32[1,1,48]{2,1,0:T(1,128)S(1)}, s32[1,1,48]{2,1,0:T(1,128)}, u32[]{:S(2)}) copy-start(s32[1,1,48]{2,1,0:T(1,128)} %param.8) | copy-start | bytes 580
  0.7 4.4 %copy-start.2 = (f32[1,1,4,128]{3,2,1,0:T(4,128)S(1)}, f32[1,1,4,128]{3,2,1,0:T(4,128)}, u32[]{:S(2)}) copy-start(f32[1,1,4,128]{3,2,1,0:T(4,128)} %param.11) | copy-start | bytes 6148
  1.5 1.8 %collective-permute-start = (bf16[8,4,128]{2,1,0:T(4,128)(2,1)S(1)}, bf16[8,4,128]{2,1,0:T(4,128)(2,1)S(1)}, u32[]{:S(2)}, u32[]{:S(2)}) collective-permute-start(bf16[8,4,128]{2,1,0:T(4,128)(2,1)S(1)} %convert_element_type.12), channel_id=1, source_target_pairs={{0,1},{1,0},{2,3},{3,2},{4,5},{5,4},{6,7},{7,6},{8,9},{9,8},{10,11... | collective-permute-start | bytes 24584 | tf_op jit(solution)/shard_map/ppermute | solution.py:9
  4.9 15.9 %copy-start.1 = (f32[8,4,128]{2,1,0:T(4,128)S(1)}, f32[8,4,128]{2,1,0:T(4,128)}, u32[]{:S(2)}) copy-start(f32[8,4,128]{2,1,0:T(4,128)} %param.6) | copy-start | bytes 49156
  5.2 4.3 %collective-permute-start.1 = (f32[8,5,128]{2,0,1:T(8,128)S(1)}, f32[8,5,128]{2,0,1:T(8,128)S(1)}, u32[]{:S(2)}, u32[]{:S(2)}) collective-permute-start(f32[8,5,128]{2,0,1:T(8,128)S(1)} %pad_maximum_fusion), channel_id=1, source_target_pairs={{0,2},{2,0},{4,6},{6,4},{8,10},{10,8},{12,14},{14,12},{1,3},{3,1},... | collective-permute-start | bytes 61448 | tf_op jit(solution)/shard_map/ppermute | solution.py:9
  9.5 3.8 %collective-permute-start.2 = (f32[8,5,128]{2,0,1:T(8,128)S(1)}, f32[8,5,128]{2,0,1:T(8,128)S(1)}, u32[]{:S(2)}, u32[]{:S(2)}) collective-permute-start(f32[8,5,128]{2,0,1:T(8,128)S(1)} %fusion.31), channel_id=1, source_target_pairs={{0,4},{2,6},{4,0},{6,2},{8,12},{10,14},{12,8},{14,10},{1,5},{3,7},... | collective-permute-start | bytes 61448 | tf_op jit(solution)/shard_map/ppermute | solution.py:9
  13.3 4.8 %collective-permute-start.3 = (f32[8,5,128]{2,0,1:T(8,128)S(1)}, f32[8,5,128]{2,0,1:T(8,128)S(1)}, u32[]{:S(2)}, u32[]{:S(2)}) collective-permute-start(f32[8,5,128]{2,0,1:T(8,128)S(1)} %add.67), channel_id=1, source_target_pairs={{0,8},{2,10},{4,12},{6,14},{8,0},{10,2},{12,4},{14,6},{1,9},{3,11}... | collective-permute-start | bytes 61448 | tf_op jit(solution)/shard_map/ppermute | solution.py:9
  19.5 1.2 %collective-permute-start.4 = (bf16[8,5,128]{2,0,1:T(8,128)(2,1)S(1)}, bf16[8,5,128]{2,0,1:T(8,128)(2,1)S(1)}, u32[]{:S(2)}, u32[]{:S(2)}) collective-permute-start(bf16[8,5,128]{2,0,1:T(8,128)(2,1)S(1)} %slice.62), channel_id=1, source_target_pairs={{0,1},{1,0},{2,3},{3,2},{4,5},{5,4},{6,7},{7,6},{8,9},{9,8},{10,11... | collective-permute-start | bytes 30728 | tf_op jit(solution)/shard_map/ppermute | solution.py:9

commit v4 on v3

--- a/solution.py
+++ b/solution.py
@@ -9,18 +9,18 @@
     return lax.ppermute(value, axis, [(i, i ^ mask) for i in range(size)])
 
 
-def radices_of(size, most):
+def radices_of(size, first):
     out = []
     while size > 1:
-        radix = min(size, most)
+        radix = min(size, 4 if out else first)
         out.append(radix)
         size //= radix
     return out
 
 
-def all_sum(value, axis, most):
+def all_sum(value, axis, first):
     stride = 1
-    for radix in radices_of(lax.axis_size(axis), most):
+    for radix in radices_of(lax.axis_size(axis), first):
         terms = [value] + [exchange(value, axis, stride * k) for k in range(1, radix)]
         while len(terms) > 1:
             terms = [a + b for a, b in zip(terms[::2], terms[1::2])]

time: 21.7 us -> 22.5 us (1.037)
  other arithmetic: 1.69 us -> 2.34 us
  waiting for transfers between devices: 5.87 us -> 6.41 us
  starting transfers between devices: 8.13 us -> 7.75 us
    select_n x1, other arithmetic: 0.01 us -> 0.66 us  [on_device(): gathered = jnp.concatenate([residual[rows], ones], axis=1)]
    ppermute x5 -> x6, waiting for transfers between devices: 5.87 us -> 6.41 us  [exchange(): return lax.ppermute(value, axis, [(i, i ^ mask) for i in range(size)])]
    ppermute x5 -> x6, starting transfers between devices: 8.13 us -> 7.75 us  [exchange(): return lax.ppermute(value, axis, [(i, i ^ mask) for i in range(size)])]
  transfers between devices with their start and end apart: 5 -> 6, of which waited for: 4 -> 4; matrix products, arithmetic and copies ran while one was open for 6% -> 9% of each run, Pallas kernels for 0% -> 0%
where the time goes in v4:
time: 22.5 us; the launch traced here: 22.2 us
  starting transfers between devices  7.75 us (34%)
  waiting for transfers between devices  6.41 us (28%)
  local copies, waits for them, and re-layouts  2.49 us (11%)
  other arithmetic  2.34 us (10%)
  matrix products  1.78 us (8%)
  between operations  1.44 us (6%)
    ppermute x6, starting transfers between devices, exchange(): return lax.ppermute(value, axis, [(i, i ^ mask) for i in range(size)])  7.75 us
    ppermute x6, waiting for transfers between devices, exchange(): return lax.ppermute(value, axis, [(i, i ^ mask) for i in range(size)])  6.41 us
    unnamed x12, local copies, waits for them, and re-layouts  1.21 us
    dot_general x1, matrix products, on_device(): jnp.einsum('nrv,ncv->ncr', block, picked, preferred_element_type=jnp.floa...  0.91 us
    convert_element_type x1, other arithmetic, on_device(): own = volume.astype(jnp.bfloat16)  0.84 us
    select_n x1, other arithmetic, on_device(): picked = jnp.concatenate([panel[place], ones], axis=1)  0.66 us
    select_n x1, other arithmetic, on_device(): gathered = jnp.concatenate([residual[rows], ones], axis=1)  0.66 us
    gather x1, local copies, waits for them, and re-layouts, on_device(): picked = jnp.concatenate([panel[place], ones], axis=1)  0.63 us
  transfers between devices with their start and end apart: 6, of which 4 were waited for; matrix products, arithmetic and copies ran while one was open for 9% of the time, Pallas kernels for 0%

profile of v4, /device:TPU:0, one launch (start us, length us, event | category | flops | bytes accessed | tf_op | source)
XLA Modules:
  0.0 22.2 jit_solution(7739212357841189047)
XLA Ops:
  0.6 0.0 copy-start
  0.6 0.0 copy-start.3
  0.7 0.0 copy-start.4
  0.7 0.0 copy-start.2
  0.7 0.8 %convert_element_type.12 = bf16[8,4,128]{2,1,0:T(4,128)(2,1)S(1)} convert(f32[8,4,128]{2,1,0:T(4,128)} %param.6) | non-fusion elementwise | flops 4096 | bytes 24576 | tf_op jit(solution)/shard_map/convert_element_type | solution.py:47
  1.5 0.5 %collective-permute-start = (bf16[8,4,128]{2,1,0:T(4,128)(2,1)S(1)}, bf16[8,4,128]{2,1,0:T(4,128)(2,1)S(1)}, u32[]{:S(2)}, u32[]{:S(2)}) collective-permute-start(bf16[8,4,128]{2,1,0:T(4,128)(2,1)S(1)} %convert_element_type.12), channel_id=1, source_target_pairs={{0,1},{1,0},{2,3},{3,2},{4,5},{5,4},{6,7},{7,6},{8,9},{9,8},{10,11... | collective-permute-start | bytes 24584 | tf_op jit(solution)/shard_map/ppermute | solution.py:9
  2.6 0.7 %fusion.27 = s32[48]{0:T(128)S(1)} fusion(s32[1,1,48]{2,1,0:T(1,128)} %param.8), kind=kLoop, calls=%fused_computation.50 | loop fusion | flops 144 | bytes 384 | tf_op jit(solution)/shard_map/select_n | solution.py:61
  3.3 0.7 %fusion.28 = s32[48]{0:T(128)S(1)} fusion(s32[1,1,48]{2,1,0:T(1,128)} %param.9, pred[]{:T(512)S(6)} %eq.41), kind=kLoop, calls=%fused_computation.55 | loop fusion | flops 528 | bytes 385 | tf_op jit(solution)/shard_map/select_n | solution.py:51
  4.0 0.0 collective-permute-done
  4.0 0.6 %gather_fusion = bf16[48,4,128]{2,1,0:T(4,128)(2,1)S(1)} fusion(bf16[16,4,128]{2,1,0:T(4,128)(2,1)S(1)} %pad_maximum_fusion.1, s32[1024]{0:T(1024)S(1)} %pad_clamp_fusion.1), kind=kCustom, calls=%fused_computation | custom fusion | bytes 98496 | tf_op jit(solution)/shard_map/gather | solution.py:51
  4.7 0.0 copy-done
  4.7 0.9 %fusion.2 = f32[48,5,128]{2,1,0:T(8,128)S(1)} fusion(bf16[1,1,48,128,128]{4,3,2,1,0:T(8,128)(2,1)S(1)} %copy-done, bf16[48,4,128]{2,1,0:T(4,128)(2,1)S(1)} %gather_fusion), kind=kOutput, calls=%fused_computation.4 | convolution fusion | flops 7864320 | bytes 1744896 | tf_op jit(solution)/shard_map/nrv,ncv->ncr/dot_general | solution.py:52
  5.6 0.0 copy-start.1
  5.6 0.0 copy-done.3
  5.6 0.2 fusion.6
  5.8 0.0 copy-done.2
  5.8 0.1 slice_subtract_fusion
  5.9 2.5 %collective-permute-start.1 = (f32[8,5,128]{2,0,1:T(8,128)S(1)}, f32[8,5,128]{2,0,1:T(8,128)S(1)}, u32[]{:S(2)}, u32[]{:S(2)}) collective-permute-start(f32[8,5,128]{2,0,1:T(8,128)S(1)} %pad_maximum_fusion), channel_id=1, source_target_pairs={{0,2},{2,0},{4,6},{6,4},{8,10},{10,8},{12,14},{14,12},{1,3},{3,1},... | collective-permute-start | bytes 61448 | tf_op jit(solution)/shard_map/ppermute | solution.py:9
  8.4 0.0 copy-done.4
  8.4 1.8 %collective-permute-done.1 = f32[8,5,128]{2,0,1:T(8,128)S(1)} collective-permute-done((f32[8,5,128]{2,0,1:T(8,128)S(1)}, f32[8,5,128]{2,0,1:T(8,128)S(1)}, u32[]{:S(2)}, u32[]{:S(2)}) %collective-permute-start.1) | collective-permute-done | bytes 20512 | tf_op jit(solution)/shard_map/ppermute | solution.py:9
  10.2 4.1 %collective-permute-start.4 = (f32[8,5,128]{2,0,1:T(8,128)S(1)}, f32[8,5,128]{2,0,1:T(8,128)S(1)}, u32[]{:S(2)}, u32[]{:S(2)}) collective-permute-start(f32[8,5,128]{2,0,1:T(8,128)S(1)} %fusion.31), channel_id=1, source_target_pairs={{0,12},{2,14},{4,8},{6,10},{8,4},{10,6},{12,0},{14,2},{1,13},{3,15... | collective-permute-start | bytes 61448 | tf_op jit(solution)/shard_map/ppermute | solution.py:9
  14.3 0.0 collective-permute-start.3
  14.3 0.6 %collective-permute-start.2 = (f32[8,5,128]{2,0,1:T(8,128)S(1)}, f32[8,5,128]{2,0,1:T(8,128)S(1)}, u32[]{:S(2)}, u32[]{:S(2)}) collective-permute-start(f32[8,5,128]{2,0,1:T(8,128)S(1)} %fusion.31), channel_id=1, source_target_pairs={{0,4},{2,6},{4,0},{6,2},{8,12},{10,14},{12,8},{14,10},{1,5},{3,7},... | collective-permute-start | bytes 61448 | tf_op jit(solution)/shard_map/ppermute | solution.py:9
  14.9 1.3 %collective-permute-done.4 = f32[8,5,128]{2,0,1:T(8,128)S(1)} collective-permute-done((f32[8,5,128]{2,0,1:T(8,128)S(1)}, f32[8,5,128]{2,0,1:T(8,128)S(1)}, u32[]{:S(2)}, u32[]{:S(2)}) %collective-permute-start.4) | collective-permute-done | bytes 20512 | tf_op jit(solution)/shard_map/ppermute | solution.py:9
  16.2 2.7 %collective-permute-done.3 = f32[8,5,128]{2,0,1:T(8,128)S(1)} collective-permute-done((f32[8,5,128]{2,0,1:T(8,128)S(1)}, f32[8,5,128]{2,0,1:T(8,128)S(1)}, u32[]{:S(2)}, u32[]{:S(2)}) %collective-permute-start.3) | collective-permute-done | bytes 20512 | tf_op jit(solution)/shard_map/ppermute | solution.py:9
  18.9 0.0 collective-permute-done.2
  19.0 0.6 %gather_fusion.1 = bf16[48,4,128]{2,1,0:T(4,128)(2,1)S(1)} fusion(bf16[8,4,128]{2,1,0:T(4,128)(2,1)S(1)} %copy.10, s32[1024]{0:T(1024)S(1)} %pad_clamp_fusion), kind=kCustom, calls=%fused_computation.1 | custom fusion | bytes 98496 | tf_op jit(solution)/shard_map/gather | solution.py:61
  19.6 0.5 %fusion = f32[48,5,128]{2,1,0:T(8,128)S(1)} fusion(bf16[1,1,48,128,128]{4,3,2,1,0:T(8,128)(2,1)S(1)} %copy-done, bf16[48,4,128]{2,1,0:T(4,128)(2,1)S(1)} %gather_fusion.1), kind=kOutput, calls=%fused_computation.2 | convolution fusion | flops 7864320 | bytes 1744896 | tf_op jit(solution)/shard_map/nrv,ncr->ncv/dot_general | solution.py:62
  20.1 0.2 fusion.4
  20.3 0.1 collective-permute-start.5
  20.4 0.6 %copy.22 = bf16[1,4,128]{2,1,0:T(4,128)(2,1)} copy(bf16[1,4,128]{2,0,1:T(2,128)(2,1)S(1)} %constant_dynamic-slice_fusion) | data formatting | bytes 2048
  21.0 0.6 %collective-permute-done.5 = bf16[8,5,128]{2,0,1:T(8,128)(2,1)S(1)} collective-permute-done((bf16[8,5,128]{2,0,1:T(8,128)(2,1)S(1)}, bf16[8,5,128]{2,0,1:T(8,128)(2,1)S(1)}, u32[]{:S(2)}, u32[]{:S(2)}) %collective-permute-start.5) | collective-permute-done | bytes 10272 | tf_op jit(solution)/shard_map/ppermute | solution.py:9
  21.6 0.0 copy-done.1
  21.6 0.6 %copy.12 = f32[8,4,128]{2,1,0:T(4,128)} copy(f32[8,4,128]{2,0,1:T(8,128)S(1)} %fusion.11) | data formatting | bytes 32768
  (18 shorter events, 0.1 us)
Async XLA Ops:
  0.6 4.0 %copy-start = (bf16[1,1,48,128,128]{4,3,2,1,0:T(8,128)(2,1)S(1)}, bf16[1,1,48,128,128]{4,3,2,1,0:T(8,128)(2,1)}, u32[]{:S(2)}) copy-start(bf16[1,1,48,128,128]{4,3,2,1,0:T(8,128)(2,1)} %param.7) | copy-start | bytes 4718596
  0.6 4.9 %copy-start.3 = (s32[1,1,48]{2,1,0:T(1,128)S(1)}, s32[1,1,48]{2,1,0:T(1,128)}, u32[]{:S(2)}) copy-start(s32[1,1,48]{2,1,0:T(1,128)} %param.8) | copy-start | bytes 580
  0.7 7.7 %copy-start.4 = (s32[1,1,48]{2,1,0:T(1,128)S(1)}, s32[1,1,48]{2,1,0:T(1,128)}, u32[]{:S(2)}) copy-start(s32[1,1,48]{2,1,0:T(1,128)} %param.9) | copy-start | bytes 580
  0.7 5.1 %copy-start.2 = (f32[1,1,4,128]{3,2,1,0:T(4,128)S(1)}, f32[1,1,4,128]{3,2,1,0:T(4,128)}, u32[]{:S(2)}) copy-start(f32[1,1,4,128]{3,2,1,0:T(4,128)} %param.11) | copy-start | bytes 6148
  1.5 2.5 %collective-permute-start = (bf16[8,4,128]{2,1,0:T(4,128)(2,1)S(1)}, bf16[8,4,128]{2,1,0:T(4,128)(2,1)S(1)}, u32[]{:S(2)}, u32[]{:S(2)}) collective-permute-start(bf16[8,4,128]{2,1,0:T(4,128)(2,1)S(1)} %convert_element_type.12), channel_id=1, source_target_pairs={{0,1},{1,0},{2,3},{3,2},{4,5},{5,4},{6,7},{7,6},{8,9},{9,8},{10,11... | collective-permute-start | bytes 24584 | tf_op jit(solution)/shard_map/ppermute | solution.py:9
  5.6 16.0 %copy-start.1 = (f32[8,4,128]{2,1,0:T(4,128)S(1)}, f32[8,4,128]{2,1,0:T(4,128)}, u32[]{:S(2)}) copy-start(f32[8,4,128]{2,1,0:T(4,128)} %param.6) | copy-start | bytes 49156
  5.9 4.3 %collective-permute-start.1 = (f32[8,5,128]{2,0,1:T(8,128)S(1)}, f32[8,5,128]{2,0,1:T(8,128)S(1)}, u32[]{:S(2)}, u32[]{:S(2)}) collective-permute-start(f32[8,5,128]{2,0,1:T(8,128)S(1)} %pad_maximum_fusion), channel_id=1, source_target_pairs={{0,2},{2,0},{4,6},{6,4},{8,10},{10,8},{12,14},{14,12},{1,3},{3,1},... | collective-permute-start | bytes 61448 | tf_op jit(solution)/shard_map/ppermute | solution.py:9
  10.2 6.1 %collective-permute-start.4 = (f32[8,5,128]{2,0,1:T(8,128)S(1)}, f32[8,5,128]{2,0,1:T(8,128)S(1)}, u32[]{:S(2)}, u32[]{:S(2)}) collective-permute-start(f32[8,5,128]{2,0,1:T(8,128)S(1)} %fusion.31), channel_id=1, source_target_pairs={{0,12},{2,14},{4,8},{6,10},{8,4},{10,6},{12,0},{14,2},{1,13},{3,15... | collective-permute-start | bytes 61448 | tf_op jit(solution)/shard_map/ppermute | solution.py:9
  14.3 4.7 %collective-permute-start.3 = (f32[8,5,128]{2,0,1:T(8,128)S(1)}, f32[8,5,128]{2,0,1:T(8,128)S(1)}, u32[]{:S(2)}, u32[]{:S(2)}) collective-permute-start(f32[8,5,128]{2,0,1:T(8,128)S(1)} %fusion.31), channel_id=1, source_target_pairs={{0,8},{2,10},{4,12},{6,14},{8,0},{10,2},{12,4},{14,6},{1,9},{3,11}... | collective-permute-start | bytes 61448 | tf_op jit(solution)/shard_map/ppermute | solution.py:9
  14.3 4.7 %collective-permute-start.2 = (f32[8,5,128]{2,0,1:T(8,128)S(1)}, f32[8,5,128]{2,0,1:T(8,128)S(1)}, u32[]{:S(2)}, u32[]{:S(2)}) collective-permute-start(f32[8,5,128]{2,0,1:T(8,128)S(1)} %fusion.31), channel_id=1, source_target_pairs={{0,4},{2,6},{4,0},{6,2},{8,12},{10,14},{12,8},{14,10},{1,5},{3,7},... | collective-permute-start | bytes 61448 | tf_op jit(solution)/shard_map/ppermute | solution.py:9
  20.3 1.2 %collective-permute-start.5 = (bf16[8,5,128]{2,0,1:T(8,128)(2,1)S(1)}, bf16[8,5,128]{2,0,1:T(8,128)(2,1)S(1)}, u32[]{:S(2)}, u32[]{:S(2)}) collective-permute-start(bf16[8,5,128]{2,0,1:T(8,128)(2,1)S(1)} %slice.62), channel_id=1, source_target_pairs={{0,1},{1,0},{2,3},{3,2},{4,5},{5,4},{6,7},{7,6},{8,9},{9,8},{10,11... | collective-permute-start | bytes 30728 | tf_op jit(solution)/shard_map/ppermute | solution.py:9

commit v5 on v2

v5 whole, which is shorter than its diff:
```python
import jax
import jax.numpy as jnp
from jax import lax
from jax.experimental import pallas as pl
from jax.experimental.pallas import tpu as pltpu
from jax.sharding import PartitionSpec as P

SUB = 8
BANKS = 4


def exchange(value, axis, mask):
    size = lax.axis_size(axis)
    return lax.ppermute(value, axis, [(i, i ^ mask) for i in range(size)])


def all_sum(value, axis):
    stride = 1
    while stride < lax.axis_size(axis):
        value = value + exchange(value, axis, stride)
        stride *= 2
    return value


def rows_of(index):
    return pl.ds(pl.multiple_of(index * SUB, SUB), SUB)


def apply_tiles(tiles, take, put, count, table, banks, contract):
    used = count[0, 0]
    for n in range(tiles.shape[2]):
        left = jnp.where(n < used, table[rows_of(take[0, 0, n]), :], 0.0).astype(jnp.bfloat16)
        prod = lax.dot_general(
            left, tiles[0, 0, n], (((1,), (contract,)), ((), ())), preferred_element_type=jnp.float32
        )
        banks[n % BANKS, rows_of(put[0, 0, n]), :] += prod


def front_kernel(tiles, rows, cols, count, own, other, measured, part, table, banks):
    half, inst, width = own.shape
    blocks = part.shape[1]
    ray = lax.axis_index("ray")
    vox = lax.axis_index("vox")
    filler = (lax.broadcasted_iota(jnp.int32, (SUB, width), 0) == inst).astype(jnp.float32)
    banks[...] = jnp.zeros_like(banks)
    for b in range(half):
        for ref, first in ((own, ray * half), (other, (1 - ray) * half)):
            table[rows_of(first + b), :] = filler
            table[pl.ds(pl.multiple_of((first + b) * SUB, SUB), inst), :] = ref[b]
    banks[0, pl.ds(pl.multiple_of(vox * SUB, SUB), inst), :] = -measured[0, 0]
    apply_tiles(tiles, cols, rows, count, table, banks, 1)
    for c in range(inst + 1):
        total = banks[0, pl.ds(c, blocks, stride=SUB), :]
        for k in range(1, BANKS):
            total = total + banks[k, pl.ds(c, blocks, stride=SUB), :]
        part[c] = total if c == inst else -total


def back_kernel(tiles, rows, cols, count, total, own, send, residual, table, banks):
    inst = total.shape[0] - 1
    blocks, width = total.shape[1:]
    half = own.shape[0] // SUB
    ray = lax.axis_index("ray")
    vox = lax.axis_index("vox")
    banks[...] = jnp.zeros_like(banks)
    weight = total[inst] + 1.0
    for c in range(SUB):
        if c < inst:
            row = (total[c] / weight).astype(jnp.bfloat16).astype(jnp.float32)
        else:
            row = jnp.full((blocks, width), 1.0 if c == inst else 0.0, jnp.float32)
        table[pl.ds(c, blocks, stride=SUB), :] = row
    residual[...] = table[rows_of(vox), :]
    apply_tiles(tiles, rows, cols, count, table, banks, 0)
    mine = pl.ds(pl.multiple_of(ray * half * SUB, SUB), half * SUB)
    theirs = pl.ds(pl.multiple_of((1 - ray) * half * SUB, SUB), half * SUB)
    own[...] = sum(banks[k, mine, :] for k in range(BANKS))
    send[...] = sum(banks[k, theirs, :] for k in range(BANKS)).astype(jnp.bfloat16)


def end_kernel(volume, own, there, residual, new_volume, own_residual):
    half, inst, _ = volume.shape
    sums = own[...] + there[...].astype(jnp.float32)
    for b in range(half):
        both = sums[b * SUB : (b + 1) * SUB]
        step = both[:inst] / (both[inst : inst + 1] + 1.0)
        new_volume[b] = jnp.maximum(volume[b] + step, 0.0)
    own_residual[0, 0] = residual[:inst, :].astype(jnp.bfloat16)


def on_device(volume, tiles, tile_row, tile_col, tile_count, measured):
    half, inst, width = volume.shape
    blocks = measured.shape[1] * lax.axis_size("vox")
    vmem = pl.BlockSpec(memory_space=pltpu.VMEM)
    smem = pl.BlockSpec(memory_space=pltpu.SMEM)
    slots = [vmem, smem, smem, smem]

    other = exchange(volume, "ray", 1)
    part = pl.pallas_call(
        front_kernel,
        out_shape=jax.ShapeDtypeStruct((inst + 1, blocks, width), jnp.float32),
        in_specs=slots + [vmem] * 3,
        out_specs=vmem,
        scratch_shapes=[
            pltpu.VMEM((2 * half * SUB, width), jnp.float32),
            pltpu.VMEM((BANKS, blocks * SUB, width), jnp.float32),
        ],
        name="project",
    )(tiles, tile_row, tile_col, tile_count, volume, other, measured)
    total = all_sum(part, "vox")
    own, send, residual = pl.pallas_call(
        back_kernel,
        out_shape=[
            jax.ShapeDtypeStruct((half * SUB, width), jnp.float32),
            jax.ShapeDtypeStruct((half * SUB, width), jnp.bfloat16),
            jax.ShapeDtypeStruct((SUB, width), jnp.float32),
        ],
        in_specs=slots + [vmem],
        out_specs=[vmem] * 3,
        scratch_shapes=[
            pltpu.VMEM((blocks * SUB, width), jnp.float32),
            pltpu.VMEM((BANKS, 2 * half * SUB, width), jnp.float32),
        ],
        name="backproject",
    )(tiles, tile_row, tile_col, tile_count, total)
    there = exchange(send, "ray", 1)
    return tuple(
        pl.pallas_call(
            end_kernel,
            out_shape=[
                jax.ShapeDtypeStruct(volume.shape, jnp.float32),
                jax.ShapeDtypeStruct(measured.shape, jnp.bfloat16),
            ],
            in_specs=[vmem] * 4,
            out_specs=[vmem] * 2,
            name="update",
        )(volume, own, there, residual)
    )


def solution(mesh):
    in_specs = (
        P(("slab", "vox", "ray"), None, None),
        P(("slab", "vox"), "ray", None, None, None),
        P(("slab", "vox"), "ray", None),
        P(("slab", "vox"), "ray", None),
        P(("slab", "vox"), "ray"),
        P("ray", ("slab", "vox"), None, None),
    )
    out_specs = (P(("slab", "vox", "ray"), None, None), P("ray", ("slab", "vox"), None, None))
    return jax.shard_map(
        on_device, mesh=mesh, in_specs=in_specs, out_specs=out_specs, check_vma=False
    )
```

time: 33.9 us -> 26.9 us (0.79)
  Pallas kernels: 0 us -> 6.95 us
  waiting for transfers between devices: 13.7 us -> 7.28 us
  starting transfers between devices: 10.7 us -> 8.5 us
  local copies, waits for them, and re-layouts: 3.13 us -> 1.2 us
  matrix products: 1.78 us -> 0 us
  other arithmetic: 2.83 us -> 1.34 us
    all_to_all x2 -> x0, waiting for transfers between devices: 13.1 us -> none  [the longest x1 6.67 us: on_device(): lax.all_to_all(sums, 'vox', 0, 0, tiled=True)]
    all_to_all x2 -> x0, starting transfers between devices: 10.1 us -> none  [the longest x1 6.8 us: on_device(): lax.all_to_all(sums, 'vox', 0, 0, tiled=True)]
    ppermute x2 -> x5, starting transfers between devices: 0.52 us -> 8.5 us  [exchange(): return lax.ppermute(value, axis, [(i, i ^ mask) for i in range(size)])]
    pallas_call x0 -> x3, Pallas kernels: none -> 6.95 us  [the longest x1 2.99 us: on_device(): pl.pallas_call(front_kernel, out_shape=jax.ShapeDtypeStruct((inst + 1, bl...]
    ppermute x2 -> x5, waiting for transfers between devices: 0.59 us -> 7.28 us  [exchange(): return lax.ppermute(value, axis, [(i, i ^ mask) for i in range(size)])]
    dot_general x4 -> x0, matrix products: 1.78 us -> none  [the longest x1 0.91 us: on_device(): jnp.einsum('nrv,ncv->ncr', block, picked, preferred_element_type=jnp.floa...]
    select_n x3 -> x0, other arithmetic: 1.33 us -> none  [the longest x1 0.66 us: on_device(): picked = jnp.concatenate([panel[place], ones], axis=1)]
    add x1 -> x3, other arithmetic: 0.01 us -> 1.34 us  [all_sum(): value = value + exchange(value, axis, stride)]
  transfers between devices with their start and end apart: 4 -> 5, of which waited for: 3 -> 5; matrix products, arithmetic and copies ran while one was open for 6% -> 0% of each run, Pallas kernels for 0% -> 0%
where the time goes in v5:
time: 26.9 us; the launch traced here: 26.6 us
  starting transfers between devices  8.5 us (32%)
  waiting for transfers between devices  7.28 us (27%)
  Pallas kernels  6.95 us (26%)
  other arithmetic  1.34 us (5%)
  between operations  1.29 us (5%)
  local copies, waits for them, and re-layouts  1.2 us (4%)
    ppermute x5, starting transfers between devices, exchange(): return lax.ppermute(value, axis, [(i, i ^ mask) for i in range(size)])  8.5 us
    ppermute x5, waiting for transfers between devices, exchange(): return lax.ppermute(value, axis, [(i, i ^ mask) for i in range(size)])  7.28 us
    pallas_call x1, Pallas kernels, on_device(): pl.pallas_call(front_kernel, out_shape=jax.ShapeDtypeStruct((inst + 1, bl...  2.99 us
    pallas_call x1, Pallas kernels, on_device(): pl.pallas_call(back_kernel, out_shape=[jax.ShapeDtypeStruct((half * SUB,...  2.58 us
    pallas_call x1, Pallas kernels, on_device(): pl.pallas_call(end_kernel, out_shape=[jax.ShapeDtypeStruct(volume.shape,...  1.39 us
    add x3, other arithmetic, all_sum(): value = value + exchange(value, axis, stride)  1.34 us
    unnamed x4, local copies, waits for them, and re-layouts  1.2 us
  transfers between devices with their start and end apart: 5, of which 5 were waited for; matrix products, arithmetic and copies ran while one was open for 0% of the time, Pallas kernels for 0%

profile of v5, /device:TPU:0, one launch (start us, length us, event | category | flops | bytes accessed | tf_op | source)
XLA Modules:
  0.0 26.6 jit_solution(10057780073085329508)
XLA Ops:
  0.6 0.5 %collective-permute-start = (f32[8,4,128]{2,1,0:T(4,128)}, f32[8,4,128]{2,1,0:T(4,128)S(1)}, u32[]{:S(2)}, u32[]{:S(2)}) collective-permute-start(f32[8,4,128]{2,1,0:T(4,128)} %volume.1), channel_id=1, source_target_pairs={{0,1},{1,0},{2,3},{3,2},{4,5},{5,4},{6,7},{7,6},{8,9},{9,8},{10,11... | collective-permute-start | bytes 49160 | tf_op jit(solution)/shard_map/ppermute | solution.py:14
  1.8 0.4 %collective-permute-done.other = f32[8,4,128]{2,1,0:T(4,128)S(1)} collective-permute-done((f32[8,4,128]{2,1,0:T(4,128)}, f32[8,4,128]{2,1,0:T(4,128)S(1)}, u32[]{:S(2)}, u32[]{:S(2)}) %collective-permute-start) | collective-permute-done | bytes 16416 | tf_op jit(solution)/shard_map/ppermute | solution.py:14
  2.2 0.0 copy-start
  2.2 0.6 %copy-done = f32[8,4,128]{2,1,0:T(4,128)} copy-done((f32[8,4,128]{2,1,0:T(4,128)}, f32[8,4,128]{2,1,0:T(4,128)S(1)}, u32[]{:S(2)}) %copy-start) | copy-done | bytes 16408
  2.8 3.0 %project.1 = f32[5,8,128]{2,1,0:T(8,128)} custom-call(bf16[1,1,48,128,128]{4,3,2,1,0:T(8,128)(2,1)} %tiles.3, s32[1,1,48]{2,1,0:T(1,128)} %rows.3, s32[1,1,48]{2,1,0:T(1,128)} %cols.3, s32[1,1]{1,0:T(1,128)S(6)} %copy.8.count, f32[8,4,128]{2,1,0:T(4,128)} %volume.1, f32[8,4,128]{2,1,0:T(4,128)} %copy-done, f32[1,1,4,128]{3,2,1,0:T(4,128)} %measured.1), custom_call_target="tpu_custom_call" | custom-call | tf_op jit(solution)/shard_map/project/pallas_call | solution.py:99
  5.8 2.8 %collective-permute-start.1 = (f32[5,8,128]{2,1,0:T(8,128)}, f32[5,8,128]{2,1,0:T(8,128)S(1)}, u32[]{:S(2)}, u32[]{:S(2)}) collective-permute-start(f32[5,8,128]{2,1,0:T(8,128)} %project.1), channel_id=1, source_target_pairs={{0,2},{2,0},{4,6},{6,4},{8,10},{10,8},{12,14},{14,12},{1,3},{3,1},... | collective-permute-start | bytes 61448 | tf_op jit(solution)/shard_map/ppermute | solution.py:14
  8.6 2.0 %collective-permute-done.1 = f32[5,8,128]{2,1,0:T(8,128)S(1)} collective-permute-done((f32[5,8,128]{2,1,0:T(8,128)}, f32[5,8,128]{2,1,0:T(8,128)S(1)}, u32[]{:S(2)}, u32[]{:S(2)}) %collective-permute-start.1) | collective-permute-done | bytes 20512 | tf_op jit(solution)/shard_map/ppermute | solution.py:14
  10.6 0.7 %add.9 = f32[5,8,128]{2,1,0:T(8,128)S(1)} add(f32[5,8,128]{2,1,0:T(8,128)} %project.1, f32[5,8,128]{2,1,0:T(8,128)S(1)} %collective-permute-done.1) | non-fusion elementwise | flops 5120 | bytes 61440 | tf_op jit(solution)/shard_map/add | solution.py:20
  11.3 2.1 %collective-permute-start.2 = (f32[5,8,128]{2,1,0:T(8,128)S(1)}, f32[5,8,128]{2,1,0:T(8,128)S(1)}, u32[]{:S(2)}, u32[]{:S(2)}) collective-permute-start(f32[5,8,128]{2,1,0:T(8,128)S(1)} %add.9), channel_id=1, source_target_pairs={{0,4},{2,6},{4,0},{6,2},{8,12},{10,14},{12,8},{14,10},{1,5},{3,7},... | collective-permute-start | bytes 61448 | tf_op jit(solution)/shard_map/ppermute | solution.py:14
  13.4 1.8 %collective-permute-done.2 = f32[5,8,128]{2,1,0:T(8,128)S(1)} collective-permute-done((f32[5,8,128]{2,1,0:T(8,128)S(1)}, f32[5,8,128]{2,1,0:T(8,128)S(1)}, u32[]{:S(2)}, u32[]{:S(2)}) %collective-permute-start.2) | collective-permute-done | bytes 20512 | tf_op jit(solution)/shard_map/ppermute | solution.py:14
  15.2 3.0 %collective-permute-start.3 = (f32[5,8,128]{2,1,0:T(8,128)S(1)}, f32[5,8,128]{2,1,0:T(8,128)S(1)}, u32[]{:S(2)}, u32[]{:S(2)}) collective-permute-start(f32[5,8,128]{2,1,0:T(8,128)S(1)} %add.10), channel_id=1, source_target_pairs={{0,8},{2,10},{4,12},{6,14},{8,0},{10,2},{12,4},{14,6},{1,9},{3,11}... | collective-permute-start | bytes 61448 | tf_op jit(solution)/shard_map/ppermute | solution.py:14
  18.2 1.8 %collective-permute-done.3 = f32[5,8,128]{2,1,0:T(8,128)S(1)} collective-permute-done((f32[5,8,128]{2,1,0:T(8,128)S(1)}, f32[5,8,128]{2,1,0:T(8,128)S(1)}, u32[]{:S(2)}, u32[]{:S(2)}) %collective-permute-start.3) | collective-permute-done | bytes 20512 | tf_op jit(solution)/shard_map/ppermute | solution.py:14
  20.0 0.6 %add.11.total = f32[5,8,128]{2,1,0:T(8,128)} add(f32[5,8,128]{2,1,0:T(8,128)S(1)} %add.10, f32[5,8,128]{2,1,0:T(8,128)S(1)} %collective-permute-done.3) | non-fusion elementwise | flops 5120 | bytes 61440 | tf_op jit(solution)/shard_map/add | solution.py:20
  20.6 2.6 %backproject.1 = (f32[64,128]{1,0:T(8,128)}, bf16[64,128]{1,0:T(8,128)(2,1)}, f32[8,128]{1,0:T(8,128)}) custom-call(bf16[1,1,48,128,128]{4,3,2,1,0:T(8,128)(2,1)} %tiles.3, s32[1,1,48]{2,1,0:T(1,128)} %rows.3, s32[1,1,48]{2,1,0:T(1,128)} %cols.3, s32[1,1]{1,0:T(1,128)S(6)} %copy.8.count, f32[5,8,128]{2,1,0:T(8,128)} %add.11.total), custom_call_target="tpu_custom_call" | custom-call | tf_op jit(solution)/shard_map/backproject/pallas_call | solution.py:111
  23.2 0.0 collective-permute-start.4
  23.2 1.4 %collective-permute-done.4.there = bf16[64,128]{1,0:T(8,128)(2,1)S(1)} collective-permute-done((bf16[64,128]{1,0:T(8,128)(2,1)}, bf16[64,128]{1,0:T(8,128)(2,1)S(1)}, u32[]{:S(2)}, u32[]{:S(2)}) %collective-permute-start.4) | collective-permute-done | bytes 16416 | tf_op jit(solution)/shard_map/ppermute | solution.py:14
  24.6 0.0 copy-start.1
  24.6 0.6 %copy-done.1 = bf16[64,128]{1,0:T(8,128)(2,1)} copy-done((bf16[64,128]{1,0:T(8,128)(2,1)}, bf16[64,128]{1,0:T(8,128)(2,1)S(1)}, u32[]{:S(2)}) %copy-start.1) | copy-done | bytes 16408
  25.2 1.4 %update.1 = (f32[8,4,128]{2,1,0:T(4,128)}, bf16[1,1,4,128]{3,2,1,0:T(4,128)(2,1)}) custom-call(f32[8,4,128]{2,1,0:T(4,128)} %volume.1, f32[64,128]{1,0:T(8,128)} %get-tuple-element.5.own, bf16[64,128]{1,0:T(8,128)(2,1)} %copy-done.1, f32[8,128]{1,0:T(8,128)} %get-tuple-element.7.residual), custom_call_target="tpu_custom_call" | custom-call | tf_op jit(solution)/shard_map/update/pallas_call | solution.py:128
  (1 shorter events, 0.0 us)
Async XLA Ops:
  0.6 1.6 %collective-permute-start = (f32[8,4,128]{2,1,0:T(4,128)}, f32[8,4,128]{2,1,0:T(4,128)S(1)}, u32[]{:S(2)}, u32[]{:S(2)}) collective-permute-start(f32[8,4,128]{2,1,0:T(4,128)} %volume.1), channel_id=1, source_target_pairs={{0,1},{1,0},{2,3},{3,2},{4,5},{5,4},{6,7},{7,6},{8,9},{9,8},{10,11... | collective-permute-start | bytes 49160 | tf_op jit(solution)/shard_map/ppermute | solution.py:14
  2.2 0.6 %copy-start = (f32[8,4,128]{2,1,0:T(4,128)}, f32[8,4,128]{2,1,0:T(4,128)S(1)}, u32[]{:S(2)}) copy-start(f32[8,4,128]{2,1,0:T(4,128)S(1)} %collective-permute-done.other) | copy-start | bytes 49156
  5.8 4.8 %collective-permute-start.1 = (f32[5,8,128]{2,1,0:T(8,128)}, f32[5,8,128]{2,1,0:T(8,128)S(1)}, u32[]{:S(2)}, u32[]{:S(2)}) collective-permute-start(f32[5,8,128]{2,1,0:T(8,128)} %project.1), channel_id=1, source_target_pairs={{0,2},{2,0},{4,6},{6,4},{8,10},{10,8},{12,14},{14,12},{1,3},{3,1},... | collective-permute-start | bytes 61448 | tf_op jit(solution)/shard_map/ppermute | solution.py:14
  11.3 3.9 %collective-permute-start.2 = (f32[5,8,128]{2,1,0:T(8,128)S(1)}, f32[5,8,128]{2,1,0:T(8,128)S(1)}, u32[]{:S(2)}, u32[]{:S(2)}) collective-permute-start(f32[5,8,128]{2,1,0:T(8,128)S(1)} %add.9), channel_id=1, source_target_pairs={{0,4},{2,6},{4,0},{6,2},{8,12},{10,14},{12,8},{14,10},{1,5},{3,7},... | collective-permute-start | bytes 61448 | tf_op jit(solution)/shard_map/ppermute | solution.py:14
  15.2 4.8 %collective-permute-start.3 = (f32[5,8,128]{2,1,0:T(8,128)S(1)}, f32[5,8,128]{2,1,0:T(8,128)S(1)}, u32[]{:S(2)}, u32[]{:S(2)}) collective-permute-start(f32[5,8,128]{2,1,0:T(8,128)S(1)} %add.10), channel_id=1, source_target_pairs={{0,8},{2,10},{4,12},{6,14},{8,0},{10,2},{12,4},{14,6},{1,9},{3,11}... | collective-permute-start | bytes 61448 | tf_op jit(solution)/shard_map/ppermute | solution.py:14
  23.2 1.4 %collective-permute-start.4 = (bf16[64,128]{1,0:T(8,128)(2,1)}, bf16[64,128]{1,0:T(8,128)(2,1)S(1)}, u32[]{:S(2)}, u32[]{:S(2)}) collective-permute-start(bf16[64,128]{1,0:T(8,128)(2,1)} %get-tuple-element.6), channel_id=1, source_target_pairs={{0,1},{1,0},{2,3},{3,2},{4,5},{5,4},{6,7},{7,6},{8,9},{9,8},{10,11... | collective-permute-start | bytes 49160 | tf_op jit(solution)/shard_map/ppermute | solution.py:14
  24.6 0.6 %copy-start.1 = (bf16[64,128]{1,0:T(8,128)(2,1)}, bf16[64,128]{1,0:T(8,128)(2,1)S(1)}, u32[]{:S(2)}) copy-start(bf16[64,128]{1,0:T(8,128)(2,1)S(1)} %collective-permute-done.4.there) | copy-start | bytes 49156

commit v6 on v5

--- a/solution.py
+++ b/solution.py
@@ -6,6 +6,7 @@
 from jax.sharding import PartitionSpec as P
 
 SUB = 8
+VMEM_BYTES = 16 << 20
 BANKS = 4
 
 
@@ -105,6 +106,7 @@
             pltpu.VMEM((2 * half * SUB, width), jnp.float32),
             pltpu.VMEM((BANKS, blocks * SUB, width), jnp.float32),
         ],
+        compiler_params=pltpu.CompilerParams(vmem_limit_bytes=VMEM_BYTES),
         name="project",
     )(tiles, tile_row, tile_col, tile_count, volume, other, measured)
     total = all_sum(part, "vox")
@@ -121,6 +123,7 @@
             pltpu.VMEM((blocks * SUB, width), jnp.float32),
             pltpu.VMEM((BANKS, 2 * half * SUB, width), jnp.float32),
         ],
+        compiler_params=pltpu.CompilerParams(vmem_limit_bytes=VMEM_BYTES),
         name="backproject",
     )(tiles, tile_row, tile_col, tile_count, total)
     there = exchange(send, "ray", 1)
@@ -133,6 +136,7 @@
             ],
             in_specs=[vmem] * 4,
             out_specs=[vmem] * 2,
+            compiler_params=pltpu.CompilerParams(vmem_limit_bytes=VMEM_BYTES),
             name="update",
         )(volume, own, there, residual)
     )

time: 26.9 us -> 24.4 us (0.907)
  Pallas kernels: 6.95 us -> 3.21 us
  local copies, waits for them, and re-layouts: 1.2 us -> 4.12 us
  other arithmetic: 1.34 us -> 0.01 us
  waiting for transfers between devices: 7.28 us -> 6.85 us
    unnamed x4 -> x12, local copies, waits for them, and re-layouts: 1.2 us -> 4.12 us
    pallas_call x1, Pallas kernels: 2.99 us -> 1.49 us  [on_device(): pl.pallas_call(front_kernel, out_shape=jax.ShapeDtypeStruct((inst + 1, bl...]
    pallas_call x1, Pallas kernels: 2.58 us -> 1.09 us  [on_device(): pl.pallas_call(back_kernel, out_shape=[jax.ShapeDtypeStruct((half * SUB,...]
    add x3, other arithmetic: 1.34 us -> 0.01 us  [all_sum(): value = value + exchange(value, axis, stride)]
    pallas_call x1, Pallas kernels: 1.39 us -> 0.63 us  [on_device(): pl.pallas_call(end_kernel, out_shape=[jax.ShapeDtypeStruct(volume.shape,...]
    ppermute x5, waiting for transfers between devices: 7.28 us -> 6.85 us  [exchange(): return lax.ppermute(value, axis, [(i, i ^ mask) for i in range(size)])]
where the time goes in v6:
time: 24.4 us; the launch traced here: 24.1 us
  starting transfers between devices  8.62 us (35%)
  waiting for transfers between devices  6.85 us (28%)
  local copies, waits for them, and re-layouts  4.12 us (17%)
  Pallas kernels  3.21 us (13%)
  between operations  1.32 us (5%)
    ppermute x5, starting transfers between devices, exchange(): return lax.ppermute(value, axis, [(i, i ^ mask) for i in range(size)])  8.62 us
    ppermute x5, waiting for transfers between devices, exchange(): return lax.ppermute(value, axis, [(i, i ^ mask) for i in range(size)])  6.85 us
    unnamed x12, local copies, waits for them, and re-layouts  4.12 us
    pallas_call x1, Pallas kernels, on_device(): pl.pallas_call(front_kernel, out_shape=jax.ShapeDtypeStruct((inst + 1, bl...  1.49 us
    pallas_call x1, Pallas kernels, on_device(): pl.pallas_call(back_kernel, out_shape=[jax.ShapeDtypeStruct((half * SUB,...  1.09 us
    pallas_call x1, Pallas kernels, on_device(): pl.pallas_call(end_kernel, out_shape=[jax.ShapeDtypeStruct(volume.shape,...  0.63 us
  transfers between devices with their start and end apart: 5, of which 5 were waited for; matrix products, arithmetic and copies ran while one was open for 0% of the time, Pallas kernels for 0%

profile of v6, /device:TPU:0, one launch (start us, length us, event | category | flops | bytes accessed | tf_op | source)
XLA Modules:
  0.0 24.1 jit_solution(2951458473679679409)
XLA Ops:
  0.6 0.5 %collective-permute-start = (f32[8,4,128]{2,1,0:T(4,128)}, f32[8,4,128]{2,1,0:T(4,128)S(1)}, u32[]{:S(2)}, u32[]{:S(2)}) collective-permute-start(f32[8,4,128]{2,1,0:T(4,128)} %volume.1), channel_id=1, source_target_pairs={{0,1},{1,0},{2,3},{3,2},{4,5},{5,4},{6,7},{7,6},{8,9},{9,8},{10,11... | collective-permute-start | bytes 49160 | tf_op jit(solution)/shard_map/ppermute | solution.py:15
  1.8 0.4 %collective-permute-done.other = f32[8,4,128]{2,1,0:T(4,128)S(1)} collective-permute-done((f32[8,4,128]{2,1,0:T(4,128)}, f32[8,4,128]{2,1,0:T(4,128)S(1)}, u32[]{:S(2)}, u32[]{:S(2)}) %collective-permute-start) | collective-permute-done | bytes 16416 | tf_op jit(solution)/shard_map/ppermute | solution.py:15
  2.2 0.0 copy-start
  2.2 1.4 %copy-done = bf16[1,1,48,128,128]{4,3,2,1,0:T(8,128)(2,1)S(1)} copy-done((bf16[1,1,48,128,128]{4,3,2,1,0:T(8,128)(2,1)S(1)}, bf16[1,1,48,128,128]{4,3,2,1,0:T(8,128)(2,1)}, u32[]{:S(2)}) %copy-start) | copy-done | bytes 1572888
  3.6 0.0 copy-start.1
  3.6 0.7 %copy-done.1 = f32[8,4,128]{2,1,0:T(4,128)S(1)} copy-done((f32[8,4,128]{2,1,0:T(4,128)S(1)}, f32[8,4,128]{2,1,0:T(4,128)}, u32[]{:S(2)}) %copy-start.1) | copy-done | bytes 16408
  4.3 0.0 copy-start.3
  4.3 0.7 %copy-done.3 = s32[1,1,48]{2,1,0:T(1,128)S(1)} copy-done((s32[1,1,48]{2,1,0:T(1,128)S(1)}, s32[1,1,48]{2,1,0:T(1,128)}, u32[]{:S(2)}) %copy-start.3) | copy-done | bytes 216
  5.0 0.0 copy-start.4
  5.0 0.7 %copy-done.4 = s32[1,1,48]{2,1,0:T(1,128)S(1)} copy-done((s32[1,1,48]{2,1,0:T(1,128)S(1)}, s32[1,1,48]{2,1,0:T(1,128)}, u32[]{:S(2)}) %copy-start.4) | copy-done | bytes 216
  5.6 0.0 copy-start.5
  5.6 0.7 %copy-done.5 = f32[1,1,4,128]{3,2,1,0:T(4,128)S(1)} copy-done((f32[1,1,4,128]{3,2,1,0:T(4,128)S(1)}, f32[1,1,4,128]{3,2,1,0:T(4,128)}, u32[]{:S(2)}) %copy-start.5) | copy-done | bytes 2072
  6.3 0.0 copy-start.2
  6.3 1.5 %project.1 = f32[5,8,128]{2,1,0:T(8,128)S(1)} custom-call(bf16[1,1,48,128,128]{4,3,2,1,0:T(8,128)(2,1)S(1)} %copy-done, s32[1,1,48]{2,1,0:T(1,128)S(1)} %copy-done.3, s32[1,1,48]{2,1,0:T(1,128)S(1)} %copy-done.4, s32[1,1]{1,0:T(1,128)S(6)} %copy.8.count, f32[8,4,128]{2,1,0:T(4,128)S(1)} %copy-done.1, f32[8,4,128]{2,1,0:T(4,128)S(1)} %collective-permute-done.other, ...), custom_call_target="tpu_custom_call" | custom-call | tf_op jit(solution)/shard_map/project/pallas_call | solution.py:100
  7.8 2.9 %collective-permute-start.1 = (f32[5,8,128]{2,1,0:T(8,128)S(1)}, f32[5,8,128]{2,1,0:T(8,128)S(1)}, u32[]{:S(2)}, u32[]{:S(2)}) collective-permute-start(f32[5,8,128]{2,1,0:T(8,128)S(1)} %project.1), channel_id=1, source_target_pairs={{0,2},{2,0},{4,6},{6,4},{8,10},{10,8},{12,14},{14,12},{1,3},{3,1},... | collective-permute-start | bytes 61448 | tf_op jit(solution)/shard_map/ppermute | solution.py:15
  10.7 1.8 %collective-permute-done.1 = f32[5,8,128]{2,1,0:T(8,128)S(1)} collective-permute-done((f32[5,8,128]{2,1,0:T(8,128)S(1)}, f32[5,8,128]{2,1,0:T(8,128)S(1)}, u32[]{:S(2)}, u32[]{:S(2)}) %collective-permute-start.1) | collective-permute-done | bytes 20512 | tf_op jit(solution)/shard_map/ppermute | solution.py:15
  12.5 2.1 %collective-permute-start.2 = (f32[5,8,128]{2,1,0:T(8,128)S(1)}, f32[5,8,128]{2,1,0:T(8,128)S(1)}, u32[]{:S(2)}, u32[]{:S(2)}) collective-permute-start(f32[5,8,128]{2,1,0:T(8,128)S(1)} %add.9), channel_id=1, source_target_pairs={{0,4},{2,6},{4,0},{6,2},{8,12},{10,14},{12,8},{14,10},{1,5},{3,7},... | collective-permute-start | bytes 61448 | tf_op jit(solution)/shard_map/ppermute | solution.py:15
  14.6 1.8 %collective-permute-done.2 = f32[5,8,128]{2,1,0:T(8,128)S(1)} collective-permute-done((f32[5,8,128]{2,1,0:T(8,128)S(1)}, f32[5,8,128]{2,1,0:T(8,128)S(1)}, u32[]{:S(2)}, u32[]{:S(2)}) %collective-permute-start.2) | collective-permute-done | bytes 20512 | tf_op jit(solution)/shard_map/ppermute | solution.py:15
  16.3 3.0 %collective-permute-start.3 = (f32[5,8,128]{2,1,0:T(8,128)S(1)}, f32[5,8,128]{2,1,0:T(8,128)S(1)}, u32[]{:S(2)}, u32[]{:S(2)}) collective-permute-start(f32[5,8,128]{2,1,0:T(8,128)S(1)} %add.10), channel_id=1, source_target_pairs={{0,8},{2,10},{4,12},{6,14},{8,0},{10,2},{12,4},{14,6},{1,9},{3,11}... | collective-permute-start | bytes 61448 | tf_op jit(solution)/shard_map/ppermute | solution.py:15
  19.4 1.8 %collective-permute-done.3 = f32[5,8,128]{2,1,0:T(8,128)S(1)} collective-permute-done((f32[5,8,128]{2,1,0:T(8,128)S(1)}, f32[5,8,128]{2,1,0:T(8,128)S(1)}, u32[]{:S(2)}, u32[]{:S(2)}) %collective-permute-start.3) | collective-permute-done | bytes 20512 | tf_op jit(solution)/shard_map/ppermute | solution.py:15
  21.1 1.1 %backproject.1 = (f32[64,128]{1,0:T(8,128)S(1)}, bf16[64,128]{1,0:T(8,128)(2,1)S(1)}, f32[8,128]{1,0:T(8,128)S(1)}) custom-call(bf16[1,1,48,128,128]{4,3,2,1,0:T(8,128)(2,1)S(1)} %copy-done, s32[1,1,48]{2,1,0:T(1,128)S(1)} %copy-done.3, s32[1,1,48]{2,1,0:T(1,128)S(1)} %copy-done.4, s32[1,1]{1,0:T(1,128)S(6)} %copy.8.count, f32[5,8,128]{2,1,0:T(8,128)S(1)} %add.11.total), custom_call_target="tpu_custom_call" | custom-call | tf_op jit(solution)/shard_map/backproject/pallas_call | solution.py:113
  22.2 0.1 collective-permute-start.4
  22.3 1.2 %collective-permute-done.4.there = bf16[64,128]{1,0:T(8,128)(2,1)S(1)} collective-permute-done((bf16[64,128]{1,0:T(8,128)(2,1)S(1)}, bf16[64,128]{1,0:T(8,128)(2,1)S(1)}, u32[]{:S(2)}, u32[]{:S(2)}) %collective-permute-start.4) | collective-permute-done | bytes 16416 | tf_op jit(solution)/shard_map/ppermute | solution.py:15
  23.5 0.0 copy-done.2
  23.5 0.6 %update.1 = (f32[8,4,128]{2,1,0:T(4,128)}, bf16[1,1,4,128]{3,2,1,0:T(4,128)(2,1)}) custom-call(f32[8,4,128]{2,1,0:T(4,128)S(1)} %copy-done.2, f32[64,128]{1,0:T(8,128)S(1)} %get-tuple-element.5.own, bf16[64,128]{1,0:T(8,128)(2,1)S(1)} %collective-permute-done.4.there, f32[8,128]{1,0:T(8,128)S(1)} %get-tuple-element.7.residual), custom_call_target="tpu_custom_call" | custom-call | tf_op jit(solution)/shard_map/update/pallas_call | solution.py:131
  (3 shorter events, 0.0 us)
Async XLA Ops:
  0.6 1.6 %collective-permute-start = (f32[8,4,128]{2,1,0:T(4,128)}, f32[8,4,128]{2,1,0:T(4,128)S(1)}, u32[]{:S(2)}, u32[]{:S(2)}) collective-permute-start(f32[8,4,128]{2,1,0:T(4,128)} %volume.1), channel_id=1, source_target_pairs={{0,1},{1,0},{2,3},{3,2},{4,5},{5,4},{6,7},{7,6},{8,9},{9,8},{10,11... | collective-permute-start | bytes 49160 | tf_op jit(solution)/shard_map/ppermute | solution.py:15
  2.2 1.4 %copy-start = (bf16[1,1,48,128,128]{4,3,2,1,0:T(8,128)(2,1)S(1)}, bf16[1,1,48,128,128]{4,3,2,1,0:T(8,128)(2,1)}, u32[]{:S(2)}) copy-start(bf16[1,1,48,128,128]{4,3,2,1,0:T(8,128)(2,1)} %tiles.3) | copy-start | bytes 4718596
  3.6 0.7 %copy-start.1 = (f32[8,4,128]{2,1,0:T(4,128)S(1)}, f32[8,4,128]{2,1,0:T(4,128)}, u32[]{:S(2)}) copy-start(f32[8,4,128]{2,1,0:T(4,128)} %volume.1) | copy-start | bytes 49156
  4.3 0.7 %copy-start.3 = (s32[1,1,48]{2,1,0:T(1,128)S(1)}, s32[1,1,48]{2,1,0:T(1,128)}, u32[]{:S(2)}) copy-start(s32[1,1,48]{2,1,0:T(1,128)} %rows.3) | copy-start | bytes 580
  5.0 0.7 %copy-start.4 = (s32[1,1,48]{2,1,0:T(1,128)S(1)}, s32[1,1,48]{2,1,0:T(1,128)}, u32[]{:S(2)}) copy-start(s32[1,1,48]{2,1,0:T(1,128)} %cols.3) | copy-start | bytes 580
  5.6 0.7 %copy-start.5 = (f32[1,1,4,128]{3,2,1,0:T(4,128)S(1)}, f32[1,1,4,128]{3,2,1,0:T(4,128)}, u32[]{:S(2)}) copy-start(f32[1,1,4,128]{3,2,1,0:T(4,128)} %measured.1) | copy-start | bytes 6148
  6.3 17.2 %copy-start.2 = (f32[8,4,128]{2,1,0:T(4,128)S(1)}, f32[8,4,128]{2,1,0:T(4,128)}, u32[]{:S(2)}) copy-start(f32[8,4,128]{2,1,0:T(4,128)} %volume.1) | copy-start | bytes 49156
  7.8 4.7 %collective-permute-start.1 = (f32[5,8,128]{2,1,0:T(8,128)S(1)}, f32[5,8,128]{2,1,0:T(8,128)S(1)}, u32[]{:S(2)}, u32[]{:S(2)}) collective-permute-start(f32[5,8,128]{2,1,0:T(8,128)S(1)} %project.1), channel_id=1, source_target_pairs={{0,2},{2,0},{4,6},{6,4},{8,10},{10,8},{12,14},{14,12},{1,3},{3,1},... | collective-permute-start | bytes 61448 | tf_op jit(solution)/shard_map/ppermute | solution.py:15
  12.5 3.9 %collective-permute-start.2 = (f32[5,8,128]{2,1,0:T(8,128)S(1)}, f32[5,8,128]{2,1,0:T(8,128)S(1)}, u32[]{:S(2)}, u32[]{:S(2)}) collective-permute-start(f32[5,8,128]{2,1,0:T(8,128)S(1)} %add.9), channel_id=1, source_target_pairs={{0,4},{2,6},{4,0},{6,2},{8,12},{10,14},{12,8},{14,10},{1,5},{3,7},... | collective-permute-start | bytes 61448 | tf_op jit(solution)/shard_map/ppermute | solution.py:15
  16.3 4.8 %collective-permute-start.3 = (f32[5,8,128]{2,1,0:T(8,128)S(1)}, f32[5,8,128]{2,1,0:T(8,128)S(1)}, u32[]{:S(2)}, u32[]{:S(2)}) collective-permute-start(f32[5,8,128]{2,1,0:T(8,128)S(1)} %add.10), channel_id=1, source_target_pairs={{0,8},{2,10},{4,12},{6,14},{8,0},{10,2},{12,4},{14,6},{1,9},{3,11}... | collective-permute-start | bytes 61448 | tf_op jit(solution)/shard_map/ppermute | solution.py:15
  22.2 1.2 %collective-permute-start.4 = (bf16[64,128]{1,0:T(8,128)(2,1)S(1)}, bf16[64,128]{1,0:T(8,128)(2,1)S(1)}, u32[]{:S(2)}, u32[]{:S(2)}) collective-permute-start(bf16[64,128]{1,0:T(8,128)(2,1)S(1)} %get-tuple-element.6), channel_id=1, source_target_pairs={{0,1},{1,0},{2,3},{3,2},{4,5},{5,4},{6,7},{7,6},{8,9},{9,8},{10,11... | collective-permute-start | bytes 49160 | tf_op jit(solution)/shard_map/ppermute | solution.py:15

commit v7 on v2

v7 whole, which is shorter than its diff:
```python
import jax
import jax.numpy as jnp
from jax import lax
from jax.sharding import PartitionSpec as P

SUB = 8


def exchange(value, axis, mask):
    size = lax.axis_size(axis)
    return lax.ppermute(value, axis, [(i, i ^ mask) for i in range(size)])


def all_sum(value, axis):
    stride = 1
    while stride < lax.axis_size(axis):
        value = value + exchange(value, axis, stride)
        stride *= 2
    return value


def picker(place, valid, blocks):
    row = place[:, None] * SUB + jnp.arange(SUB, dtype=jnp.int32)[None, :]
    row = jnp.where(valid[:, None], row, -1).reshape(-1)
    return (row[:, None] == jnp.arange(blocks * SUB, dtype=jnp.int32)[None, :]).astype(jnp.bfloat16)


def pick(matrix, table):
    blocks, inst, width = table.shape
    ones = jnp.ones((blocks, 1, width), jnp.bfloat16)
    zeros = jnp.zeros((blocks, SUB - inst - 1, width), jnp.bfloat16)
    table = jnp.concatenate([table, ones, zeros], axis=1).reshape(blocks * SUB, width)
    rows = jnp.dot(matrix, table, preferred_element_type=jnp.float32).astype(jnp.bfloat16)
    return rows.reshape(-1, SUB, width)[:, : inst + 1]


def block_sums(place, blocks, prod):
    onehot = (place[:, None] == jnp.arange(blocks, dtype=jnp.int32)[None, :]).astype(jnp.float32)
    return jnp.einsum("nb,ncr->bcr", onehot, prod, precision=lax.Precision.HIGHEST)


def on_device(volume, tiles, tile_row, tile_col, tile_count, measured):
    block = tiles[0, 0]
    rows = tile_row[0, 0]
    cols = tile_col[0, 0]
    used = tile_count[0, 0]
    half, inst, width = volume.shape
    ray_blocks = lax.axis_size("vox") * measured.shape[1]
    ray = lax.axis_index("ray")
    vox = lax.axis_index("vox")

    other = exchange(volume, "ray", 1)
    valid = jnp.arange(block.shape[0], dtype=jnp.int32) < used
    place = lax.rem(cols + ray * half, 2 * half)
    panel = jnp.concatenate([volume, other], axis=0).astype(jnp.bfloat16)
    picked = pick(picker(place, valid, 2 * half), panel)
    prod = jnp.einsum("nrv,ncv->ncr", block, picked, preferred_element_type=jnp.float32)
    sums = block_sums(rows, ray_blocks, prod)
    mine = (jnp.arange(ray_blocks, dtype=jnp.int32) == vox)[:, None, None]
    part = jnp.concatenate([jnp.where(mine, measured[0], 0.0) - sums[:, :inst], sums[:, inst:]], axis=1)
    total = all_sum(part, "vox")
    residual = (total[:, :inst] / (total[:, inst:] + 1.0)).astype(jnp.bfloat16)
    own_res = lax.dynamic_slice_in_dim(residual, vox, 1, 0)
    gathered = pick(picker(rows, valid, ray_blocks), residual)
    back = jnp.einsum("nrv,ncr->ncv", block, gathered, preferred_element_type=jnp.float32)
    bsum = block_sums(place, 2 * half, back)
    there = exchange(bsum[half:].astype(jnp.bfloat16), "ray", 1)
    bsum = bsum[:half] + there.astype(jnp.float32)
    new_volume = jnp.maximum(volume + bsum[:, :inst] / (bsum[:, inst:] + 1.0), 0.0)
    return (new_volume, own_res[None])


def solution(mesh):
    in_specs = (
        P(("slab", "vox", "ray"), None, None),
        P(("slab", "vox"), "ray", None, None, None),
        P(("slab", "vox"), "ray", None),
        P(("slab", "vox"), "ray", None),
        P(("slab", "vox"), "ray"),
        P("ray", ("slab", "vox"), None, None),
    )
    out_specs = (P(("slab", "vox", "ray"), None, None), P("ray", ("slab", "vox"), None, None))
    return jax.shard_map(
        on_device, mesh=mesh, in_specs=in_specs, out_specs=out_specs, check_vma=False
    )
```

time: 33.9 us -> 21.3 us (0.63)
  waiting for transfers between devices: 13.7 us -> 5.81 us
  starting transfers between devices: 10.7 us -> 8.13 us
  local copies, waits for them, and re-layouts: 3.13 us -> 1.55 us
  other arithmetic: 2.83 us -> 1.83 us
  matrix products: 1.78 us -> 2.27 us
    all_to_all x2 -> x0, waiting for transfers between devices: 13.1 us -> none  [the longest x1 6.67 us: on_device(): lax.all_to_all(sums, 'vox', 0, 0, tiled=True)]
    all_to_all x2 -> x0, starting transfers between devices: 10.1 us -> none  [the longest x1 6.8 us: on_device(): lax.all_to_all(sums, 'vox', 0, 0, tiled=True)]
    ppermute x2 -> x5, starting transfers between devices: 0.52 us -> 8.13 us  [exchange(): return lax.ppermute(value, axis, [(i, i ^ mask) for i in range(size)])]
    ppermute x2 -> x5, waiting for transfers between devices: 0.59 us -> 5.81 us  [exchange(): return lax.ppermute(value, axis, [(i, i ^ mask) for i in range(size)])]
    gather x2 -> x0, local copies, waits for them, and re-layouts: 1.26 us -> none  [the longest x1 0.63 us: on_device(): picked = jnp.concatenate([panel[place], ones], axis=1)]
    select_n x3 -> x1, other arithmetic: 1.33 us -> 0.08 us  [picker(): row = jnp.where(valid[:, None], row, -1).reshape(-1)]
    another operation x0 -> x1, other arithmetic: none -> 0.84 us
    convert_element_type x1, other arithmetic: 0.83 us -> 0.01 us  [on_device(): residual = (total[:, :inst] / (total[:, inst:] + 1.0)).astype(jnp.bfloat16)]
  transfers between devices with their start and end apart: 4 -> 5, of which waited for: 3 -> 4; matrix products, arithmetic and copies ran while one was open for 6% -> 8% of each run, Pallas kernels for 0% -> 0%
where the time goes in v7:
time: 21.3 us; the launch traced here: 21 us
  starting transfers between devices  8.13 us (38%)
  waiting for transfers between devices  5.81 us (27%)
  matrix products  2.27 us (11%)
  other arithmetic  1.83 us (9%)
  local copies, waits for them, and re-layouts  1.55 us (7%)
  between operations  1.44 us (7%)
    ppermute x5, starting transfers between devices, exchange(): return lax.ppermute(value, axis, [(i, i ^ mask) for i in range(size)])  8.13 us
    ppermute x5, waiting for transfers between devices, exchange(): return lax.ppermute(value, axis, [(i, i ^ mask) for i in range(size)])  5.81 us
    unnamed x10, local copies, waits for them, and re-layouts  1.2 us
    dot_general x1, matrix products, on_device(): jnp.einsum('nrv,ncv->ncr', block, picked, preferred_element_type=jnp.floa...  0.9 us
    another operation x1, other arithmetic  0.84 us
    mul x1, other arithmetic, picker(): row = place[:, None] * SUB + jnp.arange(SUB, dtype=jnp.int32)[None, :]  0.68 us
    dot_general x1, matrix products, on_device(): jnp.einsum('nrv,ncr->ncv', block, gathered, preferred_element_type=jnp.fl...  0.52 us
    dot_general x2, matrix products, pick(): jnp.dot(matrix, table, preferred_element_type=jnp.float32)  0.49 us
  transfers between devices with their start and end apart: 5, of which 4 were waited for; matrix products, arithmetic and copies ran while one was open for 8% of the time, Pallas kernels for 0%

profile of v7, /device:TPU:0, one launch (start us, length us, event | category | flops | bytes accessed | tf_op | source)
XLA Modules:
  0.0 21.0 jit_solution(15302814520849330446)
XLA Ops:
  0.6 0.0 copy-start
  0.6 0.0 copy-start.2
  0.7 0.0 copy-start.3
  0.7 0.8 %convert.16 = bf16[8,4,128]{2,1,0:T(4,128)(2,1)S(1)} convert(f32[8,4,128]{2,1,0:T(4,128)} %param.6) | non-fusion elementwise | flops 4096 | bytes 24576 | tf_op jit(solution)/shard_map/convert.1
  1.5 0.5 %collective-permute-start = (bf16[8,4,128]{2,1,0:T(4,128)(2,1)S(1)}, bf16[8,4,128]{2,1,0:T(4,128)(2,1)S(1)}, u32[]{:S(2)}, u32[]{:S(2)}) collective-permute-start(bf16[8,4,128]{2,1,0:T(4,128)(2,1)S(1)} %convert.16), channel_id=1, source_target_pairs={{0,1},{1,0},{2,3},{3,2},{4,5},{5,4},{6,7},{7,6},{8,9},{9,8},{10,11... | collective-permute-start | bytes 24584 | tf_op jit(solution)/shard_map/ppermute | solution.py:11
  2.6 0.7 %broadcast_multiply_fusion = (s32[48]{0:T(128)S(1)}, s32[48]{0:T(128)S(1)}, s32[48]{0:T(128)S(1)}) fusion(s32[1,1,48]{2,1,0:T(1,128)} %param.9, s32[]{:T(128)S(6)} %mul.19, s32[1,1,48]{2,1,0:T(1,128)} %param.8), kind=kLoop, calls=%fused_computation.55 | loop fusion | flops 432 | bytes 964 | tf_op jit(solution)/shard_map/mul | solution.py:23
  3.3 0.1 add_select_fusion
  3.4 0.1 pad.7.clone
  3.5 0.1 pad.8.clone
  3.6 0.1 select_n.32
  3.7 0.0 collective-permute-done
  3.7 0.2 %fusion.4 = bf16[48,8,128]{2,1,0:T(8,128)(2,1)S(1)} fusion(s32[384]{0:T(512)S(1)} %select_n.32, bf16[8,4,128]{2,1,0:T(4,128)(2,1)S(1)} %collective-permute-done, bf16[8,4,128]{2,1,0:T(4,128)(2,1)S(1)} %convert.16, bf16[8]{0:T(256)(128)(2,1)S(1)} %pad.8.clone, bf16[8]{0:T(256)(128)(2,1)S(1)} %pad.7.clone), kind=kOutput, calls=%fused_computation.6 | convolution fusion | flops 12812288 | bytes 116256 | tf_op jit(solution)/shard_map/dot_general | solution.py:33
  3.9 0.0 copy-done
  3.9 0.9 %fusion.2 = f32[48,5,128]{2,1,0:T(8,128)S(1)} fusion(bf16[1,1,48,128,128]{4,3,2,1,0:T(8,128)(2,1)S(1)} %copy-done, bf16[48,8,128]{2,1,0:T(8,128)(2,1)S(1)} %fusion.4), kind=kOutput, calls=%fused_computation.2 | convolution fusion | flops 7864320 | bytes 1794048 | tf_op jit(solution)/shard_map/nrv,ncv->ncr/dot_general | solution.py:57
  4.8 0.0 copy-start.1
  4.8 0.0 copy-done.2
  4.8 0.2 fusion.8
  5.0 0.0 copy-done.3
  5.1 0.1 slice_subtract_fusion
  5.1 2.5 %collective-permute-start.1 = (f32[8,5,128]{2,0,1:T(8,128)S(1)}, f32[8,5,128]{2,0,1:T(8,128)S(1)}, u32[]{:S(2)}, u32[]{:S(2)}) collective-permute-start(f32[8,5,128]{2,0,1:T(8,128)S(1)} %pad_maximum_fusion), channel_id=1, source_target_pairs={{0,2},{2,0},{4,6},{6,4},{8,10},{10,8},{12,14},{14,12},{1,3},{3,1},... | collective-permute-start | bytes 61448 | tf_op jit(solution)/shard_map/ppermute | solution.py:11
  7.6 1.8 %collective-permute-done.1 = f32[8,5,128]{2,0,1:T(8,128)S(1)} collective-permute-done((f32[8,5,128]{2,0,1:T(8,128)S(1)}, f32[8,5,128]{2,0,1:T(8,128)S(1)}, u32[]{:S(2)}, u32[]{:S(2)}) %collective-permute-start.1) | collective-permute-done | bytes 20512 | tf_op jit(solution)/shard_map/ppermute | solution.py:11
  9.4 2.1 %collective-permute-start.2 = (f32[8,5,128]{2,0,1:T(8,128)S(1)}, f32[8,5,128]{2,0,1:T(8,128)S(1)}, u32[]{:S(2)}, u32[]{:S(2)}) collective-permute-start(f32[8,5,128]{2,0,1:T(8,128)S(1)} %fusion.35), channel_id=1, source_target_pairs={{0,4},{2,6},{4,0},{6,2},{8,12},{10,14},{12,8},{14,10},{1,5},{3,7},... | collective-permute-start | bytes 61448 | tf_op jit(solution)/shard_map/ppermute | solution.py:11
  11.5 1.8 %collective-permute-done.2 = f32[8,5,128]{2,0,1:T(8,128)S(1)} collective-permute-done((f32[8,5,128]{2,0,1:T(8,128)S(1)}, f32[8,5,128]{2,0,1:T(8,128)S(1)}, u32[]{:S(2)}, u32[]{:S(2)}) %collective-permute-start.2) | collective-permute-done | bytes 20512 | tf_op jit(solution)/shard_map/ppermute | solution.py:11
  13.3 3.0 %collective-permute-start.3 = (f32[8,5,128]{2,0,1:T(8,128)S(1)}, f32[8,5,128]{2,0,1:T(8,128)S(1)}, u32[]{:S(2)}, u32[]{:S(2)}) collective-permute-start(f32[8,5,128]{2,0,1:T(8,128)S(1)} %add.89), channel_id=1, source_target_pairs={{0,8},{2,10},{4,12},{6,14},{8,0},{10,2},{12,4},{14,6},{1,9},{3,11}... | collective-permute-start | bytes 61448 | tf_op jit(solution)/shard_map/ppermute | solution.py:11
  16.3 0.1 select_n.29
  16.4 1.7 %collective-permute-done.3 = f32[8,5,128]{2,0,1:T(8,128)S(1)} collective-permute-done((f32[8,5,128]{2,0,1:T(8,128)S(1)}, f32[8,5,128]{2,0,1:T(8,128)S(1)}, u32[]{:S(2)}, u32[]{:S(2)}) %collective-permute-start.3) | collective-permute-done | bytes 20512 | tf_op jit(solution)/shard_map/ppermute | solution.py:11
  18.1 0.1 maximum_maximum_fusion
  18.2 0.2 %fusion.5 = bf16[48,8,128]{2,1,0:T(8,128)(2,1)S(1)} fusion(s32[384]{0:T(512)S(1)} %select_n.29, bf16[8,8,128]{2,0,1:T(8,128)(2,1)S(1)} %maximum_maximum_fusion), kind=kOutput, calls=%fused_computation.7 | convolution fusion | flops 6365184 | bytes 116224 | tf_op jit(solution)/shard_map/dot_general | solution.py:33
  18.4 0.5 %fusion = f32[48,5,128]{2,1,0:T(8,128)S(1)} fusion(bf16[1,1,48,128,128]{4,3,2,1,0:T(8,128)(2,1)S(1)} %copy-done, bf16[48,8,128]{2,1,0:T(8,128)(2,1)S(1)} %fusion.5), kind=kOutput, calls=%fused_computation | convolution fusion | flops 7864320 | bytes 1794048 | tf_op jit(solution)/shard_map/nrv,ncr->ncv/dot_general | solution.py:65
  18.9 0.2 fusion.6
  19.1 0.1 collective-permute-start.4
  19.2 0.6 %copy.26 = bf16[1,4,128]{2,1,0:T(4,128)(2,1)} copy(bf16[1,4,128]{2,0,1:T(2,128)(2,1)S(1)} %constant_dynamic-slice_fusion) | data formatting | bytes 2048
  19.8 0.6 %collective-permute-done.4 = bf16[8,5,128]{2,0,1:T(8,128)(2,1)S(1)} collective-permute-done((bf16[8,5,128]{2,0,1:T(8,128)(2,1)S(1)}, bf16[8,5,128]{2,0,1:T(8,128)(2,1)S(1)}, u32[]{:S(2)}, u32[]{:S(2)}) %collective-permute-start.4) | collective-permute-done | bytes 10272 | tf_op jit(solution)/shard_map/ppermute | solution.py:11
  20.4 0.0 copy-done.1
  20.4 0.6 %copy.12 = f32[8,4,128]{2,1,0:T(4,128)} copy(f32[8,4,128]{2,0,1:T(8,128)S(1)} %fusion.19) | data formatting | bytes 32768
  (15 shorter events, 0.1 us)
Async XLA Ops:
  0.6 3.3 %copy-start = (bf16[1,1,48,128,128]{4,3,2,1,0:T(8,128)(2,1)S(1)}, bf16[1,1,48,128,128]{4,3,2,1,0:T(8,128)(2,1)}, u32[]{:S(2)}) copy-start(bf16[1,1,48,128,128]{4,3,2,1,0:T(8,128)(2,1)} %param.7) | copy-start | bytes 4718596
  0.6 4.2 %copy-start.2 = (s32[1,1,48]{2,1,0:T(1,128)S(1)}, s32[1,1,48]{2,1,0:T(1,128)}, u32[]{:S(2)}) copy-start(s32[1,1,48]{2,1,0:T(1,128)} %param.8) | copy-start | bytes 580
  0.7 4.4 %copy-start.3 = (f32[1,1,4,128]{3,2,1,0:T(4,128)S(1)}, f32[1,1,4,128]{3,2,1,0:T(4,128)}, u32[]{:S(2)}) copy-start(f32[1,1,4,128]{3,2,1,0:T(4,128)} %param.11) | copy-start | bytes 6148
  1.5 2.2 %collective-permute-start = (bf16[8,4,128]{2,1,0:T(4,128)(2,1)S(1)}, bf16[8,4,128]{2,1,0:T(4,128)(2,1)S(1)}, u32[]{:S(2)}, u32[]{:S(2)}) collective-permute-start(bf16[8,4,128]{2,1,0:T(4,128)(2,1)S(1)} %convert.16), channel_id=1, source_target_pairs={{0,1},{1,0},{2,3},{3,2},{4,5},{5,4},{6,7},{7,6},{8,9},{9,8},{10,11... | collective-permute-start | bytes 24584 | tf_op jit(solution)/shard_map/ppermute | solution.py:11
  4.8 15.5 %copy-start.1 = (f32[8,4,128]{2,1,0:T(4,128)S(1)}, f32[8,4,128]{2,1,0:T(4,128)}, u32[]{:S(2)}) copy-start(f32[8,4,128]{2,1,0:T(4,128)} %param.6) | copy-start | bytes 49156
  5.1 4.3 %collective-permute-start.1 = (f32[8,5,128]{2,0,1:T(8,128)S(1)}, f32[8,5,128]{2,0,1:T(8,128)S(1)}, u32[]{:S(2)}, u32[]{:S(2)}) collective-permute-start(f32[8,5,128]{2,0,1:T(8,128)S(1)} %pad_maximum_fusion), channel_id=1, source_target_pairs={{0,2},{2,0},{4,6},{6,4},{8,10},{10,8},{12,14},{14,12},{1,3},{3,1},... | collective-permute-start | bytes 61448 | tf_op jit(solution)/shard_map/ppermute | solution.py:11
  9.4 3.8 %collective-permute-start.2 = (f32[8,5,128]{2,0,1:T(8,128)S(1)}, f32[8,5,128]{2,0,1:T(8,128)S(1)}, u32[]{:S(2)}, u32[]{:S(2)}) collective-permute-start(f32[8,5,128]{2,0,1:T(8,128)S(1)} %fusion.35), channel_id=1, source_target_pairs={{0,4},{2,6},{4,0},{6,2},{8,12},{10,14},{12,8},{14,10},{1,5},{3,7},... | collective-permute-start | bytes 61448 | tf_op jit(solution)/shard_map/ppermute | solution.py:11
  13.3 4.8 %collective-permute-start.3 = (f32[8,5,128]{2,0,1:T(8,128)S(1)}, f32[8,5,128]{2,0,1:T(8,128)S(1)}, u32[]{:S(2)}, u32[]{:S(2)}) collective-permute-start(f32[8,5,128]{2,0,1:T(8,128)S(1)} %add.89), channel_id=1, source_target_pairs={{0,8},{2,10},{4,12},{6,14},{8,0},{10,2},{12,4},{14,6},{1,9},{3,11}... | collective-permute-start | bytes 61448 | tf_op jit(solution)/shard_map/ppermute | solution.py:11
  19.1 1.2 %collective-permute-start.4 = (bf16[8,5,128]{2,0,1:T(8,128)(2,1)S(1)}, bf16[8,5,128]{2,0,1:T(8,128)(2,1)S(1)}, u32[]{:S(2)}, u32[]{:S(2)}) collective-permute-start(bf16[8,5,128]{2,0,1:T(8,128)(2,1)S(1)} %slice.72), channel_id=1, source_target_pairs={{0,1},{1,0},{2,3},{3,2},{4,5},{5,4},{6,7},{7,6},{8,9},{9,8},{10,11... | collective-permute-start | bytes 30728 | tf_op jit(solution)/shard_map/ppermute | solution.py:11

commit v8 on v7

--- a/solution.py
+++ b/solution.py
@@ -49,7 +49,7 @@
     ray = lax.axis_index("ray")
     vox = lax.axis_index("vox")
 
-    other = exchange(volume, "ray", 1)
+    other = lax.optimization_barrier(exchange(volume, "ray", 1))
     valid = jnp.arange(block.shape[0], dtype=jnp.int32) < used
     place = lax.rem(cols + ray * half, 2 * half)
     panel = jnp.concatenate([volume, other], axis=0).astype(jnp.bfloat16)

time: 21.3 us -> 21.3 us (level)
  no operation moved by 1% of the time
where the time goes in v8:
time: 21.3 us; the launch traced here: 21 us
  starting transfers between devices  8.13 us (38%)
  waiting for transfers between devices  5.81 us (27%)
  matrix products  2.27 us (11%)
  other arithmetic  1.83 us (9%)
  local copies, waits for them, and re-layouts  1.55 us (7%)
  between operations  1.44 us (7%)
    ppermute x5, starting transfers between devices, exchange(): return lax.ppermute(value, axis, [(i, i ^ mask) for i in range(size)])  8.13 us
    ppermute x5, waiting for transfers between devices, exchange(): return lax.ppermute(value, axis, [(i, i ^ mask) for i in range(size)])  5.81 us
    unnamed x10, local copies, waits for them, and re-layouts  1.2 us
    dot_general x1, matrix products, on_device(): jnp.einsum('nrv,ncv->ncr', block, picked, preferred_element_type=jnp.floa...  0.9 us
    another operation x1, other arithmetic  0.84 us
    mul x1, other arithmetic, picker(): row = place[:, None] * SUB + jnp.arange(SUB, dtype=jnp.int32)[None, :]  0.68 us
    dot_general x1, matrix products, on_device(): jnp.einsum('nrv,ncr->ncv', block, gathered, preferred_element_type=jnp.fl...  0.52 us
    dot_general x2, matrix products, pick(): jnp.dot(matrix, table, preferred_element_type=jnp.float32)  0.49 us
  transfers between devices with their start and end apart: 5, of which 4 were waited for; matrix products, arithmetic and copies ran while one was open for 8% of the time, Pallas kernels for 0%

profile of v8, /device:TPU:0, one launch (start us, length us, event | category | flops | bytes accessed | tf_op | source)
XLA Modules:
  0.0 21.0 jit_solution(15302814520849330446)
XLA Ops:
  0.6 0.0 copy-start
  0.6 0.0 copy-start.2
  0.7 0.0 copy-start.3
  0.7 0.8 %convert.16 = bf16[8,4,128]{2,1,0:T(4,128)(2,1)S(1)} convert(f32[8,4,128]{2,1,0:T(4,128)} %param.6) | non-fusion elementwise | flops 4096 | bytes 24576 | tf_op jit(solution)/shard_map/convert.1
  1.5 0.5 %collective-permute-start = (bf16[8,4,128]{2,1,0:T(4,128)(2,1)S(1)}, bf16[8,4,128]{2,1,0:T(4,128)(2,1)S(1)}, u32[]{:S(2)}, u32[]{:S(2)}) collective-permute-start(bf16[8,4,128]{2,1,0:T(4,128)(2,1)S(1)} %convert.16), channel_id=1, source_target_pairs={{0,1},{1,0},{2,3},{3,2},{4,5},{5,4},{6,7},{7,6},{8,9},{9,8},{10,11... | collective-permute-start | bytes 24584 | tf_op jit(solution)/shard_map/ppermute | solution.py:11
  2.6 0.7 %broadcast_multiply_fusion = (s32[48]{0:T(128)S(1)}, s32[48]{0:T(128)S(1)}, s32[48]{0:T(128)S(1)}) fusion(s32[1,1,48]{2,1,0:T(1,128)} %param.9, s32[]{:T(128)S(6)} %mul.19, s32[1,1,48]{2,1,0:T(1,128)} %param.8), kind=kLoop, calls=%fused_computation.55 | loop fusion | flops 432 | bytes 964 | tf_op jit(solution)/shard_map/mul | solution.py:23
  3.3 0.1 add_select_fusion
  3.4 0.1 pad.7.clone
  3.5 0.1 pad.8.clone
  3.6 0.1 select_n.32
  3.7 0.0 collective-permute-done
  3.7 0.2 %fusion.4 = bf16[48,8,128]{2,1,0:T(8,128)(2,1)S(1)} fusion(s32[384]{0:T(512)S(1)} %select_n.32, bf16[8,4,128]{2,1,0:T(4,128)(2,1)S(1)} %collective-permute-done, bf16[8,4,128]{2,1,0:T(4,128)(2,1)S(1)} %convert.16, bf16[8]{0:T(256)(128)(2,1)S(1)} %pad.8.clone, bf16[8]{0:T(256)(128)(2,1)S(1)} %pad.7.clone), kind=kOutput, calls=%fused_computation.6 | convolution fusion | flops 12812288 | bytes 116256 | tf_op jit(solution)/shard_map/dot_general | solution.py:33
  3.9 0.0 copy-done
  3.9 0.9 %fusion.2 = f32[48,5,128]{2,1,0:T(8,128)S(1)} fusion(bf16[1,1,48,128,128]{4,3,2,1,0:T(8,128)(2,1)S(1)} %copy-done, bf16[48,8,128]{2,1,0:T(8,128)(2,1)S(1)} %fusion.4), kind=kOutput, calls=%fused_computation.2 | convolution fusion | flops 7864320 | bytes 1794048 | tf_op jit(solution)/shard_map/nrv,ncv->ncr/dot_general | solution.py:57
  4.8 0.0 copy-start.1
  4.8 0.0 copy-done.2
  4.8 0.2 fusion.8
  5.0 0.0 copy-done.3
  5.1 0.1 slice_subtract_fusion
  5.1 2.5 %collective-permute-start.1 = (f32[8,5,128]{2,0,1:T(8,128)S(1)}, f32[8,5,128]{2,0,1:T(8,128)S(1)}, u32[]{:S(2)}, u32[]{:S(2)}) collective-permute-start(f32[8,5,128]{2,0,1:T(8,128)S(1)} %pad_maximum_fusion), channel_id=1, source_target_pairs={{0,2},{2,0},{4,6},{6,4},{8,10},{10,8},{12,14},{14,12},{1,3},{3,1},... | collective-permute-start | bytes 61448 | tf_op jit(solution)/shard_map/ppermute | solution.py:11
  7.6 1.8 %collective-permute-done.1 = f32[8,5,128]{2,0,1:T(8,128)S(1)} collective-permute-done((f32[8,5,128]{2,0,1:T(8,128)S(1)}, f32[8,5,128]{2,0,1:T(8,128)S(1)}, u32[]{:S(2)}, u32[]{:S(2)}) %collective-permute-start.1) | collective-permute-done | bytes 20512 | tf_op jit(solution)/shard_map/ppermute | solution.py:11
  9.4 2.1 %collective-permute-start.2 = (f32[8,5,128]{2,0,1:T(8,128)S(1)}, f32[8,5,128]{2,0,1:T(8,128)S(1)}, u32[]{:S(2)}, u32[]{:S(2)}) collective-permute-start(f32[8,5,128]{2,0,1:T(8,128)S(1)} %fusion.35), channel_id=1, source_target_pairs={{0,4},{2,6},{4,0},{6,2},{8,12},{10,14},{12,8},{14,10},{1,5},{3,7},... | collective-permute-start | bytes 61448 | tf_op jit(solution)/shard_map/ppermute | solution.py:11
  11.5 1.8 %collective-permute-done.2 = f32[8,5,128]{2,0,1:T(8,128)S(1)} collective-permute-done((f32[8,5,128]{2,0,1:T(8,128)S(1)}, f32[8,5,128]{2,0,1:T(8,128)S(1)}, u32[]{:S(2)}, u32[]{:S(2)}) %collective-permute-start.2) | collective-permute-done | bytes 20512 | tf_op jit(solution)/shard_map/ppermute | solution.py:11
  13.3 3.0 %collective-permute-start.3 = (f32[8,5,128]{2,0,1:T(8,128)S(1)}, f32[8,5,128]{2,0,1:T(8,128)S(1)}, u32[]{:S(2)}, u32[]{:S(2)}) collective-permute-start(f32[8,5,128]{2,0,1:T(8,128)S(1)} %add.89), channel_id=1, source_target_pairs={{0,8},{2,10},{4,12},{6,14},{8,0},{10,2},{12,4},{14,6},{1,9},{3,11}... | collective-permute-start | bytes 61448 | tf_op jit(solution)/shard_map/ppermute | solution.py:11
  16.3 0.1 select_n.29
  16.4 1.7 %collective-permute-done.3 = f32[8,5,128]{2,0,1:T(8,128)S(1)} collective-permute-done((f32[8,5,128]{2,0,1:T(8,128)S(1)}, f32[8,5,128]{2,0,1:T(8,128)S(1)}, u32[]{:S(2)}, u32[]{:S(2)}) %collective-permute-start.3) | collective-permute-done | bytes 20512 | tf_op jit(solution)/shard_map/ppermute | solution.py:11
  18.1 0.1 maximum_maximum_fusion
  18.2 0.2 %fusion.5 = bf16[48,8,128]{2,1,0:T(8,128)(2,1)S(1)} fusion(s32[384]{0:T(512)S(1)} %select_n.29, bf16[8,8,128]{2,0,1:T(8,128)(2,1)S(1)} %maximum_maximum_fusion), kind=kOutput, calls=%fused_computation.7 | convolution fusion | flops 6365184 | bytes 116224 | tf_op jit(solution)/shard_map/dot_general | solution.py:33
  18.4 0.5 %fusion = f32[48,5,128]{2,1,0:T(8,128)S(1)} fusion(bf16[1,1,48,128,128]{4,3,2,1,0:T(8,128)(2,1)S(1)} %copy-done, bf16[48,8,128]{2,1,0:T(8,128)(2,1)S(1)} %fusion.5), kind=kOutput, calls=%fused_computation | convolution fusion | flops 7864320 | bytes 1794048 | tf_op jit(solution)/shard_map/nrv,ncr->ncv/dot_general | solution.py:65
  18.9 0.2 fusion.6
  19.1 0.1 collective-permute-start.4
  19.2 0.6 %copy.26 = bf16[1,4,128]{2,1,0:T(4,128)(2,1)} copy(bf16[1,4,128]{2,0,1:T(2,128)(2,1)S(1)} %constant_dynamic-slice_fusion) | data formatting | bytes 2048
  19.8 0.6 %collective-permute-done.4 = bf16[8,5,128]{2,0,1:T(8,128)(2,1)S(1)} collective-permute-done((bf16[8,5,128]{2,0,1:T(8,128)(2,1)S(1)}, bf16[8,5,128]{2,0,1:T(8,128)(2,1)S(1)}, u32[]{:S(2)}, u32[]{:S(2)}) %collective-permute-start.4) | collective-permute-done | bytes 10272 | tf_op jit(solution)/shard_map/ppermute | solution.py:11
  20.4 0.0 copy-done.1
  20.4 0.6 %copy.12 = f32[8,4,128]{2,1,0:T(4,128)} copy(f32[8,4,128]{2,0,1:T(8,128)S(1)} %fusion.19) | data formatting | bytes 32768
  (15 shorter events, 0.1 us)
Async XLA Ops:
  0.6 3.3 %copy-start = (bf16[1,1,48,128,128]{4,3,2,1,0:T(8,128)(2,1)S(1)}, bf16[1,1,48,128,128]{4,3,2,1,0:T(8,128)(2,1)}, u32[]{:S(2)}) copy-start(bf16[1,1,48,128,128]{4,3,2,1,0:T(8,128)(2,1)} %param.7) | copy-start | bytes 4718596
  0.6 4.2 %copy-start.2 = (s32[1,1,48]{2,1,0:T(1,128)S(1)}, s32[1,1,48]{2,1,0:T(1,128)}, u32[]{:S(2)}) copy-start(s32[1,1,48]{2,1,0:T(1,128)} %param.8) | copy-start | bytes 580
  0.7 4.4 %copy-start.3 = (f32[1,1,4,128]{3,2,1,0:T(4,128)S(1)}, f32[1,1,4,128]{3,2,1,0:T(4,128)}, u32[]{:S(2)}) copy-start(f32[1,1,4,128]{3,2,1,0:T(4,128)} %param.11) | copy-start | bytes 6148
  1.5 2.2 %collective-permute-start = (bf16[8,4,128]{2,1,0:T(4,128)(2,1)S(1)}, bf16[8,4,128]{2,1,0:T(4,128)(2,1)S(1)}, u32[]{:S(2)}, u32[]{:S(2)}) collective-permute-start(bf16[8,4,128]{2,1,0:T(4,128)(2,1)S(1)} %convert.16), channel_id=1, source_target_pairs={{0,1},{1,0},{2,3},{3,2},{4,5},{5,4},{6,7},{7,6},{8,9},{9,8},{10,11... | collective-permute-start | bytes 24584 | tf_op jit(solution)/shard_map/ppermute | solution.py:11
  4.8 15.5 %copy-start.1 = (f32[8,4,128]{2,1,0:T(4,128)S(1)}, f32[8,4,128]{2,1,0:T(4,128)}, u32[]{:S(2)}) copy-start(f32[8,4,128]{2,1,0:T(4,128)} %param.6) | copy-start | bytes 49156
  5.1 4.3 %collective-permute-start.1 = (f32[8,5,128]{2,0,1:T(8,128)S(1)}, f32[8,5,128]{2,0,1:T(8,128)S(1)}, u32[]{:S(2)}, u32[]{:S(2)}) collective-permute-start(f32[8,5,128]{2,0,1:T(8,128)S(1)} %pad_maximum_fusion), channel_id=1, source_target_pairs={{0,2},{2,0},{4,6},{6,4},{8,10},{10,8},{12,14},{14,12},{1,3},{3,1},... | collective-permute-start | bytes 61448 | tf_op jit(solution)/shard_map/ppermute | solution.py:11
  9.4 3.8 %collective-permute-start.2 = (f32[8,5,128]{2,0,1:T(8,128)S(1)}, f32[8,5,128]{2,0,1:T(8,128)S(1)}, u32[]{:S(2)}, u32[]{:S(2)}) collective-permute-start(f32[8,5,128]{2,0,1:T(8,128)S(1)} %fusion.35), channel_id=1, source_target_pairs={{0,4},{2,6},{4,0},{6,2},{8,12},{10,14},{12,8},{14,10},{1,5},{3,7},... | collective-permute-start | bytes 61448 | tf_op jit(solution)/shard_map/ppermute | solution.py:11
  13.3 4.8 %collective-permute-start.3 = (f32[8,5,128]{2,0,1:T(8,128)S(1)}, f32[8,5,128]{2,0,1:T(8,128)S(1)}, u32[]{:S(2)}, u32[]{:S(2)}) collective-permute-start(f32[8,5,128]{2,0,1:T(8,128)S(1)} %add.89), channel_id=1, source_target_pairs={{0,8},{2,10},{4,12},{6,14},{8,0},{10,2},{12,4},{14,6},{1,9},{3,11}... | collective-permute-start | bytes 61448 | tf_op jit(solution)/shard_map/ppermute | solution.py:11
  19.1 1.2 %collective-permute-start.4 = (bf16[8,5,128]{2,0,1:T(8,128)(2,1)S(1)}, bf16[8,5,128]{2,0,1:T(8,128)(2,1)S(1)}, u32[]{:S(2)}, u32[]{:S(2)}) collective-permute-start(bf16[8,5,128]{2,0,1:T(8,128)(2,1)S(1)} %slice.72), channel_id=1, source_target_pairs={{0,1},{1,0},{2,3},{3,2},{4,5},{5,4},{6,7},{7,6},{8,9},{9,8},{10,11... | collective-permute-start | bytes 30728 | tf_op jit(solution)/shard_map/ppermute | solution.py:11

commit v9 on v7

--- a/solution.py
+++ b/solution.py
@@ -12,10 +12,17 @@
 
 
 def all_sum(value, axis):
+    size = lax.axis_size(axis)
     stride = 1
-    while stride < lax.axis_size(axis):
-        value = value + exchange(value, axis, stride)
-        stride *= 2
+    while stride < size:
+        if 2 * stride < size:
+            across = exchange(value, axis, stride)
+            both = exchange(value, axis, 3 * stride)
+            along = exchange(value, axis, 2 * stride)
+            value = (value + across) + (along + both)
+        else:
+            value = value + exchange(value, axis, stride)
+        stride *= 4
     return value
 
 

time: 21.3 us -> 20.9 us (0.981)
  starting transfers between devices: 8.13 us -> 7.3 us
  waiting for transfers between devices: 5.81 us -> 6.2 us
    ppermute x5 -> x6, starting transfers between devices: 8.13 us -> 7.3 us  [exchange(): return lax.ppermute(value, axis, [(i, i ^ mask) for i in range(size)])]
    ppermute x5 -> x6, waiting for transfers between devices: 5.81 us -> 6.2 us  [exchange(): return lax.ppermute(value, axis, [(i, i ^ mask) for i in range(size)])]
  transfers between devices with their start and end apart: 5 -> 6, of which waited for: 4 -> 5; matrix products, arithmetic and copies ran while one was open for 8% -> 8% of each run, Pallas kernels for 0% -> 0%
where the time goes in v9:
time: 20.9 us; the launch traced here: 20.6 us
  starting transfers between devices  7.3 us (35%)
  waiting for transfers between devices  6.2 us (30%)
  matrix products  2.27 us (11%)
  other arithmetic  1.83 us (9%)
  local copies, waits for them, and re-layouts  1.55 us (7%)
  between operations  1.44 us (7%)
    ppermute x6, starting transfers between devices, exchange(): return lax.ppermute(value, axis, [(i, i ^ mask) for i in range(size)])  7.3 us
    ppermute x6, waiting for transfers between devices, exchange(): return lax.ppermute(value, axis, [(i, i ^ mask) for i in range(size)])  6.2 us
    unnamed x10, local copies, waits for them, and re-layouts  1.2 us
    dot_general x1, matrix products, on_device(): jnp.einsum('nrv,ncv->ncr', block, picked, preferred_element_type=jnp.floa...  0.9 us
    another operation x1, other arithmetic  0.84 us
    mul x1, other arithmetic, picker(): row = place[:, None] * SUB + jnp.arange(SUB, dtype=jnp.int32)[None, :]  0.68 us
    dot_general x1, matrix products, on_device(): jnp.einsum('nrv,ncr->ncv', block, gathered, preferred_element_type=jnp.fl...  0.52 us
    dot_general x2, matrix products, pick(): jnp.dot(matrix, table, preferred_element_type=jnp.float32)  0.49 us
  transfers between devices with their start and end apart: 6, of which 5 were waited for; matrix products, arithmetic and copies ran while one was open for 8% of the time, Pallas kernels for 0%

profile of v9, /device:TPU:0, one launch (start us, length us, event | category | flops | bytes accessed | tf_op | source)
XLA Modules:
  0.0 20.6 jit_solution(8851796150163385450)
XLA Ops:
  0.6 0.0 copy-start
  0.6 0.0 copy-start.2
  0.7 0.0 copy-start.3
  0.7 0.8 %convert.16 = bf16[8,4,128]{2,1,0:T(4,128)(2,1)S(1)} convert(f32[8,4,128]{2,1,0:T(4,128)} %param.6) | non-fusion elementwise | flops 4096 | bytes 24576 | tf_op jit(solution)/shard_map/convert.1
  1.5 0.5 %collective-permute-start = (bf16[8,4,128]{2,1,0:T(4,128)(2,1)S(1)}, bf16[8,4,128]{2,1,0:T(4,128)(2,1)S(1)}, u32[]{:S(2)}, u32[]{:S(2)}) collective-permute-start(bf16[8,4,128]{2,1,0:T(4,128)(2,1)S(1)} %convert.16), channel_id=1, source_target_pairs={{0,1},{1,0},{2,3},{3,2},{4,5},{5,4},{6,7},{7,6},{8,9},{9,8},{10,11... | collective-permute-start | bytes 24584 | tf_op jit(solution)/shard_map/ppermute | solution.py:11
  2.6 0.7 %broadcast_multiply_fusion = (s32[48]{0:T(128)S(1)}, s32[48]{0:T(128)S(1)}, s32[48]{0:T(128)S(1)}) fusion(s32[1,1,48]{2,1,0:T(1,128)} %param.9, s32[]{:T(128)S(6)} %mul.19, s32[1,1,48]{2,1,0:T(1,128)} %param.8), kind=kLoop, calls=%fused_computation.56 | loop fusion | flops 432 | bytes 964 | tf_op jit(solution)/shard_map/mul | solution.py:30
  3.3 0.1 add_select_fusion
  3.4 0.1 pad.7.clone
  3.5 0.1 pad.8.clone
  3.6 0.1 select_n.32
  3.7 0.0 collective-permute-done
  3.7 0.2 %fusion.4 = bf16[48,8,128]{2,1,0:T(8,128)(2,1)S(1)} fusion(s32[384]{0:T(512)S(1)} %select_n.32, bf16[8,4,128]{2,1,0:T(4,128)(2,1)S(1)} %collective-permute-done, bf16[8,4,128]{2,1,0:T(4,128)(2,1)S(1)} %convert.16, bf16[8]{0:T(256)(128)(2,1)S(1)} %pad.8.clone, bf16[8]{0:T(256)(128)(2,1)S(1)} %pad.7.clone), kind=kOutput, calls=%fused_computation.6 | convolution fusion | flops 12812288 | bytes 116256 | tf_op jit(solution)/shard_map/dot_general | solution.py:40
  3.9 0.0 copy-done
  3.9 0.9 %fusion.2 = f32[48,5,128]{2,1,0:T(8,128)S(1)} fusion(bf16[1,1,48,128,128]{4,3,2,1,0:T(8,128)(2,1)S(1)} %copy-done, bf16[48,8,128]{2,1,0:T(8,128)(2,1)S(1)} %fusion.4), kind=kOutput, calls=%fused_computation.2 | convolution fusion | flops 7864320 | bytes 1794048 | tf_op jit(solution)/shard_map/nrv,ncv->ncr/dot_general | solution.py:64
  4.8 0.0 copy-start.1
  4.8 0.0 copy-done.2
  4.8 0.2 fusion.8
  5.0 0.0 copy-done.3
  5.1 0.1 slice_subtract_fusion
  5.1 2.6 %collective-permute-start.2 = (f32[8,5,128]{2,0,1:T(8,128)S(1)}, f32[8,5,128]{2,0,1:T(8,128)S(1)}, u32[]{:S(2)}, u32[]{:S(2)}) collective-permute-start(f32[8,5,128]{2,0,1:T(8,128)S(1)} %pad_maximum_fusion), channel_id=1, source_target_pairs={{0,4},{2,6},{4,0},{6,2},{8,12},{10,14},{12,8},{14,10},{1,5},{3,7},... | collective-permute-start | bytes 61448 | tf_op jit(solution)/shard_map/ppermute | solution.py:11
  7.7 1.4 %collective-permute-start.3 = (f32[8,5,128]{2,0,1:T(8,128)S(1)}, f32[8,5,128]{2,0,1:T(8,128)S(1)}, u32[]{:S(2)}, u32[]{:S(2)}) collective-permute-start(f32[8,5,128]{2,0,1:T(8,128)S(1)} %pad_maximum_fusion), channel_id=1, source_target_pairs={{0,6},{2,4},{4,2},{6,0},{8,14},{10,12},{12,10},{14,8},{1,7},{3,5},... | collective-permute-start | bytes 61448 | tf_op jit(solution)/shard_map/ppermute | solution.py:11
  9.1 0.2 collective-permute-start.1
  9.3 0.3 %collective-permute-done.2 = f32[8,5,128]{2,0,1:T(8,128)S(1)} collective-permute-done((f32[8,5,128]{2,0,1:T(8,128)S(1)}, f32[8,5,128]{2,0,1:T(8,128)S(1)}, u32[]{:S(2)}, u32[]{:S(2)}) %collective-permute-start.2) | collective-permute-done | bytes 20512 | tf_op jit(solution)/shard_map/ppermute | solution.py:11
  9.5 2.9 %collective-permute-done.3 = f32[8,5,128]{2,0,1:T(8,128)S(1)} collective-permute-done((f32[8,5,128]{2,0,1:T(8,128)S(1)}, f32[8,5,128]{2,0,1:T(8,128)S(1)}, u32[]{:S(2)}, u32[]{:S(2)}) %collective-permute-start.3) | collective-permute-done | bytes 20512 | tf_op jit(solution)/shard_map/ppermute | solution.py:11
  12.4 0.5 %collective-permute-done.1 = f32[8,5,128]{2,0,1:T(8,128)S(1)} collective-permute-done((f32[8,5,128]{2,0,1:T(8,128)S(1)}, f32[8,5,128]{2,0,1:T(8,128)S(1)}, u32[]{:S(2)}, u32[]{:S(2)}) %collective-permute-start.1) | collective-permute-done | bytes 20512 | tf_op jit(solution)/shard_map/ppermute | solution.py:11
  12.9 2.6 %collective-permute-start.4 = (f32[8,5,128]{2,0,1:T(8,128)S(1)}, f32[8,5,128]{2,0,1:T(8,128)S(1)}, u32[]{:S(2)}, u32[]{:S(2)}) collective-permute-start(f32[8,5,128]{2,0,1:T(8,128)S(1)} %add_add_fusion), channel_id=1, source_target_pairs={{0,8},{2,10},{4,12},{6,14},{8,0},{10,2},{12,4},{14,6},{1,9},{3,11}... | collective-permute-start | bytes 61448 | tf_op jit(solution)/shard_map/ppermute | solution.py:11
  15.5 0.1 select_n.29
  15.6 2.0 %collective-permute-done.4 = f32[8,5,128]{2,0,1:T(8,128)S(1)} collective-permute-done((f32[8,5,128]{2,0,1:T(8,128)S(1)}, f32[8,5,128]{2,0,1:T(8,128)S(1)}, u32[]{:S(2)}, u32[]{:S(2)}) %collective-permute-start.4) | collective-permute-done | bytes 20512 | tf_op jit(solution)/shard_map/ppermute | solution.py:11
  17.7 0.1 maximum_maximum_fusion
  17.7 0.2 %fusion.5 = bf16[48,8,128]{2,1,0:T(8,128)(2,1)S(1)} fusion(s32[384]{0:T(512)S(1)} %select_n.29, bf16[8,8,128]{2,0,1:T(8,128)(2,1)S(1)} %maximum_maximum_fusion), kind=kOutput, calls=%fused_computation.7 | convolution fusion | flops 6365184 | bytes 116224 | tf_op jit(solution)/shard_map/dot_general | solution.py:40
  18.0 0.5 %fusion = f32[48,5,128]{2,1,0:T(8,128)S(1)} fusion(bf16[1,1,48,128,128]{4,3,2,1,0:T(8,128)(2,1)S(1)} %copy-done, bf16[48,8,128]{2,1,0:T(8,128)(2,1)S(1)} %fusion.5), kind=kOutput, calls=%fused_computation | convolution fusion | flops 7864320 | bytes 1794048 | tf_op jit(solution)/shard_map/nrv,ncr->ncv/dot_general | solution.py:72
  18.5 0.2 fusion.6
  18.7 0.1 collective-permute-start.5
  18.8 0.6 %copy.26 = bf16[1,4,128]{2,1,0:T(4,128)(2,1)} copy(bf16[1,4,128]{2,0,1:T(2,128)(2,1)S(1)} %constant_dynamic-slice_fusion) | data formatting | bytes 2048
  19.4 0.6 %collective-permute-done.5 = bf16[8,5,128]{2,0,1:T(8,128)(2,1)S(1)} collective-permute-done((bf16[8,5,128]{2,0,1:T(8,128)(2,1)S(1)}, bf16[8,5,128]{2,0,1:T(8,128)(2,1)S(1)}, u32[]{:S(2)}, u32[]{:S(2)}) %collective-permute-start.5) | collective-permute-done | bytes 10272 | tf_op jit(solution)/shard_map/ppermute | solution.py:11
  20.0 0.0 copy-done.1
  20.0 0.6 %copy.12 = f32[8,4,128]{2,1,0:T(4,128)} copy(f32[8,4,128]{2,0,1:T(8,128)S(1)} %fusion.19) | data formatting | bytes 32768
  (14 shorter events, 0.1 us)
Async XLA Ops:
  0.6 3.3 %copy-start = (bf16[1,1,48,128,128]{4,3,2,1,0:T(8,128)(2,1)S(1)}, bf16[1,1,48,128,128]{4,3,2,1,0:T(8,128)(2,1)}, u32[]{:S(2)}) copy-start(bf16[1,1,48,128,128]{4,3,2,1,0:T(8,128)(2,1)} %param.7) | copy-start | bytes 4718596
  0.6 4.2 %copy-start.2 = (s32[1,1,48]{2,1,0:T(1,128)S(1)}, s32[1,1,48]{2,1,0:T(1,128)}, u32[]{:S(2)}) copy-start(s32[1,1,48]{2,1,0:T(1,128)} %param.8) | copy-start | bytes 580
  0.7 4.4 %copy-start.3 = (f32[1,1,4,128]{3,2,1,0:T(4,128)S(1)}, f32[1,1,4,128]{3,2,1,0:T(4,128)}, u32[]{:S(2)}) copy-start(f32[1,1,4,128]{3,2,1,0:T(4,128)} %param.11) | copy-start | bytes 6148
  1.5 2.2 %collective-permute-start = (bf16[8,4,128]{2,1,0:T(4,128)(2,1)S(1)}, bf16[8,4,128]{2,1,0:T(4,128)(2,1)S(1)}, u32[]{:S(2)}, u32[]{:S(2)}) collective-permute-start(bf16[8,4,128]{2,1,0:T(4,128)(2,1)S(1)} %convert.16), channel_id=1, source_target_pairs={{0,1},{1,0},{2,3},{3,2},{4,5},{5,4},{6,7},{7,6},{8,9},{9,8},{10,11... | collective-permute-start | bytes 24584 | tf_op jit(solution)/shard_map/ppermute | solution.py:11
  4.8 15.1 %copy-start.1 = (f32[8,4,128]{2,1,0:T(4,128)S(1)}, f32[8,4,128]{2,1,0:T(4,128)}, u32[]{:S(2)}) copy-start(f32[8,4,128]{2,1,0:T(4,128)} %param.6) | copy-start | bytes 49156
  5.1 4.4 %collective-permute-start.2 = (f32[8,5,128]{2,0,1:T(8,128)S(1)}, f32[8,5,128]{2,0,1:T(8,128)S(1)}, u32[]{:S(2)}, u32[]{:S(2)}) collective-permute-start(f32[8,5,128]{2,0,1:T(8,128)S(1)} %pad_maximum_fusion), channel_id=1, source_target_pairs={{0,4},{2,6},{4,0},{6,2},{8,12},{10,14},{12,8},{14,10},{1,5},{3,7},... | collective-permute-start | bytes 61448 | tf_op jit(solution)/shard_map/ppermute | solution.py:11
  7.7 4.7 %collective-permute-start.3 = (f32[8,5,128]{2,0,1:T(8,128)S(1)}, f32[8,5,128]{2,0,1:T(8,128)S(1)}, u32[]{:S(2)}, u32[]{:S(2)}) collective-permute-start(f32[8,5,128]{2,0,1:T(8,128)S(1)} %pad_maximum_fusion), channel_id=1, source_target_pairs={{0,6},{2,4},{4,2},{6,0},{8,14},{10,12},{12,10},{14,8},{1,7},{3,5},... | collective-permute-start | bytes 61448 | tf_op jit(solution)/shard_map/ppermute | solution.py:11
  9.1 3.8 %collective-permute-start.1 = (f32[8,5,128]{2,0,1:T(8,128)S(1)}, f32[8,5,128]{2,0,1:T(8,128)S(1)}, u32[]{:S(2)}, u32[]{:S(2)}) collective-permute-start(f32[8,5,128]{2,0,1:T(8,128)S(1)} %pad_maximum_fusion), channel_id=1, source_target_pairs={{0,2},{2,0},{4,6},{6,4},{8,10},{10,8},{12,14},{14,12},{1,3},{3,1},... | collective-permute-start | bytes 61448 | tf_op jit(solution)/shard_map/ppermute | solution.py:11
  12.9 4.7 %collective-permute-start.4 = (f32[8,5,128]{2,0,1:T(8,128)S(1)}, f32[8,5,128]{2,0,1:T(8,128)S(1)}, u32[]{:S(2)}, u32[]{:S(2)}) collective-permute-start(f32[8,5,128]{2,0,1:T(8,128)S(1)} %add_add_fusion), channel_id=1, source_target_pairs={{0,8},{2,10},{4,12},{6,14},{8,0},{10,2},{12,4},{14,6},{1,9},{3,11}... | collective-permute-start | bytes 61448 | tf_op jit(solution)/shard_map/ppermute | solution.py:11
  18.7 1.2 %collective-permute-start.5 = (bf16[8,5,128]{2,0,1:T(8,128)(2,1)S(1)}, bf16[8,5,128]{2,0,1:T(8,128)(2,1)S(1)}, u32[]{:S(2)}, u32[]{:S(2)}) collective-permute-start(bf16[8,5,128]{2,0,1:T(8,128)(2,1)S(1)} %slice.72), channel_id=1, source_target_pairs={{0,1},{1,0},{2,3},{3,2},{4,5},{5,4},{6,7},{7,6},{8,9},{9,8},{10,11... | collective-permute-start | bytes 30728 | tf_op jit(solution)/shard_map/ppermute | solution.py:11

commit v10 on v9

v10 whole, which is shorter than its diff:
```python
import jax
import jax.numpy as jnp
from jax import lax
from jax.experimental import pallas as pl
from jax.experimental.pallas import tpu as pltpu
from jax.sharding import PartitionSpec as P

SUB = 8
VMEM_BYTES = 16 << 20


def exchange(value, axis, mask):
    size = lax.axis_size(axis)
    return lax.ppermute(value, axis, [(i, i ^ mask) for i in range(size)])


def all_sum(value, axis):
    size = lax.axis_size(axis)
    stride = 1
    while stride < size:
        if 2 * stride < size:
            across = exchange(value, axis, stride)
            both = exchange(value, axis, 3 * stride)
            along = exchange(value, axis, 2 * stride)
            value = (value + across) + (along + both)
        else:
            value = value + exchange(value, axis, stride)
        stride *= 4
    return value


def pick_rows(key, blocks):
    shape = (SUB, blocks * SUB)
    lane = lax.broadcasted_iota(jnp.int32, shape, 1)
    same = lane % SUB == lax.broadcasted_iota(jnp.int32, shape, 0)
    block = jnp.where(same, lane // SUB, -2)
    hits = [(block == key[:, n : n + 1]).astype(jnp.float32) for n in range(key.shape[1])]
    return jnp.concatenate(hits, axis=0).astype(jnp.bfloat16)


def blocks_of(values):
    inst, width = values[0].shape
    row = lax.broadcasted_iota(jnp.int32, (SUB - inst, width), 0)
    rest = (row == 0).astype(jnp.float32)
    return jnp.concatenate([x for value in values for x in (value, rest)], axis=0).astype(jnp.bfloat16)


def load_kernel(tiles, volume, measured, rows, cols, count, *refs):
    tiles_out, volume_out, measured_out, table, pick, pick_back, add, add_back = refs[:8]
    rows_in, cols_in, sems = refs[8:]
    pairs = (
        (rows, rows_in),
        (cols, cols_in),
        (volume, volume_out),
        (measured, measured_out),
        (tiles, tiles_out),
    )
    copies = [pltpu.make_async_copy(a, b, sems.at[i]) for i, (a, b) in enumerate(pairs)]
    for copy in copies:
        copy.start()
    for copy in copies[:3]:
        copy.wait()
    half = volume.shape[0]
    slots = rows.shape[2]
    valid = lax.broadcasted_iota(jnp.int32, (1, slots), 1) < count[0, 0]
    place = cols_in[0] + lax.axis_index("ray") * half
    place = jnp.where(place < 2 * half, place, place - 2 * half)
    place = jnp.where(valid, place, -1)
    row = jnp.where(valid, rows_in[0], -1)
    for out, key in ((add, row), (add_back, place)):
        out[...] = (lax.broadcasted_iota(jnp.int32, out.shape, 0) == key).astype(jnp.float32)
    pick[...] = pick_rows(place, 2 * half)
    pick_back[...] = pick_rows(row, add.shape[0])
    table[...] = blocks_of([volume_out[b] for b in range(half)])
    for copy in copies[3:]:
        copy.wait()


def apply_tiles(picked, tiles, contract, add, prods):
    slots = tiles.shape[2]
    width = picked.shape[1]
    for n in range(slots):
        prods[pl.ds(n, SUB, stride=slots), :] = lax.dot_general(
            picked[n * SUB : (n + 1) * SUB].astype(jnp.bfloat16),
            tiles[0, 0, n],
            (((1,), (contract,)), ((), ())),
            preferred_element_type=jnp.float32,
        )
    kinds = prods.shape[0] // slots
    left = jnp.concatenate([prods[c * slots : (c + 1) * slots, :] for c in range(kinds)], axis=1)
    sums = None
    for _ in range(3):
        piece = left.astype(jnp.bfloat16)
        left = left - piece.astype(jnp.float32)
        term = jnp.dot(add[...].astype(jnp.bfloat16), piece, preferred_element_type=jnp.float32)
        sums = term if sums is None else sums + term
    return [sums[:, c * width : (c + 1) * width] for c in range(kinds)]


def project_kernel(tiles, table, pick, add, measured, other, part, prods):
    half, inst, _ = other.shape
    blocks = add.shape[0]
    panel = jnp.concatenate([table[...], blocks_of([other[b] for b in range(half)])], axis=0)
    picked = jnp.dot(pick[...], panel, preferred_element_type=jnp.float32)
    sums = apply_tiles(picked, tiles, 1, add, prods)
    mine = lax.broadcasted_iota(jnp.int32, sums[0].shape, 0) == lax.axis_index("vox")
    for c in range(inst):
        row = jnp.broadcast_to(measured[0, 0, c : c + 1, :], sums[c].shape)
        part[c * blocks : (c + 1) * blocks, :] = jnp.where(mine, row, 0.0) - sums[c]
    part[inst * blocks : (inst + 1) * blocks, :] = sums[inst]


def backproject_kernel(tiles, pick, add, total, own, send, residual, table, prods, mixed):
    blocks = pick.shape[1] // SUB
    inst = total.shape[0] // blocks - 1
    half = add.shape[0] // 2
    weight = total[inst * blocks : (inst + 1) * blocks, :] + 1.0
    for c in range(SUB):
        if c < inst:
            row = (total[c * blocks : (c + 1) * blocks, :] / weight).astype(jnp.bfloat16).astype(jnp.float32)
        else:
            row = jnp.full(weight.shape, 1.0 if c == inst else 0.0, jnp.float32)
        table[pl.ds(c, blocks, stride=SUB), :] = row
    residual[...] = table[pl.ds(pl.multiple_of(lax.axis_index("vox") * SUB, SUB), SUB), :]
    picked = jnp.dot(pick[...], table[...].astype(jnp.bfloat16), preferred_element_type=jnp.float32)
    sums = apply_tiles(picked, tiles, 0, add, prods)
    for c in range(SUB):
        own[pl.ds(c, half, stride=SUB), :] = sums[c][:half]
        mixed[pl.ds(c, half, stride=SUB), :] = sums[c][half:]
    send[...] = mixed[...].astype(jnp.bfloat16)


def update_kernel(volume, own, there, residual, new_volume, own_residual):
    half, inst, _ = volume.shape
    sums = own[...] + there[...].astype(jnp.float32)
    for b in range(half):
        both = sums[b * SUB : (b + 1) * SUB]
        step = both[:inst] / (both[inst : inst + 1] + 1.0)
        new_volume[b] = jnp.maximum(volume[b] + step, 0.0)
    own_residual[0, 0] = residual[:inst, :].astype(jnp.bfloat16)


def on_device(volume, tiles, tile_row, tile_col, tile_count, measured):
    half, inst, width = volume.shape
    slots = tiles.shape[2]
    blocks = lax.axis_size("vox") * measured.shape[1]
    f32, bf16 = jnp.float32, jnp.bfloat16
    vmem = pl.BlockSpec(memory_space=pltpu.VMEM)
    load_specs = [pl.BlockSpec(memory_space=pltpu.HBM)] * 5 + [pl.BlockSpec(memory_space=pltpu.SMEM)]
    params = pltpu.CompilerParams(vmem_limit_bytes=VMEM_BYTES)

    def call(kernel, name, outs, scratch, args, specs=None, cost=None):
        return pl.pallas_call(
            kernel,
            out_shape=[jax.ShapeDtypeStruct(shape, dtype) for shape, dtype in outs],
            in_specs=specs or [vmem] * len(args),
            out_specs=[vmem] * len(outs),
            scratch_shapes=scratch,
            compiler_params=params,
            cost_estimate=cost,
            name=name,
        )(*args)

    other = exchange(volume, "ray", 1)
    args = [pltpu.with_memory_space_constraint(x, pltpu.HBM) for x in (tiles, volume, measured, tile_row, tile_col)]
    ints = [pltpu.VMEM(x.shape, x.dtype) for x in (tile_row, tile_col)]
    tiles, volume, measured, table, pick, pick_back, add, add_back = call(
        load_kernel,
        "load",
        [
            (tiles.shape, bf16),
            (volume.shape, f32),
            (measured.shape, f32),
            ((half * SUB, width), bf16),
            ((slots * SUB, 2 * half * SUB), bf16),
            ((slots * SUB, blocks * SUB), bf16),
            ((blocks, slots), f32),
            ((2 * half, slots), f32),
        ],
        ints + [pltpu.SemaphoreType.DMA((len(args),))],
        args + [tile_count],
        specs=load_specs,
        cost=pl.CostEstimate(flops=0, bytes_accessed=4 * tiles.size, transcendentals=0),
    )
    prods = pltpu.VMEM((slots * SUB, width), f32)
    (part,) = call(
        project_kernel,
        "project",
        [(((inst + 1) * blocks, width), f32)],
        [prods],
        [tiles, table, pick, add, measured, other],
    )
    total = all_sum(part, "vox")
    flat = (half * SUB, width)
    own, send, residual = call(
        backproject_kernel,
        "backproject",
        [(flat, f32), (flat, bf16), ((SUB, width), f32)],
        [pltpu.VMEM((blocks * SUB, width), f32), prods, pltpu.VMEM(flat, f32)],
        [tiles, pick_back, add_back, total],
    )
    there = exchange(send, "ray", 1)
    return tuple(
        call(
            update_kernel,
            "update",
            [(volume.shape, f32), ((1, 1, inst, width), bf16)],
            [],
            [volume, own, there, residual],
        )
    )


def solution(mesh):
    in_specs = (
        P(("slab", "vox", "ray"), None, None),
        P(("slab", "vox"), "ray", None, None, None),
        P(("slab", "vox"), "ray", None),
        P(("slab", "vox"), "ray", None),
        P(("slab", "vox"), "ray"),
        P("ray", ("slab", "vox"), None, None),
    )
    out_specs = (P(("slab", "vox", "ray"), None, None), P("ray", ("slab", "vox"), None, None))
    return jax.shard_map(
        on_device, mesh=mesh, in_specs=in_specs, out_specs=out_specs, check_vma=False
    )
```

time: 20.9 us -> 20 us (0.957)
  Pallas kernels: 0 us -> 4.16 us
  matrix products: 2.27 us -> 0 us
  other arithmetic: 1.83 us -> 0.01 us
  local copies, waits for them, and re-layouts: 1.55 us -> 0 us
  waiting for transfers between devices: 6.2 us -> 6.85 us
    pallas_call x0 -> x4, Pallas kernels: none -> 4.16 us  [call(): pl.pallas_call(kernel, out_shape=[jax.ShapeDtypeStruct(shape, dtype) for...]
    dot_general x6 -> x0, matrix products: 2.27 us -> none  [the longest x1 0.9 us: on_device(): jnp.einsum('nrv,ncv->ncr', block, picked, preferred_element_type=jnp.floa...]
    unnamed x10 -> x0, local copies, waits for them, and re-layouts: 1.2 us -> none
    another operation x1 -> x0, other arithmetic: 0.84 us -> none
    mul x1 -> x0, other arithmetic: 0.68 us -> none  [picker(): row = place[:, None] * SUB + jnp.arange(SUB, dtype=jnp.int32)[None, :]]
    ppermute x6, waiting for transfers between devices: 6.2 us -> 6.85 us  [exchange(): return lax.ppermute(value, axis, [(i, i ^ mask) for i in range(size)])]
  transfers between devices with their start and end apart: 6 -> 6, of which waited for: 5 -> 5; matrix products, arithmetic and copies ran while one was open for 8% -> 0% of each run, Pallas kernels for 0% -> 8%
where the time goes in v10:
time: 20 us; the launch traced here: 19.8 us
  starting transfers between devices  7.45 us (37%)
  waiting for transfers between devices  6.85 us (34%)
  Pallas kernels  4.16 us (21%)
  between operations  1.34 us (7%)
    ppermute x6, starting transfers between devices, exchange(): return lax.ppermute(value, axis, [(i, i ^ mask) for i in range(size)])  7.45 us
    ppermute x6, waiting for transfers between devices, exchange(): return lax.ppermute(value, axis, [(i, i ^ mask) for i in range(size)])  6.85 us
    pallas_call x4, Pallas kernels, call(): pl.pallas_call(kernel, out_shape=[jax.ShapeDtypeStruct(shape, dtype) for...  4.16 us
  transfers between devices with their start and end apart: 6, of which 5 were waited for; matrix products, arithmetic and copies ran while one was open for 0% of the time, Pallas kernels for 8%

profile of v10, /device:TPU:0, one launch (start us, length us, event | category | flops | bytes accessed | tf_op | source)
XLA Modules:
  0.0 19.8 jit_solution(7032284166185095422)
XLA Ops:
  0.6 0.5 %collective-permute-start = (f32[8,4,128]{2,1,0:T(4,128)}, f32[8,4,128]{2,1,0:T(4,128)S(1)}, u32[]{:S(2)}, u32[]{:S(2)}) collective-permute-start(f32[8,4,128]{2,1,0:T(4,128)} %volume.1), channel_id=1, source_target_pairs={{0,1},{1,0},{2,3},{3,2},{4,5},{5,4},{6,7},{7,6},{8,9},{9,8},{10,11... | collective-permute-start | bytes 49160 | tf_op jit(solution)/shard_map/ppermute | solution.py:14
  1.8 1.5 %load.1 = (bf16[1,1,48,128,128]{4,3,2,1,0:T(8,128)(2,1)S(1)}, f32[8,4,128]{2,1,0:T(4,128)S(1)}, f32[1,1,4,128]{3,2,1,0:T(4,128)S(1)}, bf16[64,128]{1,0:T(8,128)(...) custom-call(bf16[1,1,48,128,128]{4,3,2,1,0:T(8,128)(2,1)} %tiles.1, ...), custom_call_target="tpu_custom_call" | custom-call | bytes 3145728 | tf_op jit(solution)/shard_map/load/pallas_call | solution.py:153
  3.3 0.0 collective-permute-done.other
  3.3 1.2 %project.1 = f32[40,128]{1,0:T(8,128)S(1)} custom-call(bf16[1,1,48,128,128]{4,3,2,1,0:T(8,128)(2,1)S(1)} %get-tuple-element.14.tiles, bf16[64,128]{1,0:T(8,128)(2,1)S(1)} %get-tuple-element.17.table, bf16[384,128]{1,0:T(8,128)(2,1)S(1)} %get-tuple-element.18.pick, f32[8,48]{1,0:T(8,128)S(1)} %get-tuple-element.19.add, ...), custom_call_target="tpu_custom_call" | custom-call | tf_op jit(solution)/shard_map/project/pallas_call | solution.py:153
  4.5 3.6 %collective-permute-start.3 = (f32[40,128]{1,0:T(8,128)S(1)}, f32[40,128]{1,0:T(8,128)S(1)}, u32[]{:S(2)}, u32[]{:S(2)}) collective-permute-start(f32[40,128]{1,0:T(8,128)S(1)} %project.1), channel_id=1, source_target_pairs={{0,6},{2,4},{4,2},{6,0},{8,14},{10,12},{12,10},{14,8},{1,7},{3,5},... | collective-permute-start | bytes 61448 | tf_op jit(solution)/shard_map/ppermute | solution.py:14
  8.1 0.5 %collective-permute-start.2 = (f32[40,128]{1,0:T(8,128)S(1)}, f32[40,128]{1,0:T(8,128)S(1)}, u32[]{:S(2)}, u32[]{:S(2)}) collective-permute-start(f32[40,128]{1,0:T(8,128)S(1)} %project.1), channel_id=1, source_target_pairs={{0,4},{2,6},{4,0},{6,2},{8,12},{10,14},{12,8},{14,10},{1,5},{3,7},... | collective-permute-start | bytes 61448 | tf_op jit(solution)/shard_map/ppermute | solution.py:14
  8.6 0.2 collective-permute-start.1
  8.8 1.2 %collective-permute-done.3 = f32[40,128]{1,0:T(8,128)S(1)} collective-permute-done((f32[40,128]{1,0:T(8,128)S(1)}, f32[40,128]{1,0:T(8,128)S(1)}, u32[]{:S(2)}, u32[]{:S(2)}) %collective-permute-start.3) | collective-permute-done | bytes 20512 | tf_op jit(solution)/shard_map/ppermute | solution.py:14
  9.9 2.0 %collective-permute-done.2 = f32[40,128]{1,0:T(8,128)S(1)} collective-permute-done((f32[40,128]{1,0:T(8,128)S(1)}, f32[40,128]{1,0:T(8,128)S(1)}, u32[]{:S(2)}, u32[]{:S(2)}) %collective-permute-start.2) | collective-permute-done | bytes 20512 | tf_op jit(solution)/shard_map/ppermute | solution.py:14
  11.9 0.5 %collective-permute-done.1 = f32[40,128]{1,0:T(8,128)S(1)} collective-permute-done((f32[40,128]{1,0:T(8,128)S(1)}, f32[40,128]{1,0:T(8,128)S(1)}, u32[]{:S(2)}, u32[]{:S(2)}) %collective-permute-start.1) | collective-permute-done | bytes 20512 | tf_op jit(solution)/shard_map/ppermute | solution.py:14
  12.4 2.6 %collective-permute-start.4 = (f32[40,128]{1,0:T(8,128)S(1)}, f32[40,128]{1,0:T(8,128)S(1)}, u32[]{:S(2)}, u32[]{:S(2)}) collective-permute-start(f32[40,128]{1,0:T(8,128)S(1)} %add_add_fusion), channel_id=1, source_target_pairs={{0,8},{2,10},{4,12},{6,14},{8,0},{10,2},{12,4},{14,6},{1,9},{3,11}... | collective-permute-start | bytes 61448 | tf_op jit(solution)/shard_map/ppermute | solution.py:14
  15.0 2.1 %collective-permute-done.4 = f32[40,128]{1,0:T(8,128)S(1)} collective-permute-done((f32[40,128]{1,0:T(8,128)S(1)}, f32[40,128]{1,0:T(8,128)S(1)}, u32[]{:S(2)}, u32[]{:S(2)}) %collective-permute-start.4) | collective-permute-done | bytes 20512 | tf_op jit(solution)/shard_map/ppermute | solution.py:14
  17.1 0.8 %backproject.1 = (f32[64,128]{1,0:T(8,128)S(1)}, bf16[64,128]{1,0:T(8,128)(2,1)S(1)}, f32[8,128]{1,0:T(8,128)S(1)}) custom-call(bf16[1,1,48,128,128]{4,3,2,1,0:T(8,128)(2,1)S(1)} %get-tuple-element.14.tiles, bf16[384,64]{1,0:T(8,128)(2,1)S(1)} %get-tuple-element.15.pick, f32[16,48]{1,0:T(8,128)S(1)} %get-tuple-element.16.add, f32[40,128]{1,0:T(8,128)S(1)} %add.15.total), custom_call_target="tpu_custom_call" | custom-call | tf_op jit(solution)/shard_map/backproject/pallas_call | solution.py:153
  17.9 0.1 collective-permute-start.5
  18.0 1.2 %collective-permute-done.5.there = bf16[64,128]{1,0:T(8,128)(2,1)S(1)} collective-permute-done((bf16[64,128]{1,0:T(8,128)(2,1)S(1)}, bf16[64,128]{1,0:T(8,128)(2,1)S(1)}, u32[]{:S(2)}, u32[]{:S(2)}) %collective-permute-start.5) | collective-permute-done | bytes 16416 | tf_op jit(solution)/shard_map/ppermute | solution.py:14
  19.2 0.6 %update.1 = (f32[8,4,128]{2,1,0:T(4,128)}, bf16[1,1,4,128]{3,2,1,0:T(4,128)(2,1)}) custom-call(f32[8,4,128]{2,1,0:T(4,128)S(1)} %get-tuple-element.13.volume, f32[64,128]{1,0:T(8,128)S(1)} %get-tuple-element.21.own, bf16[64,128]{1,0:T(8,128)(2,1)S(1)} %collective-permute-done.5.there, f32[8,128]{1,0:T(8,128)S(1)} %get-tuple-element.23.residual), custom_call_target="tpu_custom_call" | custom-call | tf_op jit(solution)/shard_map/update/pallas_call | solution.py:153
  (2 shorter events, 0.0 us)
Async XLA Ops:
  0.6 2.7 %collective-permute-start = (f32[8,4,128]{2,1,0:T(4,128)}, f32[8,4,128]{2,1,0:T(4,128)S(1)}, u32[]{:S(2)}, u32[]{:S(2)}) collective-permute-start(f32[8,4,128]{2,1,0:T(4,128)} %volume.1), channel_id=1, source_target_pairs={{0,1},{1,0},{2,3},{3,2},{4,5},{5,4},{6,7},{7,6},{8,9},{9,8},{10,11... | collective-permute-start | bytes 49160 | tf_op jit(solution)/shard_map/ppermute | solution.py:14
  4.5 5.4 %collective-permute-start.3 = (f32[40,128]{1,0:T(8,128)S(1)}, f32[40,128]{1,0:T(8,128)S(1)}, u32[]{:S(2)}, u32[]{:S(2)}) collective-permute-start(f32[40,128]{1,0:T(8,128)S(1)} %project.1), channel_id=1, source_target_pairs={{0,6},{2,4},{4,2},{6,0},{8,14},{10,12},{12,10},{14,8},{1,7},{3,5},... | collective-permute-start | bytes 61448 | tf_op jit(solution)/shard_map/ppermute | solution.py:14
  8.1 3.8 %collective-permute-start.2 = (f32[40,128]{1,0:T(8,128)S(1)}, f32[40,128]{1,0:T(8,128)S(1)}, u32[]{:S(2)}, u32[]{:S(2)}) collective-permute-start(f32[40,128]{1,0:T(8,128)S(1)} %project.1), channel_id=1, source_target_pairs={{0,4},{2,6},{4,0},{6,2},{8,12},{10,14},{12,8},{14,10},{1,5},{3,7},... | collective-permute-start | bytes 61448 | tf_op jit(solution)/shard_map/ppermute | solution.py:14
  8.6 3.8 %collective-permute-start.1 = (f32[40,128]{1,0:T(8,128)S(1)}, f32[40,128]{1,0:T(8,128)S(1)}, u32[]{:S(2)}, u32[]{:S(2)}) collective-permute-start(f32[40,128]{1,0:T(8,128)S(1)} %project.1), channel_id=1, source_target_pairs={{0,2},{2,0},{4,6},{6,4},{8,10},{10,8},{12,14},{14,12},{1,3},{3,1},... | collective-permute-start | bytes 61448 | tf_op jit(solution)/shard_map/ppermute | solution.py:14
  12.4 4.7 %collective-permute-start.4 = (f32[40,128]{1,0:T(8,128)S(1)}, f32[40,128]{1,0:T(8,128)S(1)}, u32[]{:S(2)}, u32[]{:S(2)}) collective-permute-start(f32[40,128]{1,0:T(8,128)S(1)} %add_add_fusion), channel_id=1, source_target_pairs={{0,8},{2,10},{4,12},{6,14},{8,0},{10,2},{12,4},{14,6},{1,9},{3,11}... | collective-permute-start | bytes 61448 | tf_op jit(solution)/shard_map/ppermute | solution.py:14
  17.9 1.2 %collective-permute-start.5 = (bf16[64,128]{1,0:T(8,128)(2,1)S(1)}, bf16[64,128]{1,0:T(8,128)(2,1)S(1)}, u32[]{:S(2)}, u32[]{:S(2)}) collective-permute-start(bf16[64,128]{1,0:T(8,128)(2,1)S(1)} %get-tuple-element.22), channel_id=1, source_target_pairs={{0,1},{1,0},{2,3},{3,2},{4,5},{5,4},{6,7},{7,6},{8,9},{9,8},{10,11... | collective-permute-start | bytes 49160 | tf_op jit(solution)/shard_map/ppermute | solution.py:14

commit v11 on v10

v11 whole, which is shorter than its diff:
```python
import jax
import jax.numpy as jnp
from jax import lax
from jax.experimental import pallas as pl
from jax.experimental.pallas import tpu as pltpu
from jax.sharding import PartitionSpec as P

SUB = 8
VMEM_BYTES = 16 << 20


def exchange(value, axis, mask):
    size = lax.axis_size(axis)
    return lax.ppermute(value, axis, [(i, i ^ mask) for i in range(size)])


def all_sum(value, axis):
    size = lax.axis_size(axis)
    stride = 1
    while stride < size:
        if 2 * stride < size:
            across = exchange(value, axis, stride)
            both = exchange(value, axis, 3 * stride)
            along = exchange(value, axis, 2 * stride)
            value = (value + across) + (along + both)
        else:
            value = value + exchange(value, axis, stride)
        stride *= 4
    return value


def load_kernel(tiles, volume, measured, rows, cols, count, *refs):
    tiles_out, volume_out, measured_out, add, add_back, rows_in, cols_in, sems = refs
    pairs = (
        (rows, rows_in),
        (cols, cols_in),
        (tiles, tiles_out),
        (volume, volume_out),
        (measured, measured_out),
    )
    copies = [pltpu.make_async_copy(a, b, sems.at[i]) for i, (a, b) in enumerate(pairs)]
    for copy in copies:
        copy.start()
    for copy in copies[:2]:
        copy.wait()
    blocks = add_back.shape[0]
    valid = lax.broadcasted_iota(jnp.int32, (1, rows.shape[2]), 1) < count[0, 0]
    place = cols_in[0] + lax.axis_index("ray") * (blocks // 2)
    place = jnp.where(place < blocks, place, place - blocks)
    for out, key in ((add, rows_in[0]), (add_back, place)):
        hit = (lax.broadcasted_iota(jnp.int32, out.shape, 0) == key) & valid
        out[...] = hit.astype(jnp.float32)
    for copy in copies[2:]:
        copy.wait()


def slot_rows(which, table, picked):
    slots, width = which.shape[1], table[0].shape[1]
    rows = lax.dot_general(
        which[...].astype(jnp.bfloat16),
        jnp.concatenate(table, axis=1).astype(jnp.bfloat16),
        (((0,), (0,)), ((), ())),
        preferred_element_type=jnp.float32,
    )
    for c in range(len(table)):
        picked[pl.ds(c, slots, stride=SUB), :] = rows[:, c * width : (c + 1) * width]
    picked[pl.ds(len(table), slots, stride=SUB), :] = jnp.ones((slots, width), jnp.float32)


def apply_tiles(picked, tiles, contract, add, prods, kinds):
    slots = tiles.shape[2]
    width = picked.shape[1]
    for n in range(slots):
        prods[pl.ds(n, SUB, stride=slots), :] = lax.dot_general(
            picked[n * SUB : (n + 1) * SUB, :].astype(jnp.bfloat16),
            tiles[0, 0, n],
            (((1,), (contract,)), ((), ())),
            preferred_element_type=jnp.float32,
        )
    left = jnp.concatenate([prods[c * slots : (c + 1) * slots, :] for c in range(kinds)], axis=1)
    onehot = add[...].astype(jnp.bfloat16)
    sums = None
    for _ in range(3):
        piece = left.astype(jnp.bfloat16)
        left = left - piece.astype(jnp.float32)
        term = jnp.dot(onehot, piece, preferred_element_type=jnp.float32)
        sums = term if sums is None else sums + term
    return [sums[:, c * width : (c + 1) * width] for c in range(kinds)]


def project_kernel(tiles, add, add_back, volume, other, measured, part, picked, prods):
    blocks = add.shape[0]
    half = add_back.shape[0] // 2
    inst = measured.shape[2]
    rows = [pl.ds(c, half, stride=inst) for c in range(inst)]
    table = [jnp.concatenate([volume[row, :], other[row, :]], axis=0) for row in rows]
    slot_rows(add_back, table, picked)
    sums = apply_tiles(picked, tiles, 1, add, prods, inst + 1)
    mine = lax.broadcasted_iota(jnp.int32, sums[0].shape, 0) == lax.axis_index("vox")
    for c in range(inst):
        row = jnp.broadcast_to(measured[0, 0, c : c + 1, :], sums[c].shape)
        part[c * blocks : (c + 1) * blocks, :] = jnp.where(mine, row, 0.0) - sums[c]
    part[inst * blocks : (inst + 1) * blocks, :] = sums[inst]


def backproject_kernel(tiles, add, add_back, total, own, send, residual, picked, prods):
    blocks = add.shape[0]
    half = add_back.shape[0] // 2
    inst = residual.shape[0]
    rows = [total[c * blocks : (c + 1) * blocks, :] for c in range(inst + 1)]
    weight = rows[inst] + 1.0
    table = [(row / weight).astype(jnp.bfloat16).astype(jnp.float32) for row in rows[:inst]]
    mine = lax.broadcasted_iota(jnp.int32, weight.shape, 0) == lax.axis_index("vox")
    for c in range(inst):
        residual[c : c + 1, :] = jnp.sum(jnp.where(mine, table[c], 0.0), axis=0, keepdims=True)
    slot_rows(add, table, picked)
    sums = apply_tiles(picked, tiles, 0, add_back, prods, inst + 1)
    filler = [jnp.zeros((half, weight.shape[1]), jnp.float32)] * (SUB - inst - 1)
    own[...] = jnp.concatenate([x[:half] for x in sums], axis=0)
    send[...] = jnp.concatenate([x[half:] for x in sums] + filler, axis=0).astype(jnp.bfloat16)


def update_kernel(volume, own, there, residual, new_volume, own_residual):
    inst = residual.shape[0]
    half = volume.shape[0] // inst
    both = own[...] + there[...].astype(jnp.float32)[: own.shape[0]]
    weight = both[inst * half :] + 1.0
    for c in range(inst):
        row = pl.ds(c, half, stride=inst)
        new_volume[row, :] = jnp.maximum(volume[row, :] + both[c * half : (c + 1) * half] / weight, 0.0)
    own_residual[0, 0] = residual[...].astype(jnp.bfloat16)


def on_device(volume, tiles, tile_row, tile_col, tile_count, measured):
    half, inst, width = volume.shape
    slots = tiles.shape[2]
    blocks = lax.axis_size("vox") * measured.shape[1]
    f32, bf16 = jnp.float32, jnp.bfloat16
    vmem = pl.BlockSpec(memory_space=pltpu.VMEM)
    load_specs = [pl.BlockSpec(memory_space=pltpu.HBM)] * 5 + [pl.BlockSpec(memory_space=pltpu.SMEM)]
    params = pltpu.CompilerParams(vmem_limit_bytes=VMEM_BYTES)

    def call(kernel, name, outs, scratch, args, specs=None, cost=None):
        return pl.pallas_call(
            kernel,
            out_shape=[jax.ShapeDtypeStruct(shape, dtype) for shape, dtype in outs],
            in_specs=specs or [vmem] * len(args),
            out_specs=[vmem] * len(outs),
            scratch_shapes=scratch,
            compiler_params=params,
            cost_estimate=cost,
            name=name,
        )(*args)

    volume = volume.reshape(half * inst, width)
    other = exchange(volume, "ray", 1)
    args = [pltpu.with_memory_space_constraint(x, pltpu.HBM) for x in (tiles, volume, measured, tile_row, tile_col)]
    ints = [pltpu.VMEM(x.shape, x.dtype) for x in (tile_row, tile_col)]
    tiles, volume, measured, add, add_back = call(
        load_kernel,
        "load",
        [
            (tiles.shape, bf16),
            (volume.shape, f32),
            (measured.shape, f32),
            ((blocks, slots), f32),
            ((2 * half, slots), f32),
        ],
        ints + [pltpu.SemaphoreType.DMA((len(args),))],
        args + [tile_count],
        specs=load_specs,
        cost=pl.CostEstimate(flops=0, bytes_accessed=4 * tiles.size, transcendentals=0),
    )
    scratch = [pltpu.VMEM((slots * SUB, width), f32)] * 2
    (part,) = call(
        project_kernel,
        "project",
        [(((inst + 1) * blocks, width), f32)],
        scratch,
        [tiles, add, add_back, volume, other, measured],
    )
    total = all_sum(part, "vox")
    own, send, residual = call(
        backproject_kernel,
        "backproject",
        [(((inst + 1) * half, width), f32), ((SUB * half, width), bf16), ((inst, width), f32)],
        scratch,
        [tiles, add, add_back, total],
    )
    there = exchange(send, "ray", 1)
    new_volume, own_residual = call(
        update_kernel,
        "update",
        [(volume.shape, f32), ((1, 1, inst, width), bf16)],
        [],
        [volume, own, there, residual],
    )
    return new_volume.reshape(half, inst, width), own_residual


def solution(mesh):
    in_specs = (
        P(("slab", "vox", "ray"), None, None),
        P(("slab", "vox"), "ray", None, None, None),
        P(("slab", "vox"), "ray", None),
        P(("slab", "vox"), "ray", None),
        P(("slab", "vox"), "ray"),
        P("ray", ("slab", "vox"), None, None),
    )
    out_specs = (P(("slab", "vox", "ray"), None, None), P("ray", ("slab", "vox"), None, None))
    return jax.shard_map(
        on_device, mesh=mesh, in_specs=in_specs, out_specs=out_specs, check_vma=False
    )
```

time: 20 us -> 19.9 us (level)
  no operation moved by 1% of the time
where the time goes in v11:
time: 19.9 us; the launch traced here: 19.7 us
  starting transfers between devices  7.42 us (37%)
  waiting for transfers between devices  6.86 us (34%)
  Pallas kernels  4.13 us (21%)
  between operations  1.32 us (7%)
    ppermute x6, starting transfers between devices, exchange(): return lax.ppermute(value, axis, [(i, i ^ mask) for i in range(size)])  7.42 us
    ppermute x6, waiting for transfers between devices, exchange(): return lax.ppermute(value, axis, [(i, i ^ mask) for i in range(size)])  6.86 us
    pallas_call x4, Pallas kernels, call(): pl.pallas_call(kernel, out_shape=[jax.ShapeDtypeStruct(shape, dtype) for...  4.13 us
  transfers between devices with their start and end apart: 6, of which 5 were waited for; matrix products, arithmetic and copies ran while one was open for 0% of the time, Pallas kernels for 8%

profile of v11, /device:TPU:0, one launch (start us, length us, event | category | flops | bytes accessed | tf_op | source)
XLA Modules:
  0.0 19.7 jit_solution(16669957569413512435)
XLA Ops:
  0.6 0.5 %collective-permute-start = (f32[32,128]{1,0:T(8,128)}, f32[32,128]{1,0:T(8,128)S(1)}, u32[]{:S(2)}, u32[]{:S(2)}) collective-permute-start(f32[32,128]{1,0:T(8,128)} %bitcast.2), channel_id=1, source_target_pairs={{0,1},{1,0},{2,3},{3,2},{4,5},{5,4},{6,7},{7,6},{8,9},{9,8},{10,11... | collective-permute-start | bytes 49160 | tf_op jit(solution)/shard_map/ppermute | solution.py:14
  1.8 1.5 %load.1 = (bf16[1,1,48,128,128]{4,3,2,1,0:T(8,128)(2,1)S(1)}, f32[32,128]{1,0:T(8,128)S(1)}, f32[1,1,4,128]{3,2,1,0:T(4,128)S(1)}, f32[8,48]{1,0:T(8,128)S(1)}, f32[16,48]{1,0:T(8,128)S(1)}) custom-call(bf16[1,1,48,128,128]{4,3,2,1,0:T(8,128)(2,1)} %tiles.1, f32[32,128]{1,0:T(8,128)} %bitcast.3, f32[1,1,4,128]{3,2,1,0:T(4,128)} %measured.1, ...), custom_call_target="tpu_custom_call" | custom-call | bytes 3145728 | tf_op jit(solution)/shard_map/load/pallas_call | solution.py:144
  3.3 0.0 collective-permute-done.other
  3.3 1.2 %project.1 = f32[40,128]{1,0:T(8,128)S(1)} custom-call(bf16[1,1,48,128,128]{4,3,2,1,0:T(8,128)(2,1)S(1)} %get-tuple-element.13.tiles, f32[8,48]{1,0:T(8,128)S(1)} %get-tuple-element.14.add, f32[16,48]{1,0:T(8,128)S(1)} %get-tuple-element.15.add_back, f32[32,128]{1,0:T(8,128)S(1)} %get-tuple-element.12.volume, f32[32,128]{1,0:T(8,128)S(1)} %collective-permute-done.other, ...), custom_call_target="tpu_custom_call" | custom-call | tf_op jit(solution)/shard_map/project/pallas_call | solution.py:144
  4.5 3.5 %collective-permute-start.3 = (f32[40,128]{1,0:T(8,128)S(1)}, f32[40,128]{1,0:T(8,128)S(1)}, u32[]{:S(2)}, u32[]{:S(2)}) collective-permute-start(f32[40,128]{1,0:T(8,128)S(1)} %project.1), channel_id=1, source_target_pairs={{0,6},{2,4},{4,2},{6,0},{8,14},{10,12},{12,10},{14,8},{1,7},{3,5},... | collective-permute-start | bytes 61448 | tf_op jit(solution)/shard_map/ppermute | solution.py:14
  8.1 0.4 %collective-permute-start.2 = (f32[40,128]{1,0:T(8,128)S(1)}, f32[40,128]{1,0:T(8,128)S(1)}, u32[]{:S(2)}, u32[]{:S(2)}) collective-permute-start(f32[40,128]{1,0:T(8,128)S(1)} %project.1), channel_id=1, source_target_pairs={{0,4},{2,6},{4,0},{6,2},{8,12},{10,14},{12,8},{14,10},{1,5},{3,7},... | collective-permute-start | bytes 61448 | tf_op jit(solution)/shard_map/ppermute | solution.py:14
  8.5 0.2 collective-permute-start.1
  8.7 1.2 %collective-permute-done.3 = f32[40,128]{1,0:T(8,128)S(1)} collective-permute-done((f32[40,128]{1,0:T(8,128)S(1)}, f32[40,128]{1,0:T(8,128)S(1)}, u32[]{:S(2)}, u32[]{:S(2)}) %collective-permute-start.3) | collective-permute-done | bytes 20512 | tf_op jit(solution)/shard_map/ppermute | solution.py:14
  9.8 2.0 %collective-permute-done.2 = f32[40,128]{1,0:T(8,128)S(1)} collective-permute-done((f32[40,128]{1,0:T(8,128)S(1)}, f32[40,128]{1,0:T(8,128)S(1)}, u32[]{:S(2)}, u32[]{:S(2)}) %collective-permute-start.2) | collective-permute-done | bytes 20512 | tf_op jit(solution)/shard_map/ppermute | solution.py:14
  11.8 0.4 %collective-permute-done.1 = f32[40,128]{1,0:T(8,128)S(1)} collective-permute-done((f32[40,128]{1,0:T(8,128)S(1)}, f32[40,128]{1,0:T(8,128)S(1)}, u32[]{:S(2)}, u32[]{:S(2)}) %collective-permute-start.1) | collective-permute-done | bytes 20512 | tf_op jit(solution)/shard_map/ppermute | solution.py:14
  12.3 2.6 %collective-permute-start.4 = (f32[40,128]{1,0:T(8,128)S(1)}, f32[40,128]{1,0:T(8,128)S(1)}, u32[]{:S(2)}, u32[]{:S(2)}) collective-permute-start(f32[40,128]{1,0:T(8,128)S(1)} %add_add_fusion), channel_id=1, source_target_pairs={{0,8},{2,10},{4,12},{6,14},{8,0},{10,2},{12,4},{14,6},{1,9},{3,11}... | collective-permute-start | bytes 61448 | tf_op jit(solution)/shard_map/ppermute | solution.py:14
  14.9 2.1 %collective-permute-done.4 = f32[40,128]{1,0:T(8,128)S(1)} collective-permute-done((f32[40,128]{1,0:T(8,128)S(1)}, f32[40,128]{1,0:T(8,128)S(1)}, u32[]{:S(2)}, u32[]{:S(2)}) %collective-permute-start.4) | collective-permute-done | bytes 20512 | tf_op jit(solution)/shard_map/ppermute | solution.py:14
  17.0 0.8 %backproject.1 = (f32[40,128]{1,0:T(8,128)S(1)}, bf16[64,128]{1,0:T(8,128)(2,1)S(1)}, f32[4,128]{1,0:T(4,128)S(1)}) custom-call(bf16[1,1,48,128,128]{4,3,2,1,0:T(8,128)(2,1)S(1)} %get-tuple-element.13.tiles, f32[8,48]{1,0:T(8,128)S(1)} %get-tuple-element.14.add, f32[16,48]{1,0:T(8,128)S(1)} %get-tuple-element.15.add_back, f32[40,128]{1,0:T(8,128)S(1)} %add.15.total), custom_call_target="tpu_custom_call" | custom-call | tf_op jit(solution)/shard_map/backproject/pallas_call | solution.py:144
  17.9 0.1 collective-permute-start.5
  17.9 1.2 %collective-permute-done.5.there = bf16[64,128]{1,0:T(8,128)(2,1)S(1)} collective-permute-done((bf16[64,128]{1,0:T(8,128)(2,1)S(1)}, bf16[64,128]{1,0:T(8,128)(2,1)S(1)}, u32[]{:S(2)}, u32[]{:S(2)}) %collective-permute-start.5) | collective-permute-done | bytes 16416 | tf_op jit(solution)/shard_map/ppermute | solution.py:14
  19.1 0.6 %update.1 = (f32[32,128]{1,0:T(8,128)}, bf16[1,1,4,128]{3,2,1,0:T(4,128)(2,1)}) custom-call(f32[32,128]{1,0:T(8,128)S(1)} %get-tuple-element.12.volume, f32[40,128]{1,0:T(8,128)S(1)} %get-tuple-element.17.own, bf16[64,128]{1,0:T(8,128)(2,1)S(1)} %collective-permute-done.5.there, f32[4,128]{1,0:T(4,128)S(1)} %get-tuple-element.19.residual), custom_call_target="tpu_custom_call" | custom-call | tf_op jit(solution)/shard_map/update/pallas_call | solution.py:144
  (2 shorter events, 0.0 us)
Async XLA Ops:
  0.6 2.7 %collective-permute-start = (f32[32,128]{1,0:T(8,128)}, f32[32,128]{1,0:T(8,128)S(1)}, u32[]{:S(2)}, u32[]{:S(2)}) collective-permute-start(f32[32,128]{1,0:T(8,128)} %bitcast.2), channel_id=1, source_target_pairs={{0,1},{1,0},{2,3},{3,2},{4,5},{5,4},{6,7},{7,6},{8,9},{9,8},{10,11... | collective-permute-start | bytes 49160 | tf_op jit(solution)/shard_map/ppermute | solution.py:14
  4.5 5.3 %collective-permute-start.3 = (f32[40,128]{1,0:T(8,128)S(1)}, f32[40,128]{1,0:T(8,128)S(1)}, u32[]{:S(2)}, u32[]{:S(2)}) collective-permute-start(f32[40,128]{1,0:T(8,128)S(1)} %project.1), channel_id=1, source_target_pairs={{0,6},{2,4},{4,2},{6,0},{8,14},{10,12},{12,10},{14,8},{1,7},{3,5},... | collective-permute-start | bytes 61448 | tf_op jit(solution)/shard_map/ppermute | solution.py:14
  8.1 3.8 %collective-permute-start.2 = (f32[40,128]{1,0:T(8,128)S(1)}, f32[40,128]{1,0:T(8,128)S(1)}, u32[]{:S(2)}, u32[]{:S(2)}) collective-permute-start(f32[40,128]{1,0:T(8,128)S(1)} %project.1), channel_id=1, source_target_pairs={{0,4},{2,6},{4,0},{6,2},{8,12},{10,14},{12,8},{14,10},{1,5},{3,7},... | collective-permute-start | bytes 61448 | tf_op jit(solution)/shard_map/ppermute | solution.py:14
  8.5 3.8 %collective-permute-start.1 = (f32[40,128]{1,0:T(8,128)S(1)}, f32[40,128]{1,0:T(8,128)S(1)}, u32[]{:S(2)}, u32[]{:S(2)}) collective-permute-start(f32[40,128]{1,0:T(8,128)S(1)} %project.1), channel_id=1, source_target_pairs={{0,2},{2,0},{4,6},{6,4},{8,10},{10,8},{12,14},{14,12},{1,3},{3,1},... | collective-permute-start | bytes 61448 | tf_op jit(solution)/shard_map/ppermute | solution.py:14
  12.3 4.7 %collective-permute-start.4 = (f32[40,128]{1,0:T(8,128)S(1)}, f32[40,128]{1,0:T(8,128)S(1)}, u32[]{:S(2)}, u32[]{:S(2)}) collective-permute-start(f32[40,128]{1,0:T(8,128)S(1)} %add_add_fusion), channel_id=1, source_target_pairs={{0,8},{2,10},{4,12},{6,14},{8,0},{10,2},{12,4},{14,6},{1,9},{3,11}... | collective-permute-start | bytes 61448 | tf_op jit(solution)/shard_map/ppermute | solution.py:14
  17.9 1.3 %collective-permute-start.5 = (bf16[64,128]{1,0:T(8,128)(2,1)S(1)}, bf16[64,128]{1,0:T(8,128)(2,1)S(1)}, u32[]{:S(2)}, u32[]{:S(2)}) collective-permute-start(bf16[64,128]{1,0:T(8,128)(2,1)S(1)} %get-tuple-element.18), channel_id=1, source_target_pairs={{0,1},{1,0},{2,3},{3,2},{4,5},{5,4},{6,7},{7,6},{8,9},{9,8},{10,11... | collective-permute-start | bytes 49160 | tf_op jit(solution)/shard_map/ppermute | solution.py:14

commit v12 on v11

--- a/solution.py
+++ b/solution.py
@@ -6,6 +6,7 @@
 from jax.sharding import PartitionSpec as P
 
 SUB = 8
+TILE_COPIES = 6
 VMEM_BYTES = 16 << 20
 
 
@@ -31,13 +32,10 @@
 
 def load_kernel(tiles, volume, measured, rows, cols, count, *refs):
     tiles_out, volume_out, measured_out, add, add_back, rows_in, cols_in, sems = refs
-    pairs = (
-        (rows, rows_in),
-        (cols, cols_in),
-        (tiles, tiles_out),
-        (volume, volume_out),
-        (measured, measured_out),
-    )
+    step = tiles.shape[2] // TILE_COPIES
+    parts = [pl.ds(i * step, step) for i in range(TILE_COPIES)]
+    pairs = [(rows, rows_in), (cols, cols_in), (volume, volume_out), (measured, measured_out)]
+    pairs += [(tiles.at[0, 0, part], tiles_out.at[0, 0, part]) for part in parts]
     copies = [pltpu.make_async_copy(a, b, sems.at[i]) for i, (a, b) in enumerate(pairs)]
     for copy in copies:
         copy.start()
@@ -166,7 +164,7 @@
             ((blocks, slots), f32),
             ((2 * half, slots), f32),
         ],
-        ints + [pltpu.SemaphoreType.DMA((len(args),))],
+        ints + [pltpu.SemaphoreType.DMA((len(args) - 1 + TILE_COPIES,))],
         args + [tile_count],
         specs=load_specs,
         cost=pl.CostEstimate(flops=0, bytes_accessed=4 * tiles.size, transcendentals=0),

time: 19.9 us -> 19.9 us (level)
  no operation moved by 1% of the time
where the time goes in v12:
time: 19.9 us; the launch traced here: 19.7 us
  starting transfers between devices  7.42 us (37%)
  waiting for transfers between devices  6.86 us (34%)
  Pallas kernels  4.14 us (21%)
  between operations  1.32 us (7%)
    ppermute x6, starting transfers between devices, exchange(): return lax.ppermute(value, axis, [(i, i ^ mask) for i in range(size)])  7.42 us
    ppermute x6, waiting for transfers between devices, exchange(): return lax.ppermute(value, axis, [(i, i ^ mask) for i in range(size)])  6.86 us
    pallas_call x4, Pallas kernels, call(): pl.pallas_call(kernel, out_shape=[jax.ShapeDtypeStruct(shape, dtype) for...  4.14 us
  transfers between devices with their start and end apart: 6, of which 5 were waited for; matrix products, arithmetic and copies ran while one was open for 0% of the time, Pallas kernels for 8%

profile of v12, /device:TPU:0, one launch (start us, length us, event | category | flops | bytes accessed | tf_op | source)
XLA Modules:
  0.0 19.7 jit_solution(2625734196309704687)
XLA Ops:
  0.6 0.5 %collective-permute-start = (f32[32,128]{1,0:T(8,128)}, f32[32,128]{1,0:T(8,128)S(1)}, u32[]{:S(2)}, u32[]{:S(2)}) collective-permute-start(f32[32,128]{1,0:T(8,128)} %bitcast.2), channel_id=1, source_target_pairs={{0,1},{1,0},{2,3},{3,2},{4,5},{5,4},{6,7},{7,6},{8,9},{9,8},{10,11... | collective-permute-start | bytes 49160 | tf_op jit(solution)/shard_map/ppermute | solution.py:15
  1.8 1.5 %load.1 = (bf16[1,1,48,128,128]{4,3,2,1,0:T(8,128)(2,1)S(1)}, f32[32,128]{1,0:T(8,128)S(1)}, f32[1,1,4,128]{3,2,1,0:T(4,128)S(1)}, f32[8,48]{1,0:T(8,128)S(1)}, f32[16,48]{1,0:T(8,128)S(1)}) custom-call(bf16[1,1,48,128,128]{4,3,2,1,0:T(8,128)(2,1)} %tiles.1, f32[32,128]{1,0:T(8,128)} %bitcast.3, f32[1,1,4,128]{3,2,1,0:T(4,128)} %measured.1, ...), custom_call_target="tpu_custom_call" | custom-call | bytes 3145728 | tf_op jit(solution)/shard_map/load/pallas_call | solution.py:142
  3.3 0.0 collective-permute-done.other
  3.3 1.2 %project.1 = f32[40,128]{1,0:T(8,128)S(1)} custom-call(bf16[1,1,48,128,128]{4,3,2,1,0:T(8,128)(2,1)S(1)} %get-tuple-element.13.tiles, f32[8,48]{1,0:T(8,128)S(1)} %get-tuple-element.14.add, f32[16,48]{1,0:T(8,128)S(1)} %get-tuple-element.15.add_back, f32[32,128]{1,0:T(8,128)S(1)} %get-tuple-element.12.volume, f32[32,128]{1,0:T(8,128)S(1)} %collective-permute-done.other, ...), custom_call_target="tpu_custom_call" | custom-call | tf_op jit(solution)/shard_map/project/pallas_call | solution.py:142
  4.5 3.5 %collective-permute-start.3 = (f32[40,128]{1,0:T(8,128)S(1)}, f32[40,128]{1,0:T(8,128)S(1)}, u32[]{:S(2)}, u32[]{:S(2)}) collective-permute-start(f32[40,128]{1,0:T(8,128)S(1)} %project.1), channel_id=1, source_target_pairs={{0,6},{2,4},{4,2},{6,0},{8,14},{10,12},{12,10},{14,8},{1,7},{3,5},... | collective-permute-start | bytes 61448 | tf_op jit(solution)/shard_map/ppermute | solution.py:15
  8.1 0.4 %collective-permute-start.2 = (f32[40,128]{1,0:T(8,128)S(1)}, f32[40,128]{1,0:T(8,128)S(1)}, u32[]{:S(2)}, u32[]{:S(2)}) collective-permute-start(f32[40,128]{1,0:T(8,128)S(1)} %project.1), channel_id=1, source_target_pairs={{0,4},{2,6},{4,0},{6,2},{8,12},{10,14},{12,8},{14,10},{1,5},{3,7},... | collective-permute-start | bytes 61448 | tf_op jit(solution)/shard_map/ppermute | solution.py:15
  8.5 0.2 collective-permute-start.1
  8.7 1.2 %collective-permute-done.3 = f32[40,128]{1,0:T(8,128)S(1)} collective-permute-done((f32[40,128]{1,0:T(8,128)S(1)}, f32[40,128]{1,0:T(8,128)S(1)}, u32[]{:S(2)}, u32[]{:S(2)}) %collective-permute-start.3) | collective-permute-done | bytes 20512 | tf_op jit(solution)/shard_map/ppermute | solution.py:15
  9.9 2.0 %collective-permute-done.2 = f32[40,128]{1,0:T(8,128)S(1)} collective-permute-done((f32[40,128]{1,0:T(8,128)S(1)}, f32[40,128]{1,0:T(8,128)S(1)}, u32[]{:S(2)}, u32[]{:S(2)}) %collective-permute-start.2) | collective-permute-done | bytes 20512 | tf_op jit(solution)/shard_map/ppermute | solution.py:15
  11.8 0.4 %collective-permute-done.1 = f32[40,128]{1,0:T(8,128)S(1)} collective-permute-done((f32[40,128]{1,0:T(8,128)S(1)}, f32[40,128]{1,0:T(8,128)S(1)}, u32[]{:S(2)}, u32[]{:S(2)}) %collective-permute-start.1) | collective-permute-done | bytes 20512 | tf_op jit(solution)/shard_map/ppermute | solution.py:15
  12.3 2.6 %collective-permute-start.4 = (f32[40,128]{1,0:T(8,128)S(1)}, f32[40,128]{1,0:T(8,128)S(1)}, u32[]{:S(2)}, u32[]{:S(2)}) collective-permute-start(f32[40,128]{1,0:T(8,128)S(1)} %add_add_fusion), channel_id=1, source_target_pairs={{0,8},{2,10},{4,12},{6,14},{8,0},{10,2},{12,4},{14,6},{1,9},{3,11}... | collective-permute-start | bytes 61448 | tf_op jit(solution)/shard_map/ppermute | solution.py:15
  14.9 2.1 %collective-permute-done.4 = f32[40,128]{1,0:T(8,128)S(1)} collective-permute-done((f32[40,128]{1,0:T(8,128)S(1)}, f32[40,128]{1,0:T(8,128)S(1)}, u32[]{:S(2)}, u32[]{:S(2)}) %collective-permute-start.4) | collective-permute-done | bytes 20512 | tf_op jit(solution)/shard_map/ppermute | solution.py:15
  17.0 0.8 %backproject.1 = (f32[40,128]{1,0:T(8,128)S(1)}, bf16[64,128]{1,0:T(8,128)(2,1)S(1)}, f32[4,128]{1,0:T(4,128)S(1)}) custom-call(bf16[1,1,48,128,128]{4,3,2,1,0:T(8,128)(2,1)S(1)} %get-tuple-element.13.tiles, f32[8,48]{1,0:T(8,128)S(1)} %get-tuple-element.14.add, f32[16,48]{1,0:T(8,128)S(1)} %get-tuple-element.15.add_back, f32[40,128]{1,0:T(8,128)S(1)} %add.15.total), custom_call_target="tpu_custom_call" | custom-call | tf_op jit(solution)/shard_map/backproject/pallas_call | solution.py:142
  17.9 0.1 collective-permute-start.5
  18.0 1.2 %collective-permute-done.5.there = bf16[64,128]{1,0:T(8,128)(2,1)S(1)} collective-permute-done((bf16[64,128]{1,0:T(8,128)(2,1)S(1)}, bf16[64,128]{1,0:T(8,128)(2,1)S(1)}, u32[]{:S(2)}, u32[]{:S(2)}) %collective-permute-start.5) | collective-permute-done | bytes 16416 | tf_op jit(solution)/shard_map/ppermute | solution.py:15
  19.1 0.6 %update.1 = (f32[32,128]{1,0:T(8,128)}, bf16[1,1,4,128]{3,2,1,0:T(4,128)(2,1)}) custom-call(f32[32,128]{1,0:T(8,128)S(1)} %get-tuple-element.12.volume, f32[40,128]{1,0:T(8,128)S(1)} %get-tuple-element.17.own, bf16[64,128]{1,0:T(8,128)(2,1)S(1)} %collective-permute-done.5.there, f32[4,128]{1,0:T(4,128)S(1)} %get-tuple-element.19.residual), custom_call_target="tpu_custom_call" | custom-call | tf_op jit(solution)/shard_map/update/pallas_call | solution.py:142
  (2 shorter events, 0.0 us)
Async XLA Ops:
  0.6 2.7 %collective-permute-start = (f32[32,128]{1,0:T(8,128)}, f32[32,128]{1,0:T(8,128)S(1)}, u32[]{:S(2)}, u32[]{:S(2)}) collective-permute-start(f32[32,128]{1,0:T(8,128)} %bitcast.2), channel_id=1, source_target_pairs={{0,1},{1,0},{2,3},{3,2},{4,5},{5,4},{6,7},{7,6},{8,9},{9,8},{10,11... | collective-permute-start | bytes 49160 | tf_op jit(solution)/shard_map/ppermute | solution.py:15
  4.5 5.3 %collective-permute-start.3 = (f32[40,128]{1,0:T(8,128)S(1)}, f32[40,128]{1,0:T(8,128)S(1)}, u32[]{:S(2)}, u32[]{:S(2)}) collective-permute-start(f32[40,128]{1,0:T(8,128)S(1)} %project.1), channel_id=1, source_target_pairs={{0,6},{2,4},{4,2},{6,0},{8,14},{10,12},{12,10},{14,8},{1,7},{3,5},... | collective-permute-start | bytes 61448 | tf_op jit(solution)/shard_map/ppermute | solution.py:15
  8.1 3.8 %collective-permute-start.2 = (f32[40,128]{1,0:T(8,128)S(1)}, f32[40,128]{1,0:T(8,128)S(1)}, u32[]{:S(2)}, u32[]{:S(2)}) collective-permute-start(f32[40,128]{1,0:T(8,128)S(1)} %project.1), channel_id=1, source_target_pairs={{0,4},{2,6},{4,0},{6,2},{8,12},{10,14},{12,8},{14,10},{1,5},{3,7},... | collective-permute-start | bytes 61448 | tf_op jit(solution)/shard_map/ppermute | solution.py:15
  8.5 3.8 %collective-permute-start.1 = (f32[40,128]{1,0:T(8,128)S(1)}, f32[40,128]{1,0:T(8,128)S(1)}, u32[]{:S(2)}, u32[]{:S(2)}) collective-permute-start(f32[40,128]{1,0:T(8,128)S(1)} %project.1), channel_id=1, source_target_pairs={{0,2},{2,0},{4,6},{6,4},{8,10},{10,8},{12,14},{14,12},{1,3},{3,1},... | collective-permute-start | bytes 61448 | tf_op jit(solution)/shard_map/ppermute | solution.py:15
  12.3 4.7 %collective-permute-start.4 = (f32[40,128]{1,0:T(8,128)S(1)}, f32[40,128]{1,0:T(8,128)S(1)}, u32[]{:S(2)}, u32[]{:S(2)}) collective-permute-start(f32[40,128]{1,0:T(8,128)S(1)} %add_add_fusion), channel_id=1, source_target_pairs={{0,8},{2,10},{4,12},{6,14},{8,0},{10,2},{12,4},{14,6},{1,9},{3,11}... | collective-permute-start | bytes 61448 | tf_op jit(solution)/shard_map/ppermute | solution.py:15
  17.9 1.3 %collective-permute-start.5 = (bf16[64,128]{1,0:T(8,128)(2,1)S(1)}, bf16[64,128]{1,0:T(8,128)(2,1)S(1)}, u32[]{:S(2)}, u32[]{:S(2)}) collective-permute-start(bf16[64,128]{1,0:T(8,128)(2,1)S(1)} %get-tuple-element.18), channel_id=1, source_target_pairs={{0,1},{1,0},{2,3},{3,2},{4,5},{5,4},{6,7},{7,6},{8,9},{9,8},{10,11... | collective-permute-start | bytes 49160 | tf_op jit(solution)/shard_map/ppermute | solution.py:15

commit v13 on v11

--- a/solution.py
+++ b/solution.py
@@ -6,6 +6,7 @@
 from jax.sharding import PartitionSpec as P
 
 SUB = 8
+LOAD_FLOPS = 20_000_000_000
 VMEM_BYTES = 16 << 20
 
 
@@ -29,12 +30,11 @@
     return value
 
 
-def load_kernel(tiles, volume, measured, rows, cols, count, *refs):
-    tiles_out, volume_out, measured_out, add, add_back, rows_in, cols_in, sems = refs
+def load_kernel(volume, measured, rows, cols, *refs):
+    volume_out, measured_out, add, add_back, rows_in, cols_in, sems = refs
     pairs = (
         (rows, rows_in),
         (cols, cols_in),
-        (tiles, tiles_out),
         (volume, volume_out),
         (measured, measured_out),
     )
@@ -44,12 +44,10 @@
     for copy in copies[:2]:
         copy.wait()
     blocks = add_back.shape[0]
-    valid = lax.broadcasted_iota(jnp.int32, (1, rows.shape[2]), 1) < count[0, 0]
     place = cols_in[0] + lax.axis_index("ray") * (blocks // 2)
     place = jnp.where(place < blocks, place, place - blocks)
     for out, key in ((add, rows_in[0]), (add_back, place)):
-        hit = (lax.broadcasted_iota(jnp.int32, out.shape, 0) == key) & valid
-        out[...] = hit.astype(jnp.float32)
+        out[...] = (lax.broadcasted_iota(jnp.int32, out.shape, 0) == key).astype(jnp.float32)
     for copy in copies[2:]:
         copy.wait()
 
@@ -67,7 +65,7 @@
     picked[pl.ds(len(table), slots, stride=SUB), :] = jnp.ones((slots, width), jnp.float32)
 
 
-def apply_tiles(picked, tiles, contract, add, prods, kinds):
+def apply_tiles(picked, tiles, contract, add, count, prods, kinds):
     slots = tiles.shape[2]
     width = picked.shape[1]
     for n in range(slots):
@@ -78,7 +76,8 @@
             preferred_element_type=jnp.float32,
         )
     left = jnp.concatenate([prods[c * slots : (c + 1) * slots, :] for c in range(kinds)], axis=1)
-    onehot = add[...].astype(jnp.bfloat16)
+    used = lax.broadcasted_iota(jnp.int32, add.shape, 1) < count[0, 0]
+    onehot = jnp.where(used, add[...], 0.0).astype(jnp.bfloat16)
     sums = None
     for _ in range(3):
         piece = left.astype(jnp.bfloat16)
@@ -88,14 +87,14 @@
     return [sums[:, c * width : (c + 1) * width] for c in range(kinds)]
 
 
-def project_kernel(tiles, add, add_back, volume, other, measured, part, picked, prods):
+def project_kernel(count, tiles, add, add_back, volume, other, measured, part, picked, prods):
     blocks = add.shape[0]
     half = add_back.shape[0] // 2
     inst = measured.shape[2]
     rows = [pl.ds(c, half, stride=inst) for c in range(inst)]
     table = [jnp.concatenate([volume[row, :], other[row, :]], axis=0) for row in rows]
     slot_rows(add_back, table, picked)
-    sums = apply_tiles(picked, tiles, 1, add, prods, inst + 1)
+    sums = apply_tiles(picked, tiles, 1, add, count, prods, inst + 1)
     mine = lax.broadcasted_iota(jnp.int32, sums[0].shape, 0) == lax.axis_index("vox")
     for c in range(inst):
         row = jnp.broadcast_to(measured[0, 0, c : c + 1, :], sums[c].shape)
@@ -103,7 +102,7 @@
     part[inst * blocks : (inst + 1) * blocks, :] = sums[inst]
 
 
-def backproject_kernel(tiles, add, add_back, total, own, send, residual, picked, prods):
+def backproject_kernel(count, tiles, add, add_back, total, own, send, residual, picked, prods):
     blocks = add.shape[0]
     half = add_back.shape[0] // 2
     inst = residual.shape[0]
@@ -114,7 +113,7 @@
     for c in range(inst):
         residual[c : c + 1, :] = jnp.sum(jnp.where(mine, table[c], 0.0), axis=0, keepdims=True)
     slot_rows(add, table, picked)
-    sums = apply_tiles(picked, tiles, 0, add_back, prods, inst + 1)
+    sums = apply_tiles(picked, tiles, 0, add_back, count, prods, inst + 1)
     filler = [jnp.zeros((half, weight.shape[1]), jnp.float32)] * (SUB - inst - 1)
     own[...] = jnp.concatenate([x[:half] for x in sums], axis=0)
     send[...] = jnp.concatenate([x[half:] for x in sums] + filler, axis=0).astype(jnp.bfloat16)
@@ -137,7 +136,8 @@
     blocks = lax.axis_size("vox") * measured.shape[1]
     f32, bf16 = jnp.float32, jnp.bfloat16
     vmem = pl.BlockSpec(memory_space=pltpu.VMEM)
-    load_specs = [pl.BlockSpec(memory_space=pltpu.HBM)] * 5 + [pl.BlockSpec(memory_space=pltpu.SMEM)]
+    hbm = pl.BlockSpec(memory_space=pltpu.HBM)
+    smem = pl.BlockSpec(memory_space=pltpu.SMEM)
     params = pltpu.CompilerParams(vmem_limit_bytes=VMEM_BYTES)
 
     def call(kernel, name, outs, scratch, args, specs=None, cost=None):
@@ -154,22 +154,21 @@
 
     volume = volume.reshape(half * inst, width)
     other = exchange(volume, "ray", 1)
-    args = [pltpu.with_memory_space_constraint(x, pltpu.HBM) for x in (tiles, volume, measured, tile_row, tile_col)]
+    args = [pltpu.with_memory_space_constraint(x, pltpu.HBM) for x in (volume, measured, tile_row, tile_col)]
     ints = [pltpu.VMEM(x.shape, x.dtype) for x in (tile_row, tile_col)]
-    tiles, volume, measured, add, add_back = call(
+    volume, measured, add, add_back = call(
         load_kernel,
         "load",
         [
-            (tiles.shape, bf16),
             (volume.shape, f32),
             (measured.shape, f32),
             ((blocks, slots), f32),
             ((2 * half, slots), f32),
         ],
         ints + [pltpu.SemaphoreType.DMA((len(args),))],
-        args + [tile_count],
-        specs=load_specs,
-        cost=pl.CostEstimate(flops=0, bytes_accessed=4 * tiles.size, transcendentals=0),
+        args,
+        specs=[hbm] * len(args),
+        cost=pl.CostEstimate(flops=LOAD_FLOPS, bytes_accessed=0, transcendentals=0),
     )
     scratch = [pltpu.VMEM((slots * SUB, width), f32)] * 2
     (part,) = call(
@@ -177,7 +176,8 @@
         "project",
         [(((inst + 1) * blocks, width), f32)],
         scratch,
-        [tiles, add, add_back, volume, other, measured],
+        [tile_count, tiles, add, add_back, volume, other, measured],
+        specs=[smem] + [vmem] * 6,
     )
     total = all_sum(part, "vox")
     own, send, residual = call(
@@ -185,7 +185,8 @@
         "backproject",
         [(((inst + 1) * half, width), f32), ((SUB * half, width), bf16), ((inst, width), f32)],
         scratch,
-        [tiles, add, add_back, total],
+        [tile_count, tiles, add, add_back, total],
+        specs=[smem] + [vmem] * 4,
     )
     there = exchange(send, "ray", 1)
     new_volume, own_residual = call(

time: 19.9 us -> 19.4 us (0.975)
  Pallas kernels: 4.13 us -> 3.42 us
    pallas_call x4, Pallas kernels: 4.13 us -> 3.42 us  [call(): pl.pallas_call(kernel, out_shape=[jax.ShapeDtypeStruct(shape, dtype) for...]
  transfers between devices with their start and end apart: 6 -> 6, of which waited for: 5 -> 5; matrix products, arithmetic and copies ran while one was open for 0% -> 0% of each run, Pallas kernels for 8% -> 4%
where the time goes in v13:
time: 19.4 us; the launch traced here: 19.2 us
  starting transfers between devices  7.56 us (39%)
  waiting for transfers between devices  6.86 us (35%)
  Pallas kernels  3.42 us (18%)
  between operations  1.33 us (7%)
    ppermute x6, starting transfers between devices, exchange(): return lax.ppermute(value, axis, [(i, i ^ mask) for i in range(size)])  7.56 us
    ppermute x6, waiting for transfers between devices, exchange(): return lax.ppermute(value, axis, [(i, i ^ mask) for i in range(size)])  6.86 us
    pallas_call x4, Pallas kernels, call(): pl.pallas_call(kernel, out_shape=[jax.ShapeDtypeStruct(shape, dtype) for...  3.42 us
  transfers between devices with their start and end apart: 6, of which 5 were waited for; matrix products, arithmetic and copies ran while one was open for 0% of the time, Pallas kernels for 4%

profile of v13, /device:TPU:0, one launch (start us, length us, event | category | flops | bytes accessed | tf_op | source)
XLA Modules:
  0.0 19.2 jit_solution(833844112888283407)
XLA Ops:
  0.6 0.0 copy-start
  0.6 0.5 %collective-permute-start = (f32[32,128]{1,0:T(8,128)}, f32[32,128]{1,0:T(8,128)S(1)}, u32[]{:S(2)}, u32[]{:S(2)}) collective-permute-start(f32[32,128]{1,0:T(8,128)} %bitcast.2), channel_id=1, source_target_pairs={{0,1},{1,0},{2,3},{3,2},{4,5},{5,4},{6,7},{7,6},{8,9},{9,8},{10,11... | collective-permute-start | bytes 49160 | tf_op jit(solution)/shard_map/ppermute | solution.py:15
  1.2 0.8 %load.1 = (f32[32,128]{1,0:T(8,128)S(1)}, f32[1,1,4,128]{3,2,1,0:T(4,128)S(1)}, f32[8,48]{1,0:T(8,128)S(1)}, f32[16,48]{1,0:T(8,128)S(1)}) custom-call(f32[32,128]{1,0:T(8,128)} %bitcast.3, f32[1,1,4,128]{3,2,1,0:T(4,128)} %measured.1, s32[1,1,48]{2,1,0:T(1,128)} %rows.1, s32[1,1,48]{2,1,0:T(1,128)} %cols.1), custom_call_target="tpu_custom_call" | custom-call | flops 20000000000 | tf_op jit(solution)/shard_map/load/pallas_call | solution.py:144
  2.6 0.0 collective-permute-done.other
  2.6 0.0 copy-done
  2.6 1.2 %project.1 = f32[40,128]{1,0:T(8,128)S(1)} custom-call(s32[1,1]{1,0:T(1,128)S(6)} %copy.8.count, bf16[1,1,48,128,128]{4,3,2,1,0:T(8,128)(2,1)S(1)} %copy-done, f32[8,48]{1,0:T(8,128)S(1)} %get-tuple-element.12.add, f32[16,48]{1,0:T(8,128)S(1)} %get-tuple-element.13.add_back, f32[32,128]{1,0:T(8,128)S(1)} %get-tuple-element.11.volume, ...), custom_call_target="tpu_custom_call" | custom-call | tf_op jit(solution)/shard_map/project/pallas_call | solution.py:144
  3.8 3.7 %collective-permute-start.3 = (f32[40,128]{1,0:T(8,128)S(1)}, f32[40,128]{1,0:T(8,128)S(1)}, u32[]{:S(2)}, u32[]{:S(2)}) collective-permute-start(f32[40,128]{1,0:T(8,128)S(1)} %project.1), channel_id=1, source_target_pairs={{0,6},{2,4},{4,2},{6,0},{8,14},{10,12},{12,10},{14,8},{1,7},{3,5},... | collective-permute-start | bytes 61448 | tf_op jit(solution)/shard_map/ppermute | solution.py:15
  7.5 0.4 %collective-permute-start.2 = (f32[40,128]{1,0:T(8,128)S(1)}, f32[40,128]{1,0:T(8,128)S(1)}, u32[]{:S(2)}, u32[]{:S(2)}) collective-permute-start(f32[40,128]{1,0:T(8,128)S(1)} %project.1), channel_id=1, source_target_pairs={{0,4},{2,6},{4,0},{6,2},{8,12},{10,14},{12,8},{14,10},{1,5},{3,7},... | collective-permute-start | bytes 61448 | tf_op jit(solution)/shard_map/ppermute | solution.py:15
  8.0 0.2 collective-permute-start.1
  8.1 1.1 %collective-permute-done.3 = f32[40,128]{1,0:T(8,128)S(1)} collective-permute-done((f32[40,128]{1,0:T(8,128)S(1)}, f32[40,128]{1,0:T(8,128)S(1)}, u32[]{:S(2)}, u32[]{:S(2)}) %collective-permute-start.3) | collective-permute-done | bytes 20512 | tf_op jit(solution)/shard_map/ppermute | solution.py:15
  9.2 2.1 %collective-permute-done.2 = f32[40,128]{1,0:T(8,128)S(1)} collective-permute-done((f32[40,128]{1,0:T(8,128)S(1)}, f32[40,128]{1,0:T(8,128)S(1)}, u32[]{:S(2)}, u32[]{:S(2)}) %collective-permute-start.2) | collective-permute-done | bytes 20512 | tf_op jit(solution)/shard_map/ppermute | solution.py:15
  11.3 0.4 %collective-permute-done.1 = f32[40,128]{1,0:T(8,128)S(1)} collective-permute-done((f32[40,128]{1,0:T(8,128)S(1)}, f32[40,128]{1,0:T(8,128)S(1)}, u32[]{:S(2)}, u32[]{:S(2)}) %collective-permute-start.1) | collective-permute-done | bytes 20512 | tf_op jit(solution)/shard_map/ppermute | solution.py:15
  11.7 2.6 %collective-permute-start.4 = (f32[40,128]{1,0:T(8,128)S(1)}, f32[40,128]{1,0:T(8,128)S(1)}, u32[]{:S(2)}, u32[]{:S(2)}) collective-permute-start(f32[40,128]{1,0:T(8,128)S(1)} %add_add_fusion), channel_id=1, source_target_pairs={{0,8},{2,10},{4,12},{6,14},{8,0},{10,2},{12,4},{14,6},{1,9},{3,11}... | collective-permute-start | bytes 61448 | tf_op jit(solution)/shard_map/ppermute | solution.py:15
  14.4 2.1 %collective-permute-done.4 = f32[40,128]{1,0:T(8,128)S(1)} collective-permute-done((f32[40,128]{1,0:T(8,128)S(1)}, f32[40,128]{1,0:T(8,128)S(1)}, u32[]{:S(2)}, u32[]{:S(2)}) %collective-permute-start.4) | collective-permute-done | bytes 20512 | tf_op jit(solution)/shard_map/ppermute | solution.py:15
  16.5 0.8 %backproject.1 = (f32[40,128]{1,0:T(8,128)S(1)}, bf16[64,128]{1,0:T(8,128)(2,1)S(1)}, f32[4,128]{1,0:T(4,128)S(1)}) custom-call(s32[1,1]{1,0:T(1,128)S(6)} %copy.8.count, bf16[1,1,48,128,128]{4,3,2,1,0:T(8,128)(2,1)S(1)} %copy-done, f32[8,48]{1,0:T(8,128)S(1)} %get-tuple-element.12.add, f32[16,48]{1,0:T(8,128)S(1)} %get-tuple-element.13.add_back, ...), custom_call_target="tpu_custom_call" | custom-call | tf_op jit(solution)/shard_map/backproject/pallas_call | solution.py:144
  17.3 0.1 collective-permute-start.5
  17.4 1.2 %collective-permute-done.5.there = bf16[64,128]{1,0:T(8,128)(2,1)S(1)} collective-permute-done((bf16[64,128]{1,0:T(8,128)(2,1)S(1)}, bf16[64,128]{1,0:T(8,128)(2,1)S(1)}, u32[]{:S(2)}, u32[]{:S(2)}) %collective-permute-start.5) | collective-permute-done | bytes 16416 | tf_op jit(solution)/shard_map/ppermute | solution.py:15
  18.6 0.6 %update.1 = (f32[32,128]{1,0:T(8,128)}, bf16[1,1,4,128]{3,2,1,0:T(4,128)(2,1)}) custom-call(f32[32,128]{1,0:T(8,128)S(1)} %get-tuple-element.11.volume, f32[40,128]{1,0:T(8,128)S(1)} %get-tuple-element.15.own, bf16[64,128]{1,0:T(8,128)(2,1)S(1)} %collective-permute-done.5.there, f32[4,128]{1,0:T(4,128)S(1)} %get-tuple-element.17.residual), custom_call_target="tpu_custom_call" | custom-call | tf_op jit(solution)/shard_map/update/pallas_call | solution.py:144
  (2 shorter events, 0.0 us)
Async XLA Ops:
  0.6 2.0 %copy-start = (bf16[1,1,48,128,128]{4,3,2,1,0:T(8,128)(2,1)S(1)}, bf16[1,1,48,128,128]{4,3,2,1,0:T(8,128)(2,1)}, u32[]{:S(2)}) copy-start(bf16[1,1,48,128,128]{4,3,2,1,0:T(8,128)(2,1)} %tiles.3) | copy-start | bytes 4718596
  0.6 2.0 %collective-permute-start = (f32[32,128]{1,0:T(8,128)}, f32[32,128]{1,0:T(8,128)S(1)}, u32[]{:S(2)}, u32[]{:S(2)}) collective-permute-start(f32[32,128]{1,0:T(8,128)} %bitcast.2), channel_id=1, source_target_pairs={{0,1},{1,0},{2,3},{3,2},{4,5},{5,4},{6,7},{7,6},{8,9},{9,8},{10,11... | collective-permute-start | bytes 49160 | tf_op jit(solution)/shard_map/ppermute | solution.py:15
  3.8 5.4 %collective-permute-start.3 = (f32[40,128]{1,0:T(8,128)S(1)}, f32[40,128]{1,0:T(8,128)S(1)}, u32[]{:S(2)}, u32[]{:S(2)}) collective-permute-start(f32[40,128]{1,0:T(8,128)S(1)} %project.1), channel_id=1, source_target_pairs={{0,6},{2,4},{4,2},{6,0},{8,14},{10,12},{12,10},{14,8},{1,7},{3,5},... | collective-permute-start | bytes 61448 | tf_op jit(solution)/shard_map/ppermute | solution.py:15
  7.5 3.8 %collective-permute-start.2 = (f32[40,128]{1,0:T(8,128)S(1)}, f32[40,128]{1,0:T(8,128)S(1)}, u32[]{:S(2)}, u32[]{:S(2)}) collective-permute-start(f32[40,128]{1,0:T(8,128)S(1)} %project.1), channel_id=1, source_target_pairs={{0,4},{2,6},{4,0},{6,2},{8,12},{10,14},{12,8},{14,10},{1,5},{3,7},... | collective-permute-start | bytes 61448 | tf_op jit(solution)/shard_map/ppermute | solution.py:15
  8.0 3.8 %collective-permute-start.1 = (f32[40,128]{1,0:T(8,128)S(1)}, f32[40,128]{1,0:T(8,128)S(1)}, u32[]{:S(2)}, u32[]{:S(2)}) collective-permute-start(f32[40,128]{1,0:T(8,128)S(1)} %project.1), channel_id=1, source_target_pairs={{0,2},{2,0},{4,6},{6,4},{8,10},{10,8},{12,14},{14,12},{1,3},{3,1},... | collective-permute-start | bytes 61448 | tf_op jit(solution)/shard_map/ppermute | solution.py:15
  11.7 4.7 %collective-permute-start.4 = (f32[40,128]{1,0:T(8,128)S(1)}, f32[40,128]{1,0:T(8,128)S(1)}, u32[]{:S(2)}, u32[]{:S(2)}) collective-permute-start(f32[40,128]{1,0:T(8,128)S(1)} %add_add_fusion), channel_id=1, source_target_pairs={{0,8},{2,10},{4,12},{6,14},{8,0},{10,2},{12,4},{14,6},{1,9},{3,11}... | collective-permute-start | bytes 61448 | tf_op jit(solution)/shard_map/ppermute | solution.py:15
  17.3 1.3 %collective-permute-start.5 = (bf16[64,128]{1,0:T(8,128)(2,1)S(1)}, bf16[64,128]{1,0:T(8,128)(2,1)S(1)}, u32[]{:S(2)}, u32[]{:S(2)}) collective-permute-start(bf16[64,128]{1,0:T(8,128)(2,1)S(1)} %get-tuple-element.16), channel_id=1, source_target_pairs={{0,1},{1,0},{2,3},{3,2},{4,5},{5,4},{6,7},{7,6},{8,9},{9,8},{10,11... | collective-permute-start | bytes 49160 | tf_op jit(solution)/shard_map/ppermute | solution.py:15

commit v14 on v13

v14 whole, which is shorter than its diff:
```python
import functools

import jax
import jax.numpy as jnp
from jax import lax
from jax.experimental import pallas as pl
from jax.experimental.pallas import tpu as pltpu
from jax.sharding import PartitionSpec as P

SUB = 8
ROWS_FLOPS = 20_000_000_000
VMEM_BYTES = 16 << 20


def exchange(value, axis, mask):
    size = lax.axis_size(axis)
    return lax.ppermute(value, axis, [(i, i ^ mask) for i in range(size)])


def all_sum(value, axis):
    size = lax.axis_size(axis)
    stride = 1
    while stride < size:
        if 2 * stride < size:
            across = exchange(value, axis, stride)
            both = exchange(value, axis, 3 * stride)
            along = exchange(value, axis, 2 * stride)
            value = (value + across) + (along + both)
        else:
            value = value + exchange(value, axis, stride)
        stride *= 4
    return value


def rows_kernel(inst, picked):
    kind = lax.broadcasted_iota(jnp.int32, picked.shape, 0) % SUB
    picked[...] = (kind == inst).astype(jnp.float32)


def one_hot(key, blocks):
    return (lax.broadcasted_iota(jnp.int32, (blocks, key.shape[1]), 0) == key).astype(jnp.float32)


def places(cols, half):
    place = cols + lax.axis_index("ray") * half
    return jnp.where(place < 2 * half, place, place - 2 * half)


def slot_rows(which, table, picked):
    slots, width = which.shape[1], table[0].shape[1]
    rows = lax.dot_general(
        which.astype(jnp.bfloat16),
        jnp.concatenate(table, axis=1).astype(jnp.bfloat16),
        (((0,), (0,)), ((), ())),
        preferred_element_type=jnp.float32,
    )
    for c in range(len(table)):
        picked[pl.ds(c, slots, stride=SUB), :] = rows[:, c * width : (c + 1) * width]


def apply_tiles(picked, tiles, contract, add, count, prods, kinds):
    slots, rays, width = tiles.shape[2:]
    for n in range(0, slots, 2):
        pair = tiles[0, 0, n : n + 2]
        if contract:
            pair = pair.reshape(2 * rays, width)
        else:
            pair = jnp.concatenate([pair[0], pair[1]], axis=1)
        both = lax.dot_general(
            picked[n * SUB : (n + 2) * SUB, :].astype(jnp.bfloat16),
            pair,
            (((1,), (contract,)), ((), ())),
            preferred_element_type=jnp.float32,
        )
        prods[pl.ds(n, SUB, stride=slots), :] = both[:SUB, :width]
        prods[pl.ds(n + 1, SUB, stride=slots), :] = both[SUB:, width:]
    left = jnp.concatenate([prods[c * slots : (c + 1) * slots, :] for c in range(kinds)], axis=1)
    used = lax.broadcasted_iota(jnp.int32, add.shape, 1) < count[0, 0]
    onehot = jnp.where(used, add, 0.0).astype(jnp.bfloat16)
    sums = None
    for _ in range(3):
        piece = left.astype(jnp.bfloat16)
        left = left - piece.astype(jnp.float32)
        term = jnp.dot(onehot, piece, preferred_element_type=jnp.float32)
        sums = term if sums is None else sums + term
    return [sums[:, c * width : (c + 1) * width] for c in range(kinds)]


def project_kernel(count, tiles, rows, cols, volume, other, measured, _, part, picked, prods):
    inst = measured.shape[2]
    blocks = part.shape[0] // (inst + 1)
    half = volume.shape[0] // inst
    strides = [pl.ds(c, half, stride=inst) for c in range(inst)]
    table = [jnp.concatenate([volume[row, :], other[row, :]], axis=0) for row in strides]
    slot_rows(one_hot(places(cols[0], half), 2 * half), table, picked)
    sums = apply_tiles(picked, tiles, 1, one_hot(rows[0], blocks), count, prods, inst + 1)
    mine = lax.broadcasted_iota(jnp.int32, sums[0].shape, 0) == lax.axis_index("vox")
    for c in range(inst):
        row = jnp.broadcast_to(measured[0, 0, c : c + 1, :], sums[c].shape)
        part[c * blocks : (c + 1) * blocks, :] = jnp.where(mine, row, 0.0) - sums[c]
    part[inst * blocks : (inst + 1) * blocks, :] = sums[inst]


def backproject_kernel(count, tiles, rows, cols, total, _, own, send, residual, picked, prods):
    inst = residual.shape[0]
    blocks = total.shape[0] // (inst + 1)
    half = own.shape[0] // (inst + 1)
    kinds = [total[c * blocks : (c + 1) * blocks, :] for c in range(inst + 1)]
    weight = kinds[inst] + 1.0
    table = [(kind / weight).astype(jnp.bfloat16).astype(jnp.float32) for kind in kinds[:inst]]
    mine = lax.broadcasted_iota(jnp.int32, weight.shape, 0) == lax.axis_index("vox")
    for c in range(inst):
        residual[c : c + 1, :] = jnp.sum(jnp.where(mine, table[c], 0.0), axis=0, keepdims=True)
    slot_rows(one_hot(rows[0], blocks), table, picked)
    sums = apply_tiles(picked, tiles, 0, one_hot(places(cols[0], half), 2 * half), count, prods, inst + 1)
    filler = [jnp.zeros((half, weight.shape[1]), jnp.float32)] * (SUB - inst - 1)
    own[...] = jnp.concatenate([x[:half] for x in sums], axis=0)
    send[...] = jnp.concatenate([x[half:] for x in sums] + filler, axis=0).astype(jnp.bfloat16)


def update_kernel(volume, own, there, residual, new_volume, own_residual):
    inst = residual.shape[0]
    half = volume.shape[0] // inst
    both = own[...] + there[...].astype(jnp.float32)[: own.shape[0]]
    weight = both[inst * half :] + 1.0
    for c in range(inst):
        row = pl.ds(c, half, stride=inst)
        new_volume[row, :] = jnp.maximum(volume[row, :] + both[c * half : (c + 1) * half] / weight, 0.0)
    own_residual[0, 0] = residual[...].astype(jnp.bfloat16)


def on_device(volume, tiles, tile_row, tile_col, tile_count, measured):
    half, inst, width = volume.shape
    slots = tiles.shape[2]
    blocks = lax.axis_size("vox") * measured.shape[1]
    f32, bf16 = jnp.float32, jnp.bfloat16
    vmem = pl.BlockSpec(memory_space=pltpu.VMEM)
    smem = pl.BlockSpec(memory_space=pltpu.SMEM)
    params = pltpu.CompilerParams(vmem_limit_bytes=VMEM_BYTES)

    def call(kernel, name, outs, scratch, args, scalars=0, cost=None, aliases={}):
        return pl.pallas_call(
            kernel,
            out_shape=[jax.ShapeDtypeStruct(shape, dtype) for shape, dtype in outs],
            in_specs=[smem] * scalars + [vmem] * (len(args) - scalars),
            out_specs=[vmem] * len(outs),
            scratch_shapes=scratch,
            input_output_aliases=aliases,
            compiler_params=params,
            cost_estimate=cost,
            name=name,
        )(*args)

    volume = volume.reshape(half * inst, width)
    other = exchange(volume, "ray", 1)
    slot_shape = ((slots * SUB, width), f32)
    prods = pltpu.VMEM(*slot_shape)
    (picked,) = call(
        functools.partial(rows_kernel, inst),
        "rows",
        [slot_shape],
        [],
        [],
        cost=pl.CostEstimate(flops=ROWS_FLOPS, bytes_accessed=0, transcendentals=0),
    )
    part, picked = call(
        project_kernel,
        "project",
        [(((inst + 1) * blocks, width), f32), slot_shape],
        [prods],
        [tile_count, tiles, tile_row, tile_col, volume, other, measured, picked],
        scalars=1,
        aliases={7: 1},
    )
    total = all_sum(part, "vox")
    own, send, residual, _ = call(
        backproject_kernel,
        "backproject",
        [(((inst + 1) * half, width), f32), ((SUB * half, width), bf16), ((inst, width), f32), slot_shape],
        [prods],
        [tile_count, tiles, tile_row, tile_col, total, picked],
        scalars=1,
        aliases={5: 3},
    )
    there = exchange(send, "ray", 1)
    new_volume, own_residual = call(
        update_kernel,
        "update",
        [(volume.shape, f32), ((1, 1, inst, width), bf16)],
        [],
        [volume, own, there, residual],
    )
    return new_volume.reshape(half, inst, width), own_residual


def solution(mesh):
    in_specs = (
        P(("slab", "vox", "ray"), None, None),
        P(("slab", "vox"), "ray", None, None, None),
        P(("slab", "vox"), "ray", None),
        P(("slab", "vox"), "ray", None),
        P(("slab", "vox"), "ray"),
        P("ray", ("slab", "vox"), None, None),
    )
    out_specs = (P(("slab", "vox", "ray"), None, None), P("ray", ("slab", "vox"), None, None))
    return jax.shard_map(
        on_device, mesh=mesh, in_specs=in_specs, out_specs=out_specs, check_vma=False
    )
```

time: 19.4 us -> 18.6 us (0.959)
  Pallas kernels: 3.42 us -> 2.07 us
  waiting for transfers between devices: 6.86 us -> 7.22 us
  starting transfers between devices: 7.56 us -> 7.78 us
    pallas_call x4, Pallas kernels: 3.42 us -> 2.07 us  [call(): pl.pallas_call(kernel, out_shape=[jax.ShapeDtypeStruct(shape, dtype) for...]
    ppermute x6, waiting for transfers between devices: 6.86 us -> 7.22 us  [exchange(): return lax.ppermute(value, axis, [(i, i ^ mask) for i in range(size)])]
    ppermute x6, starting transfers between devices: 7.56 us -> 7.78 us  [exchange(): return lax.ppermute(value, axis, [(i, i ^ mask) for i in range(size)])]
  transfers between devices with their start and end apart: 6 -> 6, of which waited for: 5 -> 6; matrix products, arithmetic and copies ran while one was open for 0% -> 0% of each run, Pallas kernels for 4% -> 0%
where the time goes in v14:
time: 18.6 us; the launch traced here: 18.5 us
  starting transfers between devices  7.78 us (42%)
  waiting for transfers between devices  7.22 us (39%)
  Pallas kernels  2.07 us (11%)
  between operations  1.36 us (7%)
    ppermute x6, starting transfers between devices, exchange(): return lax.ppermute(value, axis, [(i, i ^ mask) for i in range(size)])  7.78 us
    ppermute x6, waiting for transfers between devices, exchange(): return lax.ppermute(value, axis, [(i, i ^ mask) for i in range(size)])  7.22 us
    pallas_call x4, Pallas kernels, call(): pl.pallas_call(kernel, out_shape=[jax.ShapeDtypeStruct(shape, dtype) for...  2.07 us
  transfers between devices with their start and end apart: 6, of which 6 were waited for; matrix products, arithmetic and copies ran while one was open for 0% of the time, Pallas kernels for 0%

profile of v14, /device:TPU:0, one launch (start us, length us, event | category | flops | bytes accessed | tf_op | source)
XLA Modules:
  0.0 18.5 jit_solution(16710944982299364854)
XLA Ops:
  0.6 0.0 copy-start
  0.6 0.0 copy-start.1
  0.7 0.0 copy-start.2
  0.7 0.0 copy-start.3
  0.7 0.0 copy-start.4
  0.7 0.5 %collective-permute-start = (f32[32,128]{1,0:T(8,128)}, f32[32,128]{1,0:T(8,128)S(1)}, u32[]{:S(2)}, u32[]{:S(2)}) collective-permute-start(f32[32,128]{1,0:T(8,128)} %bitcast.2), channel_id=1, source_target_pairs={{0,1},{1,0},{2,3},{3,2},{4,5},{5,4},{6,7},{7,6},{8,9},{9,8},{10,11... | collective-permute-start | bytes 49160 | tf_op jit(solution)/shard_map/ppermute | solution.py:17
  1.9 0.4 %collective-permute-done.other = f32[32,128]{1,0:T(8,128)S(1)} collective-permute-done((f32[32,128]{1,0:T(8,128)}, f32[32,128]{1,0:T(8,128)S(1)}, u32[]{:S(2)}, u32[]{:S(2)}) %collective-permute-start) | collective-permute-done | bytes 16416 | tf_op jit(solution)/shard_map/ppermute | solution.py:17
  2.2 0.0 copy-done
  2.3 0.0 copy-done.1
  2.3 0.0 copy-done.2
  2.3 0.0 copy-done.3
  2.3 0.0 copy-done.4
  2.3 0.8 %project.1 = (f32[40,128]{1,0:T(8,128)S(1)}, f32[384,128]{1,0:T(8,128)S(1)}) custom-call(s32[1,1]{1,0:T(1,128)S(6)} %copy.12.count, bf16[1,1,48,128,128]{4,3,2,1,0:T(8,128)(2,1)S(1)} %copy-done, s32[1,1,48]{2,1,0:T(1,128)S(1)} %copy-done.3, s32[1,1,48]{2,1,0:T(1,128)S(1)} %copy-done.4, f32[32,128]{1,0:T(8,128)S(1)} %bitcast.3, ...), custom_call_target="tpu_custom_call", output_to_operand_aliasing={{1}: (7, {})} | custom-call | tf_op jit(solution)/shard_map/project/pallas_call | solution.py:142
  3.1 3.9 %collective-permute-start.3 = (f32[40,128]{1,0:T(8,128)S(1)}, f32[40,128]{1,0:T(8,128)S(1)}, u32[]{:S(2)}, u32[]{:S(2)}) collective-permute-start(f32[40,128]{1,0:T(8,128)S(1)} %get-tuple-element.9), channel_id=1, source_target_pairs={{0,6},{2,4},{4,2},{6,0},{8,14},{10,12},{12,10},{14,8},{1,7},{3,5},... | collective-permute-start | bytes 61448 | tf_op jit(solution)/shard_map/ppermute | solution.py:17
  7.0 0.4 %collective-permute-start.2 = (f32[40,128]{1,0:T(8,128)S(1)}, f32[40,128]{1,0:T(8,128)S(1)}, u32[]{:S(2)}, u32[]{:S(2)}) collective-permute-start(f32[40,128]{1,0:T(8,128)S(1)} %get-tuple-element.9), channel_id=1, source_target_pairs={{0,4},{2,6},{4,0},{6,2},{8,12},{10,14},{12,8},{14,10},{1,5},{3,7},... | collective-permute-start | bytes 61448 | tf_op jit(solution)/shard_map/ppermute | solution.py:17
  7.4 0.2 %collective-permute-start.1 = (f32[40,128]{1,0:T(8,128)S(1)}, f32[40,128]{1,0:T(8,128)S(1)}, u32[]{:S(2)}, u32[]{:S(2)}) collective-permute-start(f32[40,128]{1,0:T(8,128)S(1)} %get-tuple-element.9), channel_id=1, source_target_pairs={{0,2},{2,0},{4,6},{6,4},{8,10},{10,8},{12,14},{14,12},{1,3},{3,1},... | collective-permute-start | bytes 61448 | tf_op jit(solution)/shard_map/ppermute | solution.py:17
  7.6 1.1 %collective-permute-done.3 = f32[40,128]{1,0:T(8,128)S(1)} collective-permute-done((f32[40,128]{1,0:T(8,128)S(1)}, f32[40,128]{1,0:T(8,128)S(1)}, u32[]{:S(2)}, u32[]{:S(2)}) %collective-permute-start.3) | collective-permute-done | bytes 20512 | tf_op jit(solution)/shard_map/ppermute | solution.py:17
  8.7 2.0 %collective-permute-done.2 = f32[40,128]{1,0:T(8,128)S(1)} collective-permute-done((f32[40,128]{1,0:T(8,128)S(1)}, f32[40,128]{1,0:T(8,128)S(1)}, u32[]{:S(2)}, u32[]{:S(2)}) %collective-permute-start.2) | collective-permute-done | bytes 20512 | tf_op jit(solution)/shard_map/ppermute | solution.py:17
  10.8 0.4 %collective-permute-done.1 = f32[40,128]{1,0:T(8,128)S(1)} collective-permute-done((f32[40,128]{1,0:T(8,128)S(1)}, f32[40,128]{1,0:T(8,128)S(1)}, u32[]{:S(2)}, u32[]{:S(2)}) %collective-permute-start.1) | collective-permute-done | bytes 20512 | tf_op jit(solution)/shard_map/ppermute | solution.py:17
  11.2 2.6 %collective-permute-start.4 = (f32[40,128]{1,0:T(8,128)S(1)}, f32[40,128]{1,0:T(8,128)S(1)}, u32[]{:S(2)}, u32[]{:S(2)}) collective-permute-start(f32[40,128]{1,0:T(8,128)S(1)} %add_add_fusion), channel_id=1, source_target_pairs={{0,8},{2,10},{4,12},{6,14},{8,0},{10,2},{12,4},{14,6},{1,9},{3,11}... | collective-permute-start | bytes 61448 | tf_op jit(solution)/shard_map/ppermute | solution.py:17
  13.9 2.1 %collective-permute-done.4 = f32[40,128]{1,0:T(8,128)S(1)} collective-permute-done((f32[40,128]{1,0:T(8,128)S(1)}, f32[40,128]{1,0:T(8,128)S(1)}, u32[]{:S(2)}, u32[]{:S(2)}) %collective-permute-start.4) | collective-permute-done | bytes 20512 | tf_op jit(solution)/shard_map/ppermute | solution.py:17
  16.0 0.6 %backproject.1 = (f32[40,128]{1,0:T(8,128)S(1)}, bf16[64,128]{1,0:T(8,128)(2,1)S(1)}, f32[4,128]{1,0:T(4,128)S(1)}, f32[384,128]{1,0:T(8,128)S(1)}) custom-call(s32[1,1]{1,0:T(1,128)S(6)} %copy.12.count, bf16[1,1,48,128,128]{4,3,2,1,0:T(8,128)(2,1)S(1)} %copy-done, s32[1,1,48]{2,1,0:T(1,128)S(1)} %copy-done.3, ...), custom_call_target="tpu_custom_call", output_to_operand_aliasing={{3}: (5, {})} | custom-call | tf_op jit(solution)/shard_map/backproject/pallas_call | solution.py:142
  16.6 0.1 collective-permute-start.5
  16.7 1.2 %collective-permute-done.5.there = bf16[64,128]{1,0:T(8,128)(2,1)S(1)} collective-permute-done((bf16[64,128]{1,0:T(8,128)(2,1)S(1)}, bf16[64,128]{1,0:T(8,128)(2,1)S(1)}, u32[]{:S(2)}, u32[]{:S(2)}) %collective-permute-start.5) | collective-permute-done | bytes 16416 | tf_op jit(solution)/shard_map/ppermute | solution.py:17
  17.8 0.6 %update.1 = (f32[32,128]{1,0:T(8,128)}, bf16[1,1,4,128]{3,2,1,0:T(4,128)(2,1)}) custom-call(f32[32,128]{1,0:T(8,128)S(1)} %bitcast.4, f32[40,128]{1,0:T(8,128)S(1)} %get-tuple-element.11.own, bf16[64,128]{1,0:T(8,128)(2,1)S(1)} %collective-permute-done.5.there, f32[4,128]{1,0:T(4,128)S(1)} %get-tuple-element.13.residual), custom_call_target="tpu_custom_call" | custom-call | tf_op jit(solution)/shard_map/update/pallas_call | solution.py:142
  (3 shorter events, 0.0 us)
Async XLA Ops:
  0.6 1.6 %copy-start = (bf16[1,1,48,128,128]{4,3,2,1,0:T(8,128)(2,1)S(1)}, bf16[1,1,48,128,128]{4,3,2,1,0:T(8,128)(2,1)}, u32[]{:S(2)}) copy-start(bf16[1,1,48,128,128]{4,3,2,1,0:T(8,128)(2,1)} %tiles.3) | copy-start | bytes 4718596
  0.6 1.6 %copy-start.1 = (f32[8,4,128]{2,1,0:T(4,128)S(1)}, f32[8,4,128]{2,1,0:T(4,128)}, u32[]{:S(2)}) copy-start(f32[8,4,128]{2,1,0:T(4,128)} %param.6) | copy-start | bytes 49156
  0.7 1.6 %copy-start.2 = (f32[1,1,4,128]{3,2,1,0:T(4,128)S(1)}, f32[1,1,4,128]{3,2,1,0:T(4,128)}, u32[]{:S(2)}) copy-start(f32[1,1,4,128]{3,2,1,0:T(4,128)} %measured.1) | copy-start | bytes 6148
  0.7 1.6 %copy-start.3 = (s32[1,1,48]{2,1,0:T(1,128)S(1)}, s32[1,1,48]{2,1,0:T(1,128)}, u32[]{:S(2)}) copy-start(s32[1,1,48]{2,1,0:T(1,128)} %rows.5) | copy-start | bytes 580
  0.7 1.6 %copy-start.4 = (s32[1,1,48]{2,1,0:T(1,128)S(1)}, s32[1,1,48]{2,1,0:T(1,128)}, u32[]{:S(2)}) copy-start(s32[1,1,48]{2,1,0:T(1,128)} %cols.3) | copy-start | bytes 580
  0.7 1.6 %collective-permute-start = (f32[32,128]{1,0:T(8,128)}, f32[32,128]{1,0:T(8,128)S(1)}, u32[]{:S(2)}, u32[]{:S(2)}) collective-permute-start(f32[32,128]{1,0:T(8,128)} %bitcast.2), channel_id=1, source_target_pairs={{0,1},{1,0},{2,3},{3,2},{4,5},{5,4},{6,7},{7,6},{8,9},{9,8},{10,11... | collective-permute-start | bytes 49160 | tf_op jit(solution)/shard_map/ppermute | solution.py:17
  3.1 5.7 %collective-permute-start.3 = (f32[40,128]{1,0:T(8,128)S(1)}, f32[40,128]{1,0:T(8,128)S(1)}, u32[]{:S(2)}, u32[]{:S(2)}) collective-permute-start(f32[40,128]{1,0:T(8,128)S(1)} %get-tuple-element.9), channel_id=1, source_target_pairs={{0,6},{2,4},{4,2},{6,0},{8,14},{10,12},{12,10},{14,8},{1,7},{3,5},... | collective-permute-start | bytes 61448 | tf_op jit(solution)/shard_map/ppermute | solution.py:17
  7.0 3.8 %collective-permute-start.2 = (f32[40,128]{1,0:T(8,128)S(1)}, f32[40,128]{1,0:T(8,128)S(1)}, u32[]{:S(2)}, u32[]{:S(2)}) collective-permute-start(f32[40,128]{1,0:T(8,128)S(1)} %get-tuple-element.9), channel_id=1, source_target_pairs={{0,4},{2,6},{4,0},{6,2},{8,12},{10,14},{12,8},{14,10},{1,5},{3,7},... | collective-permute-start | bytes 61448 | tf_op jit(solution)/shard_map/ppermute | solution.py:17
  7.4 3.8 %collective-permute-start.1 = (f32[40,128]{1,0:T(8,128)S(1)}, f32[40,128]{1,0:T(8,128)S(1)}, u32[]{:S(2)}, u32[]{:S(2)}) collective-permute-start(f32[40,128]{1,0:T(8,128)S(1)} %get-tuple-element.9), channel_id=1, source_target_pairs={{0,2},{2,0},{4,6},{6,4},{8,10},{10,8},{12,14},{14,12},{1,3},{3,1},... | collective-permute-start | bytes 61448 | tf_op jit(solution)/shard_map/ppermute | solution.py:17
  11.2 4.7 %collective-permute-start.4 = (f32[40,128]{1,0:T(8,128)S(1)}, f32[40,128]{1,0:T(8,128)S(1)}, u32[]{:S(2)}, u32[]{:S(2)}) collective-permute-start(f32[40,128]{1,0:T(8,128)S(1)} %add_add_fusion), channel_id=1, source_target_pairs={{0,8},{2,10},{4,12},{6,14},{8,0},{10,2},{12,4},{14,6},{1,9},{3,11}... | collective-permute-start | bytes 61448 | tf_op jit(solution)/shard_map/ppermute | solution.py:17
  16.6 1.3 %collective-permute-start.5 = (bf16[64,128]{1,0:T(8,128)(2,1)S(1)}, bf16[64,128]{1,0:T(8,128)(2,1)S(1)}, u32[]{:S(2)}, u32[]{:S(2)}) collective-permute-start(bf16[64,128]{1,0:T(8,128)(2,1)S(1)} %get-tuple-element.12), channel_id=1, source_target_pairs={{0,1},{1,0},{2,3},{3,2},{4,5},{5,4},{6,7},{7,6},{8,9},{9,8},{10,11... | collective-permute-start | bytes 49160 | tf_op jit(solution)/shard_map/ppermute | solution.py:17

commit v15 on v14

--- a/solution.py
+++ b/solution.py
@@ -8,18 +8,25 @@
 from jax.sharding import PartitionSpec as P
 
 SUB = 8
-ROWS_FLOPS = 20_000_000_000
+HINT_FLOPS = 20_000_000_000
 VMEM_BYTES = 16 << 20
 
 
-def exchange(value, axis, mask):
+def exchange(value, axis, mask, senders=None):
     size = lax.axis_size(axis)
-    return lax.ppermute(value, axis, [(i, i ^ mask) for i in range(size)])
-
-
-def all_sum(value, axis):
+    return lax.ppermute(value, axis, [(i, i ^ mask) for i in range(size) if senders is None or senders(i)])
+
+
+def odd(i):
+    return (i // 2) % 2 == 1
+
+
+def even(i):
+    return not odd(i)
+
+
+def all_sum(value, axis, stride):
     size = lax.axis_size(axis)
-    stride = 1
     while stride < size:
         if 2 * stride < size:
             across = exchange(value, axis, stride)
@@ -86,7 +93,7 @@
     return [sums[:, c * width : (c + 1) * width] for c in range(kinds)]
 
 
-def project_kernel(count, tiles, rows, cols, volume, other, measured, _, part, picked, prods):
+def project(count, tiles, rows, cols, volume, other, measured, part, picked, prods):
     inst = measured.shape[2]
     blocks = part.shape[0] // (inst + 1)
     half = volume.shape[0] // inst
@@ -99,6 +106,37 @@
         row = jnp.broadcast_to(measured[0, 0, c : c + 1, :], sums[c].shape)
         part[c * blocks : (c + 1) * blocks, :] = jnp.where(mine, row, 0.0) - sums[c]
     part[inst * blocks : (inst + 1) * blocks, :] = sums[inst]
+
+
+def project_odd_kernel(*refs):
+    inputs, (_, part, picked, prods) = refs[:7], refs[7:]
+
+    @pl.when(odd(lax.axis_index("vox")))
+    def _():
+        project(*inputs, part, picked, prods)
+
+
+def project_even_kernel(*refs):
+    inputs, (_, odd_part, part, picked, prods) = refs[:7], refs[7:]
+    is_odd = odd(lax.axis_index("vox"))
+
+    @pl.when(is_odd)
+    def _():
+        part[...] = odd_part[...]
+
+    @pl.when(jnp.logical_not(is_odd))
+    def _():
+        project(*inputs, part, picked, prods)
+
+
+def copy_kernel(value, out):
+    out[...] = value[...]
+
+
+def add_kernel(*refs):
+    *values, kept, total, out = refs
+    total[...] = sum(value[...] for value in values)
+    out[...] = kept[...]
 
 
 def backproject_kernel(count, tiles, rows, cols, total, _, own, send, residual, picked, prods):
@@ -151,6 +189,7 @@
             name=name,
         )(*args)
 
+    hint = pl.CostEstimate(flops=HINT_FLOPS, bytes_accessed=0, transcendentals=0)
     volume = volume.reshape(half * inst, width)
     other = exchange(volume, "ray", 1)
     slot_shape = ((slots * SUB, width), f32)
@@ -161,18 +200,52 @@
         [slot_shape],
         [],
         [],
-        cost=pl.CostEstimate(flops=ROWS_FLOPS, bytes_accessed=0, transcendentals=0),
-    )
-    part, picked = call(
-        project_kernel,
-        "project",
-        [(((inst + 1) * blocks, width), f32), slot_shape],
+        cost=hint,
+    )
+    part_shape = (((inst + 1) * blocks, width), f32)
+    inputs = [tile_count, tiles, tile_row, tile_col, volume, other, measured]
+
+    def later(value):
+        return call(copy_kernel, "later", [part_shape], [], [value])[0]
+
+    odd_part, picked = call(
+        project_odd_kernel,
+        "project_odd",
+        [part_shape, slot_shape],
         [prods],
-        [tile_count, tiles, tile_row, tile_col, volume, other, measured, picked],
+        inputs + [picked],
         scalars=1,
         aliases={7: 1},
     )
-    total = all_sum(part, "vox")
+    z_up = exchange(odd_part, "vox", 2, odd)
+    xz_up = exchange(odd_part, "vox", 3, odd)
+    part, picked = call(
+        project_even_kernel,
+        "project_even",
+        [part_shape, slot_shape],
+        [prods],
+        inputs + [picked, odd_part],
+        scalars=1,
+        cost=hint,
+        aliases={7: 1},
+    )
+    x_even = exchange(part, "vox", 1, even)
+    step = later(part)
+    z_down = exchange(step, "vox", 2, even)
+    step = later(step)
+    xz_down = exchange(step, "vox", 3, even)
+    step = later(step)
+    x_odd = exchange(step, "vox", 1, odd)
+
+    def add(*values):
+        return call(add_kernel, "add", [part_shape] * 2, [], values)
+
+    along, own = add(z_up, xz_up, part)
+    across, along = add(own, x_even, along)
+    along, across = add(along, z_down, across)
+    along, across = add(along, xz_down, across)
+    total = (across + x_odd) + along
+    total = all_sum(total, "vox", 4)
     own, send, residual, _ = call(
         backproject_kernel,
         "backproject",

time: 18.6 us -> 23.6 us (1.27)
  the two profiles are of different devices: /device:TPU:0 before, /device:TPU:9 now
where the time goes in v15:
time: 23.6 us; the launch traced here: 23.4 us
  starting transfers between devices  15 us (64%)
  waiting for transfers between devices  4.65 us (20%)
  Pallas kernels  2.17 us (9%)
  between operations  1.48 us (6%)
    ppermute x9, starting transfers between devices, exchange(): lax.ppermute(value, axis, [(i, i ^ mask) for i in range(size) if senders...  15 us
    ppermute x9, waiting for transfers between devices, exchange(): lax.ppermute(value, axis, [(i, i ^ mask) for i in range(size) if senders...  4.65 us
    pallas_call x12, Pallas kernels, call(): pl.pallas_call(kernel, out_shape=[jax.ShapeDtypeStruct(shape, dtype) for...  2.17 us
  transfers between devices with their start and end apart: 9, of which 5 were waited for; matrix products, arithmetic and copies ran while one was open for 0% of the time, Pallas kernels for 0%

profile of v15, /device:TPU:9, one launch (start us, length us, event | category | flops | bytes accessed | tf_op | source)
XLA Modules:
  0.0 23.4 jit_solution(15512164150112800417)
XLA Ops:
  0.6 0.0 copy-start
  0.6 0.0 copy-start.1
  0.7 0.0 copy-start.2
  0.7 0.0 copy-start.3
  0.7 0.0 copy-start.4
  0.7 0.7 %collective-permute-start = (f32[32,128]{1,0:T(8,128)}, f32[32,128]{1,0:T(8,128)S(1)}, u32[]{:S(2)}, u32[]{:S(2)}) collective-permute-start(f32[32,128]{1,0:T(8,128)} %bitcast.2), channel_id=1, source_target_pairs={{0,1},{1,0},{2,3},{3,2},{4,5},{5,4},{6,7},{7,6},{8,9},{9,8},{10,11... | collective-permute-start | bytes 49160 | tf_op jit(solution)/shard_map/ppermute | solution.py:17
  2.1 0.4 %collective-permute-done.refs_5_ = f32[32,128]{1,0:T(8,128)S(1)} collective-permute-done((f32[32,128]{1,0:T(8,128)}, f32[32,128]{1,0:T(8,128)S(1)}, u32[]{:S(2)}, u32[]{:S(2)}) %collective-permute-start) | collective-permute-done | bytes 16416 | tf_op jit(solution)/shard_map/ppermute | solution.py:17
  2.5 0.0 copy-done
  2.5 0.0 copy-done.1
  2.5 0.0 copy-done.2
  2.5 0.0 copy-done.3
  2.5 0.0 copy-done.4
  2.5 0.8 %project_odd.1 = (f32[40,128]{1,0:T(8,128)S(1)}, f32[384,128]{1,0:T(8,128)S(1)}) custom-call(s32[1,1]{1,0:T(1,128)S(6)} %copy.14.refs_0_.count, bf16[1,1,48,128,128]{4,3,2,1,0:T(8,128)(2,1)S(1)} %copy-done, s32[1,1,48]{2,1,0:T(1,128)S(1)} %copy-done.3, s32[1,1,48]{2,1,0:T(1,128)S(1)} %copy-done.4, ...), custom_call_target="tpu_custom_call", output_to_operand_aliasing={{1}: (7, {})} | custom-call | tf_op jit(solution)/shard_map/project_odd/pallas_call | solution.py:180
  3.3 2.2 %collective-permute-start.2 = (f32[40,128]{1,0:T(8,128)S(1)}, f32[40,128]{1,0:T(8,128)S(1)}, u32[]{:S(2)}, u32[]{:S(2)}) collective-permute-start(f32[40,128]{1,0:T(8,128)S(1)} %get-tuple-element.19.refs_8_), channel_id=1, source_target_pairs={{4,2},{6,0},{12,10},{14,8},{5,3},{7,1},{13,11},{15,9},{20,18},{22,... | collective-permute-start | bytes 61448 | tf_op jit(solution)/shard_map/ppermute | solution.py:17
  5.5 1.3 %collective-permute-start.1 = (f32[40,128]{1,0:T(8,128)S(1)}, f32[40,128]{1,0:T(8,128)S(1)}, u32[]{:S(2)}, u32[]{:S(2)}) collective-permute-start(f32[40,128]{1,0:T(8,128)S(1)} %get-tuple-element.19.refs_8_), channel_id=1, source_target_pairs={{4,0},{6,2},{12,8},{14,10},{5,1},{7,3},{13,9},{15,11},{20,16},{22,... | collective-permute-start | bytes 61448 | tf_op jit(solution)/shard_map/ppermute | solution.py:17
  6.9 0.7 %collective-permute-start.3 = (f32[40,128]{1,0:T(8,128)S(1)}, f32[40,128]{1,0:T(8,128)S(1)}, u32[]{:S(2)}, u32[]{:S(2)}) collective-permute-start(f32[40,128]{1,0:T(8,128)S(1)} %get-tuple-element.21.refs_2_.value), channel_id=1, source_target_pairs={{0,2},{2,0},{8,10},{10,8},{1,3},{3,1},{9,11},{11,9},{16,18},{18,16... | collective-permute-start | bytes 61448 | tf_op jit(solution)/shard_map/ppermute | solution.py:17
  7.6 1.3 %collective-permute-start.4 = (f32[40,128]{1,0:T(8,128)S(1)}, f32[40,128]{1,0:T(8,128)S(1)}, u32[]{:S(2)}, u32[]{:S(2)}) collective-permute-start(f32[40,128]{1,0:T(8,128)S(1)} %later.3.value), channel_id=1, source_target_pairs={{0,4},{2,6},{8,12},{10,14},{1,5},{3,7},{9,13},{11,15},{16,20},{18,... | collective-permute-start | bytes 61448 | tf_op jit(solution)/shard_map/ppermute | solution.py:17
  8.9 1.3 %collective-permute-start.5 = (f32[40,128]{1,0:T(8,128)S(1)}, f32[40,128]{1,0:T(8,128)S(1)}, u32[]{:S(2)}, u32[]{:S(2)}) collective-permute-start(f32[40,128]{1,0:T(8,128)S(1)} %later.4.value), channel_id=1, source_target_pairs={{0,6},{2,4},{8,14},{10,12},{1,7},{3,5},{9,15},{11,13},{16,22},{18,... | collective-permute-start | bytes 61448 | tf_op jit(solution)/shard_map/ppermute | solution.py:17
  10.2 0.0 collective-permute-done.2.refs_1_
  10.2 2.2 %collective-permute-start.6 = (f32[40,128]{1,0:T(8,128)S(1)}, f32[40,128]{1,0:T(8,128)S(1)}, u32[]{:S(2)}, u32[]{:S(2)}) collective-permute-start(f32[40,128]{1,0:T(8,128)S(1)} %later.5), channel_id=1, source_target_pairs={{4,6},{6,4},{12,14},{14,12},{5,7},{7,5},{13,15},{15,13},{20,22},{2... | collective-permute-start | bytes 61448 | tf_op jit(solution)/shard_map/ppermute | solution.py:17
  12.4 0.0 collective-permute-done.1.refs_0_
  12.5 0.0 collective-permute-done.3.refs_1_
  12.5 0.0 collective-permute-done.4.refs_1_
  12.5 1.8 %collective-permute-done.5.refs_1_ = f32[40,128]{1,0:T(8,128)S(1)} collective-permute-done((f32[40,128]{1,0:T(8,128)S(1)}, f32[40,128]{1,0:T(8,128)S(1)}, u32[]{:S(2)}, u32[]{:S(2)}) %collective-permute-start.5) | collective-permute-done | bytes 20512 | tf_op jit(solution)/shard_map/ppermute | solution.py:17
  14.3 0.4 %collective-permute-done.6 = f32[40,128]{1,0:T(8,128)S(1)} collective-permute-done((f32[40,128]{1,0:T(8,128)S(1)}, f32[40,128]{1,0:T(8,128)S(1)}, u32[]{:S(2)}, u32[]{:S(2)}) %collective-permute-start.6) | collective-permute-done | bytes 20512 | tf_op jit(solution)/shard_map/ppermute | solution.py:17
  14.7 2.3 %collective-permute-start.7 = (f32[40,128]{1,0:T(8,128)S(1)}, f32[40,128]{1,0:T(8,128)S(1)}, u32[]{:S(2)}, u32[]{:S(2)}) collective-permute-start(f32[40,128]{1,0:T(8,128)S(1)} %add_add_fusion), channel_id=1, source_target_pairs={{0,8},{2,10},{4,12},{6,14},{8,0},{10,2},{12,4},{14,6},{1,9},{3,11}... | collective-permute-start | bytes 61448 | tf_op jit(solution)/shard_map/ppermute | solution.py:17
  17.0 1.2 %collective-permute-done.7 = f32[40,128]{1,0:T(8,128)S(1)} collective-permute-done((f32[40,128]{1,0:T(8,128)S(1)}, f32[40,128]{1,0:T(8,128)S(1)}, u32[]{:S(2)}, u32[]{:S(2)}) %collective-permute-start.7) | collective-permute-done | bytes 20512 | tf_op jit(solution)/shard_map/ppermute | solution.py:17
  18.3 0.6 %backproject.1 = (f32[40,128]{1,0:T(8,128)S(1)}, bf16[64,128]{1,0:T(8,128)(2,1)S(1)}, f32[4,128]{1,0:T(4,128)S(1)}, f32[384,128]{1,0:T(8,128)S(1)}) custom-call(s32[1,1]{1,0:T(1,128)S(6)} %copy.14.refs_0_.count, bf16[1,1,48,128,128]{4,3,2,1,0:T(8,128)(2,1)S(1)} %copy-done, s32[1,1,48]{2,1,0:T(1,128)S(1)} %copy-done.3, ...), custom_call_target="tpu_custom_call", output_to_operand_aliasing={{3}: (5, {})} | custom-call | tf_op jit(solution)/shard_map/backproject/pallas_call | solution.py:180
  18.9 3.0 %collective-permute-start.8 = (bf16[64,128]{1,0:T(8,128)(2,1)S(1)}, bf16[64,128]{1,0:T(8,128)(2,1)S(1)}, u32[]{:S(2)}, u32[]{:S(2)}) collective-permute-start(bf16[64,128]{1,0:T(8,128)(2,1)S(1)} %get-tuple-element.32), channel_id=1, source_target_pairs={{0,1},{1,0},{2,3},{3,2},{4,5},{5,4},{6,7},{7,6},{8,9},{9,8},{10,11... | collective-permute-start | bytes 49160 | tf_op jit(solution)/shard_map/ppermute | solution.py:17
  21.9 0.8 %collective-permute-done.8.there = bf16[64,128]{1,0:T(8,128)(2,1)S(1)} collective-permute-done((bf16[64,128]{1,0:T(8,128)(2,1)S(1)}, bf16[64,128]{1,0:T(8,128)(2,1)S(1)}, u32[]{:S(2)}, u32[]{:S(2)}) %collective-permute-start.8) | collective-permute-done | bytes 16416 | tf_op jit(solution)/shard_map/ppermute | solution.py:17
  22.7 0.6 %update.1 = (f32[32,128]{1,0:T(8,128)}, bf16[1,1,4,128]{3,2,1,0:T(4,128)(2,1)}) custom-call(f32[32,128]{1,0:T(8,128)S(1)} %bitcast.5, f32[40,128]{1,0:T(8,128)S(1)} %get-tuple-element.31.own, bf16[64,128]{1,0:T(8,128)(2,1)S(1)} %collective-permute-done.8.there, f32[4,128]{1,0:T(4,128)S(1)} %get-tuple-element.33.residual), custom_call_target="tpu_custom_call" | custom-call | tf_op jit(solution)/shard_map/update/pallas_call | solution.py:180
  (11 shorter events, 0.1 us)
Async XLA Ops:
  0.6 1.8 %copy-start = (bf16[1,1,48,128,128]{4,3,2,1,0:T(8,128)(2,1)S(1)}, bf16[1,1,48,128,128]{4,3,2,1,0:T(8,128)(2,1)}, u32[]{:S(2)}) copy-start(bf16[1,1,48,128,128]{4,3,2,1,0:T(8,128)(2,1)} %tiles.1) | copy-start | bytes 4718596
  0.6 1.8 %copy-start.1 = (f32[8,4,128]{2,1,0:T(4,128)S(1)}, f32[8,4,128]{2,1,0:T(4,128)}, u32[]{:S(2)}) copy-start(f32[8,4,128]{2,1,0:T(4,128)} %param.6) | copy-start | bytes 49156
  0.7 1.8 %copy-start.2 = (f32[1,1,4,128]{3,2,1,0:T(4,128)S(1)}, f32[1,1,4,128]{3,2,1,0:T(4,128)}, u32[]{:S(2)}) copy-start(f32[1,1,4,128]{3,2,1,0:T(4,128)} %refs_6_.3) | copy-start | bytes 6148
  0.7 1.8 %copy-start.3 = (s32[1,1,48]{2,1,0:T(1,128)S(1)}, s32[1,1,48]{2,1,0:T(1,128)}, u32[]{:S(2)}) copy-start(s32[1,1,48]{2,1,0:T(1,128)} %rows.3) | copy-start | bytes 580
  0.7 1.8 %copy-start.4 = (s32[1,1,48]{2,1,0:T(1,128)S(1)}, s32[1,1,48]{2,1,0:T(1,128)}, u32[]{:S(2)}) copy-start(s32[1,1,48]{2,1,0:T(1,128)} %cols.1) | copy-start | bytes 580
  0.7 1.8 %collective-permute-start = (f32[32,128]{1,0:T(8,128)}, f32[32,128]{1,0:T(8,128)S(1)}, u32[]{:S(2)}, u32[]{:S(2)}) collective-permute-start(f32[32,128]{1,0:T(8,128)} %bitcast.2), channel_id=1, source_target_pairs={{0,1},{1,0},{2,3},{3,2},{4,5},{5,4},{6,7},{7,6},{8,9},{9,8},{10,11... | collective-permute-start | bytes 49160 | tf_op jit(solution)/shard_map/ppermute | solution.py:17
  3.3 6.9 %collective-permute-start.2 = (f32[40,128]{1,0:T(8,128)S(1)}, f32[40,128]{1,0:T(8,128)S(1)}, u32[]{:S(2)}, u32[]{:S(2)}) collective-permute-start(f32[40,128]{1,0:T(8,128)S(1)} %get-tuple-element.19.refs_8_), channel_id=1, source_target_pairs={{4,2},{6,0},{12,10},{14,8},{5,3},{7,1},{13,11},{15,9},{20,18},{22,... | collective-permute-start | bytes 61448 | tf_op jit(solution)/shard_map/ppermute | solution.py:17
  5.5 6.9 %collective-permute-start.1 = (f32[40,128]{1,0:T(8,128)S(1)}, f32[40,128]{1,0:T(8,128)S(1)}, u32[]{:S(2)}, u32[]{:S(2)}) collective-permute-start(f32[40,128]{1,0:T(8,128)S(1)} %get-tuple-element.19.refs_8_), channel_id=1, source_target_pairs={{4,0},{6,2},{12,8},{14,10},{5,1},{7,3},{13,9},{15,11},{20,16},{22,... | collective-permute-start | bytes 61448 | tf_op jit(solution)/shard_map/ppermute | solution.py:17
  6.9 5.6 %collective-permute-start.3 = (f32[40,128]{1,0:T(8,128)S(1)}, f32[40,128]{1,0:T(8,128)S(1)}, u32[]{:S(2)}, u32[]{:S(2)}) collective-permute-start(f32[40,128]{1,0:T(8,128)S(1)} %get-tuple-element.21.refs_2_.value), channel_id=1, source_target_pairs={{0,2},{2,0},{8,10},{10,8},{1,3},{3,1},{9,11},{11,9},{16,18},{18,16... | collective-permute-start | bytes 61448 | tf_op jit(solution)/shard_map/ppermute | solution.py:17
  7.6 4.9 %collective-permute-start.4 = (f32[40,128]{1,0:T(8,128)S(1)}, f32[40,128]{1,0:T(8,128)S(1)}, u32[]{:S(2)}, u32[]{:S(2)}) collective-permute-start(f32[40,128]{1,0:T(8,128)S(1)} %later.3.value), channel_id=1, source_target_pairs={{0,4},{2,6},{8,12},{10,14},{1,5},{3,7},{9,13},{11,15},{16,20},{18,... | collective-permute-start | bytes 61448 | tf_op jit(solution)/shard_map/ppermute | solution.py:17
  8.9 5.4 %collective-permute-start.5 = (f32[40,128]{1,0:T(8,128)S(1)}, f32[40,128]{1,0:T(8,128)S(1)}, u32[]{:S(2)}, u32[]{:S(2)}) collective-permute-start(f32[40,128]{1,0:T(8,128)S(1)} %later.4.value), channel_id=1, source_target_pairs={{0,6},{2,4},{8,14},{10,12},{1,7},{3,5},{9,15},{11,13},{16,22},{18,... | collective-permute-start | bytes 61448 | tf_op jit(solution)/shard_map/ppermute | solution.py:17
  10.2 4.5 %collective-permute-start.6 = (f32[40,128]{1,0:T(8,128)S(1)}, f32[40,128]{1,0:T(8,128)S(1)}, u32[]{:S(2)}, u32[]{:S(2)}) collective-permute-start(f32[40,128]{1,0:T(8,128)S(1)} %later.5), channel_id=1, source_target_pairs={{4,6},{6,4},{12,14},{14,12},{5,7},{7,5},{13,15},{15,13},{20,22},{2... | collective-permute-start | bytes 61448 | tf_op jit(solution)/shard_map/ppermute | solution.py:17
  14.7 3.5 %collective-permute-start.7 = (f32[40,128]{1,0:T(8,128)S(1)}, f32[40,128]{1,0:T(8,128)S(1)}, u32[]{:S(2)}, u32[]{:S(2)}) collective-permute-start(f32[40,128]{1,0:T(8,128)S(1)} %add_add_fusion), channel_id=1, source_target_pairs={{0,8},{2,10},{4,12},{6,14},{8,0},{10,2},{12,4},{14,6},{1,9},{3,11}... | collective-permute-start | bytes 61448 | tf_op jit(solution)/shard_map/ppermute | solution.py:17
  18.9 3.8 %collective-permute-start.8 = (bf16[64,128]{1,0:T(8,128)(2,1)S(1)}, bf16[64,128]{1,0:T(8,128)(2,1)S(1)}, u32[]{:S(2)}, u32[]{:S(2)}) collective-permute-start(bf16[64,128]{1,0:T(8,128)(2,1)S(1)} %get-tuple-element.32), channel_id=1, source_target_pairs={{0,1},{1,0},{2,3},{3,2},{4,5},{5,4},{6,7},{7,6},{8,9},{9,8},{10,11... | collective-permute-start | bytes 49160 | tf_op jit(solution)/shard_map/ppermute | solution.py:17

commit v16 on v14

--- a/solution.py
+++ b/solution.py
@@ -22,10 +22,12 @@
     stride = 1
     while stride < size:
         if 2 * stride < size:
-            across = exchange(value, axis, stride)
-            both = exchange(value, axis, 3 * stride)
-            along = exchange(value, axis, 2 * stride)
-            value = (value + across) + (along + both)
+            firsts = [i for i in range(size) if (i // stride) % 4 == 0]
+            groups = [[i + k * stride for k in range(4)] for i in firsts]
+            copies = jnp.concatenate([value] * 4, axis=0)
+            got = lax.all_to_all(copies, axis, 0, 0, axis_index_groups=groups, tiled=True)
+            got = got.reshape((4,) + value.shape)
+            value = (got[0] + got[1]) + (got[2] + got[3])
         else:
             value = value + exchange(value, axis, stride)
         stride *= 4

time: 18.6 us -> 20.4 us (1.097)
  blocking collectives: 0 us -> 9.81 us
  starting transfers between devices: 7.78 us -> 3.24 us
  waiting for transfers between devices: 7.22 us -> 3.63 us
    all_to_all x0 -> x1, blocking collectives: none -> 9.81 us  [all_sum(): lax.all_to_all(copies, axis, 0, 0, axis_index_groups=groups, tiled=True)]
    ppermute x6 -> x3, starting transfers between devices: 7.78 us -> 3.24 us  [exchange(): return lax.ppermute(value, axis, [(i, i ^ mask) for i in range(size)])]
    ppermute x6 -> x3, waiting for transfers between devices: 7.22 us -> 3.63 us  [exchange(): return lax.ppermute(value, axis, [(i, i ^ mask) for i in range(size)])]
  transfers between devices with their start and end apart: 6 -> 3, of which waited for: 6 -> 3; matrix products, arithmetic and copies ran while one was open for 0% -> 0% of each run, Pallas kernels for 0% -> 0%
where the time goes in v16:
time: 20.4 us; the launch traced here: 20.2 us
  blocking collectives  9.81 us (48%)
  waiting for transfers between devices  3.63 us (18%)
  starting transfers between devices  3.24 us (16%)
  Pallas kernels  2.07 us (10%)
  between operations  1.37 us (7%)
    all_to_all x1, blocking collectives, all_sum(): lax.all_to_all(copies, axis, 0, 0, axis_index_groups=groups, tiled=True)  9.81 us
    ppermute x3, waiting for transfers between devices, exchange(): return lax.ppermute(value, axis, [(i, i ^ mask) for i in range(size)])  3.63 us
    ppermute x3, starting transfers between devices, exchange(): return lax.ppermute(value, axis, [(i, i ^ mask) for i in range(size)])  3.24 us
    pallas_call x4, Pallas kernels, call(): pl.pallas_call(kernel, out_shape=[jax.ShapeDtypeStruct(shape, dtype) for...  2.07 us
  transfers between devices with their start and end apart: 3, of which 3 were waited for; matrix products, arithmetic and copies ran while one was open for 0% of the time, Pallas kernels for 0%

profile of v16, /device:TPU:0, one launch (start us, length us, event | category | flops | bytes accessed | tf_op | source)
XLA Modules:
  0.0 20.2 jit_solution(8436337200384732618)
XLA Ops:
  0.6 0.0 copy-start
  0.6 0.0 copy-start.1
  0.7 0.0 copy-start.2
  0.7 0.0 copy-start.3
  0.7 0.0 copy-start.4
  0.7 0.5 %collective-permute-start = (f32[32,128]{1,0:T(8,128)}, f32[32,128]{1,0:T(8,128)S(1)}, u32[]{:S(2)}, u32[]{:S(2)}) collective-permute-start(f32[32,128]{1,0:T(8,128)} %bitcast.7), channel_id=1, source_target_pairs={{0,1},{1,0},{2,3},{3,2},{4,5},{5,4},{6,7},{7,6},{8,9},{9,8},{10,11... | collective-permute-start | bytes 49160 | tf_op jit(solution)/shard_map/ppermute | solution.py:17
  1.9 0.4 %collective-permute-done.other = f32[32,128]{1,0:T(8,128)S(1)} collective-permute-done((f32[32,128]{1,0:T(8,128)}, f32[32,128]{1,0:T(8,128)S(1)}, u32[]{:S(2)}, u32[]{:S(2)}) %collective-permute-start) | collective-permute-done | bytes 16416 | tf_op jit(solution)/shard_map/ppermute | solution.py:17
  2.2 0.0 copy-done
  2.3 0.0 copy-done.1
  2.3 0.0 copy-done.2
  2.3 0.0 copy-done.3
  2.3 0.0 copy-done.4
  2.3 0.8 %project.1 = (f32[40,128]{1,0:T(8,128)S(1)}, f32[384,128]{1,0:T(8,128)S(1)}) custom-call(s32[1,1]{1,0:T(1,128)S(6)} %copy.12.count, bf16[1,1,48,128,128]{4,3,2,1,0:T(8,128)(2,1)S(1)} %copy-done, s32[1,1,48]{2,1,0:T(1,128)S(1)} %copy-done.3, s32[1,1,48]{2,1,0:T(1,128)S(1)} %copy-done.4, f32[32,128]{1,0:T(8,128)S(1)} %bitcast.8, ...), custom_call_target="tpu_custom_call", output_to_operand_aliasing={{1}: (7, {})} | custom-call | tf_op jit(solution)/shard_map/project/pallas_call | solution.py:144
  3.1 9.8 %all_to_all.9 = f32[4,40,128]{2,1,0:T(8,128)S(1)} all-to-all(f32[4,40,128]{2,1,0:T(8,128)S(1)} %bitcast.10), channel_id=1, replica_groups={{0,2,4,6},{8,10,12,14},{1,3,5,7},{9,11,13,15},{16,18,20,22},{24,26,28,3..., dimensions={0} | all-to-all | bytes 163840 | tf_op jit(solution)/shard_map/all_to_all | solution.py:28
  12.9 2.6 %collective-permute-start.1 = (f32[40,128]{1,0:T(8,128)S(1)}, f32[40,128]{1,0:T(8,128)S(1)}, u32[]{:S(2)}, u32[]{:S(2)}) collective-permute-start(f32[40,128]{1,0:T(8,128)S(1)} %fusion.1), channel_id=1, source_target_pairs={{0,8},{2,10},{4,12},{6,14},{8,0},{10,2},{12,4},{14,6},{1,9},{3,11}... | collective-permute-start | bytes 61448 | tf_op jit(solution)/shard_map/ppermute | solution.py:17
  15.6 2.1 %collective-permute-done.1 = f32[40,128]{1,0:T(8,128)S(1)} collective-permute-done((f32[40,128]{1,0:T(8,128)S(1)}, f32[40,128]{1,0:T(8,128)S(1)}, u32[]{:S(2)}, u32[]{:S(2)}) %collective-permute-start.1) | collective-permute-done | bytes 20512 | tf_op jit(solution)/shard_map/ppermute | solution.py:17
  17.7 0.6 %backproject.1 = (f32[40,128]{1,0:T(8,128)S(1)}, bf16[64,128]{1,0:T(8,128)(2,1)S(1)}, f32[4,128]{1,0:T(4,128)S(1)}, f32[384,128]{1,0:T(8,128)S(1)}) custom-call(s32[1,1]{1,0:T(1,128)S(6)} %copy.12.count, bf16[1,1,48,128,128]{4,3,2,1,0:T(8,128)(2,1)S(1)} %copy-done, s32[1,1,48]{2,1,0:T(1,128)S(1)} %copy-done.3, ...), custom_call_target="tpu_custom_call", output_to_operand_aliasing={{3}: (5, {})} | custom-call | tf_op jit(solution)/shard_map/backproject/pallas_call | solution.py:144
  18.3 0.1 collective-permute-start.2
  18.4 1.2 %collective-permute-done.2.there = bf16[64,128]{1,0:T(8,128)(2,1)S(1)} collective-permute-done((bf16[64,128]{1,0:T(8,128)(2,1)S(1)}, bf16[64,128]{1,0:T(8,128)(2,1)S(1)}, u32[]{:S(2)}, u32[]{:S(2)}) %collective-permute-start.2) | collective-permute-done | bytes 16416 | tf_op jit(solution)/shard_map/ppermute | solution.py:17
  19.6 0.6 %update.1 = (f32[32,128]{1,0:T(8,128)}, bf16[1,1,4,128]{3,2,1,0:T(4,128)(2,1)}) custom-call(f32[32,128]{1,0:T(8,128)S(1)} %bitcast.9, f32[40,128]{1,0:T(8,128)S(1)} %get-tuple-element.11.own, bf16[64,128]{1,0:T(8,128)(2,1)S(1)} %collective-permute-done.2.there, f32[4,128]{1,0:T(4,128)S(1)} %get-tuple-element.13.residual), custom_call_target="tpu_custom_call" | custom-call | tf_op jit(solution)/shard_map/update/pallas_call | solution.py:144
  (4 shorter events, 0.1 us)
Async XLA Ops:
  0.6 1.6 %copy-start = (bf16[1,1,48,128,128]{4,3,2,1,0:T(8,128)(2,1)S(1)}, bf16[1,1,48,128,128]{4,3,2,1,0:T(8,128)(2,1)}, u32[]{:S(2)}) copy-start(bf16[1,1,48,128,128]{4,3,2,1,0:T(8,128)(2,1)} %tiles.3) | copy-start | bytes 4718596
  0.6 1.6 %copy-start.1 = (f32[8,4,128]{2,1,0:T(4,128)S(1)}, f32[8,4,128]{2,1,0:T(4,128)}, u32[]{:S(2)}) copy-start(f32[8,4,128]{2,1,0:T(4,128)} %param.6) | copy-start | bytes 49156
  0.7 1.6 %copy-start.2 = (f32[1,1,4,128]{3,2,1,0:T(4,128)S(1)}, f32[1,1,4,128]{3,2,1,0:T(4,128)}, u32[]{:S(2)}) copy-start(f32[1,1,4,128]{3,2,1,0:T(4,128)} %measured.1) | copy-start | bytes 6148
  0.7 1.6 %copy-start.3 = (s32[1,1,48]{2,1,0:T(1,128)S(1)}, s32[1,1,48]{2,1,0:T(1,128)}, u32[]{:S(2)}) copy-start(s32[1,1,48]{2,1,0:T(1,128)} %rows.5) | copy-start | bytes 580
  0.7 1.6 %copy-start.4 = (s32[1,1,48]{2,1,0:T(1,128)S(1)}, s32[1,1,48]{2,1,0:T(1,128)}, u32[]{:S(2)}) copy-start(s32[1,1,48]{2,1,0:T(1,128)} %cols.3) | copy-start | bytes 580
  0.7 1.6 %collective-permute-start = (f32[32,128]{1,0:T(8,128)}, f32[32,128]{1,0:T(8,128)S(1)}, u32[]{:S(2)}, u32[]{:S(2)}) collective-permute-start(f32[32,128]{1,0:T(8,128)} %bitcast.7), channel_id=1, source_target_pairs={{0,1},{1,0},{2,3},{3,2},{4,5},{5,4},{6,7},{7,6},{8,9},{9,8},{10,11... | collective-permute-start | bytes 49160 | tf_op jit(solution)/shard_map/ppermute | solution.py:17
  12.9 4.7 %collective-permute-start.1 = (f32[40,128]{1,0:T(8,128)S(1)}, f32[40,128]{1,0:T(8,128)S(1)}, u32[]{:S(2)}, u32[]{:S(2)}) collective-permute-start(f32[40,128]{1,0:T(8,128)S(1)} %fusion.1), channel_id=1, source_target_pairs={{0,8},{2,10},{4,12},{6,14},{8,0},{10,2},{12,4},{14,6},{1,9},{3,11}... | collective-permute-start | bytes 61448 | tf_op jit(solution)/shard_map/ppermute | solution.py:17
  18.3 1.3 %collective-permute-start.2 = (bf16[64,128]{1,0:T(8,128)(2,1)S(1)}, bf16[64,128]{1,0:T(8,128)(2,1)S(1)}, u32[]{:S(2)}, u32[]{:S(2)}) collective-permute-start(bf16[64,128]{1,0:T(8,128)(2,1)S(1)} %get-tuple-element.12), channel_id=1, source_target_pairs={{0,1},{1,0},{2,3},{3,2},{4,5},{5,4},{6,7},{7,6},{8,9},{9,8},{10,11... | collective-permute-start | bytes 49160 | tf_op jit(solution)/shard_map/ppermute | solution.py:17

commit v17 on v14

v17 whole, which is shorter than its diff:
```python
import functools

import jax
import jax.numpy as jnp
from jax import lax
from jax.experimental import pallas as pl
from jax.experimental.pallas import tpu as pltpu
from jax.sharding import PartitionSpec as P

SUB = 8
HINT_FLOPS = 20_000_000_000
VMEM_BYTES = 16 << 20


def exchange(value, axis, mask):
    size = lax.axis_size(axis)
    return lax.ppermute(value, axis, [(i, i ^ mask) for i in range(size)])


def all_sum(value, axis, add):
    size = lax.axis_size(axis)
    stride = 1
    while stride < size:
        if 2 * stride < size:
            across = exchange(value, axis, stride)
            both = exchange(value, axis, 3 * stride)
            along = exchange(value, axis, 2 * stride)
            value = (value + across) + add(along, both)
        else:
            value = value + exchange(value, axis, stride)
        stride *= 4
    return value


def spread_kernel(spread):
    slot = lax.broadcasted_iota(jnp.int32, spread.shape, 0)
    column = lax.broadcasted_iota(jnp.int32, spread.shape, 1)
    spread[...] = (column // SUB == slot).astype(jnp.float32)


def pick_matrix(key, blocks, kinds):
    shape = (SUB, kinds * blocks)
    lane = lax.broadcasted_iota(jnp.int32, shape, 1)
    same = lane // blocks == lax.broadcasted_iota(jnp.int32, shape, 0)
    block = jnp.where(same, lane % blocks, -2)
    hits = [(block == key[:, n : n + 1]).astype(jnp.float32) for n in range(key.shape[1])]
    return jnp.concatenate(hits, axis=0).astype(jnp.bfloat16)


def add_matrix(key, first, blocks, kinds, spread):
    hit = lax.broadcasted_iota(jnp.int32, (blocks, key.shape[1]), 0) + first == key
    hit = jnp.dot(
        hit.astype(jnp.float32).astype(jnp.bfloat16),
        spread[...].astype(jnp.bfloat16),
        preferred_element_type=jnp.float32,
    )
    kind = lax.broadcasted_iota(jnp.int32, hit.shape, 1) % SUB
    return jnp.concatenate([jnp.where(kind == c, hit, 0.0) for c in range(kinds)], axis=0)


def prepare_kernel(kinds, count, rows, cols, spread, pick, pick_back, add, add_back):
    blocks = add.shape[0] // kinds
    half = add_back.shape[0] // (2 * kinds)
    valid = lax.broadcasted_iota(jnp.int32, rows.shape[1:], 1) < count[0, 0]
    row = jnp.where(valid, rows[0], -1)
    place = cols[0] + lax.axis_index("ray") * half
    place = jnp.where(place < 2 * half, place, place - 2 * half)
    place = jnp.where(valid, place, -1)
    pick[...] = pick_matrix(place, 2 * half, kinds)
    pick_back[...] = pick_matrix(row, blocks, kinds)
    add[...] = add_matrix(row, 0, blocks, kinds, spread).astype(jnp.bfloat16)
    own = add_matrix(place, 0, half, kinds, spread)
    theirs = add_matrix(place, half, half, kinds, spread)
    add_back[...] = jnp.concatenate([own, theirs], axis=0).astype(jnp.bfloat16)


def add_kernel(left, right, out):
    out[...] = left[...] + right[...]


def apply_tiles(pick, table, tiles, contract, add):
    slots, rays, width = tiles.shape[2:]
    picked = jnp.dot(pick[...], table.astype(jnp.bfloat16), preferred_element_type=jnp.float32)
    prods = []
    for n in range(0, slots, 2):
        pair = tiles[0, 0, n : n + 2]
        if contract:
            pair = pair.reshape(2 * rays, width)
        else:
            pair = jnp.concatenate([pair[0], pair[1]], axis=1)
        both = lax.dot_general(
            picked[n * SUB : (n + 2) * SUB].astype(jnp.bfloat16),
            pair,
            (((1,), (contract,)), ((), ())),
            preferred_element_type=jnp.float32,
        )
        prods += [both[:SUB, :width], both[SUB:, width:]]
    left = jnp.concatenate(prods, axis=0)
    sums = None
    for _ in range(3):
        piece = left.astype(jnp.bfloat16)
        left = left - piece.astype(jnp.float32)
        term = jnp.dot(add[...], piece, preferred_element_type=jnp.float32)
        sums = term if sums is None else sums + term
    return sums


def project_kernel(tiles, pick, add, volume, other, measured, part):
    inst = measured.shape[2]
    blocks = part.shape[0] // (inst + 1)
    half = volume.shape[0] // inst
    table = []
    for c in range(inst):
        row = pl.ds(c, half, stride=inst)
        table += [volume[row, :], other[row, :]]
    table.append(jnp.ones((2 * half, part.shape[1]), jnp.float32))
    sums = apply_tiles(pick, jnp.concatenate(table, axis=0), tiles, 1, add)
    mine = lax.broadcasted_iota(jnp.int32, (blocks, part.shape[1]), 0) == lax.axis_index("vox")
    for c in range(inst):
        row = jnp.broadcast_to(measured[0, 0, c : c + 1, :], mine.shape)
        part[c * blocks : (c + 1) * blocks, :] = jnp.where(mine, row, 0.0) - sums[c * blocks : (c + 1) * blocks]
    part[inst * blocks : (inst + 1) * blocks, :] = sums[inst * blocks :]


def backproject_kernel(tiles, pick, add, total, own, send, residual):
    inst = residual.shape[0]
    blocks = total.shape[0] // (inst + 1)
    kinds = [total[c * blocks : (c + 1) * blocks, :] for c in range(inst + 1)]
    weight = kinds[inst] + 1.0
    table = [(kind / weight).astype(jnp.bfloat16).astype(jnp.float32) for kind in kinds[:inst]]
    mine = lax.broadcasted_iota(jnp.int32, weight.shape, 0) == lax.axis_index("vox")
    for c in range(inst):
        residual[c : c + 1, :] = jnp.sum(jnp.where(mine, table[c], 0.0), axis=0, keepdims=True)
    table = jnp.concatenate(table + [jnp.ones_like(weight)], axis=0)
    sums = apply_tiles(pick, table, tiles, 0, add)
    rows = own.shape[0]
    own[...] = sums[:rows]
    filler = jnp.zeros((send.shape[0] - rows, weight.shape[1]), jnp.float32)
    send[...] = jnp.concatenate([sums[rows:], filler], axis=0).astype(jnp.bfloat16)


def update_kernel(volume, own, there, residual, new_volume, own_residual):
    inst = residual.shape[0]
    half = volume.shape[0] // inst
    both = own[...] + there[...].astype(jnp.float32)[: own.shape[0]]
    weight = both[inst * half :] + 1.0
    for c in range(inst):
        row = pl.ds(c, half, stride=inst)
        new_volume[row, :] = jnp.maximum(volume[row, :] + both[c * half : (c + 1) * half] / weight, 0.0)
    own_residual[0, 0] = residual[...].astype(jnp.bfloat16)


def on_device(volume, tiles, tile_row, tile_col, tile_count, measured):
    half, inst, width = volume.shape
    slots = tiles.shape[2]
    blocks = lax.axis_size("vox") * measured.shape[1]
    f32, bf16 = jnp.float32, jnp.bfloat16
    vmem = pl.BlockSpec(memory_space=pltpu.VMEM)
    smem = pl.BlockSpec(memory_space=pltpu.SMEM)
    params = pltpu.CompilerParams(vmem_limit_bytes=VMEM_BYTES)

    def call(kernel, name, outs, scratch, args, scalars=0, cost=None):
        return pl.pallas_call(
            kernel,
            out_shape=[jax.ShapeDtypeStruct(shape, dtype) for shape, dtype in outs],
            in_specs=[smem] * scalars + [vmem] * (len(args) - scalars),
            out_specs=[vmem] * len(outs),
            scratch_shapes=scratch,
            compiler_params=params,
            cost_estimate=cost,
            name=name,
        )(*args)

    volume = volume.reshape(half * inst, width)
    other = exchange(volume, "ray", 1)
    kinds = inst + 1
    (spread,) = call(
        spread_kernel,
        "spread",
        [((slots, slots * SUB), f32)],
        [],
        [],
        cost=pl.CostEstimate(flops=HINT_FLOPS, bytes_accessed=0, transcendentals=0),
    )
    pick, pick_back, add, add_back = call(
        functools.partial(prepare_kernel, kinds),
        "prepare",
        [
            ((slots * SUB, 2 * half * kinds), bf16),
            ((slots * SUB, blocks * kinds), bf16),
            ((blocks * kinds, slots * SUB), bf16),
            ((2 * half * kinds, slots * SUB), bf16),
        ],
        [],
        [tile_count, tile_row, tile_col, spread],
        scalars=1,
    )
    (part,) = call(
        project_kernel,
        "project",
        [((kinds * blocks, width), f32)],
        [],
        [tiles, pick, add, volume, other, measured],
    )

    def add_parts(left, right):
        return call(add_kernel, "add", [((kinds * blocks, width), f32)], [], [left, right])[0]

    total = all_sum(part, "vox", add_parts)
    padded = -(-kinds * half // 16) * 16
    own, send, residual = call(
        backproject_kernel,
        "backproject",
        [((kinds * half, width), f32), ((padded, width), bf16), ((inst, width), f32)],
        [],
        [tiles, pick_back, add_back, total],
    )
    there = exchange(send, "ray", 1)
    new_volume, own_residual = call(
        update_kernel,
        "update",
        [(volume.shape, f32), ((1, 1, inst, width), bf16)],
        [],
        [volume, own, there, residual],
    )
    return new_volume.reshape(half, inst, width), own_residual


def solution(mesh):
    in_specs = (
        P(("slab", "vox", "ray"), None, None),
        P(("slab", "vox"), "ray", None, None, None),
        P(("slab", "vox"), "ray", None),
        P(("slab", "vox"), "ray", None),
        P(("slab", "vox"), "ray"),
        P("ray", ("slab", "vox"), None, None),
    )
    out_specs = (P(("slab", "vox", "ray"), None, None), P("ray", ("slab", "vox"), None, None))
    return jax.shard_map(
        on_device, mesh=mesh, in_specs=in_specs, out_specs=out_specs, check_vma=False
    )
```

time: 18.6 us -> 18.5 us (level)
  waiting for transfers between devices: 7.22 us -> 6.98 us
  Pallas kernels: 2.07 us -> 2.3 us
    ppermute x6, waiting for transfers between devices: 7.22 us -> 6.98 us  [exchange(): return lax.ppermute(value, axis, [(i, i ^ mask) for i in range(size)])]
    pallas_call x4 -> x6, Pallas kernels: 2.07 us -> 2.3 us  [call(): pl.pallas_call(kernel, out_shape=[jax.ShapeDtypeStruct(shape, dtype) for...]
  transfers between devices with their start and end apart: 6 -> 6, of which waited for: 6 -> 6; matrix products, arithmetic and copies ran while one was open for 0% -> 0% of each run, Pallas kernels for 0% -> 1%
where the time goes in v17:
time: 18.5 us; the launch traced here: 18.3 us
  starting transfers between devices  7.66 us (41%)
  waiting for transfers between devices  6.98 us (38%)
  Pallas kernels  2.3 us (12%)
  between operations  1.37 us (7%)
    ppermute x6, starting transfers between devices, exchange(): return lax.ppermute(value, axis, [(i, i ^ mask) for i in range(size)])  7.66 us
    ppermute x6, waiting for transfers between devices, exchange(): return lax.ppermute(value, axis, [(i, i ^ mask) for i in range(size)])  6.98 us
    pallas_call x6, Pallas kernels, call(): pl.pallas_call(kernel, out_shape=[jax.ShapeDtypeStruct(shape, dtype) for...  2.3 us
  transfers between devices with their start and end apart: 6, of which 6 were waited for; matrix products, arithmetic and copies ran while one was open for 0% of the time, Pallas kernels for 1%

profile of v17, /device:TPU:0, one launch (start us, length us, event | category | flops | bytes accessed | tf_op | source)
XLA Modules:
  0.0 18.3 jit_solution(6806602873886963728)
XLA Ops:
  0.6 0.0 copy-start.3
  0.6 0.0 copy-start.4
  0.7 0.0 copy-start
  0.7 0.0 copy-start.1
  0.7 0.0 copy-start.2
  0.7 0.5 %collective-permute-start = (f32[32,128]{1,0:T(8,128)}, f32[32,128]{1,0:T(8,128)S(1)}, u32[]{:S(2)}, u32[]{:S(2)}) collective-permute-start(f32[32,128]{1,0:T(8,128)} %bitcast.2), channel_id=1, source_target_pairs={{0,1},{1,0},{2,3},{3,2},{4,5},{5,4},{6,7},{7,6},{8,9},{9,8},{10,11... | collective-permute-start | bytes 49160 | tf_op jit(solution)/shard_map/ppermute | solution.py:17
  1.9 0.0 copy-done.3
  1.9 0.0 copy-done.4
  1.9 0.2 %prepare.1 = (bf16[384,80]{1,0:T(8,128)(2,1)S(1)}, bf16[384,40]{1,0:T(8,128)(2,1)S(1)}, bf16[40,384]{1,0:T(8,128)(2,1)S(1)}, bf16[80,384]{1,0:T(8,128)(2,1)S(1)}) custom-call(s32[1,1]{1,0:T(1,128)S(6)} %copy.8.count, s32[1,1,48]{2,1,0:T(1,128)S(1)} %copy-done.3, s32[1,1,48]{2,1,0:T(1,128)S(1)} %copy-done.4, f32[48,384]{1,0:T(8,128)S(1)} %spread.1), custom_call_target="tpu_custom_call" | custom-call | tf_op jit(solution)/shard_map/prepare/pallas_call | solution.py:163
  2.1 0.1 collective-permute-done.other
  2.2 0.0 copy-done
  2.3 0.0 copy-done.1
  2.3 0.0 copy-done.2
  2.3 0.8 %project.1 = f32[40,128]{1,0:T(8,128)S(1)} custom-call(bf16[1,1,48,128,128]{4,3,2,1,0:T(8,128)(2,1)S(1)} %copy-done, bf16[384,80]{1,0:T(8,128)(2,1)S(1)} %get-tuple-element.13.pick, bf16[40,384]{1,0:T(8,128)(2,1)S(1)} %get-tuple-element.14.add, f32[32,128]{1,0:T(8,128)S(1)} %bitcast.3, f32[32,128]{1,0:T(8,128)S(1)} %collective-permute-done.other, ...), custom_call_target="tpu_custom_call" | custom-call | tf_op jit(solution)/shard_map/project/pallas_call | solution.py:163
  3.0 2.9 %collective-permute-start.2 = (f32[40,128]{1,0:T(8,128)S(1)}, f32[40,128]{1,0:T(8,128)S(1)}, u32[]{:S(2)}, u32[]{:S(2)}) collective-permute-start(f32[40,128]{1,0:T(8,128)S(1)} %project.1), channel_id=1, source_target_pairs={{0,4},{2,6},{4,0},{6,2},{8,12},{10,14},{12,8},{14,10},{1,5},{3,7},... | collective-permute-start | bytes 61448 | tf_op jit(solution)/shard_map/ppermute | solution.py:17
  6.0 1.4 %collective-permute-start.3 = (f32[40,128]{1,0:T(8,128)S(1)}, f32[40,128]{1,0:T(8,128)S(1)}, u32[]{:S(2)}, u32[]{:S(2)}) collective-permute-start(f32[40,128]{1,0:T(8,128)S(1)} %project.1), channel_id=1, source_target_pairs={{0,6},{2,4},{4,2},{6,0},{8,14},{10,12},{12,10},{14,8},{1,7},{3,5},... | collective-permute-start | bytes 61448 | tf_op jit(solution)/shard_map/ppermute | solution.py:17
  7.4 0.2 collective-permute-start.1
  7.5 0.2 %collective-permute-done.2.left = f32[40,128]{1,0:T(8,128)S(1)} collective-permute-done((f32[40,128]{1,0:T(8,128)S(1)}, f32[40,128]{1,0:T(8,128)S(1)}, u32[]{:S(2)}, u32[]{:S(2)}) %collective-permute-start.2) | collective-permute-done | bytes 20512 | tf_op jit(solution)/shard_map/ppermute | solution.py:17
  7.7 2.9 %collective-permute-done.3.right = f32[40,128]{1,0:T(8,128)S(1)} collective-permute-done((f32[40,128]{1,0:T(8,128)S(1)}, f32[40,128]{1,0:T(8,128)S(1)}, u32[]{:S(2)}, u32[]{:S(2)}) %collective-permute-start.3) | collective-permute-done | bytes 20512 | tf_op jit(solution)/shard_map/ppermute | solution.py:17
  10.7 0.5 %collective-permute-done.1 = f32[40,128]{1,0:T(8,128)S(1)} collective-permute-done((f32[40,128]{1,0:T(8,128)S(1)}, f32[40,128]{1,0:T(8,128)S(1)}, u32[]{:S(2)}, u32[]{:S(2)}) %collective-permute-start.1) | collective-permute-done | bytes 20512 | tf_op jit(solution)/shard_map/ppermute | solution.py:17
  11.2 2.6 %collective-permute-start.4 = (f32[40,128]{1,0:T(8,128)S(1)}, f32[40,128]{1,0:T(8,128)S(1)}, u32[]{:S(2)}, u32[]{:S(2)}) collective-permute-start(f32[40,128]{1,0:T(8,128)S(1)} %add_add_fusion), channel_id=1, source_target_pairs={{0,8},{2,10},{4,12},{6,14},{8,0},{10,2},{12,4},{14,6},{1,9},{3,11}... | collective-permute-start | bytes 61448 | tf_op jit(solution)/shard_map/ppermute | solution.py:17
  13.7 2.1 %collective-permute-done.4 = f32[40,128]{1,0:T(8,128)S(1)} collective-permute-done((f32[40,128]{1,0:T(8,128)S(1)}, f32[40,128]{1,0:T(8,128)S(1)}, u32[]{:S(2)}, u32[]{:S(2)}) %collective-permute-start.4) | collective-permute-done | bytes 20512 | tf_op jit(solution)/shard_map/ppermute | solution.py:17
  15.8 0.6 %backproject.1 = (f32[40,128]{1,0:T(8,128)S(1)}, bf16[48,128]{1,0:T(8,128)(2,1)S(1)}, f32[4,128]{1,0:T(4,128)S(1)}) custom-call(bf16[1,1,48,128,128]{4,3,2,1,0:T(8,128)(2,1)S(1)} %copy-done, bf16[384,40]{1,0:T(8,128)(2,1)S(1)} %get-tuple-element.11.pick, bf16[80,384]{1,0:T(8,128)(2,1)S(1)} %get-tuple-element.12.add, f32[40,128]{1,0:T(8,128)S(1)} %add.12.total), custom_call_target="tpu_custom_call" | custom-call | tf_op jit(solution)/shard_map/backproject/pallas_call | solution.py:163
  16.5 0.1 collective-permute-start.5
  16.6 1.2 %collective-permute-done.5.there = bf16[48,128]{1,0:T(8,128)(2,1)S(1)} collective-permute-done((bf16[48,128]{1,0:T(8,128)(2,1)S(1)}, bf16[48,128]{1,0:T(8,128)(2,1)S(1)}, u32[]{:S(2)}, u32[]{:S(2)}) %collective-permute-start.5) | collective-permute-done | bytes 12320 | tf_op jit(solution)/shard_map/ppermute | solution.py:17
  17.7 0.6 %update.1 = (f32[32,128]{1,0:T(8,128)}, bf16[1,1,4,128]{3,2,1,0:T(4,128)(2,1)}) custom-call(f32[32,128]{1,0:T(8,128)S(1)} %bitcast.4, f32[40,128]{1,0:T(8,128)S(1)} %get-tuple-element.15.own, bf16[48,128]{1,0:T(8,128)(2,1)S(1)} %collective-permute-done.5.there, f32[4,128]{1,0:T(4,128)S(1)} %get-tuple-element.17.residual), custom_call_target="tpu_custom_call" | custom-call | tf_op jit(solution)/shard_map/update/pallas_call | solution.py:163
  (4 shorter events, 0.0 us)
Async XLA Ops:
  0.6 1.2 %copy-start.3 = (s32[1,1,48]{2,1,0:T(1,128)S(1)}, s32[1,1,48]{2,1,0:T(1,128)}, u32[]{:S(2)}) copy-start(s32[1,1,48]{2,1,0:T(1,128)} %rows.1) | copy-start | bytes 580
  0.6 1.2 %copy-start.4 = (s32[1,1,48]{2,1,0:T(1,128)S(1)}, s32[1,1,48]{2,1,0:T(1,128)}, u32[]{:S(2)}) copy-start(s32[1,1,48]{2,1,0:T(1,128)} %cols.1) | copy-start | bytes 580
  0.7 1.6 %copy-start = (bf16[1,1,48,128,128]{4,3,2,1,0:T(8,128)(2,1)S(1)}, bf16[1,1,48,128,128]{4,3,2,1,0:T(8,128)(2,1)}, u32[]{:S(2)}) copy-start(bf16[1,1,48,128,128]{4,3,2,1,0:T(8,128)(2,1)} %tiles.3) | copy-start | bytes 4718596
  0.7 1.6 %copy-start.1 = (f32[8,4,128]{2,1,0:T(4,128)S(1)}, f32[8,4,128]{2,1,0:T(4,128)}, u32[]{:S(2)}) copy-start(f32[8,4,128]{2,1,0:T(4,128)} %param.6) | copy-start | bytes 49156
  0.7 1.6 %copy-start.2 = (f32[1,1,4,128]{3,2,1,0:T(4,128)S(1)}, f32[1,1,4,128]{3,2,1,0:T(4,128)}, u32[]{:S(2)}) copy-start(f32[1,1,4,128]{3,2,1,0:T(4,128)} %measured.1) | copy-start | bytes 6148
  0.7 1.6 %collective-permute-start = (f32[32,128]{1,0:T(8,128)}, f32[32,128]{1,0:T(8,128)S(1)}, u32[]{:S(2)}, u32[]{:S(2)}) collective-permute-start(f32[32,128]{1,0:T(8,128)} %bitcast.2), channel_id=1, source_target_pairs={{0,1},{1,0},{2,3},{3,2},{4,5},{5,4},{6,7},{7,6},{8,9},{9,8},{10,11... | collective-permute-start | bytes 49160 | tf_op jit(solution)/shard_map/ppermute | solution.py:17
  3.0 4.7 %collective-permute-start.2 = (f32[40,128]{1,0:T(8,128)S(1)}, f32[40,128]{1,0:T(8,128)S(1)}, u32[]{:S(2)}, u32[]{:S(2)}) collective-permute-start(f32[40,128]{1,0:T(8,128)S(1)} %project.1), channel_id=1, source_target_pairs={{0,4},{2,6},{4,0},{6,2},{8,12},{10,14},{12,8},{14,10},{1,5},{3,7},... | collective-permute-start | bytes 61448 | tf_op jit(solution)/shard_map/ppermute | solution.py:17
  6.0 4.7 %collective-permute-start.3 = (f32[40,128]{1,0:T(8,128)S(1)}, f32[40,128]{1,0:T(8,128)S(1)}, u32[]{:S(2)}, u32[]{:S(2)}) collective-permute-start(f32[40,128]{1,0:T(8,128)S(1)} %project.1), channel_id=1, source_target_pairs={{0,6},{2,4},{4,2},{6,0},{8,14},{10,12},{12,10},{14,8},{1,7},{3,5},... | collective-permute-start | bytes 61448 | tf_op jit(solution)/shard_map/ppermute | solution.py:17
  7.4 3.8 %collective-permute-start.1 = (f32[40,128]{1,0:T(8,128)S(1)}, f32[40,128]{1,0:T(8,128)S(1)}, u32[]{:S(2)}, u32[]{:S(2)}) collective-permute-start(f32[40,128]{1,0:T(8,128)S(1)} %project.1), channel_id=1, source_target_pairs={{0,2},{2,0},{4,6},{6,4},{8,10},{10,8},{12,14},{14,12},{1,3},{3,1},... | collective-permute-start | bytes 61448 | tf_op jit(solution)/shard_map/ppermute | solution.py:17
  11.2 4.7 %collective-permute-start.4 = (f32[40,128]{1,0:T(8,128)S(1)}, f32[40,128]{1,0:T(8,128)S(1)}, u32[]{:S(2)}, u32[]{:S(2)}) collective-permute-start(f32[40,128]{1,0:T(8,128)S(1)} %add_add_fusion), channel_id=1, source_target_pairs={{0,8},{2,10},{4,12},{6,14},{8,0},{10,2},{12,4},{14,6},{1,9},{3,11}... | collective-permute-start | bytes 61448 | tf_op jit(solution)/shard_map/ppermute | solution.py:17
  16.5 1.2 %collective-permute-start.5 = (bf16[48,128]{1,0:T(8,128)(2,1)S(1)}, bf16[48,128]{1,0:T(8,128)(2,1)S(1)}, u32[]{:S(2)}, u32[]{:S(2)}) collective-permute-start(bf16[48,128]{1,0:T(8,128)(2,1)S(1)} %get-tuple-element.16), channel_id=1, source_target_pairs={{0,1},{1,0},{2,3},{3,2},{4,5},{5,4},{6,7},{7,6},{8,9},{9,8},{10,11... | collective-permute-start | bytes 36872 | tf_op jit(solution)/shard_map/ppermute | solution.py:17

commit v18 on v14

--- a/solution.py
+++ b/solution.py
@@ -13,19 +13,39 @@
 
 
 def exchange(value, axis, mask):
+    return permute(value, axis, lambda i: i ^ mask)
+
+
+def permute(value, axis, target):
+    return lax.ppermute(value, axis, [(i, target(i)) for i in range(lax.axis_size(axis))])
+
+
+QUAD = ((1, 0, 2, 3), (2, 3, 1, 0), (3, 2, 0, 1), (0, 1, 3, 2))
+
+
+def copy_kernel(value, out):
+    out[...] = value[...]
+
+
+def add_kernel(kept, left, right, kept_out, out):
+    kept_out[...] = kept[...]
+    out[...] = left[...] + right[...]
+
+
+def all_sum(value, axis, call):
     size = lax.axis_size(axis)
-    return lax.ppermute(value, axis, [(i, i ^ mask) for i in range(size)])
-
-
-def all_sum(value, axis):
-    size = lax.axis_size(axis)
+    shape = (value.shape, value.dtype)
     stride = 1
     while stride < size:
         if 2 * stride < size:
-            across = exchange(value, axis, stride)
-            both = exchange(value, axis, 3 * stride)
-            along = exchange(value, axis, 2 * stride)
-            value = (value + across) + (along + both)
+            place = [(i // stride) % 4 for i in range(size)]
+            first, right, left, last = (
+                permute(value, axis, lambda i: i + (to[place[i]] - place[i]) * stride) for to in QUAD
+            )
+            (first,) = call(copy_kernel, "kept", [shape], [], [first])
+            first, both = call(add_kernel, "add", [shape] * 2, [], [first, left, right])
+            low = (lax.axis_index(axis) // stride) % 4 < 2
+            value = (value + jnp.where(low, first, last)) + both
         else:
             value = value + exchange(value, axis, stride)
         stride *= 4
@@ -172,7 +192,7 @@
         scalars=1,
         aliases={7: 1},
     )
-    total = all_sum(part, "vox")
+    total = all_sum(part, "vox", call)
     own, send, residual, _ = call(
         backproject_kernel,
         "backproject",

time: 18.6 us -> 20.4 us (1.097)
  the two profiles are of different devices: /device:TPU:0 before, /device:TPU:25 now
where the time goes in v18:
time: 20.4 us; the launch traced here: 20.2 us
  starting transfers between devices  10.3 us (50%)
  waiting for transfers between devices  6.46 us (32%)
  Pallas kernels  2.08 us (10%)
  between operations  1.41 us (7%)
    ppermute x7, starting transfers between devices, permute(): lax.ppermute(value, axis, [(i, target(i)) for i in range(lax.axis_size(ax...  10.3 us
    ppermute x7, waiting for transfers between devices, permute(): lax.ppermute(value, axis, [(i, target(i)) for i in range(lax.axis_size(ax...  6.46 us
    pallas_call x6, Pallas kernels, call(): pl.pallas_call(kernel, out_shape=[jax.ShapeDtypeStruct(shape, dtype) for...  2.08 us
  transfers between devices with their start and end apart: 7, of which 5 were waited for; matrix products, arithmetic and copies ran while one was open for 0% of the time, Pallas kernels for 0%

profile of v18, /device:TPU:25, one launch (start us, length us, event | category | flops | bytes accessed | tf_op | source)
XLA Modules:
  0.0 20.2 jit_solution(3266327960632272479)
XLA Ops:
  0.6 0.0 copy-start
  0.6 0.0 copy-start.1
  0.7 0.0 copy-start.2
  0.7 0.0 copy-start.3
  0.7 0.0 copy-start.4
  0.7 0.7 %collective-permute-start = (f32[32,128]{1,0:T(8,128)}, f32[32,128]{1,0:T(8,128)S(1)}, u32[]{:S(2)}, u32[]{:S(2)}) collective-permute-start(f32[32,128]{1,0:T(8,128)} %bitcast.2), channel_id=1, source_target_pairs={{0,1},{1,0},{2,3},{3,2},{4,5},{5,4},{6,7},{7,6},{8,9},{9,8},{10,11... | collective-permute-start | bytes 49160 | tf_op jit(solution)/shard_map/ppermute | solution.py:20
  2.1 0.4 %collective-permute-done.other = f32[32,128]{1,0:T(8,128)S(1)} collective-permute-done((f32[32,128]{1,0:T(8,128)}, f32[32,128]{1,0:T(8,128)S(1)}, u32[]{:S(2)}, u32[]{:S(2)}) %collective-permute-start) | collective-permute-done | bytes 16416 | tf_op jit(solution)/shard_map/ppermute | solution.py:20
  2.5 0.0 copy-done
  2.5 0.0 copy-done.1
  2.5 0.0 copy-done.2
  2.5 0.0 copy-done.3
  2.5 0.0 copy-done.4
  2.5 0.8 %project.1 = (f32[40,128]{1,0:T(8,128)S(1)}, f32[384,128]{1,0:T(8,128)S(1)}) custom-call(s32[1,1]{1,0:T(1,128)S(6)} %copy.12.count, bf16[1,1,48,128,128]{4,3,2,1,0:T(8,128)(2,1)S(1)} %copy-done, s32[1,1,48]{2,1,0:T(1,128)S(1)} %copy-done.3, s32[1,1,48]{2,1,0:T(1,128)S(1)} %copy-done.4, f32[32,128]{1,0:T(8,128)S(1)} %bitcast.3, ...), custom_call_target="tpu_custom_call", output_to_operand_aliasing={{1}: (7, {})} | custom-call | tf_op jit(solution)/shard_map/project/pallas_call | solution.py:162
  3.3 0.7 %collective-permute-start.1 = (f32[40,128]{1,0:T(8,128)S(1)}, f32[40,128]{1,0:T(8,128)S(1)}, u32[]{:S(2)}, u32[]{:S(2)}) collective-permute-start(f32[40,128]{1,0:T(8,128)S(1)} %get-tuple-element.11), channel_id=1, source_target_pairs={{0,2},{2,0},{4,4},{6,6},{8,10},{10,8},{12,12},{14,14},{1,3},{3,1},... | collective-permute-start | bytes 61448 | tf_op jit(solution)/shard_map/ppermute | solution.py:20
  4.0 2.6 %collective-permute-start.3 = (f32[40,128]{1,0:T(8,128)S(1)}, f32[40,128]{1,0:T(8,128)S(1)}, u32[]{:S(2)}, u32[]{:S(2)}) collective-permute-start(f32[40,128]{1,0:T(8,128)S(1)} %get-tuple-element.11), channel_id=1, source_target_pairs={{0,4},{2,6},{4,2},{6,0},{8,12},{10,14},{12,10},{14,8},{1,5},{3,7},... | collective-permute-start | bytes 61448 | tf_op jit(solution)/shard_map/ppermute | solution.py:20
  6.7 0.1 collective-permute-start.2
  6.7 3.0 %collective-permute-start.4 = (f32[40,128]{1,0:T(8,128)S(1)}, f32[40,128]{1,0:T(8,128)S(1)}, u32[]{:S(2)}, u32[]{:S(2)}) collective-permute-start(f32[40,128]{1,0:T(8,128)S(1)} %get-tuple-element.11), channel_id=1, source_target_pairs={{0,0},{2,2},{4,6},{6,4},{8,8},{10,10},{12,14},{14,12},{1,1},{3,3},... | collective-permute-start | bytes 61448 | tf_op jit(solution)/shard_map/ppermute | solution.py:20
  9.8 0.0 collective-permute-done.1.value
  9.8 0.0 collective-permute-done.3.right
  9.8 0.4 %collective-permute-done.2.left = f32[40,128]{1,0:T(8,128)S(1)} collective-permute-done((f32[40,128]{1,0:T(8,128)S(1)}, f32[40,128]{1,0:T(8,128)S(1)}, u32[]{:S(2)}, u32[]{:S(2)}) %collective-permute-start.2) | collective-permute-done | bytes 20512 | tf_op jit(solution)/shard_map/ppermute | solution.py:20
  10.2 1.4 %collective-permute-done.4 = f32[40,128]{1,0:T(8,128)S(1)} collective-permute-done((f32[40,128]{1,0:T(8,128)S(1)}, f32[40,128]{1,0:T(8,128)S(1)}, u32[]{:S(2)}, u32[]{:S(2)}) %collective-permute-start.4) | collective-permute-done | bytes 20512 | tf_op jit(solution)/shard_map/ppermute | solution.py:20
  11.6 0.1 collective-permute-start.5
  11.6 3.5 %collective-permute-done.5 = f32[40,128]{1,0:T(8,128)S(1)} collective-permute-done((f32[40,128]{1,0:T(8,128)S(1)}, f32[40,128]{1,0:T(8,128)S(1)}, u32[]{:S(2)}, u32[]{:S(2)}) %collective-permute-start.5) | collective-permute-done | bytes 20512 | tf_op jit(solution)/shard_map/ppermute | solution.py:20
  15.2 0.6 %backproject.1 = (f32[40,128]{1,0:T(8,128)S(1)}, bf16[64,128]{1,0:T(8,128)(2,1)S(1)}, f32[4,128]{1,0:T(4,128)S(1)}, f32[384,128]{1,0:T(8,128)S(1)}) custom-call(s32[1,1]{1,0:T(1,128)S(6)} %copy.12.count, bf16[1,1,48,128,128]{4,3,2,1,0:T(8,128)(2,1)S(1)} %copy-done, s32[1,1,48]{2,1,0:T(1,128)S(1)} %copy-done.3, ...), custom_call_target="tpu_custom_call", output_to_operand_aliasing={{3}: (5, {})} | custom-call | tf_op jit(solution)/shard_map/backproject/pallas_call | solution.py:162
  15.8 3.0 %collective-permute-start.6 = (bf16[64,128]{1,0:T(8,128)(2,1)S(1)}, bf16[64,128]{1,0:T(8,128)(2,1)S(1)}, u32[]{:S(2)}, u32[]{:S(2)}) collective-permute-start(bf16[64,128]{1,0:T(8,128)(2,1)S(1)} %get-tuple-element.16), channel_id=1, source_target_pairs={{0,1},{1,0},{2,3},{3,2},{4,5},{5,4},{6,7},{7,6},{8,9},{9,8},{10,11... | collective-permute-start | bytes 49160 | tf_op jit(solution)/shard_map/ppermute | solution.py:20
  18.8 0.8 %collective-permute-done.6.there = bf16[64,128]{1,0:T(8,128)(2,1)S(1)} collective-permute-done((bf16[64,128]{1,0:T(8,128)(2,1)S(1)}, bf16[64,128]{1,0:T(8,128)(2,1)S(1)}, u32[]{:S(2)}, u32[]{:S(2)}) %collective-permute-start.6) | collective-permute-done | bytes 16416 | tf_op jit(solution)/shard_map/ppermute | solution.py:20
  19.6 0.6 %update.1 = (f32[32,128]{1,0:T(8,128)}, bf16[1,1,4,128]{3,2,1,0:T(4,128)(2,1)}) custom-call(f32[32,128]{1,0:T(8,128)S(1)} %bitcast.4, f32[40,128]{1,0:T(8,128)S(1)} %get-tuple-element.15.own, bf16[64,128]{1,0:T(8,128)(2,1)S(1)} %collective-permute-done.6.there, f32[4,128]{1,0:T(4,128)S(1)} %get-tuple-element.17.residual), custom_call_target="tpu_custom_call" | custom-call | tf_op jit(solution)/shard_map/update/pallas_call | solution.py:162
  (5 shorter events, 0.0 us)
Async XLA Ops:
  0.6 1.8 %copy-start = (bf16[1,1,48,128,128]{4,3,2,1,0:T(8,128)(2,1)S(1)}, bf16[1,1,48,128,128]{4,3,2,1,0:T(8,128)(2,1)}, u32[]{:S(2)}) copy-start(bf16[1,1,48,128,128]{4,3,2,1,0:T(8,128)(2,1)} %tiles.3) | copy-start | bytes 4718596
  0.6 1.8 %copy-start.1 = (f32[8,4,128]{2,1,0:T(4,128)S(1)}, f32[8,4,128]{2,1,0:T(4,128)}, u32[]{:S(2)}) copy-start(f32[8,4,128]{2,1,0:T(4,128)} %param.6) | copy-start | bytes 49156
  0.7 1.8 %copy-start.2 = (f32[1,1,4,128]{3,2,1,0:T(4,128)S(1)}, f32[1,1,4,128]{3,2,1,0:T(4,128)}, u32[]{:S(2)}) copy-start(f32[1,1,4,128]{3,2,1,0:T(4,128)} %measured.1) | copy-start | bytes 6148
  0.7 1.8 %copy-start.3 = (s32[1,1,48]{2,1,0:T(1,128)S(1)}, s32[1,1,48]{2,1,0:T(1,128)}, u32[]{:S(2)}) copy-start(s32[1,1,48]{2,1,0:T(1,128)} %rows.5) | copy-start | bytes 580
  0.7 1.8 %copy-start.4 = (s32[1,1,48]{2,1,0:T(1,128)S(1)}, s32[1,1,48]{2,1,0:T(1,128)}, u32[]{:S(2)}) copy-start(s32[1,1,48]{2,1,0:T(1,128)} %cols.3) | copy-start | bytes 580
  0.7 1.8 %collective-permute-start = (f32[32,128]{1,0:T(8,128)}, f32[32,128]{1,0:T(8,128)S(1)}, u32[]{:S(2)}, u32[]{:S(2)}) collective-permute-start(f32[32,128]{1,0:T(8,128)} %bitcast.2), channel_id=1, source_target_pairs={{0,1},{1,0},{2,3},{3,2},{4,5},{5,4},{6,7},{7,6},{8,9},{9,8},{10,11... | collective-permute-start | bytes 49160 | tf_op jit(solution)/shard_map/ppermute | solution.py:20
  3.3 6.5 %collective-permute-start.1 = (f32[40,128]{1,0:T(8,128)S(1)}, f32[40,128]{1,0:T(8,128)S(1)}, u32[]{:S(2)}, u32[]{:S(2)}) collective-permute-start(f32[40,128]{1,0:T(8,128)S(1)} %get-tuple-element.11), channel_id=1, source_target_pairs={{0,2},{2,0},{4,4},{6,6},{8,10},{10,8},{12,12},{14,14},{1,3},{3,1},... | collective-permute-start | bytes 61448 | tf_op jit(solution)/shard_map/ppermute | solution.py:20
  4.0 5.8 %collective-permute-start.3 = (f32[40,128]{1,0:T(8,128)S(1)}, f32[40,128]{1,0:T(8,128)S(1)}, u32[]{:S(2)}, u32[]{:S(2)}) collective-permute-start(f32[40,128]{1,0:T(8,128)S(1)} %get-tuple-element.11), channel_id=1, source_target_pairs={{0,4},{2,6},{4,2},{6,0},{8,12},{10,14},{12,10},{14,8},{1,5},{3,7},... | collective-permute-start | bytes 61448 | tf_op jit(solution)/shard_map/ppermute | solution.py:20
  6.7 3.5 %collective-permute-start.2 = (f32[40,128]{1,0:T(8,128)S(1)}, f32[40,128]{1,0:T(8,128)S(1)}, u32[]{:S(2)}, u32[]{:S(2)}) collective-permute-start(f32[40,128]{1,0:T(8,128)S(1)} %get-tuple-element.11), channel_id=1, source_target_pairs={{0,6},{2,4},{4,0},{6,2},{8,14},{10,12},{12,8},{14,10},{1,7},{3,5},... | collective-permute-start | bytes 61448 | tf_op jit(solution)/shard_map/ppermute | solution.py:20
  6.7 4.8 %collective-permute-start.4 = (f32[40,128]{1,0:T(8,128)S(1)}, f32[40,128]{1,0:T(8,128)S(1)}, u32[]{:S(2)}, u32[]{:S(2)}) collective-permute-start(f32[40,128]{1,0:T(8,128)S(1)} %get-tuple-element.11), channel_id=1, source_target_pairs={{0,0},{2,2},{4,6},{6,4},{8,8},{10,10},{12,14},{14,12},{1,1},{3,3},... | collective-permute-start | bytes 61448 | tf_op jit(solution)/shard_map/ppermute | solution.py:20
  11.6 3.6 %collective-permute-start.5 = (f32[40,128]{1,0:T(8,128)S(1)}, f32[40,128]{1,0:T(8,128)S(1)}, u32[]{:S(2)}, u32[]{:S(2)}) collective-permute-start(f32[40,128]{1,0:T(8,128)S(1)} %add_add_fusion), channel_id=1, source_target_pairs={{0,8},{2,10},{4,12},{6,14},{8,0},{10,2},{12,4},{14,6},{1,9},{3,11}... | collective-permute-start | bytes 61448 | tf_op jit(solution)/shard_map/ppermute | solution.py:20
  15.8 3.8 %collective-permute-start.6 = (bf16[64,128]{1,0:T(8,128)(2,1)S(1)}, bf16[64,128]{1,0:T(8,128)(2,1)S(1)}, u32[]{:S(2)}, u32[]{:S(2)}) collective-permute-start(bf16[64,128]{1,0:T(8,128)(2,1)S(1)} %get-tuple-element.16), channel_id=1, source_target_pairs={{0,1},{1,0},{2,3},{3,2},{4,5},{5,4},{6,7},{7,6},{8,9},{9,8},{10,11... | collective-permute-start | bytes 49160 | tf_op jit(solution)/shard_map/ppermute | solution.py:20

commit v19 on v14

--- a/solution.py
+++ b/solution.py
@@ -59,21 +59,25 @@
 
 
 def apply_tiles(picked, tiles, contract, add, count, prods, kinds):
-    slots, rays, width = tiles.shape[2:]
-    for n in range(0, slots, 2):
-        pair = tiles[0, 0, n : n + 2]
-        if contract:
-            pair = pair.reshape(2 * rays, width)
-        else:
-            pair = jnp.concatenate([pair[0], pair[1]], axis=1)
+    slots, _, width = tiles.shape[2:]
+    zeros = jnp.zeros((SUB, width), jnp.float32)
+    for n in range(0, slots, 4):
+        rows = [picked[k * SUB : (k + 1) * SUB, :] for k in range(n, n + 4)]
+        first = jnp.concatenate([rows[0], zeros, rows[2], zeros], axis=0)
+        second = jnp.concatenate([zeros, rows[1], zeros, rows[3]], axis=0)
+        four = [tiles[0, 0, k] for k in range(n, n + 4)]
+        order = (0, 1, 2, 3) if contract else (0, 2, 1, 3)
+        upper = jnp.concatenate([four[order[0]], four[order[1]]], axis=1)
+        lower = jnp.concatenate([four[order[2]], four[order[3]]], axis=1)
         both = lax.dot_general(
-            picked[n * SUB : (n + 2) * SUB, :].astype(jnp.bfloat16),
-            pair,
+            jnp.concatenate([first, second], axis=1).astype(jnp.bfloat16),
+            jnp.concatenate([upper, lower], axis=0),
             (((1,), (contract,)), ((), ())),
             preferred_element_type=jnp.float32,
         )
-        prods[pl.ds(n, SUB, stride=slots), :] = both[:SUB, :width]
-        prods[pl.ds(n + 1, SUB, stride=slots), :] = both[SUB:, width:]
+        for k in range(4):
+            columns = slice(0, width) if k < 2 else slice(width, 2 * width)
+            prods[pl.ds(n + k, SUB, stride=slots), :] = both[k * SUB : (k + 1) * SUB, columns]
     left = jnp.concatenate([prods[c * slots : (c + 1) * slots, :] for c in range(kinds)], axis=1)
     used = lax.broadcasted_iota(jnp.int32, add.shape, 1) < count[0, 0]
     onehot = jnp.where(used, add, 0.0).astype(jnp.bfloat16)

time: 18.6 us -> 18.7 us (level)
  no operation moved by 1% of the time
where the time goes in v19:
time: 18.7 us; the launch traced here: 18.5 us
  starting transfers between devices  7.77 us (42%)
  waiting for transfers between devices  7.23 us (39%)
  Pallas kernels  2.14 us (11%)
  between operations  1.36 us (7%)
    ppermute x6, starting transfers between devices, exchange(): return lax.ppermute(value, axis, [(i, i ^ mask) for i in range(size)])  7.77 us
    ppermute x6, waiting for transfers between devices, exchange(): return lax.ppermute(value, axis, [(i, i ^ mask) for i in range(size)])  7.23 us
    pallas_call x4, Pallas kernels, call(): pl.pallas_call(kernel, out_shape=[jax.ShapeDtypeStruct(shape, dtype) for...  2.14 us
  transfers between devices with their start and end apart: 6, of which 6 were waited for; matrix products, arithmetic and copies ran while one was open for 0% of the time, Pallas kernels for 0%

profile of v19, /device:TPU:0, one launch (start us, length us, event | category | flops | bytes accessed | tf_op | source)
XLA Modules:
  0.0 18.5 jit_solution(11971905009402355482)
XLA Ops:
  0.6 0.0 copy-start
  0.6 0.0 copy-start.1
  0.7 0.0 copy-start.2
  0.7 0.0 copy-start.3
  0.7 0.0 copy-start.4
  0.7 0.5 %collective-permute-start = (f32[32,128]{1,0:T(8,128)}, f32[32,128]{1,0:T(8,128)S(1)}, u32[]{:S(2)}, u32[]{:S(2)}) collective-permute-start(f32[32,128]{1,0:T(8,128)} %bitcast.2), channel_id=1, source_target_pairs={{0,1},{1,0},{2,3},{3,2},{4,5},{5,4},{6,7},{7,6},{8,9},{9,8},{10,11... | collective-permute-start | bytes 49160 | tf_op jit(solution)/shard_map/ppermute | solution.py:17
  1.9 0.4 %collective-permute-done.other = f32[32,128]{1,0:T(8,128)S(1)} collective-permute-done((f32[32,128]{1,0:T(8,128)}, f32[32,128]{1,0:T(8,128)S(1)}, u32[]{:S(2)}, u32[]{:S(2)}) %collective-permute-start) | collective-permute-done | bytes 16416 | tf_op jit(solution)/shard_map/ppermute | solution.py:17
  2.2 0.0 copy-done
  2.3 0.0 copy-done.1
  2.3 0.0 copy-done.2
  2.3 0.0 copy-done.3
  2.3 0.0 copy-done.4
  2.3 0.8 %project.1 = (f32[40,128]{1,0:T(8,128)S(1)}, f32[384,128]{1,0:T(8,128)S(1)}) custom-call(s32[1,1]{1,0:T(1,128)S(6)} %copy.12.count, bf16[1,1,48,128,128]{4,3,2,1,0:T(8,128)(2,1)S(1)} %copy-done, s32[1,1,48]{2,1,0:T(1,128)S(1)} %copy-done.3, s32[1,1,48]{2,1,0:T(1,128)S(1)} %copy-done.4, f32[32,128]{1,0:T(8,128)S(1)} %bitcast.3, ...), custom_call_target="tpu_custom_call", output_to_operand_aliasing={{1}: (7, {})} | custom-call | tf_op jit(solution)/shard_map/project/pallas_call | solution.py:146
  3.1 3.9 %collective-permute-start.3 = (f32[40,128]{1,0:T(8,128)S(1)}, f32[40,128]{1,0:T(8,128)S(1)}, u32[]{:S(2)}, u32[]{:S(2)}) collective-permute-start(f32[40,128]{1,0:T(8,128)S(1)} %get-tuple-element.9), channel_id=1, source_target_pairs={{0,6},{2,4},{4,2},{6,0},{8,14},{10,12},{12,10},{14,8},{1,7},{3,5},... | collective-permute-start | bytes 61448 | tf_op jit(solution)/shard_map/ppermute | solution.py:17
  7.0 0.4 %collective-permute-start.2 = (f32[40,128]{1,0:T(8,128)S(1)}, f32[40,128]{1,0:T(8,128)S(1)}, u32[]{:S(2)}, u32[]{:S(2)}) collective-permute-start(f32[40,128]{1,0:T(8,128)S(1)} %get-tuple-element.9), channel_id=1, source_target_pairs={{0,4},{2,6},{4,0},{6,2},{8,12},{10,14},{12,8},{14,10},{1,5},{3,7},... | collective-permute-start | bytes 61448 | tf_op jit(solution)/shard_map/ppermute | solution.py:17
  7.4 0.2 %collective-permute-start.1 = (f32[40,128]{1,0:T(8,128)S(1)}, f32[40,128]{1,0:T(8,128)S(1)}, u32[]{:S(2)}, u32[]{:S(2)}) collective-permute-start(f32[40,128]{1,0:T(8,128)S(1)} %get-tuple-element.9), channel_id=1, source_target_pairs={{0,2},{2,0},{4,6},{6,4},{8,10},{10,8},{12,14},{14,12},{1,3},{3,1},... | collective-permute-start | bytes 61448 | tf_op jit(solution)/shard_map/ppermute | solution.py:17
  7.6 1.1 %collective-permute-done.3 = f32[40,128]{1,0:T(8,128)S(1)} collective-permute-done((f32[40,128]{1,0:T(8,128)S(1)}, f32[40,128]{1,0:T(8,128)S(1)}, u32[]{:S(2)}, u32[]{:S(2)}) %collective-permute-start.3) | collective-permute-done | bytes 20512 | tf_op jit(solution)/shard_map/ppermute | solution.py:17
  8.8 2.0 %collective-permute-done.2 = f32[40,128]{1,0:T(8,128)S(1)} collective-permute-done((f32[40,128]{1,0:T(8,128)S(1)}, f32[40,128]{1,0:T(8,128)S(1)}, u32[]{:S(2)}, u32[]{:S(2)}) %collective-permute-start.2) | collective-permute-done | bytes 20512 | tf_op jit(solution)/shard_map/ppermute | solution.py:17
  10.8 0.4 %collective-permute-done.1 = f32[40,128]{1,0:T(8,128)S(1)} collective-permute-done((f32[40,128]{1,0:T(8,128)S(1)}, f32[40,128]{1,0:T(8,128)S(1)}, u32[]{:S(2)}, u32[]{:S(2)}) %collective-permute-start.1) | collective-permute-done | bytes 20512 | tf_op jit(solution)/shard_map/ppermute | solution.py:17
  11.2 2.6 %collective-permute-start.4 = (f32[40,128]{1,0:T(8,128)S(1)}, f32[40,128]{1,0:T(8,128)S(1)}, u32[]{:S(2)}, u32[]{:S(2)}) collective-permute-start(f32[40,128]{1,0:T(8,128)S(1)} %add_add_fusion), channel_id=1, source_target_pairs={{0,8},{2,10},{4,12},{6,14},{8,0},{10,2},{12,4},{14,6},{1,9},{3,11}... | collective-permute-start | bytes 61448 | tf_op jit(solution)/shard_map/ppermute | solution.py:17
  13.9 2.1 %collective-permute-done.4 = f32[40,128]{1,0:T(8,128)S(1)} collective-permute-done((f32[40,128]{1,0:T(8,128)S(1)}, f32[40,128]{1,0:T(8,128)S(1)}, u32[]{:S(2)}, u32[]{:S(2)}) %collective-permute-start.4) | collective-permute-done | bytes 20512 | tf_op jit(solution)/shard_map/ppermute | solution.py:17
  16.0 0.7 %backproject.1 = (f32[40,128]{1,0:T(8,128)S(1)}, bf16[64,128]{1,0:T(8,128)(2,1)S(1)}, f32[4,128]{1,0:T(4,128)S(1)}, f32[384,128]{1,0:T(8,128)S(1)}) custom-call(s32[1,1]{1,0:T(1,128)S(6)} %copy.12.count, bf16[1,1,48,128,128]{4,3,2,1,0:T(8,128)(2,1)S(1)} %copy-done, s32[1,1,48]{2,1,0:T(1,128)S(1)} %copy-done.3, ...), custom_call_target="tpu_custom_call", output_to_operand_aliasing={{3}: (5, {})} | custom-call | tf_op jit(solution)/shard_map/backproject/pallas_call | solution.py:146
  16.7 0.1 collective-permute-start.5
  16.7 1.2 %collective-permute-done.5.there = bf16[64,128]{1,0:T(8,128)(2,1)S(1)} collective-permute-done((bf16[64,128]{1,0:T(8,128)(2,1)S(1)}, bf16[64,128]{1,0:T(8,128)(2,1)S(1)}, u32[]{:S(2)}, u32[]{:S(2)}) %collective-permute-start.5) | collective-permute-done | bytes 16416 | tf_op jit(solution)/shard_map/ppermute | solution.py:17
  17.9 0.6 %update.1 = (f32[32,128]{1,0:T(8,128)}, bf16[1,1,4,128]{3,2,1,0:T(4,128)(2,1)}) custom-call(f32[32,128]{1,0:T(8,128)S(1)} %bitcast.4, f32[40,128]{1,0:T(8,128)S(1)} %get-tuple-element.11.own, bf16[64,128]{1,0:T(8,128)(2,1)S(1)} %collective-permute-done.5.there, f32[4,128]{1,0:T(4,128)S(1)} %get-tuple-element.13.residual), custom_call_target="tpu_custom_call" | custom-call | tf_op jit(solution)/shard_map/update/pallas_call | solution.py:146
  (3 shorter events, 0.0 us)
Async XLA Ops:
  0.6 1.6 %copy-start = (bf16[1,1,48,128,128]{4,3,2,1,0:T(8,128)(2,1)S(1)}, bf16[1,1,48,128,128]{4,3,2,1,0:T(8,128)(2,1)}, u32[]{:S(2)}) copy-start(bf16[1,1,48,128,128]{4,3,2,1,0:T(8,128)(2,1)} %tiles.3) | copy-start | bytes 4718596
  0.6 1.6 %copy-start.1 = (f32[8,4,128]{2,1,0:T(4,128)S(1)}, f32[8,4,128]{2,1,0:T(4,128)}, u32[]{:S(2)}) copy-start(f32[8,4,128]{2,1,0:T(4,128)} %param.6) | copy-start | bytes 49156
  0.7 1.6 %copy-start.2 = (f32[1,1,4,128]{3,2,1,0:T(4,128)S(1)}, f32[1,1,4,128]{3,2,1,0:T(4,128)}, u32[]{:S(2)}) copy-start(f32[1,1,4,128]{3,2,1,0:T(4,128)} %measured.1) | copy-start | bytes 6148
  0.7 1.6 %copy-start.3 = (s32[1,1,48]{2,1,0:T(1,128)S(1)}, s32[1,1,48]{2,1,0:T(1,128)}, u32[]{:S(2)}) copy-start(s32[1,1,48]{2,1,0:T(1,128)} %rows.5) | copy-start | bytes 580
  0.7 1.6 %copy-start.4 = (s32[1,1,48]{2,1,0:T(1,128)S(1)}, s32[1,1,48]{2,1,0:T(1,128)}, u32[]{:S(2)}) copy-start(s32[1,1,48]{2,1,0:T(1,128)} %cols.3) | copy-start | bytes 580
  0.7 1.6 %collective-permute-start = (f32[32,128]{1,0:T(8,128)}, f32[32,128]{1,0:T(8,128)S(1)}, u32[]{:S(2)}, u32[]{:S(2)}) collective-permute-start(f32[32,128]{1,0:T(8,128)} %bitcast.2), channel_id=1, source_target_pairs={{0,1},{1,0},{2,3},{3,2},{4,5},{5,4},{6,7},{7,6},{8,9},{9,8},{10,11... | collective-permute-start | bytes 49160 | tf_op jit(solution)/shard_map/ppermute | solution.py:17
  3.1 5.7 %collective-permute-start.3 = (f32[40,128]{1,0:T(8,128)S(1)}, f32[40,128]{1,0:T(8,128)S(1)}, u32[]{:S(2)}, u32[]{:S(2)}) collective-permute-start(f32[40,128]{1,0:T(8,128)S(1)} %get-tuple-element.9), channel_id=1, source_target_pairs={{0,6},{2,4},{4,2},{6,0},{8,14},{10,12},{12,10},{14,8},{1,7},{3,5},... | collective-permute-start | bytes 61448 | tf_op jit(solution)/shard_map/ppermute | solution.py:17
  7.0 3.8 %collective-permute-start.2 = (f32[40,128]{1,0:T(8,128)S(1)}, f32[40,128]{1,0:T(8,128)S(1)}, u32[]{:S(2)}, u32[]{:S(2)}) collective-permute-start(f32[40,128]{1,0:T(8,128)S(1)} %get-tuple-element.9), channel_id=1, source_target_pairs={{0,4},{2,6},{4,0},{6,2},{8,12},{10,14},{12,8},{14,10},{1,5},{3,7},... | collective-permute-start | bytes 61448 | tf_op jit(solution)/shard_map/ppermute | solution.py:17
  7.4 3.8 %collective-permute-start.1 = (f32[40,128]{1,0:T(8,128)S(1)}, f32[40,128]{1,0:T(8,128)S(1)}, u32[]{:S(2)}, u32[]{:S(2)}) collective-permute-start(f32[40,128]{1,0:T(8,128)S(1)} %get-tuple-element.9), channel_id=1, source_target_pairs={{0,2},{2,0},{4,6},{6,4},{8,10},{10,8},{12,14},{14,12},{1,3},{3,1},... | collective-permute-start | bytes 61448 | tf_op jit(solution)/shard_map/ppermute | solution.py:17
  11.2 4.7 %collective-permute-start.4 = (f32[40,128]{1,0:T(8,128)S(1)}, f32[40,128]{1,0:T(8,128)S(1)}, u32[]{:S(2)}, u32[]{:S(2)}) collective-permute-start(f32[40,128]{1,0:T(8,128)S(1)} %add_add_fusion), channel_id=1, source_target_pairs={{0,8},{2,10},{4,12},{6,14},{8,0},{10,2},{12,4},{14,6},{1,9},{3,11}... | collective-permute-start | bytes 61448 | tf_op jit(solution)/shard_map/ppermute | solution.py:17
  16.7 1.3 %collective-permute-start.5 = (bf16[64,128]{1,0:T(8,128)(2,1)S(1)}, bf16[64,128]{1,0:T(8,128)(2,1)S(1)}, u32[]{:S(2)}, u32[]{:S(2)}) collective-permute-start(bf16[64,128]{1,0:T(8,128)(2,1)S(1)} %get-tuple-element.12), channel_id=1, source_target_pairs={{0,1},{1,0},{2,3},{3,2},{4,5},{5,4},{6,7},{7,6},{8,9},{9,8},{10,11... | collective-permute-start | bytes 49160 | tf_op jit(solution)/shard_map/ppermute | solution.py:17

commit v20 on v14

--- a/solution.py
+++ b/solution.py
@@ -58,20 +58,15 @@
         picked[pl.ds(c, slots, stride=SUB), :] = rows[:, c * width : (c + 1) * width]
 
 
-def apply_tiles(picked, tiles, contract, add, count, prods, kinds):
-    slots, rays, width = tiles.shape[2:]
+def apply_tiles(picked, tiles, transposed, add, count, prods, kinds):
+    slots, _, width = tiles.shape[2:]
     for n in range(0, slots, 2):
-        pair = tiles[0, 0, n : n + 2]
-        if contract:
-            pair = pair.reshape(2 * rays, width)
-        else:
-            pair = jnp.concatenate([pair[0], pair[1]], axis=1)
-        both = lax.dot_general(
-            picked[n * SUB : (n + 2) * SUB, :].astype(jnp.bfloat16),
-            pair,
-            (((1,), (contract,)), ((), ())),
-            preferred_element_type=jnp.float32,
-        )
+        pair = [tiles[0, 0, k] for k in (n, n + 1)]
+        if transposed:
+            pair = [tile.T for tile in pair]
+        pair = jnp.concatenate(pair, axis=1)
+        left = picked[n * SUB : (n + 2) * SUB, :].astype(jnp.bfloat16)
+        both = jnp.dot(left, pair, preferred_element_type=jnp.float32)
         prods[pl.ds(n, SUB, stride=slots), :] = both[:SUB, :width]
         prods[pl.ds(n + 1, SUB, stride=slots), :] = both[SUB:, width:]
     left = jnp.concatenate([prods[c * slots : (c + 1) * slots, :] for c in range(kinds)], axis=1)
@@ -93,7 +88,7 @@
     strides = [pl.ds(c, half, stride=inst) for c in range(inst)]
     table = [jnp.concatenate([volume[row, :], other[row, :]], axis=0) for row in strides]
     slot_rows(one_hot(places(cols[0], half), 2 * half), table, picked)
-    sums = apply_tiles(picked, tiles, 1, one_hot(rows[0], blocks), count, prods, inst + 1)
+    sums = apply_tiles(picked, tiles, True, one_hot(rows[0], blocks), count, prods, inst + 1)
     mine = lax.broadcasted_iota(jnp.int32, sums[0].shape, 0) == lax.axis_index("vox")
     for c in range(inst):
         row = jnp.broadcast_to(measured[0, 0, c : c + 1, :], sums[c].shape)
@@ -112,7 +107,7 @@
     for c in range(inst):
         residual[c : c + 1, :] = jnp.sum(jnp.where(mine, table[c], 0.0), axis=0, keepdims=True)
     slot_rows(one_hot(rows[0], blocks), table, picked)
-    sums = apply_tiles(picked, tiles, 0, one_hot(places(cols[0], half), 2 * half), count, prods, inst + 1)
+    sums = apply_tiles(picked, tiles, False, one_hot(places(cols[0], half), 2 * half), count, prods, inst + 1)
     filler = [jnp.zeros((half, weight.shape[1]), jnp.float32)] * (SUB - inst - 1)
     own[...] = jnp.concatenate([x[:half] for x in sums], axis=0)
     send[...] = jnp.concatenate([x[half:] for x in sums] + filler, axis=0).astype(jnp.bfloat16)

time: 18.6 us -> 18.5 us (level)
  no operation moved by 1% of the time
where the time goes in v20:
time: 18.5 us; the launch traced here: 18.4 us
  starting transfers between devices  7.77 us (42%)
  waiting for transfers between devices  7.22 us (39%)
  Pallas kernels  2.02 us (11%)
  between operations  1.36 us (7%)
    ppermute x6, starting transfers between devices, exchange(): return lax.ppermute(value, axis, [(i, i ^ mask) for i in range(size)])  7.77 us
    ppermute x6, waiting for transfers between devices, exchange(): return lax.ppermute(value, axis, [(i, i ^ mask) for i in range(size)])  7.22 us
    pallas_call x4, Pallas kernels, call(): pl.pallas_call(kernel, out_shape=[jax.ShapeDtypeStruct(shape, dtype) for...  2.02 us
  transfers between devices with their start and end apart: 6, of which 6 were waited for; matrix products, arithmetic and copies ran while one was open for 0% of the time, Pallas kernels for 0%

profile of v20, /device:TPU:0, one launch (start us, length us, event | category | flops | bytes accessed | tf_op | source)
XLA Modules:
  0.0 18.4 jit_solution(13601916090228560528)
XLA Ops:
  0.6 0.0 copy-start
  0.6 0.0 copy-start.1
  0.7 0.0 copy-start.2
  0.7 0.0 copy-start.3
  0.7 0.0 copy-start.4
  0.7 0.5 %collective-permute-start = (f32[32,128]{1,0:T(8,128)}, f32[32,128]{1,0:T(8,128)S(1)}, u32[]{:S(2)}, u32[]{:S(2)}) collective-permute-start(f32[32,128]{1,0:T(8,128)} %bitcast.2), channel_id=1, source_target_pairs={{0,1},{1,0},{2,3},{3,2},{4,5},{5,4},{6,7},{7,6},{8,9},{9,8},{10,11... | collective-permute-start | bytes 49160 | tf_op jit(solution)/shard_map/ppermute | solution.py:17
  1.9 0.4 %collective-permute-done.other = f32[32,128]{1,0:T(8,128)S(1)} collective-permute-done((f32[32,128]{1,0:T(8,128)}, f32[32,128]{1,0:T(8,128)S(1)}, u32[]{:S(2)}, u32[]{:S(2)}) %collective-permute-start) | collective-permute-done | bytes 16416 | tf_op jit(solution)/shard_map/ppermute | solution.py:17
  2.2 0.0 copy-done
  2.3 0.0 copy-done.1
  2.3 0.0 copy-done.2
  2.3 0.0 copy-done.3
  2.3 0.0 copy-done.4
  2.3 0.8 %project.1 = (f32[40,128]{1,0:T(8,128)S(1)}, f32[384,128]{1,0:T(8,128)S(1)}) custom-call(s32[1,1]{1,0:T(1,128)S(6)} %copy.12.count, bf16[1,1,48,128,128]{4,3,2,1,0:T(8,128)(2,1)S(1)} %copy-done, s32[1,1,48]{2,1,0:T(1,128)S(1)} %copy-done.3, s32[1,1,48]{2,1,0:T(1,128)S(1)} %copy-done.4, f32[32,128]{1,0:T(8,128)S(1)} %bitcast.3, ...), custom_call_target="tpu_custom_call", output_to_operand_aliasing={{1}: (7, {})} | custom-call | tf_op jit(solution)/shard_map/project/pallas_call | solution.py:137
  3.0 3.9 %collective-permute-start.3 = (f32[40,128]{1,0:T(8,128)S(1)}, f32[40,128]{1,0:T(8,128)S(1)}, u32[]{:S(2)}, u32[]{:S(2)}) collective-permute-start(f32[40,128]{1,0:T(8,128)S(1)} %get-tuple-element.9), channel_id=1, source_target_pairs={{0,6},{2,4},{4,2},{6,0},{8,14},{10,12},{12,10},{14,8},{1,7},{3,5},... | collective-permute-start | bytes 61448 | tf_op jit(solution)/shard_map/ppermute | solution.py:17
  6.9 0.4 %collective-permute-start.2 = (f32[40,128]{1,0:T(8,128)S(1)}, f32[40,128]{1,0:T(8,128)S(1)}, u32[]{:S(2)}, u32[]{:S(2)}) collective-permute-start(f32[40,128]{1,0:T(8,128)S(1)} %get-tuple-element.9), channel_id=1, source_target_pairs={{0,4},{2,6},{4,0},{6,2},{8,12},{10,14},{12,8},{14,10},{1,5},{3,7},... | collective-permute-start | bytes 61448 | tf_op jit(solution)/shard_map/ppermute | solution.py:17
  7.4 0.2 %collective-permute-start.1 = (f32[40,128]{1,0:T(8,128)S(1)}, f32[40,128]{1,0:T(8,128)S(1)}, u32[]{:S(2)}, u32[]{:S(2)}) collective-permute-start(f32[40,128]{1,0:T(8,128)S(1)} %get-tuple-element.9), channel_id=1, source_target_pairs={{0,2},{2,0},{4,6},{6,4},{8,10},{10,8},{12,14},{14,12},{1,3},{3,1},... | collective-permute-start | bytes 61448 | tf_op jit(solution)/shard_map/ppermute | solution.py:17
  7.5 1.1 %collective-permute-done.3 = f32[40,128]{1,0:T(8,128)S(1)} collective-permute-done((f32[40,128]{1,0:T(8,128)S(1)}, f32[40,128]{1,0:T(8,128)S(1)}, u32[]{:S(2)}, u32[]{:S(2)}) %collective-permute-start.3) | collective-permute-done | bytes 20512 | tf_op jit(solution)/shard_map/ppermute | solution.py:17
  8.7 2.0 %collective-permute-done.2 = f32[40,128]{1,0:T(8,128)S(1)} collective-permute-done((f32[40,128]{1,0:T(8,128)S(1)}, f32[40,128]{1,0:T(8,128)S(1)}, u32[]{:S(2)}, u32[]{:S(2)}) %collective-permute-start.2) | collective-permute-done | bytes 20512 | tf_op jit(solution)/shard_map/ppermute | solution.py:17
  10.7 0.4 %collective-permute-done.1 = f32[40,128]{1,0:T(8,128)S(1)} collective-permute-done((f32[40,128]{1,0:T(8,128)S(1)}, f32[40,128]{1,0:T(8,128)S(1)}, u32[]{:S(2)}, u32[]{:S(2)}) %collective-permute-start.1) | collective-permute-done | bytes 20512 | tf_op jit(solution)/shard_map/ppermute | solution.py:17
  11.2 2.6 %collective-permute-start.4 = (f32[40,128]{1,0:T(8,128)S(1)}, f32[40,128]{1,0:T(8,128)S(1)}, u32[]{:S(2)}, u32[]{:S(2)}) collective-permute-start(f32[40,128]{1,0:T(8,128)S(1)} %add_add_fusion), channel_id=1, source_target_pairs={{0,8},{2,10},{4,12},{6,14},{8,0},{10,2},{12,4},{14,6},{1,9},{3,11}... | collective-permute-start | bytes 61448 | tf_op jit(solution)/shard_map/ppermute | solution.py:17
  13.8 2.1 %collective-permute-done.4 = f32[40,128]{1,0:T(8,128)S(1)} collective-permute-done((f32[40,128]{1,0:T(8,128)S(1)}, f32[40,128]{1,0:T(8,128)S(1)}, u32[]{:S(2)}, u32[]{:S(2)}) %collective-permute-start.4) | collective-permute-done | bytes 20512 | tf_op jit(solution)/shard_map/ppermute | solution.py:17
  15.9 0.6 %backproject.1 = (f32[40,128]{1,0:T(8,128)S(1)}, bf16[64,128]{1,0:T(8,128)(2,1)S(1)}, f32[4,128]{1,0:T(4,128)S(1)}, f32[384,128]{1,0:T(8,128)S(1)}) custom-call(s32[1,1]{1,0:T(1,128)S(6)} %copy.12.count, bf16[1,1,48,128,128]{4,3,2,1,0:T(8,128)(2,1)S(1)} %copy-done, s32[1,1,48]{2,1,0:T(1,128)S(1)} %copy-done.3, ...), custom_call_target="tpu_custom_call", output_to_operand_aliasing={{3}: (5, {})} | custom-call | tf_op jit(solution)/shard_map/backproject/pallas_call | solution.py:137
  16.5 0.1 collective-permute-start.5
  16.6 1.2 %collective-permute-done.5.there = bf16[64,128]{1,0:T(8,128)(2,1)S(1)} collective-permute-done((bf16[64,128]{1,0:T(8,128)(2,1)S(1)}, bf16[64,128]{1,0:T(8,128)(2,1)S(1)}, u32[]{:S(2)}, u32[]{:S(2)}) %collective-permute-start.5) | collective-permute-done | bytes 16416 | tf_op jit(solution)/shard_map/ppermute | solution.py:17
  17.8 0.6 %update.1 = (f32[32,128]{1,0:T(8,128)}, bf16[1,1,4,128]{3,2,1,0:T(4,128)(2,1)}) custom-call(f32[32,128]{1,0:T(8,128)S(1)} %bitcast.4, f32[40,128]{1,0:T(8,128)S(1)} %get-tuple-element.11.own, bf16[64,128]{1,0:T(8,128)(2,1)S(1)} %collective-permute-done.5.there, f32[4,128]{1,0:T(4,128)S(1)} %get-tuple-element.13.residual), custom_call_target="tpu_custom_call" | custom-call | tf_op jit(solution)/shard_map/update/pallas_call | solution.py:137
  (3 shorter events, 0.0 us)
Async XLA Ops:
  0.6 1.6 %copy-start = (bf16[1,1,48,128,128]{4,3,2,1,0:T(8,128)(2,1)S(1)}, bf16[1,1,48,128,128]{4,3,2,1,0:T(8,128)(2,1)}, u32[]{:S(2)}) copy-start(bf16[1,1,48,128,128]{4,3,2,1,0:T(8,128)(2,1)} %tiles.3) | copy-start | bytes 4718596
  0.6 1.6 %copy-start.1 = (f32[8,4,128]{2,1,0:T(4,128)S(1)}, f32[8,4,128]{2,1,0:T(4,128)}, u32[]{:S(2)}) copy-start(f32[8,4,128]{2,1,0:T(4,128)} %param.6) | copy-start | bytes 49156
  0.7 1.6 %copy-start.2 = (f32[1,1,4,128]{3,2,1,0:T(4,128)S(1)}, f32[1,1,4,128]{3,2,1,0:T(4,128)}, u32[]{:S(2)}) copy-start(f32[1,1,4,128]{3,2,1,0:T(4,128)} %measured.1) | copy-start | bytes 6148
  0.7 1.6 %copy-start.3 = (s32[1,1,48]{2,1,0:T(1,128)S(1)}, s32[1,1,48]{2,1,0:T(1,128)}, u32[]{:S(2)}) copy-start(s32[1,1,48]{2,1,0:T(1,128)} %rows.5) | copy-start | bytes 580
  0.7 1.6 %copy-start.4 = (s32[1,1,48]{2,1,0:T(1,128)S(1)}, s32[1,1,48]{2,1,0:T(1,128)}, u32[]{:S(2)}) copy-start(s32[1,1,48]{2,1,0:T(1,128)} %cols.3) | copy-start | bytes 580
  0.7 1.6 %collective-permute-start = (f32[32,128]{1,0:T(8,128)}, f32[32,128]{1,0:T(8,128)S(1)}, u32[]{:S(2)}, u32[]{:S(2)}) collective-permute-start(f32[32,128]{1,0:T(8,128)} %bitcast.2), channel_id=1, source_target_pairs={{0,1},{1,0},{2,3},{3,2},{4,5},{5,4},{6,7},{7,6},{8,9},{9,8},{10,11... | collective-permute-start | bytes 49160 | tf_op jit(solution)/shard_map/ppermute | solution.py:17
  3.0 5.6 %collective-permute-start.3 = (f32[40,128]{1,0:T(8,128)S(1)}, f32[40,128]{1,0:T(8,128)S(1)}, u32[]{:S(2)}, u32[]{:S(2)}) collective-permute-start(f32[40,128]{1,0:T(8,128)S(1)} %get-tuple-element.9), channel_id=1, source_target_pairs={{0,6},{2,4},{4,2},{6,0},{8,14},{10,12},{12,10},{14,8},{1,7},{3,5},... | collective-permute-start | bytes 61448 | tf_op jit(solution)/shard_map/ppermute | solution.py:17
  6.9 3.8 %collective-permute-start.2 = (f32[40,128]{1,0:T(8,128)S(1)}, f32[40,128]{1,0:T(8,128)S(1)}, u32[]{:S(2)}, u32[]{:S(2)}) collective-permute-start(f32[40,128]{1,0:T(8,128)S(1)} %get-tuple-element.9), channel_id=1, source_target_pairs={{0,4},{2,6},{4,0},{6,2},{8,12},{10,14},{12,8},{14,10},{1,5},{3,7},... | collective-permute-start | bytes 61448 | tf_op jit(solution)/shard_map/ppermute | solution.py:17
  7.4 3.8 %collective-permute-start.1 = (f32[40,128]{1,0:T(8,128)S(1)}, f32[40,128]{1,0:T(8,128)S(1)}, u32[]{:S(2)}, u32[]{:S(2)}) collective-permute-start(f32[40,128]{1,0:T(8,128)S(1)} %get-tuple-element.9), channel_id=1, source_target_pairs={{0,2},{2,0},{4,6},{6,4},{8,10},{10,8},{12,14},{14,12},{1,3},{3,1},... | collective-permute-start | bytes 61448 | tf_op jit(solution)/shard_map/ppermute | solution.py:17
  11.2 4.7 %collective-permute-start.4 = (f32[40,128]{1,0:T(8,128)S(1)}, f32[40,128]{1,0:T(8,128)S(1)}, u32[]{:S(2)}, u32[]{:S(2)}) collective-permute-start(f32[40,128]{1,0:T(8,128)S(1)} %add_add_fusion), channel_id=1, source_target_pairs={{0,8},{2,10},{4,12},{6,14},{8,0},{10,2},{12,4},{14,6},{1,9},{3,11}... | collective-permute-start | bytes 61448 | tf_op jit(solution)/shard_map/ppermute | solution.py:17
  16.5 1.3 %collective-permute-start.5 = (bf16[64,128]{1,0:T(8,128)(2,1)S(1)}, bf16[64,128]{1,0:T(8,128)(2,1)S(1)}, u32[]{:S(2)}, u32[]{:S(2)}) collective-permute-start(bf16[64,128]{1,0:T(8,128)(2,1)S(1)} %get-tuple-element.12), channel_id=1, source_target_pairs={{0,1},{1,0},{2,3},{3,2},{4,5},{5,4},{6,7},{7,6},{8,9},{9,8},{10,11... | collective-permute-start | bytes 49160 | tf_op jit(solution)/shard_map/ppermute | solution.py:17

commit v21 on v20

--- a/solution.py
+++ b/solution.py
@@ -37,28 +37,30 @@
     picked[...] = (kind == inst).astype(jnp.float32)
 
 
-def one_hot(key, blocks):
-    return (lax.broadcasted_iota(jnp.int32, (blocks, key.shape[1]), 0) == key).astype(jnp.float32)
-
-
-def places(cols, half):
-    place = cols + lax.axis_index("ray") * half
-    return jnp.where(place < 2 * half, place, place - 2 * half)
-
-
-def slot_rows(which, table, picked):
-    slots, width = which.shape[1], table[0].shape[1]
-    rows = lax.dot_general(
-        which.astype(jnp.bfloat16),
+def prepare_kernel(count, rows, cols, pick, pick_back, add, add_back):
+    blocks, half = add.shape[0], add_back.shape[0] // 2
+    used = lax.broadcasted_iota(jnp.int32, rows.shape[1:], 1) < count[0, 0]
+    place = cols[0] + lax.axis_index("ray") * half
+    place = jnp.where(place < 2 * half, place, place - 2 * half)
+    for key, one_way, other_way in ((rows[0], add, pick_back), (place, add_back, pick)):
+        hit = (lax.broadcasted_iota(jnp.int32, one_way.shape, 0) == key) & used
+        hit = hit.astype(jnp.float32)
+        one_way[...] = hit
+        other_way[...] = hit.T
+
+
+def slot_rows(pick, table, picked):
+    slots, width = pick.shape[0], table[0].shape[1]
+    rows = jnp.dot(
+        pick[...].astype(jnp.bfloat16),
         jnp.concatenate(table, axis=1).astype(jnp.bfloat16),
-        (((0,), (0,)), ((), ())),
         preferred_element_type=jnp.float32,
     )
     for c in range(len(table)):
         picked[pl.ds(c, slots, stride=SUB), :] = rows[:, c * width : (c + 1) * width]
 
 
-def apply_tiles(picked, tiles, transposed, add, count, prods, kinds):
+def apply_tiles(picked, tiles, transposed, add, prods, kinds):
     slots, _, width = tiles.shape[2:]
     for n in range(0, slots, 2):
         pair = [tiles[0, 0, k] for k in (n, n + 1)]
@@ -70,8 +72,7 @@
         prods[pl.ds(n, SUB, stride=slots), :] = both[:SUB, :width]
         prods[pl.ds(n + 1, SUB, stride=slots), :] = both[SUB:, width:]
     left = jnp.concatenate([prods[c * slots : (c + 1) * slots, :] for c in range(kinds)], axis=1)
-    used = lax.broadcasted_iota(jnp.int32, add.shape, 1) < count[0, 0]
-    onehot = jnp.where(used, add, 0.0).astype(jnp.bfloat16)
+    onehot = add[...].astype(jnp.bfloat16)
     sums = None
     for _ in range(3):
         piece = left.astype(jnp.bfloat16)
@@ -81,14 +82,14 @@
     return [sums[:, c * width : (c + 1) * width] for c in range(kinds)]
 
 
-def project_kernel(count, tiles, rows, cols, volume, other, measured, _, part, picked, prods):
+def project_kernel(tiles, pick, add, volume, other, measured, _, part, picked, prods):
     inst = measured.shape[2]
     blocks = part.shape[0] // (inst + 1)
     half = volume.shape[0] // inst
     strides = [pl.ds(c, half, stride=inst) for c in range(inst)]
     table = [jnp.concatenate([volume[row, :], other[row, :]], axis=0) for row in strides]
-    slot_rows(one_hot(places(cols[0], half), 2 * half), table, picked)
-    sums = apply_tiles(picked, tiles, True, one_hot(rows[0], blocks), count, prods, inst + 1)
+    slot_rows(pick, table, picked)
+    sums = apply_tiles(picked, tiles, True, add, prods, inst + 1)
     mine = lax.broadcasted_iota(jnp.int32, sums[0].shape, 0) == lax.axis_index("vox")
     for c in range(inst):
         row = jnp.broadcast_to(measured[0, 0, c : c + 1, :], sums[c].shape)
@@ -96,7 +97,7 @@
     part[inst * blocks : (inst + 1) * blocks, :] = sums[inst]
 
 
-def backproject_kernel(count, tiles, rows, cols, total, _, own, send, residual, picked, prods):
+def backproject_kernel(tiles, pick, add, total, _, own, send, residual, picked, prods):
     inst = residual.shape[0]
     blocks = total.shape[0] // (inst + 1)
     half = own.shape[0] // (inst + 1)
@@ -106,8 +107,8 @@
     mine = lax.broadcasted_iota(jnp.int32, weight.shape, 0) == lax.axis_index("vox")
     for c in range(inst):
         residual[c : c + 1, :] = jnp.sum(jnp.where(mine, table[c], 0.0), axis=0, keepdims=True)
-    slot_rows(one_hot(rows[0], blocks), table, picked)
-    sums = apply_tiles(picked, tiles, False, one_hot(places(cols[0], half), 2 * half), count, prods, inst + 1)
+    slot_rows(pick, table, picked)
+    sums = apply_tiles(picked, tiles, False, add, prods, inst + 1)
     filler = [jnp.zeros((half, weight.shape[1]), jnp.float32)] * (SUB - inst - 1)
     own[...] = jnp.concatenate([x[:half] for x in sums], axis=0)
     send[...] = jnp.concatenate([x[half:] for x in sums] + filler, axis=0).astype(jnp.bfloat16)
@@ -158,14 +159,21 @@
         [],
         cost=pl.CostEstimate(flops=ROWS_FLOPS, bytes_accessed=0, transcendentals=0),
     )
+    pick, pick_back, add, add_back = call(
+        prepare_kernel,
+        "prepare",
+        [((slots, 2 * half), f32), ((slots, blocks), f32), ((blocks, slots), f32), ((2 * half, slots), f32)],
+        [],
+        [tile_count, tile_row, tile_col],
+        scalars=1,
+    )
     part, picked = call(
         project_kernel,
         "project",
         [(((inst + 1) * blocks, width), f32), slot_shape],
         [prods],
-        [tile_count, tiles, tile_row, tile_col, volume, other, measured, picked],
-        scalars=1,
-        aliases={7: 1},
+        [tiles, pick, add, volume, other, measured, picked],
+        aliases={6: 1},
     )
     total = all_sum(part, "vox")
     own, send, residual, _ = call(
@@ -173,9 +181,8 @@
         "backproject",
         [(((inst + 1) * half, width), f32), ((SUB * half, width), bf16), ((inst, width), f32), slot_shape],
         [prods],
-        [tile_count, tiles, tile_row, tile_col, total, picked],
-        scalars=1,
-        aliases={5: 3},
+        [tiles, pick_back, add_back, total, picked],
+        aliases={4: 3},
     )
     there = exchange(send, "ray", 1)
     new_volume, own_residual = call(

time: 18.5 us -> 18.5 us (level)
    pallas_call x4 -> x5, Pallas kernels: 2.02 us -> 2.04 us  [call(): pl.pallas_call(kernel, out_shape=[jax.ShapeDtypeStruct(shape, dtype) for...]
  transfers between devices with their start and end apart: 6 -> 6, of which waited for: 6 -> 6; matrix products, arithmetic and copies ran while one was open for 0% -> 0% of each run, Pallas kernels for 0% -> 1%
where the time goes in v21:
time: 18.5 us; the launch traced here: 18.3 us
  starting transfers between devices  7.77 us (42%)
  waiting for transfers between devices  7.11 us (38%)
  Pallas kernels  2.04 us (11%)
  between operations  1.36 us (7%)
    ppermute x6, starting transfers between devices, exchange(): return lax.ppermute(value, axis, [(i, i ^ mask) for i in range(size)])  7.77 us
    ppermute x6, waiting for transfers between devices, exchange(): return lax.ppermute(value, axis, [(i, i ^ mask) for i in range(size)])  7.11 us
    pallas_call x5, Pallas kernels, call(): pl.pallas_call(kernel, out_shape=[jax.ShapeDtypeStruct(shape, dtype) for...  2.04 us
  transfers between devices with their start and end apart: 6, of which 6 were waited for; matrix products, arithmetic and copies ran while one was open for 0% of the time, Pallas kernels for 1%

profile of v21, /device:TPU:0, one launch (start us, length us, event | category | flops | bytes accessed | tf_op | source)
XLA Modules:
  0.0 18.3 jit_solution(12166862640758458248)
XLA Ops:
  0.6 0.0 copy-start.3
  0.6 0.0 copy-start.4
  0.7 0.0 copy-start
  0.7 0.0 copy-start.1
  0.7 0.0 copy-start.2
  0.7 0.5 %collective-permute-start = (f32[32,128]{1,0:T(8,128)}, f32[32,128]{1,0:T(8,128)S(1)}, u32[]{:S(2)}, u32[]{:S(2)}) collective-permute-start(f32[32,128]{1,0:T(8,128)} %bitcast.2), channel_id=1, source_target_pairs={{0,1},{1,0},{2,3},{3,2},{4,5},{5,4},{6,7},{7,6},{8,9},{9,8},{10,11... | collective-permute-start | bytes 49160 | tf_op jit(solution)/shard_map/ppermute | solution.py:17
  1.9 0.0 copy-done.3
  1.9 0.0 copy-done.4
  1.9 0.1 prepare.1
  2.0 0.3 %collective-permute-done.other = f32[32,128]{1,0:T(8,128)S(1)} collective-permute-done((f32[32,128]{1,0:T(8,128)}, f32[32,128]{1,0:T(8,128)S(1)}, u32[]{:S(2)}, u32[]{:S(2)}) %collective-permute-start) | collective-permute-done | bytes 16416 | tf_op jit(solution)/shard_map/ppermute | solution.py:17
  2.2 0.0 copy-done
  2.3 0.0 copy-done.1
  2.3 0.0 copy-done.2
  2.3 0.7 %project.1 = (f32[40,128]{1,0:T(8,128)S(1)}, f32[384,128]{1,0:T(8,128)S(1)}) custom-call(bf16[1,1,48,128,128]{4,3,2,1,0:T(8,128)(2,1)S(1)} %copy-done, f32[48,16]{1,0:T(8,128)S(1)} %get-tuple-element.15.pick, f32[8,48]{1,0:T(8,128)S(1)} %get-tuple-element.16.add, f32[32,128]{1,0:T(8,128)S(1)} %bitcast.3, ...), custom_call_target="tpu_custom_call", output_to_operand_aliasing={{1}: (6, {})} | custom-call | tf_op jit(solution)/shard_map/project/pallas_call | solution.py:138
  3.0 3.9 %collective-permute-start.3 = (f32[40,128]{1,0:T(8,128)S(1)}, f32[40,128]{1,0:T(8,128)S(1)}, u32[]{:S(2)}, u32[]{:S(2)}) collective-permute-start(f32[40,128]{1,0:T(8,128)S(1)} %get-tuple-element.17), channel_id=1, source_target_pairs={{0,6},{2,4},{4,2},{6,0},{8,14},{10,12},{12,10},{14,8},{1,7},{3,5},... | collective-permute-start | bytes 61448 | tf_op jit(solution)/shard_map/ppermute | solution.py:17
  6.9 0.4 %collective-permute-start.2 = (f32[40,128]{1,0:T(8,128)S(1)}, f32[40,128]{1,0:T(8,128)S(1)}, u32[]{:S(2)}, u32[]{:S(2)}) collective-permute-start(f32[40,128]{1,0:T(8,128)S(1)} %get-tuple-element.17), channel_id=1, source_target_pairs={{0,4},{2,6},{4,0},{6,2},{8,12},{10,14},{12,8},{14,10},{1,5},{3,7},... | collective-permute-start | bytes 61448 | tf_op jit(solution)/shard_map/ppermute | solution.py:17
  7.3 0.2 %collective-permute-start.1 = (f32[40,128]{1,0:T(8,128)S(1)}, f32[40,128]{1,0:T(8,128)S(1)}, u32[]{:S(2)}, u32[]{:S(2)}) collective-permute-start(f32[40,128]{1,0:T(8,128)S(1)} %get-tuple-element.17), channel_id=1, source_target_pairs={{0,2},{2,0},{4,6},{6,4},{8,10},{10,8},{12,14},{14,12},{1,3},{3,1},... | collective-permute-start | bytes 61448 | tf_op jit(solution)/shard_map/ppermute | solution.py:17
  7.5 1.1 %collective-permute-done.3 = f32[40,128]{1,0:T(8,128)S(1)} collective-permute-done((f32[40,128]{1,0:T(8,128)S(1)}, f32[40,128]{1,0:T(8,128)S(1)}, u32[]{:S(2)}, u32[]{:S(2)}) %collective-permute-start.3) | collective-permute-done | bytes 20512 | tf_op jit(solution)/shard_map/ppermute | solution.py:17
  8.6 2.0 %collective-permute-done.2 = f32[40,128]{1,0:T(8,128)S(1)} collective-permute-done((f32[40,128]{1,0:T(8,128)S(1)}, f32[40,128]{1,0:T(8,128)S(1)}, u32[]{:S(2)}, u32[]{:S(2)}) %collective-permute-start.2) | collective-permute-done | bytes 20512 | tf_op jit(solution)/shard_map/ppermute | solution.py:17
  10.6 0.4 %collective-permute-done.1 = f32[40,128]{1,0:T(8,128)S(1)} collective-permute-done((f32[40,128]{1,0:T(8,128)S(1)}, f32[40,128]{1,0:T(8,128)S(1)}, u32[]{:S(2)}, u32[]{:S(2)}) %collective-permute-start.1) | collective-permute-done | bytes 20512 | tf_op jit(solution)/shard_map/ppermute | solution.py:17
  11.1 2.6 %collective-permute-start.4 = (f32[40,128]{1,0:T(8,128)S(1)}, f32[40,128]{1,0:T(8,128)S(1)}, u32[]{:S(2)}, u32[]{:S(2)}) collective-permute-start(f32[40,128]{1,0:T(8,128)S(1)} %add_add_fusion), channel_id=1, source_target_pairs={{0,8},{2,10},{4,12},{6,14},{8,0},{10,2},{12,4},{14,6},{1,9},{3,11}... | collective-permute-start | bytes 61448 | tf_op jit(solution)/shard_map/ppermute | solution.py:17
  13.8 2.1 %collective-permute-done.4 = f32[40,128]{1,0:T(8,128)S(1)} collective-permute-done((f32[40,128]{1,0:T(8,128)S(1)}, f32[40,128]{1,0:T(8,128)S(1)}, u32[]{:S(2)}, u32[]{:S(2)}) %collective-permute-start.4) | collective-permute-done | bytes 20512 | tf_op jit(solution)/shard_map/ppermute | solution.py:17
  15.9 0.6 %backproject.1 = (f32[40,128]{1,0:T(8,128)S(1)}, bf16[64,128]{1,0:T(8,128)(2,1)S(1)}, f32[4,128]{1,0:T(4,128)S(1)}, f32[384,128]{1,0:T(8,128)S(1)}) custom-call(bf16[1,1,48,128,128]{4,3,2,1,0:T(8,128)(2,1)S(1)} %copy-done, f32[48,8]{1,0:T(8,128)S(1)} %get-tuple-element.13.pick, f32[16,48]{1,0:T(8,128)S(1)} %get-tuple-element.14.add, ...), custom_call_target="tpu_custom_call", output_to_operand_aliasing={{3}: (4, {})} | custom-call | tf_op jit(solution)/shard_map/backproject/pallas_call | solution.py:138
  16.4 0.1 collective-permute-start.5
  16.5 1.2 %collective-permute-done.5.there = bf16[64,128]{1,0:T(8,128)(2,1)S(1)} collective-permute-done((bf16[64,128]{1,0:T(8,128)(2,1)S(1)}, bf16[64,128]{1,0:T(8,128)(2,1)S(1)}, u32[]{:S(2)}, u32[]{:S(2)}) %collective-permute-start.5) | collective-permute-done | bytes 16416 | tf_op jit(solution)/shard_map/ppermute | solution.py:17
  17.7 0.6 %update.1 = (f32[32,128]{1,0:T(8,128)}, bf16[1,1,4,128]{3,2,1,0:T(4,128)(2,1)}) custom-call(f32[32,128]{1,0:T(8,128)S(1)} %bitcast.4, f32[40,128]{1,0:T(8,128)S(1)} %get-tuple-element.19.own, bf16[64,128]{1,0:T(8,128)(2,1)S(1)} %collective-permute-done.5.there, f32[4,128]{1,0:T(4,128)S(1)} %get-tuple-element.21.residual), custom_call_target="tpu_custom_call" | custom-call | tf_op jit(solution)/shard_map/update/pallas_call | solution.py:138
  (3 shorter events, 0.0 us)
Async XLA Ops:
  0.6 1.3 %copy-start.3 = (s32[1,1,48]{2,1,0:T(1,128)S(1)}, s32[1,1,48]{2,1,0:T(1,128)}, u32[]{:S(2)}) copy-start(s32[1,1,48]{2,1,0:T(1,128)} %rows.2) | copy-start | bytes 580
  0.6 1.3 %copy-start.4 = (s32[1,1,48]{2,1,0:T(1,128)S(1)}, s32[1,1,48]{2,1,0:T(1,128)}, u32[]{:S(2)}) copy-start(s32[1,1,48]{2,1,0:T(1,128)} %cols.1) | copy-start | bytes 580
  0.7 1.6 %copy-start = (bf16[1,1,48,128,128]{4,3,2,1,0:T(8,128)(2,1)S(1)}, bf16[1,1,48,128,128]{4,3,2,1,0:T(8,128)(2,1)}, u32[]{:S(2)}) copy-start(bf16[1,1,48,128,128]{4,3,2,1,0:T(8,128)(2,1)} %tiles.3) | copy-start | bytes 4718596
  0.7 1.6 %copy-start.1 = (f32[8,4,128]{2,1,0:T(4,128)S(1)}, f32[8,4,128]{2,1,0:T(4,128)}, u32[]{:S(2)}) copy-start(f32[8,4,128]{2,1,0:T(4,128)} %param.6) | copy-start | bytes 49156
  0.7 1.6 %copy-start.2 = (f32[1,1,4,128]{3,2,1,0:T(4,128)S(1)}, f32[1,1,4,128]{3,2,1,0:T(4,128)}, u32[]{:S(2)}) copy-start(f32[1,1,4,128]{3,2,1,0:T(4,128)} %measured.1) | copy-start | bytes 6148
  0.7 1.6 %collective-permute-start = (f32[32,128]{1,0:T(8,128)}, f32[32,128]{1,0:T(8,128)S(1)}, u32[]{:S(2)}, u32[]{:S(2)}) collective-permute-start(f32[32,128]{1,0:T(8,128)} %bitcast.2), channel_id=1, source_target_pairs={{0,1},{1,0},{2,3},{3,2},{4,5},{5,4},{6,7},{7,6},{8,9},{9,8},{10,11... | collective-permute-start | bytes 49160 | tf_op jit(solution)/shard_map/ppermute | solution.py:17
  3.0 5.6 %collective-permute-start.3 = (f32[40,128]{1,0:T(8,128)S(1)}, f32[40,128]{1,0:T(8,128)S(1)}, u32[]{:S(2)}, u32[]{:S(2)}) collective-permute-start(f32[40,128]{1,0:T(8,128)S(1)} %get-tuple-element.17), channel_id=1, source_target_pairs={{0,6},{2,4},{4,2},{6,0},{8,14},{10,12},{12,10},{14,8},{1,7},{3,5},... | collective-permute-start | bytes 61448 | tf_op jit(solution)/shard_map/ppermute | solution.py:17
  6.9 3.8 %collective-permute-start.2 = (f32[40,128]{1,0:T(8,128)S(1)}, f32[40,128]{1,0:T(8,128)S(1)}, u32[]{:S(2)}, u32[]{:S(2)}) collective-permute-start(f32[40,128]{1,0:T(8,128)S(1)} %get-tuple-element.17), channel_id=1, source_target_pairs={{0,4},{2,6},{4,0},{6,2},{8,12},{10,14},{12,8},{14,10},{1,5},{3,7},... | collective-permute-start | bytes 61448 | tf_op jit(solution)/shard_map/ppermute | solution.py:17
  7.3 3.8 %collective-permute-start.1 = (f32[40,128]{1,0:T(8,128)S(1)}, f32[40,128]{1,0:T(8,128)S(1)}, u32[]{:S(2)}, u32[]{:S(2)}) collective-permute-start(f32[40,128]{1,0:T(8,128)S(1)} %get-tuple-element.17), channel_id=1, source_target_pairs={{0,2},{2,0},{4,6},{6,4},{8,10},{10,8},{12,14},{14,12},{1,3},{3,1},... | collective-permute-start | bytes 61448 | tf_op jit(solution)/shard_map/ppermute | solution.py:17
  11.1 4.7 %collective-permute-start.4 = (f32[40,128]{1,0:T(8,128)S(1)}, f32[40,128]{1,0:T(8,128)S(1)}, u32[]{:S(2)}, u32[]{:S(2)}) collective-permute-start(f32[40,128]{1,0:T(8,128)S(1)} %add_add_fusion), channel_id=1, source_target_pairs={{0,8},{2,10},{4,12},{6,14},{8,0},{10,2},{12,4},{14,6},{1,9},{3,11}... | collective-permute-start | bytes 61448 | tf_op jit(solution)/shard_map/ppermute | solution.py:17
  16.4 1.3 %collective-permute-start.5 = (bf16[64,128]{1,0:T(8,128)(2,1)S(1)}, bf16[64,128]{1,0:T(8,128)(2,1)S(1)}, u32[]{:S(2)}, u32[]{:S(2)}) collective-permute-start(bf16[64,128]{1,0:T(8,128)(2,1)S(1)} %get-tuple-element.20), channel_id=1, source_target_pairs={{0,1},{1,0},{2,3},{3,2},{4,5},{5,4},{6,7},{7,6},{8,9},{9,8},{10,11... | collective-permute-start | bytes 49160 | tf_op jit(solution)/shard_map/ppermute | solution.py:17

commit v22 on v21

--- a/solution.py
+++ b/solution.py
@@ -18,17 +18,17 @@
 
 
 def all_sum(value, axis):
-    size = lax.axis_size(axis)
-    stride = 1
-    while stride < size:
-        if 2 * stride < size:
-            across = exchange(value, axis, stride)
-            both = exchange(value, axis, 3 * stride)
-            along = exchange(value, axis, 2 * stride)
-            value = (value + across) + (along + both)
-        else:
-            value = value + exchange(value, axis, stride)
-        stride *= 4
+    bits = (lax.axis_size(axis) - 1).bit_length()
+    if bits % 2:
+        bits -= 1
+        value = value + exchange(value, axis, 1 << bits)
+    while bits:
+        bits -= 2
+        stride = 1 << bits
+        across = exchange(value, axis, stride)
+        both = exchange(value, axis, 3 * stride)
+        along = exchange(value, axis, 2 * stride)
+        value = (value + across) + (along + both)
     return value
 
 

time: 18.5 us -> 18.4 us (level)
  waiting for transfers between devices: 7.11 us -> 6.78 us
  starting transfers between devices: 7.77 us -> 8.05 us
    ppermute x6, waiting for transfers between devices: 7.11 us -> 6.78 us  [exchange(): return lax.ppermute(value, axis, [(i, i ^ mask) for i in range(size)])]
    ppermute x6, starting transfers between devices: 7.77 us -> 8.05 us  [exchange(): return lax.ppermute(value, axis, [(i, i ^ mask) for i in range(size)])]
where the time goes in v22:
time: 18.4 us; the launch traced here: 18.3 us
  starting transfers between devices  8.05 us (44%)
  waiting for transfers between devices  6.78 us (37%)
  Pallas kernels  2.04 us (11%)
  between operations  1.36 us (7%)
    ppermute x6, starting transfers between devices, exchange(): return lax.ppermute(value, axis, [(i, i ^ mask) for i in range(size)])  8.05 us
    ppermute x6, waiting for transfers between devices, exchange(): return lax.ppermute(value, axis, [(i, i ^ mask) for i in range(size)])  6.78 us
    pallas_call x5, Pallas kernels, call(): pl.pallas_call(kernel, out_shape=[jax.ShapeDtypeStruct(shape, dtype) for...  2.04 us
  transfers between devices with their start and end apart: 6, of which 6 were waited for; matrix products, arithmetic and copies ran while one was open for 0% of the time, Pallas kernels for 1%

profile of v22, /device:TPU:0, one launch (start us, length us, event | category | flops | bytes accessed | tf_op | source)
XLA Modules:
  0.0 18.3 jit_solution(4616414508837717077)
XLA Ops:
  0.6 0.0 copy-start.3
  0.6 0.0 copy-start.4
  0.7 0.0 copy-start
  0.7 0.0 copy-start.1
  0.7 0.0 copy-start.2
  0.7 0.5 %collective-permute-start = (f32[32,128]{1,0:T(8,128)}, f32[32,128]{1,0:T(8,128)S(1)}, u32[]{:S(2)}, u32[]{:S(2)}) collective-permute-start(f32[32,128]{1,0:T(8,128)} %bitcast.2), channel_id=1, source_target_pairs={{0,1},{1,0},{2,3},{3,2},{4,5},{5,4},{6,7},{7,6},{8,9},{9,8},{10,11... | collective-permute-start | bytes 49160 | tf_op jit(solution)/shard_map/ppermute | solution.py:17
  1.9 0.0 copy-done.3
  1.9 0.0 copy-done.4
  1.9 0.1 prepare.1
  2.0 0.3 %collective-permute-done.other = f32[32,128]{1,0:T(8,128)S(1)} collective-permute-done((f32[32,128]{1,0:T(8,128)}, f32[32,128]{1,0:T(8,128)S(1)}, u32[]{:S(2)}, u32[]{:S(2)}) %collective-permute-start) | collective-permute-done | bytes 16416 | tf_op jit(solution)/shard_map/ppermute | solution.py:17
  2.2 0.0 copy-done
  2.3 0.0 copy-done.1
  2.3 0.0 copy-done.2
  2.3 0.7 %project.1 = (f32[40,128]{1,0:T(8,128)S(1)}, f32[384,128]{1,0:T(8,128)S(1)}) custom-call(bf16[1,1,48,128,128]{4,3,2,1,0:T(8,128)(2,1)S(1)} %copy-done, f32[48,16]{1,0:T(8,128)S(1)} %get-tuple-element.15.pick, f32[8,48]{1,0:T(8,128)S(1)} %get-tuple-element.16.add, f32[32,128]{1,0:T(8,128)S(1)} %bitcast.3, ...), custom_call_target="tpu_custom_call", output_to_operand_aliasing={{1}: (6, {})} | custom-call | tf_op jit(solution)/shard_map/project/pallas_call | solution.py:138
  3.0 4.0 %collective-permute-start.1 = (f32[40,128]{1,0:T(8,128)S(1)}, f32[40,128]{1,0:T(8,128)S(1)}, u32[]{:S(2)}, u32[]{:S(2)}) collective-permute-start(f32[40,128]{1,0:T(8,128)S(1)} %get-tuple-element.17), channel_id=1, source_target_pairs={{0,8},{2,10},{4,12},{6,14},{8,0},{10,2},{12,4},{14,6},{1,9},{3,11}... | collective-permute-start | bytes 61448 | tf_op jit(solution)/shard_map/ppermute | solution.py:17
  6.9 1.8 %collective-permute-done.1 = f32[40,128]{1,0:T(8,128)S(1)} collective-permute-done((f32[40,128]{1,0:T(8,128)S(1)}, f32[40,128]{1,0:T(8,128)S(1)}, u32[]{:S(2)}, u32[]{:S(2)}) %collective-permute-start.1) | collective-permute-done | bytes 20512 | tf_op jit(solution)/shard_map/ppermute | solution.py:17
  8.7 2.8 %collective-permute-start.4 = (f32[40,128]{1,0:T(8,128)S(1)}, f32[40,128]{1,0:T(8,128)S(1)}, u32[]{:S(2)}, u32[]{:S(2)}) collective-permute-start(f32[40,128]{1,0:T(8,128)S(1)} %add.12), channel_id=1, source_target_pairs={{0,6},{2,4},{4,2},{6,0},{8,14},{10,12},{12,10},{14,8},{1,7},{3,5},... | collective-permute-start | bytes 61448 | tf_op jit(solution)/shard_map/ppermute | solution.py:17
  11.5 0.5 %collective-permute-start.3 = (f32[40,128]{1,0:T(8,128)S(1)}, f32[40,128]{1,0:T(8,128)S(1)}, u32[]{:S(2)}, u32[]{:S(2)}) collective-permute-start(f32[40,128]{1,0:T(8,128)S(1)} %add.12), channel_id=1, source_target_pairs={{0,4},{2,6},{4,0},{6,2},{8,12},{10,14},{12,8},{14,10},{1,5},{3,7},... | collective-permute-start | bytes 61448 | tf_op jit(solution)/shard_map/ppermute | solution.py:17
  12.0 0.2 %collective-permute-start.2 = (f32[40,128]{1,0:T(8,128)S(1)}, f32[40,128]{1,0:T(8,128)S(1)}, u32[]{:S(2)}, u32[]{:S(2)}) collective-permute-start(f32[40,128]{1,0:T(8,128)S(1)} %add.12), channel_id=1, source_target_pairs={{0,2},{2,0},{4,6},{6,4},{8,10},{10,8},{12,14},{14,12},{1,3},{3,1},... | collective-permute-start | bytes 61448 | tf_op jit(solution)/shard_map/ppermute | solution.py:17
  12.2 1.3 %collective-permute-done.4 = f32[40,128]{1,0:T(8,128)S(1)} collective-permute-done((f32[40,128]{1,0:T(8,128)S(1)}, f32[40,128]{1,0:T(8,128)S(1)}, u32[]{:S(2)}, u32[]{:S(2)}) %collective-permute-start.4) | collective-permute-done | bytes 20512 | tf_op jit(solution)/shard_map/ppermute | solution.py:17
  13.5 1.8 %collective-permute-done.3 = f32[40,128]{1,0:T(8,128)S(1)} collective-permute-done((f32[40,128]{1,0:T(8,128)S(1)}, f32[40,128]{1,0:T(8,128)S(1)}, u32[]{:S(2)}, u32[]{:S(2)}) %collective-permute-start.3) | collective-permute-done | bytes 20512 | tf_op jit(solution)/shard_map/ppermute | solution.py:17
  15.3 0.5 %collective-permute-done.2 = f32[40,128]{1,0:T(8,128)S(1)} collective-permute-done((f32[40,128]{1,0:T(8,128)S(1)}, f32[40,128]{1,0:T(8,128)S(1)}, u32[]{:S(2)}, u32[]{:S(2)}) %collective-permute-start.2) | collective-permute-done | bytes 20512 | tf_op jit(solution)/shard_map/ppermute | solution.py:17
  15.8 0.6 %backproject.1 = (f32[40,128]{1,0:T(8,128)S(1)}, bf16[64,128]{1,0:T(8,128)(2,1)S(1)}, f32[4,128]{1,0:T(4,128)S(1)}, f32[384,128]{1,0:T(8,128)S(1)}) custom-call(bf16[1,1,48,128,128]{4,3,2,1,0:T(8,128)(2,1)S(1)} %copy-done, f32[48,8]{1,0:T(8,128)S(1)} %get-tuple-element.13.pick, f32[16,48]{1,0:T(8,128)S(1)} %get-tuple-element.14.add, ...), custom_call_target="tpu_custom_call", output_to_operand_aliasing={{3}: (4, {})} | custom-call | tf_op jit(solution)/shard_map/backproject/pallas_call | solution.py:138
  16.4 0.1 collective-permute-start.5
  16.5 1.2 %collective-permute-done.5.there = bf16[64,128]{1,0:T(8,128)(2,1)S(1)} collective-permute-done((bf16[64,128]{1,0:T(8,128)(2,1)S(1)}, bf16[64,128]{1,0:T(8,128)(2,1)S(1)}, u32[]{:S(2)}, u32[]{:S(2)}) %collective-permute-start.5) | collective-permute-done | bytes 16416 | tf_op jit(solution)/shard_map/ppermute | solution.py:17
  17.6 0.6 %update.1 = (f32[32,128]{1,0:T(8,128)}, bf16[1,1,4,128]{3,2,1,0:T(4,128)(2,1)}) custom-call(f32[32,128]{1,0:T(8,128)S(1)} %bitcast.4, f32[40,128]{1,0:T(8,128)S(1)} %get-tuple-element.19.own, bf16[64,128]{1,0:T(8,128)(2,1)S(1)} %collective-permute-done.5.there, f32[4,128]{1,0:T(4,128)S(1)} %get-tuple-element.21.residual), custom_call_target="tpu_custom_call" | custom-call | tf_op jit(solution)/shard_map/update/pallas_call | solution.py:138
  (3 shorter events, 0.0 us)
Async XLA Ops:
  0.6 1.3 %copy-start.3 = (s32[1,1,48]{2,1,0:T(1,128)S(1)}, s32[1,1,48]{2,1,0:T(1,128)}, u32[]{:S(2)}) copy-start(s32[1,1,48]{2,1,0:T(1,128)} %rows.2) | copy-start | bytes 580
  0.6 1.3 %copy-start.4 = (s32[1,1,48]{2,1,0:T(1,128)S(1)}, s32[1,1,48]{2,1,0:T(1,128)}, u32[]{:S(2)}) copy-start(s32[1,1,48]{2,1,0:T(1,128)} %cols.1) | copy-start | bytes 580
  0.7 1.6 %copy-start = (bf16[1,1,48,128,128]{4,3,2,1,0:T(8,128)(2,1)S(1)}, bf16[1,1,48,128,128]{4,3,2,1,0:T(8,128)(2,1)}, u32[]{:S(2)}) copy-start(bf16[1,1,48,128,128]{4,3,2,1,0:T(8,128)(2,1)} %tiles.3) | copy-start | bytes 4718596
  0.7 1.6 %copy-start.1 = (f32[8,4,128]{2,1,0:T(4,128)S(1)}, f32[8,4,128]{2,1,0:T(4,128)}, u32[]{:S(2)}) copy-start(f32[8,4,128]{2,1,0:T(4,128)} %param.6) | copy-start | bytes 49156
  0.7 1.6 %copy-start.2 = (f32[1,1,4,128]{3,2,1,0:T(4,128)S(1)}, f32[1,1,4,128]{3,2,1,0:T(4,128)}, u32[]{:S(2)}) copy-start(f32[1,1,4,128]{3,2,1,0:T(4,128)} %measured.1) | copy-start | bytes 6148
  0.7 1.6 %collective-permute-start = (f32[32,128]{1,0:T(8,128)}, f32[32,128]{1,0:T(8,128)S(1)}, u32[]{:S(2)}, u32[]{:S(2)}) collective-permute-start(f32[32,128]{1,0:T(8,128)} %bitcast.2), channel_id=1, source_target_pairs={{0,1},{1,0},{2,3},{3,2},{4,5},{5,4},{6,7},{7,6},{8,9},{9,8},{10,11... | collective-permute-start | bytes 49160 | tf_op jit(solution)/shard_map/ppermute | solution.py:17
  3.0 5.7 %collective-permute-start.1 = (f32[40,128]{1,0:T(8,128)S(1)}, f32[40,128]{1,0:T(8,128)S(1)}, u32[]{:S(2)}, u32[]{:S(2)}) collective-permute-start(f32[40,128]{1,0:T(8,128)S(1)} %get-tuple-element.17), channel_id=1, source_target_pairs={{0,8},{2,10},{4,12},{6,14},{8,0},{10,2},{12,4},{14,6},{1,9},{3,11}... | collective-permute-start | bytes 61448 | tf_op jit(solution)/shard_map/ppermute | solution.py:17
  8.7 4.8 %collective-permute-start.4 = (f32[40,128]{1,0:T(8,128)S(1)}, f32[40,128]{1,0:T(8,128)S(1)}, u32[]{:S(2)}, u32[]{:S(2)}) collective-permute-start(f32[40,128]{1,0:T(8,128)S(1)} %add.12), channel_id=1, source_target_pairs={{0,6},{2,4},{4,2},{6,0},{8,14},{10,12},{12,10},{14,8},{1,7},{3,5},... | collective-permute-start | bytes 61448 | tf_op jit(solution)/shard_map/ppermute | solution.py:17
  11.5 3.8 %collective-permute-start.3 = (f32[40,128]{1,0:T(8,128)S(1)}, f32[40,128]{1,0:T(8,128)S(1)}, u32[]{:S(2)}, u32[]{:S(2)}) collective-permute-start(f32[40,128]{1,0:T(8,128)S(1)} %add.12), channel_id=1, source_target_pairs={{0,4},{2,6},{4,0},{6,2},{8,12},{10,14},{12,8},{14,10},{1,5},{3,7},... | collective-permute-start | bytes 61448 | tf_op jit(solution)/shard_map/ppermute | solution.py:17
  12.0 3.8 %collective-permute-start.2 = (f32[40,128]{1,0:T(8,128)S(1)}, f32[40,128]{1,0:T(8,128)S(1)}, u32[]{:S(2)}, u32[]{:S(2)}) collective-permute-start(f32[40,128]{1,0:T(8,128)S(1)} %add.12), channel_id=1, source_target_pairs={{0,2},{2,0},{4,6},{6,4},{8,10},{10,8},{12,14},{14,12},{1,3},{3,1},... | collective-permute-start | bytes 61448 | tf_op jit(solution)/shard_map/ppermute | solution.py:17
  16.4 1.3 %collective-permute-start.5 = (bf16[64,128]{1,0:T(8,128)(2,1)S(1)}, bf16[64,128]{1,0:T(8,128)(2,1)S(1)}, u32[]{:S(2)}, u32[]{:S(2)}) collective-permute-start(bf16[64,128]{1,0:T(8,128)(2,1)S(1)} %get-tuple-element.20), channel_id=1, source_target_pairs={{0,1},{1,0},{2,3},{3,2},{4,5},{5,4},{6,7},{7,6},{8,9},{9,8},{10,11... | collective-permute-start | bytes 49160 | tf_op jit(solution)/shard_map/ppermute | solution.py:17

commit v23 on v22

--- a/solution.py
+++ b/solution.py
@@ -9,6 +9,7 @@
 
 SUB = 8
 ROWS_FLOPS = 20_000_000_000
+PARTS = 3
 VMEM_BYTES = 16 << 20
 
 
@@ -43,9 +44,10 @@
     place = cols[0] + lax.axis_index("ray") * half
     place = jnp.where(place < 2 * half, place, place - 2 * half)
     for key, one_way, other_way in ((rows[0], add, pick_back), (place, add_back, pick)):
-        hit = (lax.broadcasted_iota(jnp.int32, one_way.shape, 0) == key) & used
+        shape = (one_way.shape[0], key.shape[1])
+        hit = (lax.broadcasted_iota(jnp.int32, shape, 0) == key) & used
         hit = hit.astype(jnp.float32)
-        one_way[...] = hit
+        one_way[...] = jnp.concatenate([hit] * PARTS, axis=1)
         other_way[...] = hit.T
 
 
@@ -72,13 +74,13 @@
         prods[pl.ds(n, SUB, stride=slots), :] = both[:SUB, :width]
         prods[pl.ds(n + 1, SUB, stride=slots), :] = both[SUB:, width:]
     left = jnp.concatenate([prods[c * slots : (c + 1) * slots, :] for c in range(kinds)], axis=1)
-    onehot = add[...].astype(jnp.bfloat16)
-    sums = None
-    for _ in range(3):
-        piece = left.astype(jnp.bfloat16)
-        left = left - piece.astype(jnp.float32)
-        term = jnp.dot(onehot, piece, preferred_element_type=jnp.float32)
-        sums = term if sums is None else sums + term
+    parts = []
+    for _ in range(PARTS):
+        parts.append(left.astype(jnp.bfloat16))
+        left = left - parts[-1].astype(jnp.float32)
+    sums = jnp.dot(
+        add[...].astype(jnp.bfloat16), jnp.concatenate(parts, axis=0), preferred_element_type=jnp.float32
+    )
     return [sums[:, c * width : (c + 1) * width] for c in range(kinds)]
 
 
@@ -162,7 +164,12 @@
     pick, pick_back, add, add_back = call(
         prepare_kernel,
         "prepare",
-        [((slots, 2 * half), f32), ((slots, blocks), f32), ((blocks, slots), f32), ((2 * half, slots), f32)],
+        [
+            ((slots, 2 * half), f32),
+            ((slots, blocks), f32),
+            ((blocks, PARTS * slots), f32),
+            ((2 * half, PARTS * slots), f32),
+        ],
         [],
         [tile_count, tile_row, tile_col],
         scalars=1,

time: 18.4 us -> 18.4 us (level)
  no operation moved by 1% of the time
where the time goes in v23:
time: 18.4 us; the launch traced here: 18.2 us
  starting transfers between devices  7.95 us (43%)
  waiting for transfers between devices  6.79 us (37%)
  Pallas kernels  2.09 us (11%)
  between operations  1.35 us (7%)
    ppermute x6, starting transfers between devices, exchange(): return lax.ppermute(value, axis, [(i, i ^ mask) for i in range(size)])  7.95 us
    ppermute x6, waiting for transfers between devices, exchange(): return lax.ppermute(value, axis, [(i, i ^ mask) for i in range(size)])  6.79 us
    pallas_call x5, Pallas kernels, call(): pl.pallas_call(kernel, out_shape=[jax.ShapeDtypeStruct(shape, dtype) for...  2.09 us
  transfers between devices with their start and end apart: 6, of which 6 were waited for; matrix products, arithmetic and copies ran while one was open for 0% of the time, Pallas kernels for 1%

profile of v23, /device:TPU:0, one launch (start us, length us, event | category | flops | bytes accessed | tf_op | source)
XLA Modules:
  0.0 18.2 jit_solution(1585124540708521824)
XLA Ops:
  0.6 0.0 copy-start.3
  0.6 0.0 copy-start.4
  0.7 0.0 copy-start
  0.7 0.0 copy-start.1
  0.7 0.0 copy-start.2
  0.7 0.5 %collective-permute-start = (f32[32,128]{1,0:T(8,128)}, f32[32,128]{1,0:T(8,128)S(1)}, u32[]{:S(2)}, u32[]{:S(2)}) collective-permute-start(f32[32,128]{1,0:T(8,128)} %bitcast.2), channel_id=1, source_target_pairs={{0,1},{1,0},{2,3},{3,2},{4,5},{5,4},{6,7},{7,6},{8,9},{9,8},{10,11... | collective-permute-start | bytes 49160 | tf_op jit(solution)/shard_map/ppermute | solution.py:18
  1.9 0.0 copy-done.3
  1.9 0.0 copy-done.4
  1.9 0.1 prepare.1
  2.0 0.2 %collective-permute-done.other = f32[32,128]{1,0:T(8,128)S(1)} collective-permute-done((f32[32,128]{1,0:T(8,128)}, f32[32,128]{1,0:T(8,128)S(1)}, u32[]{:S(2)}, u32[]{:S(2)}) %collective-permute-start) | collective-permute-done | bytes 16416 | tf_op jit(solution)/shard_map/ppermute | solution.py:18
  2.2 0.0 copy-done
  2.3 0.0 copy-done.1
  2.3 0.0 copy-done.2
  2.3 0.7 %project.1 = (f32[40,128]{1,0:T(8,128)S(1)}, f32[384,128]{1,0:T(8,128)S(1)}) custom-call(bf16[1,1,48,128,128]{4,3,2,1,0:T(8,128)(2,1)S(1)} %copy-done, f32[48,16]{1,0:T(8,128)S(1)} %get-tuple-element.15.pick, f32[8,144]{1,0:T(8,128)S(1)} %get-tuple-element.16.add, f32[32,128]{1,0:T(8,128)S(1)} %bitcast.3, ...), custom_call_target="tpu_custom_call", output_to_operand_aliasing={{1}: (6, {})} | custom-call | tf_op jit(solution)/shard_map/project/pallas_call | solution.py:140
  3.0 3.9 %collective-permute-start.1 = (f32[40,128]{1,0:T(8,128)S(1)}, f32[40,128]{1,0:T(8,128)S(1)}, u32[]{:S(2)}, u32[]{:S(2)}) collective-permute-start(f32[40,128]{1,0:T(8,128)S(1)} %get-tuple-element.17), channel_id=1, source_target_pairs={{0,8},{2,10},{4,12},{6,14},{8,0},{10,2},{12,4},{14,6},{1,9},{3,11}... | collective-permute-start | bytes 61448 | tf_op jit(solution)/shard_map/ppermute | solution.py:18
  6.9 1.8 %collective-permute-done.1 = f32[40,128]{1,0:T(8,128)S(1)} collective-permute-done((f32[40,128]{1,0:T(8,128)S(1)}, f32[40,128]{1,0:T(8,128)S(1)}, u32[]{:S(2)}, u32[]{:S(2)}) %collective-permute-start.1) | collective-permute-done | bytes 20512 | tf_op jit(solution)/shard_map/ppermute | solution.py:18
  8.7 2.8 %collective-permute-start.4 = (f32[40,128]{1,0:T(8,128)S(1)}, f32[40,128]{1,0:T(8,128)S(1)}, u32[]{:S(2)}, u32[]{:S(2)}) collective-permute-start(f32[40,128]{1,0:T(8,128)S(1)} %add.12), channel_id=1, source_target_pairs={{0,6},{2,4},{4,2},{6,0},{8,14},{10,12},{12,10},{14,8},{1,7},{3,5},... | collective-permute-start | bytes 61448 | tf_op jit(solution)/shard_map/ppermute | solution.py:18
  11.5 0.5 %collective-permute-start.3 = (f32[40,128]{1,0:T(8,128)S(1)}, f32[40,128]{1,0:T(8,128)S(1)}, u32[]{:S(2)}, u32[]{:S(2)}) collective-permute-start(f32[40,128]{1,0:T(8,128)S(1)} %add.12), channel_id=1, source_target_pairs={{0,4},{2,6},{4,0},{6,2},{8,12},{10,14},{12,8},{14,10},{1,5},{3,7},... | collective-permute-start | bytes 61448 | tf_op jit(solution)/shard_map/ppermute | solution.py:18
  12.0 0.2 %collective-permute-start.2 = (f32[40,128]{1,0:T(8,128)S(1)}, f32[40,128]{1,0:T(8,128)S(1)}, u32[]{:S(2)}, u32[]{:S(2)}) collective-permute-start(f32[40,128]{1,0:T(8,128)S(1)} %add.12), channel_id=1, source_target_pairs={{0,2},{2,0},{4,6},{6,4},{8,10},{10,8},{12,14},{14,12},{1,3},{3,1},... | collective-permute-start | bytes 61448 | tf_op jit(solution)/shard_map/ppermute | solution.py:18
  12.2 1.3 %collective-permute-done.4 = f32[40,128]{1,0:T(8,128)S(1)} collective-permute-done((f32[40,128]{1,0:T(8,128)S(1)}, f32[40,128]{1,0:T(8,128)S(1)}, u32[]{:S(2)}, u32[]{:S(2)}) %collective-permute-start.4) | collective-permute-done | bytes 20512 | tf_op jit(solution)/shard_map/ppermute | solution.py:18
  13.5 1.8 %collective-permute-done.3 = f32[40,128]{1,0:T(8,128)S(1)} collective-permute-done((f32[40,128]{1,0:T(8,128)S(1)}, f32[40,128]{1,0:T(8,128)S(1)}, u32[]{:S(2)}, u32[]{:S(2)}) %collective-permute-start.3) | collective-permute-done | bytes 20512 | tf_op jit(solution)/shard_map/ppermute | solution.py:18
  15.3 0.5 %collective-permute-done.2 = f32[40,128]{1,0:T(8,128)S(1)} collective-permute-done((f32[40,128]{1,0:T(8,128)S(1)}, f32[40,128]{1,0:T(8,128)S(1)}, u32[]{:S(2)}, u32[]{:S(2)}) %collective-permute-start.2) | collective-permute-done | bytes 20512 | tf_op jit(solution)/shard_map/ppermute | solution.py:18
  15.8 0.6 %backproject.1 = (f32[40,128]{1,0:T(8,128)S(1)}, bf16[64,128]{1,0:T(8,128)(2,1)S(1)}, f32[4,128]{1,0:T(4,128)S(1)}, f32[384,128]{1,0:T(8,128)S(1)}) custom-call(bf16[1,1,48,128,128]{4,3,2,1,0:T(8,128)(2,1)S(1)} %copy-done, f32[48,8]{1,0:T(8,128)S(1)} %get-tuple-element.13.pick, ...), custom_call_target="tpu_custom_call", output_to_operand_aliasing={{3}: (4, {})} | custom-call | tf_op jit(solution)/shard_map/backproject/pallas_call | solution.py:140
  16.4 0.0 collective-permute-start.5
  16.4 1.2 %collective-permute-done.5.there = bf16[64,128]{1,0:T(8,128)(2,1)S(1)} collective-permute-done((bf16[64,128]{1,0:T(8,128)(2,1)S(1)}, bf16[64,128]{1,0:T(8,128)(2,1)S(1)}, u32[]{:S(2)}, u32[]{:S(2)}) %collective-permute-start.5) | collective-permute-done | bytes 16416 | tf_op jit(solution)/shard_map/ppermute | solution.py:18
  17.6 0.6 %update.1 = (f32[32,128]{1,0:T(8,128)}, bf16[1,1,4,128]{3,2,1,0:T(4,128)(2,1)}) custom-call(f32[32,128]{1,0:T(8,128)S(1)} %bitcast.4, f32[40,128]{1,0:T(8,128)S(1)} %get-tuple-element.19.own, bf16[64,128]{1,0:T(8,128)(2,1)S(1)} %collective-permute-done.5.there, f32[4,128]{1,0:T(4,128)S(1)} %get-tuple-element.21.residual), custom_call_target="tpu_custom_call" | custom-call | tf_op jit(solution)/shard_map/update/pallas_call | solution.py:140
  (3 shorter events, 0.0 us)
Async XLA Ops:
  0.6 1.3 %copy-start.3 = (s32[1,1,48]{2,1,0:T(1,128)S(1)}, s32[1,1,48]{2,1,0:T(1,128)}, u32[]{:S(2)}) copy-start(s32[1,1,48]{2,1,0:T(1,128)} %rows.2) | copy-start | bytes 580
  0.6 1.3 %copy-start.4 = (s32[1,1,48]{2,1,0:T(1,128)S(1)}, s32[1,1,48]{2,1,0:T(1,128)}, u32[]{:S(2)}) copy-start(s32[1,1,48]{2,1,0:T(1,128)} %cols.1) | copy-start | bytes 580
  0.7 1.6 %copy-start = (bf16[1,1,48,128,128]{4,3,2,1,0:T(8,128)(2,1)S(1)}, bf16[1,1,48,128,128]{4,3,2,1,0:T(8,128)(2,1)}, u32[]{:S(2)}) copy-start(bf16[1,1,48,128,128]{4,3,2,1,0:T(8,128)(2,1)} %tiles.3) | copy-start | bytes 4718596
  0.7 1.6 %copy-start.1 = (f32[8,4,128]{2,1,0:T(4,128)S(1)}, f32[8,4,128]{2,1,0:T(4,128)}, u32[]{:S(2)}) copy-start(f32[8,4,128]{2,1,0:T(4,128)} %param.6) | copy-start | bytes 49156
  0.7 1.6 %copy-start.2 = (f32[1,1,4,128]{3,2,1,0:T(4,128)S(1)}, f32[1,1,4,128]{3,2,1,0:T(4,128)}, u32[]{:S(2)}) copy-start(f32[1,1,4,128]{3,2,1,0:T(4,128)} %measured.1) | copy-start | bytes 6148
  0.7 1.6 %collective-permute-start = (f32[32,128]{1,0:T(8,128)}, f32[32,128]{1,0:T(8,128)S(1)}, u32[]{:S(2)}, u32[]{:S(2)}) collective-permute-start(f32[32,128]{1,0:T(8,128)} %bitcast.2), channel_id=1, source_target_pairs={{0,1},{1,0},{2,3},{3,2},{4,5},{5,4},{6,7},{7,6},{8,9},{9,8},{10,11... | collective-permute-start | bytes 49160 | tf_op jit(solution)/shard_map/ppermute | solution.py:18
  3.0 5.7 %collective-permute-start.1 = (f32[40,128]{1,0:T(8,128)S(1)}, f32[40,128]{1,0:T(8,128)S(1)}, u32[]{:S(2)}, u32[]{:S(2)}) collective-permute-start(f32[40,128]{1,0:T(8,128)S(1)} %get-tuple-element.17), channel_id=1, source_target_pairs={{0,8},{2,10},{4,12},{6,14},{8,0},{10,2},{12,4},{14,6},{1,9},{3,11}... | collective-permute-start | bytes 61448 | tf_op jit(solution)/shard_map/ppermute | solution.py:18
  8.7 4.8 %collective-permute-start.4 = (f32[40,128]{1,0:T(8,128)S(1)}, f32[40,128]{1,0:T(8,128)S(1)}, u32[]{:S(2)}, u32[]{:S(2)}) collective-permute-start(f32[40,128]{1,0:T(8,128)S(1)} %add.12), channel_id=1, source_target_pairs={{0,6},{2,4},{4,2},{6,0},{8,14},{10,12},{12,10},{14,8},{1,7},{3,5},... | collective-permute-start | bytes 61448 | tf_op jit(solution)/shard_map/ppermute | solution.py:18
  11.5 3.8 %collective-permute-start.3 = (f32[40,128]{1,0:T(8,128)S(1)}, f32[40,128]{1,0:T(8,128)S(1)}, u32[]{:S(2)}, u32[]{:S(2)}) collective-permute-start(f32[40,128]{1,0:T(8,128)S(1)} %add.12), channel_id=1, source_target_pairs={{0,4},{2,6},{4,0},{6,2},{8,12},{10,14},{12,8},{14,10},{1,5},{3,7},... | collective-permute-start | bytes 61448 | tf_op jit(solution)/shard_map/ppermute | solution.py:18
  12.0 3.8 %collective-permute-start.2 = (f32[40,128]{1,0:T(8,128)S(1)}, f32[40,128]{1,0:T(8,128)S(1)}, u32[]{:S(2)}, u32[]{:S(2)}) collective-permute-start(f32[40,128]{1,0:T(8,128)S(1)} %add.12), channel_id=1, source_target_pairs={{0,2},{2,0},{4,6},{6,4},{8,10},{10,8},{12,14},{14,12},{1,3},{3,1},... | collective-permute-start | bytes 61448 | tf_op jit(solution)/shard_map/ppermute | solution.py:18
  16.4 1.2 %collective-permute-start.5 = (bf16[64,128]{1,0:T(8,128)(2,1)S(1)}, bf16[64,128]{1,0:T(8,128)(2,1)S(1)}, u32[]{:S(2)}, u32[]{:S(2)}) collective-permute-start(bf16[64,128]{1,0:T(8,128)(2,1)S(1)} %get-tuple-element.20), channel_id=1, source_target_pairs={{0,1},{1,0},{2,3},{3,2},{4,5},{5,4},{6,7},{7,6},{8,9},{9,8},{10,11... | collective-permute-start | bytes 49160 | tf_op jit(solution)/shard_map/ppermute | solution.py:18

commit v24 on v23

--- a/solution.py
+++ b/solution.py
@@ -87,9 +87,7 @@
 def project_kernel(tiles, pick, add, volume, other, measured, _, part, picked, prods):
     inst = measured.shape[2]
     blocks = part.shape[0] // (inst + 1)
-    half = volume.shape[0] // inst
-    strides = [pl.ds(c, half, stride=inst) for c in range(inst)]
-    table = [jnp.concatenate([volume[row, :], other[row, :]], axis=0) for row in strides]
+    table = [jnp.concatenate([volume[:, c, :], other[:, c, :]], axis=0) for c in range(inst)]
     slot_rows(pick, table, picked)
     sums = apply_tiles(picked, tiles, True, add, prods, inst + 1)
     mine = lax.broadcasted_iota(jnp.int32, sums[0].shape, 0) == lax.axis_index("vox")
@@ -117,13 +115,11 @@
 
 
 def update_kernel(volume, own, there, residual, new_volume, own_residual):
-    inst = residual.shape[0]
-    half = volume.shape[0] // inst
+    half, inst, _ = volume.shape
     both = own[...] + there[...].astype(jnp.float32)[: own.shape[0]]
     weight = both[inst * half :] + 1.0
     for c in range(inst):
-        row = pl.ds(c, half, stride=inst)
-        new_volume[row, :] = jnp.maximum(volume[row, :] + both[c * half : (c + 1) * half] / weight, 0.0)
+        new_volume[:, c, :] = jnp.maximum(volume[:, c, :] + both[c * half : (c + 1) * half] / weight, 0.0)
     own_residual[0, 0] = residual[...].astype(jnp.bfloat16)
 
 
@@ -149,10 +145,9 @@
             name=name,
         )(*args)
 
-    volume = volume.reshape(half * inst, width)
     other = exchange(volume, "ray", 1)
-    slot_shape = ((slots * SUB, width), f32)
-    prods = pltpu.VMEM(*slot_shape)
+    slot_shape = (((slots + 1) * SUB, width), f32)
+    prods = pltpu.VMEM((slots * (SUB + 1), width), f32)
     (picked,) = call(
         functools.partial(rows_kernel, inst),
         "rows",
@@ -199,7 +194,7 @@
         [],
         [volume, own, there, residual],
     )
-    return new_volume.reshape(half, inst, width), own_residual
+    return new_volume, own_residual
 
 
 def solution(mesh):

time: 18.4 us -> 18.4 us (level)
  no operation moved by 1% of the time
where the time goes in v24:
time: 18.4 us; the launch traced here: 18.2 us
  starting transfers between devices  7.95 us (43%)
  waiting for transfers between devices  6.78 us (37%)
  Pallas kernels  2.11 us (11%)
  between operations  1.35 us (7%)
    ppermute x6, starting transfers between devices, exchange(): return lax.ppermute(value, axis, [(i, i ^ mask) for i in range(size)])  7.95 us
    ppermute x6, waiting for transfers between devices, exchange(): return lax.ppermute(value, axis, [(i, i ^ mask) for i in range(size)])  6.78 us
    pallas_call x5, Pallas kernels, call(): pl.pallas_call(kernel, out_shape=[jax.ShapeDtypeStruct(shape, dtype) for...  2.11 us
  transfers between devices with their start and end apart: 6, of which 6 were waited for; matrix products, arithmetic and copies ran while one was open for 0% of the time, Pallas kernels for 1%

profile of v24, /device:TPU:0, one launch (start us, length us, event | category | flops | bytes accessed | tf_op | source)
XLA Modules:
  0.0 18.2 jit_solution(98981911853425933)
XLA Ops:
  0.6 0.0 copy-start.1
  0.6 0.0 copy-start.4
  0.7 0.0 copy-start.3
  0.7 0.0 copy-start
  0.7 0.0 copy-start.2
  0.7 0.5 %collective-permute-start = (f32[8,4,128]{2,1,0:T(4,128)}, f32[8,4,128]{2,1,0:T(4,128)S(1)}, u32[]{:S(2)}, u32[]{:S(2)}) collective-permute-start(f32[8,4,128]{2,1,0:T(4,128)} %volume.3), channel_id=1, source_target_pairs={{0,1},{1,0},{2,3},{3,2},{4,5},{5,4},{6,7},{7,6},{8,9},{9,8},{10,11... | collective-permute-start | bytes 49160 | tf_op jit(solution)/shard_map/ppermute | solution.py:18
  1.9 0.0 copy-done.4
  1.9 0.0 copy-done.3
  1.9 0.1 prepare.1
  2.0 0.2 %collective-permute-done.other = f32[8,4,128]{2,1,0:T(4,128)S(1)} collective-permute-done((f32[8,4,128]{2,1,0:T(4,128)}, f32[8,4,128]{2,1,0:T(4,128)S(1)}, u32[]{:S(2)}, u32[]{:S(2)}) %collective-permute-start) | collective-permute-done | bytes 16416 | tf_op jit(solution)/shard_map/ppermute | solution.py:18
  2.2 0.0 copy-done.1
  2.3 0.0 copy-done
  2.3 0.0 copy-done.2
  2.3 0.7 %project.1 = (f32[40,128]{1,0:T(8,128)S(1)}, f32[392,128]{1,0:T(8,128)S(1)}) custom-call(bf16[1,1,48,128,128]{4,3,2,1,0:T(8,128)(2,1)S(1)} %copy-done, f32[48,16]{1,0:T(8,128)S(1)} %get-tuple-element.13.pick, f32[8,144]{1,0:T(8,128)S(1)} %get-tuple-element.14.add, f32[8,4,128]{2,1,0:T(4,128)S(1)} %copy-done.1, ...), custom_call_target="tpu_custom_call", output_to_operand_aliasing={{1}: (6, {})} | custom-call | tf_op jit(solution)/shard_map/project/pallas_call | solution.py:136
  3.0 3.9 %collective-permute-start.1 = (f32[40,128]{1,0:T(8,128)S(1)}, f32[40,128]{1,0:T(8,128)S(1)}, u32[]{:S(2)}, u32[]{:S(2)}) collective-permute-start(f32[40,128]{1,0:T(8,128)S(1)} %get-tuple-element.15), channel_id=1, source_target_pairs={{0,8},{2,10},{4,12},{6,14},{8,0},{10,2},{12,4},{14,6},{1,9},{3,11}... | collective-permute-start | bytes 61448 | tf_op jit(solution)/shard_map/ppermute | solution.py:18
  6.9 1.8 %collective-permute-done.1 = f32[40,128]{1,0:T(8,128)S(1)} collective-permute-done((f32[40,128]{1,0:T(8,128)S(1)}, f32[40,128]{1,0:T(8,128)S(1)}, u32[]{:S(2)}, u32[]{:S(2)}) %collective-permute-start.1) | collective-permute-done | bytes 20512 | tf_op jit(solution)/shard_map/ppermute | solution.py:18
  8.7 2.8 %collective-permute-start.4 = (f32[40,128]{1,0:T(8,128)S(1)}, f32[40,128]{1,0:T(8,128)S(1)}, u32[]{:S(2)}, u32[]{:S(2)}) collective-permute-start(f32[40,128]{1,0:T(8,128)S(1)} %add.12), channel_id=1, source_target_pairs={{0,6},{2,4},{4,2},{6,0},{8,14},{10,12},{12,10},{14,8},{1,7},{3,5},... | collective-permute-start | bytes 61448 | tf_op jit(solution)/shard_map/ppermute | solution.py:18
  11.5 0.5 %collective-permute-start.3 = (f32[40,128]{1,0:T(8,128)S(1)}, f32[40,128]{1,0:T(8,128)S(1)}, u32[]{:S(2)}, u32[]{:S(2)}) collective-permute-start(f32[40,128]{1,0:T(8,128)S(1)} %add.12), channel_id=1, source_target_pairs={{0,4},{2,6},{4,0},{6,2},{8,12},{10,14},{12,8},{14,10},{1,5},{3,7},... | collective-permute-start | bytes 61448 | tf_op jit(solution)/shard_map/ppermute | solution.py:18
  12.0 0.2 %collective-permute-start.2 = (f32[40,128]{1,0:T(8,128)S(1)}, f32[40,128]{1,0:T(8,128)S(1)}, u32[]{:S(2)}, u32[]{:S(2)}) collective-permute-start(f32[40,128]{1,0:T(8,128)S(1)} %add.12), channel_id=1, source_target_pairs={{0,2},{2,0},{4,6},{6,4},{8,10},{10,8},{12,14},{14,12},{1,3},{3,1},... | collective-permute-start | bytes 61448 | tf_op jit(solution)/shard_map/ppermute | solution.py:18
  12.2 1.3 %collective-permute-done.4 = f32[40,128]{1,0:T(8,128)S(1)} collective-permute-done((f32[40,128]{1,0:T(8,128)S(1)}, f32[40,128]{1,0:T(8,128)S(1)}, u32[]{:S(2)}, u32[]{:S(2)}) %collective-permute-start.4) | collective-permute-done | bytes 20512 | tf_op jit(solution)/shard_map/ppermute | solution.py:18
  13.5 1.8 %collective-permute-done.3 = f32[40,128]{1,0:T(8,128)S(1)} collective-permute-done((f32[40,128]{1,0:T(8,128)S(1)}, f32[40,128]{1,0:T(8,128)S(1)}, u32[]{:S(2)}, u32[]{:S(2)}) %collective-permute-start.3) | collective-permute-done | bytes 20512 | tf_op jit(solution)/shard_map/ppermute | solution.py:18
  15.3 0.5 %collective-permute-done.2 = f32[40,128]{1,0:T(8,128)S(1)} collective-permute-done((f32[40,128]{1,0:T(8,128)S(1)}, f32[40,128]{1,0:T(8,128)S(1)}, u32[]{:S(2)}, u32[]{:S(2)}) %collective-permute-start.2) | collective-permute-done | bytes 20512 | tf_op jit(solution)/shard_map/ppermute | solution.py:18
  15.8 0.6 %backproject.1 = (f32[40,128]{1,0:T(8,128)S(1)}, bf16[64,128]{1,0:T(8,128)(2,1)S(1)}, f32[4,128]{1,0:T(4,128)S(1)}, f32[392,128]{1,0:T(8,128)S(1)}) custom-call(bf16[1,1,48,128,128]{4,3,2,1,0:T(8,128)(2,1)S(1)} %copy-done, f32[48,8]{1,0:T(8,128)S(1)} %get-tuple-element.11.pick, ...), custom_call_target="tpu_custom_call", output_to_operand_aliasing={{3}: (4, {})} | custom-call | tf_op jit(solution)/shard_map/backproject/pallas_call | solution.py:136
  16.4 0.0 collective-permute-start.5
  16.4 1.2 %collective-permute-done.5.there = bf16[64,128]{1,0:T(8,128)(2,1)S(1)} collective-permute-done((bf16[64,128]{1,0:T(8,128)(2,1)S(1)}, bf16[64,128]{1,0:T(8,128)(2,1)S(1)}, u32[]{:S(2)}, u32[]{:S(2)}) %collective-permute-start.5) | collective-permute-done | bytes 16416 | tf_op jit(solution)/shard_map/ppermute | solution.py:18
  17.6 0.6 %update.1 = (f32[8,4,128]{2,1,0:T(4,128)}, bf16[1,1,4,128]{3,2,1,0:T(4,128)(2,1)}) custom-call(f32[8,4,128]{2,1,0:T(4,128)S(1)} %copy-done.1, f32[40,128]{1,0:T(8,128)S(1)} %get-tuple-element.17.own, bf16[64,128]{1,0:T(8,128)(2,1)S(1)} %collective-permute-done.5.there, f32[4,128]{1,0:T(4,128)S(1)} %get-tuple-element.19.residual), custom_call_target="tpu_custom_call" | custom-call | tf_op jit(solution)/shard_map/update/pallas_call | solution.py:136
  (3 shorter events, 0.0 us)
Async XLA Ops:
  0.6 1.6 %copy-start.1 = (f32[8,4,128]{2,1,0:T(4,128)S(1)}, f32[8,4,128]{2,1,0:T(4,128)}, u32[]{:S(2)}) copy-start(f32[8,4,128]{2,1,0:T(4,128)} %volume.3) | copy-start | bytes 49156
  0.6 1.2 %copy-start.4 = (s32[1,1,48]{2,1,0:T(1,128)S(1)}, s32[1,1,48]{2,1,0:T(1,128)}, u32[]{:S(2)}) copy-start(s32[1,1,48]{2,1,0:T(1,128)} %cols.1) | copy-start | bytes 580
  0.7 1.2 %copy-start.3 = (s32[1,1,48]{2,1,0:T(1,128)S(1)}, s32[1,1,48]{2,1,0:T(1,128)}, u32[]{:S(2)}) copy-start(s32[1,1,48]{2,1,0:T(1,128)} %rows.2) | copy-start | bytes 580
  0.7 1.6 %copy-start = (bf16[1,1,48,128,128]{4,3,2,1,0:T(8,128)(2,1)S(1)}, bf16[1,1,48,128,128]{4,3,2,1,0:T(8,128)(2,1)}, u32[]{:S(2)}) copy-start(bf16[1,1,48,128,128]{4,3,2,1,0:T(8,128)(2,1)} %tiles.3) | copy-start | bytes 4718596
  0.7 1.6 %copy-start.2 = (f32[1,1,4,128]{3,2,1,0:T(4,128)S(1)}, f32[1,1,4,128]{3,2,1,0:T(4,128)}, u32[]{:S(2)}) copy-start(f32[1,1,4,128]{3,2,1,0:T(4,128)} %measured.1) | copy-start | bytes 6148
  0.7 1.6 %collective-permute-start = (f32[8,4,128]{2,1,0:T(4,128)}, f32[8,4,128]{2,1,0:T(4,128)S(1)}, u32[]{:S(2)}, u32[]{:S(2)}) collective-permute-start(f32[8,4,128]{2,1,0:T(4,128)} %volume.3), channel_id=1, source_target_pairs={{0,1},{1,0},{2,3},{3,2},{4,5},{5,4},{6,7},{7,6},{8,9},{9,8},{10,11... | collective-permute-start | bytes 49160 | tf_op jit(solution)/shard_map/ppermute | solution.py:18
  3.0 5.7 %collective-permute-start.1 = (f32[40,128]{1,0:T(8,128)S(1)}, f32[40,128]{1,0:T(8,128)S(1)}, u32[]{:S(2)}, u32[]{:S(2)}) collective-permute-start(f32[40,128]{1,0:T(8,128)S(1)} %get-tuple-element.15), channel_id=1, source_target_pairs={{0,8},{2,10},{4,12},{6,14},{8,0},{10,2},{12,4},{14,6},{1,9},{3,11}... | collective-permute-start | bytes 61448 | tf_op jit(solution)/shard_map/ppermute | solution.py:18
  8.7 4.8 %collective-permute-start.4 = (f32[40,128]{1,0:T(8,128)S(1)}, f32[40,128]{1,0:T(8,128)S(1)}, u32[]{:S(2)}, u32[]{:S(2)}) collective-permute-start(f32[40,128]{1,0:T(8,128)S(1)} %add.12), channel_id=1, source_target_pairs={{0,6},{2,4},{4,2},{6,0},{8,14},{10,12},{12,10},{14,8},{1,7},{3,5},... | collective-permute-start | bytes 61448 | tf_op jit(solution)/shard_map/ppermute | solution.py:18
  11.5 3.8 %collective-permute-start.3 = (f32[40,128]{1,0:T(8,128)S(1)}, f32[40,128]{1,0:T(8,128)S(1)}, u32[]{:S(2)}, u32[]{:S(2)}) collective-permute-start(f32[40,128]{1,0:T(8,128)S(1)} %add.12), channel_id=1, source_target_pairs={{0,4},{2,6},{4,0},{6,2},{8,12},{10,14},{12,8},{14,10},{1,5},{3,7},... | collective-permute-start | bytes 61448 | tf_op jit(solution)/shard_map/ppermute | solution.py:18
  12.0 3.8 %collective-permute-start.2 = (f32[40,128]{1,0:T(8,128)S(1)}, f32[40,128]{1,0:T(8,128)S(1)}, u32[]{:S(2)}, u32[]{:S(2)}) collective-permute-start(f32[40,128]{1,0:T(8,128)S(1)} %add.12), channel_id=1, source_target_pairs={{0,2},{2,0},{4,6},{6,4},{8,10},{10,8},{12,14},{14,12},{1,3},{3,1},... | collective-permute-start | bytes 61448 | tf_op jit(solution)/shard_map/ppermute | solution.py:18
  16.4 1.2 %collective-permute-start.5 = (bf16[64,128]{1,0:T(8,128)(2,1)S(1)}, bf16[64,128]{1,0:T(8,128)(2,1)S(1)}, u32[]{:S(2)}, u32[]{:S(2)}) collective-permute-start(bf16[64,128]{1,0:T(8,128)(2,1)S(1)} %get-tuple-element.18), channel_id=1, source_target_pairs={{0,1},{1,0},{2,3},{3,2},{4,5},{5,4},{6,7},{7,6},{8,9},{9,8},{10,11... | collective-permute-start | bytes 49160 | tf_op jit(solution)/shard_map/ppermute | solution.py:18

commit v25 on v24

--- a/solution.py
+++ b/solution.py
@@ -29,8 +29,9 @@
         across = exchange(value, axis, stride)
         both = exchange(value, axis, 3 * stride)
         along = exchange(value, axis, 2 * stride)
+        terms = (value, across, along, both)
         value = (value + across) + (along + both)
-    return value
+    return terms
 
 
 def rows_kernel(inst, picked):
@@ -97,16 +98,17 @@
     part[inst * blocks : (inst + 1) * blocks, :] = sums[inst]
 
 
-def backproject_kernel(tiles, pick, add, total, _, own, send, residual, picked, prods):
+def backproject_kernel(tiles, pick, add, a, b, c, d, _, own, send, residual, picked, prods):
     inst = residual.shape[0]
+    total = (a[...] + b[...]) + (c[...] + d[...])
     blocks = total.shape[0] // (inst + 1)
     half = own.shape[0] // (inst + 1)
-    kinds = [total[c * blocks : (c + 1) * blocks, :] for c in range(inst + 1)]
+    kinds = [total[k * blocks : (k + 1) * blocks] for k in range(inst + 1)]
     weight = kinds[inst] + 1.0
     table = [(kind / weight).astype(jnp.bfloat16).astype(jnp.float32) for kind in kinds[:inst]]
     mine = lax.broadcasted_iota(jnp.int32, weight.shape, 0) == lax.axis_index("vox")
-    for c in range(inst):
-        residual[c : c + 1, :] = jnp.sum(jnp.where(mine, table[c], 0.0), axis=0, keepdims=True)
+    for k in range(inst):
+        residual[k : k + 1, :] = jnp.sum(jnp.where(mine, table[k], 0.0), axis=0, keepdims=True)
     slot_rows(pick, table, picked)
     sums = apply_tiles(picked, tiles, False, add, prods, inst + 1)
     filler = [jnp.zeros((half, weight.shape[1]), jnp.float32)] * (SUB - inst - 1)
@@ -177,14 +179,14 @@
         [tiles, pick, add, volume, other, measured, picked],
         aliases={6: 1},
     )
-    total = all_sum(part, "vox")
+    terms = all_sum(part, "vox")
     own, send, residual, _ = call(
         backproject_kernel,
         "backproject",
         [(((inst + 1) * half, width), f32), ((SUB * half, width), bf16), ((inst, width), f32), slot_shape],
         [prods],
-        [tiles, pick_back, add_back, total, picked],
-        aliases={4: 3},
+        [tiles, pick_back, add_back, *terms, picked],
+        aliases={7: 3},
     )
     there = exchange(send, "ray", 1)
     new_volume, own_residual = call(

time: 18.4 us -> 18.4 us (level)
  no operation moved by 1% of the time
where the time goes in v25:
time: 18.4 us; the launch traced here: 18.2 us
  starting transfers between devices  7.95 us (43%)
  waiting for transfers between devices  6.78 us (37%)
  Pallas kernels  2.12 us (12%)
  between operations  1.35 us (7%)
    ppermute x6, starting transfers between devices, exchange(): return lax.ppermute(value, axis, [(i, i ^ mask) for i in range(size)])  7.95 us
    ppermute x6, waiting for transfers between devices, exchange(): return lax.ppermute(value, axis, [(i, i ^ mask) for i in range(size)])  6.78 us
    pallas_call x5, Pallas kernels, call(): pl.pallas_call(kernel, out_shape=[jax.ShapeDtypeStruct(shape, dtype) for...  2.12 us
  transfers between devices with their start and end apart: 6, of which 6 were waited for; matrix products, arithmetic and copies ran while one was open for 0% of the time, Pallas kernels for 1%

profile of v25, /device:TPU:0, one launch (start us, length us, event | category | flops | bytes accessed | tf_op | source)
XLA Modules:
  0.0 18.2 jit_solution(5229039565872311316)
XLA Ops:
  0.6 0.0 copy-start.1
  0.6 0.0 copy-start.4
  0.7 0.0 copy-start.3
  0.7 0.0 copy-start
  0.7 0.0 copy-start.2
  0.7 0.5 %collective-permute-start = (f32[8,4,128]{2,1,0:T(4,128)}, f32[8,4,128]{2,1,0:T(4,128)S(1)}, u32[]{:S(2)}, u32[]{:S(2)}) collective-permute-start(f32[8,4,128]{2,1,0:T(4,128)} %volume.3), channel_id=1, source_target_pairs={{0,1},{1,0},{2,3},{3,2},{4,5},{5,4},{6,7},{7,6},{8,9},{9,8},{10,11... | collective-permute-start | bytes 49160 | tf_op jit(solution)/shard_map/ppermute | solution.py:18
  1.9 0.0 copy-done.4
  1.9 0.0 copy-done.3
  1.9 0.1 prepare.1
  2.0 0.2 %collective-permute-done.other = f32[8,4,128]{2,1,0:T(4,128)S(1)} collective-permute-done((f32[8,4,128]{2,1,0:T(4,128)}, f32[8,4,128]{2,1,0:T(4,128)S(1)}, u32[]{:S(2)}, u32[]{:S(2)}) %collective-permute-start) | collective-permute-done | bytes 16416 | tf_op jit(solution)/shard_map/ppermute | solution.py:18
  2.2 0.0 copy-done.1
  2.3 0.0 copy-done
  2.3 0.0 copy-done.2
  2.3 0.7 %project.1 = (f32[40,128]{1,0:T(8,128)S(1)}, f32[392,128]{1,0:T(8,128)S(1)}) custom-call(bf16[1,1,48,128,128]{4,3,2,1,0:T(8,128)(2,1)S(1)} %copy-done, f32[48,16]{1,0:T(8,128)S(1)} %get-tuple-element.13.pick, f32[8,144]{1,0:T(8,128)S(1)} %get-tuple-element.14.add, f32[8,4,128]{2,1,0:T(4,128)S(1)} %copy-done.1, ...), custom_call_target="tpu_custom_call", output_to_operand_aliasing={{1}: (6, {})} | custom-call | tf_op jit(solution)/shard_map/project/pallas_call | solution.py:138
  3.0 3.9 %collective-permute-start.1 = (f32[40,128]{1,0:T(8,128)S(1)}, f32[40,128]{1,0:T(8,128)S(1)}, u32[]{:S(2)}, u32[]{:S(2)}) collective-permute-start(f32[40,128]{1,0:T(8,128)S(1)} %get-tuple-element.15), channel_id=1, source_target_pairs={{0,8},{2,10},{4,12},{6,14},{8,0},{10,2},{12,4},{14,6},{1,9},{3,11}... | collective-permute-start | bytes 61448 | tf_op jit(solution)/shard_map/ppermute | solution.py:18
  6.9 1.8 %collective-permute-done.1 = f32[40,128]{1,0:T(8,128)S(1)} collective-permute-done((f32[40,128]{1,0:T(8,128)S(1)}, f32[40,128]{1,0:T(8,128)S(1)}, u32[]{:S(2)}, u32[]{:S(2)}) %collective-permute-start.1) | collective-permute-done | bytes 20512 | tf_op jit(solution)/shard_map/ppermute | solution.py:18
  8.7 2.8 %collective-permute-start.4 = (f32[40,128]{1,0:T(8,128)S(1)}, f32[40,128]{1,0:T(8,128)S(1)}, u32[]{:S(2)}, u32[]{:S(2)}) collective-permute-start(f32[40,128]{1,0:T(8,128)S(1)} %add.3.a), channel_id=1, source_target_pairs={{0,6},{2,4},{4,2},{6,0},{8,14},{10,12},{12,10},{14,8},{1,7},{3,5},... | collective-permute-start | bytes 61448 | tf_op jit(solution)/shard_map/ppermute | solution.py:18
  11.5 0.5 %collective-permute-start.3 = (f32[40,128]{1,0:T(8,128)S(1)}, f32[40,128]{1,0:T(8,128)S(1)}, u32[]{:S(2)}, u32[]{:S(2)}) collective-permute-start(f32[40,128]{1,0:T(8,128)S(1)} %add.3.a), channel_id=1, source_target_pairs={{0,4},{2,6},{4,0},{6,2},{8,12},{10,14},{12,8},{14,10},{1,5},{3,7},... | collective-permute-start | bytes 61448 | tf_op jit(solution)/shard_map/ppermute | solution.py:18
  12.0 0.2 %collective-permute-start.2 = (f32[40,128]{1,0:T(8,128)S(1)}, f32[40,128]{1,0:T(8,128)S(1)}, u32[]{:S(2)}, u32[]{:S(2)}) collective-permute-start(f32[40,128]{1,0:T(8,128)S(1)} %add.3.a), channel_id=1, source_target_pairs={{0,2},{2,0},{4,6},{6,4},{8,10},{10,8},{12,14},{14,12},{1,3},{3,1},... | collective-permute-start | bytes 61448 | tf_op jit(solution)/shard_map/ppermute | solution.py:18
  12.2 1.3 %collective-permute-done.4.d = f32[40,128]{1,0:T(8,128)S(1)} collective-permute-done((f32[40,128]{1,0:T(8,128)S(1)}, f32[40,128]{1,0:T(8,128)S(1)}, u32[]{:S(2)}, u32[]{:S(2)}) %collective-permute-start.4) | collective-permute-done | bytes 20512 | tf_op jit(solution)/shard_map/ppermute | solution.py:18
  13.5 1.8 %collective-permute-done.3.c = f32[40,128]{1,0:T(8,128)S(1)} collective-permute-done((f32[40,128]{1,0:T(8,128)S(1)}, f32[40,128]{1,0:T(8,128)S(1)}, u32[]{:S(2)}, u32[]{:S(2)}) %collective-permute-start.3) | collective-permute-done | bytes 20512 | tf_op jit(solution)/shard_map/ppermute | solution.py:18
  15.3 0.5 %collective-permute-done.2.b = f32[40,128]{1,0:T(8,128)S(1)} collective-permute-done((f32[40,128]{1,0:T(8,128)S(1)}, f32[40,128]{1,0:T(8,128)S(1)}, u32[]{:S(2)}, u32[]{:S(2)}) %collective-permute-start.2) | collective-permute-done | bytes 20512 | tf_op jit(solution)/shard_map/ppermute | solution.py:18
  15.8 0.6 %backproject.1 = (f32[40,128]{1,0:T(8,128)S(1)}, bf16[64,128]{1,0:T(8,128)(2,1)S(1)}, f32[4,128]{1,0:T(4,128)S(1)}, f32[392,128]{1,0:T(8,128)S(1)}) custom-call(bf16[1,1,48,128,128]{4,3,2,1,0:T(8,128)(2,1)S(1)} %copy-done, f32[48,8]{1,0:T(8,128)S(1)} %get-tuple-element.11.pick, ...), custom_call_target="tpu_custom_call", output_to_operand_aliasing={{3}: (7, {})} | custom-call | tf_op jit(solution)/shard_map/backproject/pallas_call | solution.py:138
  16.4 0.0 collective-permute-start.5
  16.4 1.2 %collective-permute-done.5.there = bf16[64,128]{1,0:T(8,128)(2,1)S(1)} collective-permute-done((bf16[64,128]{1,0:T(8,128)(2,1)S(1)}, bf16[64,128]{1,0:T(8,128)(2,1)S(1)}, u32[]{:S(2)}, u32[]{:S(2)}) %collective-permute-start.5) | collective-permute-done | bytes 16416 | tf_op jit(solution)/shard_map/ppermute | solution.py:18
  17.6 0.6 %update.1 = (f32[8,4,128]{2,1,0:T(4,128)}, bf16[1,1,4,128]{3,2,1,0:T(4,128)(2,1)}) custom-call(f32[8,4,128]{2,1,0:T(4,128)S(1)} %copy-done.1, f32[40,128]{1,0:T(8,128)S(1)} %get-tuple-element.17.own, bf16[64,128]{1,0:T(8,128)(2,1)S(1)} %collective-permute-done.5.there, f32[4,128]{1,0:T(4,128)S(1)} %get-tuple-element.19.residual), custom_call_target="tpu_custom_call" | custom-call | tf_op jit(solution)/shard_map/update/pallas_call | solution.py:138
  (2 shorter events, 0.0 us)
Async XLA Ops:
  0.6 1.6 %copy-start.1 = (f32[8,4,128]{2,1,0:T(4,128)S(1)}, f32[8,4,128]{2,1,0:T(4,128)}, u32[]{:S(2)}) copy-start(f32[8,4,128]{2,1,0:T(4,128)} %volume.3) | copy-start | bytes 49156
  0.6 1.2 %copy-start.4 = (s32[1,1,48]{2,1,0:T(1,128)S(1)}, s32[1,1,48]{2,1,0:T(1,128)}, u32[]{:S(2)}) copy-start(s32[1,1,48]{2,1,0:T(1,128)} %cols.1) | copy-start | bytes 580
  0.7 1.2 %copy-start.3 = (s32[1,1,48]{2,1,0:T(1,128)S(1)}, s32[1,1,48]{2,1,0:T(1,128)}, u32[]{:S(2)}) copy-start(s32[1,1,48]{2,1,0:T(1,128)} %rows.2) | copy-start | bytes 580
  0.7 1.6 %copy-start = (bf16[1,1,48,128,128]{4,3,2,1,0:T(8,128)(2,1)S(1)}, bf16[1,1,48,128,128]{4,3,2,1,0:T(8,128)(2,1)}, u32[]{:S(2)}) copy-start(bf16[1,1,48,128,128]{4,3,2,1,0:T(8,128)(2,1)} %tiles.3) | copy-start | bytes 4718596
  0.7 1.6 %copy-start.2 = (f32[1,1,4,128]{3,2,1,0:T(4,128)S(1)}, f32[1,1,4,128]{3,2,1,0:T(4,128)}, u32[]{:S(2)}) copy-start(f32[1,1,4,128]{3,2,1,0:T(4,128)} %measured.1) | copy-start | bytes 6148
  0.7 1.6 %collective-permute-start = (f32[8,4,128]{2,1,0:T(4,128)}, f32[8,4,128]{2,1,0:T(4,128)S(1)}, u32[]{:S(2)}, u32[]{:S(2)}) collective-permute-start(f32[8,4,128]{2,1,0:T(4,128)} %volume.3), channel_id=1, source_target_pairs={{0,1},{1,0},{2,3},{3,2},{4,5},{5,4},{6,7},{7,6},{8,9},{9,8},{10,11... | collective-permute-start | bytes 49160 | tf_op jit(solution)/shard_map/ppermute | solution.py:18
  3.0 5.7 %collective-permute-start.1 = (f32[40,128]{1,0:T(8,128)S(1)}, f32[40,128]{1,0:T(8,128)S(1)}, u32[]{:S(2)}, u32[]{:S(2)}) collective-permute-start(f32[40,128]{1,0:T(8,128)S(1)} %get-tuple-element.15), channel_id=1, source_target_pairs={{0,8},{2,10},{4,12},{6,14},{8,0},{10,2},{12,4},{14,6},{1,9},{3,11}... | collective-permute-start | bytes 61448 | tf_op jit(solution)/shard_map/ppermute | solution.py:18
  8.7 4.8 %collective-permute-start.4 = (f32[40,128]{1,0:T(8,128)S(1)}, f32[40,128]{1,0:T(8,128)S(1)}, u32[]{:S(2)}, u32[]{:S(2)}) collective-permute-start(f32[40,128]{1,0:T(8,128)S(1)} %add.3.a), channel_id=1, source_target_pairs={{0,6},{2,4},{4,2},{6,0},{8,14},{10,12},{12,10},{14,8},{1,7},{3,5},... | collective-permute-start | bytes 61448 | tf_op jit(solution)/shard_map/ppermute | solution.py:18
  11.5 3.8 %collective-permute-start.3 = (f32[40,128]{1,0:T(8,128)S(1)}, f32[40,128]{1,0:T(8,128)S(1)}, u32[]{:S(2)}, u32[]{:S(2)}) collective-permute-start(f32[40,128]{1,0:T(8,128)S(1)} %add.3.a), channel_id=1, source_target_pairs={{0,4},{2,6},{4,0},{6,2},{8,12},{10,14},{12,8},{14,10},{1,5},{3,7},... | collective-permute-start | bytes 61448 | tf_op jit(solution)/shard_map/ppermute | solution.py:18
  12.0 3.8 %collective-permute-start.2 = (f32[40,128]{1,0:T(8,128)S(1)}, f32[40,128]{1,0:T(8,128)S(1)}, u32[]{:S(2)}, u32[]{:S(2)}) collective-permute-start(f32[40,128]{1,0:T(8,128)S(1)} %add.3.a), channel_id=1, source_target_pairs={{0,2},{2,0},{4,6},{6,4},{8,10},{10,8},{12,14},{14,12},{1,3},{3,1},... | collective-permute-start | bytes 61448 | tf_op jit(solution)/shard_map/ppermute | solution.py:18
  16.4 1.2 %collective-permute-start.5 = (bf16[64,128]{1,0:T(8,128)(2,1)S(1)}, bf16[64,128]{1,0:T(8,128)(2,1)S(1)}, u32[]{:S(2)}, u32[]{:S(2)}) collective-permute-start(bf16[64,128]{1,0:T(8,128)(2,1)S(1)} %get-tuple-element.18), channel_id=1, source_target_pairs={{0,1},{1,0},{2,3},{3,2},{4,5},{5,4},{6,7},{7,6},{8,9},{9,8},{10,11... | collective-permute-start | bytes 49160 | tf_op jit(solution)/shard_map/ppermute | solution.py:18

commit v26 on v25

--- a/solution.py
+++ b/solution.py
@@ -18,7 +18,7 @@
     return lax.ppermute(value, axis, [(i, i ^ mask) for i in range(size)])
 
 
-def all_sum(value, axis):
+def all_sum(value, axis, keep):
     bits = (lax.axis_size(axis) - 1).bit_length()
     if bits % 2:
         bits -= 1
@@ -29,9 +29,13 @@
         across = exchange(value, axis, stride)
         both = exchange(value, axis, 3 * stride)
         along = exchange(value, axis, 2 * stride)
-        terms = (value, across, along, both)
-        value = (value + across) + (along + both)
+        terms = (value, across, keep(along), both)
+        value = (value + across) + (terms[2] + both)
     return terms
+
+
+def keep_kernel(value, out):
+    out[...] = value[...]
 
 
 def rows_kernel(inst, picked):
@@ -179,7 +183,8 @@
         [tiles, pick, add, volume, other, measured, picked],
         aliases={6: 1},
     )
-    terms = all_sum(part, "vox")
+    part_shape = (((inst + 1) * blocks, width), f32)
+    terms = all_sum(part, "vox", lambda x: call(keep_kernel, "keep", [part_shape], [], [x])[0])
     own, send, residual, _ = call(
         backproject_kernel,
         "backproject",

time: 18.4 us -> 18.4 us (level)
    pallas_call x5 -> x6, Pallas kernels: 2.12 us -> 2.12 us  [call(): pl.pallas_call(kernel, out_shape=[jax.ShapeDtypeStruct(shape, dtype) for...]
where the time goes in v26:
time: 18.4 us; the launch traced here: 18.2 us
  starting transfers between devices  7.95 us (43%)
  waiting for transfers between devices  6.78 us (37%)
  Pallas kernels  2.12 us (12%)
  between operations  1.35 us (7%)
    ppermute x6, starting transfers between devices, exchange(): return lax.ppermute(value, axis, [(i, i ^ mask) for i in range(size)])  7.95 us
    ppermute x6, waiting for transfers between devices, exchange(): return lax.ppermute(value, axis, [(i, i ^ mask) for i in range(size)])  6.78 us
    pallas_call x6, Pallas kernels, call(): pl.pallas_call(kernel, out_shape=[jax.ShapeDtypeStruct(shape, dtype) for...  2.12 us
  transfers between devices with their start and end apart: 6, of which 6 were waited for; matrix products, arithmetic and copies ran while one was open for 0% of the time, Pallas kernels for 1%

profile of v26, /device:TPU:0, one launch (start us, length us, event | category | flops | bytes accessed | tf_op | source)
XLA Modules:
  0.0 18.2 jit_solution(3520068981289301554)
XLA Ops:
  0.6 0.0 copy-start.1
  0.6 0.0 copy-start.4
  0.7 0.0 copy-start.3
  0.7 0.0 copy-start
  0.7 0.0 copy-start.2
  0.7 0.5 %collective-permute-start = (f32[8,4,128]{2,1,0:T(4,128)}, f32[8,4,128]{2,1,0:T(4,128)S(1)}, u32[]{:S(2)}, u32[]{:S(2)}) collective-permute-start(f32[8,4,128]{2,1,0:T(4,128)} %volume.3), channel_id=1, source_target_pairs={{0,1},{1,0},{2,3},{3,2},{4,5},{5,4},{6,7},{7,6},{8,9},{9,8},{10,11... | collective-permute-start | bytes 49160 | tf_op jit(solution)/shard_map/ppermute | solution.py:18
  1.9 0.0 copy-done.4
  1.9 0.0 copy-done.3
  1.9 0.1 prepare.1
  2.0 0.2 %collective-permute-done.other = f32[8,4,128]{2,1,0:T(4,128)S(1)} collective-permute-done((f32[8,4,128]{2,1,0:T(4,128)}, f32[8,4,128]{2,1,0:T(4,128)S(1)}, u32[]{:S(2)}, u32[]{:S(2)}) %collective-permute-start) | collective-permute-done | bytes 16416 | tf_op jit(solution)/shard_map/ppermute | solution.py:18
  2.2 0.0 copy-done.1
  2.3 0.0 copy-done
  2.3 0.0 copy-done.2
  2.3 0.7 %project.1 = (f32[40,128]{1,0:T(8,128)S(1)}, f32[392,128]{1,0:T(8,128)S(1)}) custom-call(bf16[1,1,48,128,128]{4,3,2,1,0:T(8,128)(2,1)S(1)} %copy-done, f32[48,16]{1,0:T(8,128)S(1)} %get-tuple-element.13.pick, f32[8,144]{1,0:T(8,128)S(1)} %get-tuple-element.14.add, f32[8,4,128]{2,1,0:T(4,128)S(1)} %copy-done.1, ...), custom_call_target="tpu_custom_call", output_to_operand_aliasing={{1}: (6, {})} | custom-call | tf_op jit(solution)/shard_map/project/pallas_call | solution.py:142
  3.0 3.9 %collective-permute-start.1 = (f32[40,128]{1,0:T(8,128)S(1)}, f32[40,128]{1,0:T(8,128)S(1)}, u32[]{:S(2)}, u32[]{:S(2)}) collective-permute-start(f32[40,128]{1,0:T(8,128)S(1)} %get-tuple-element.15), channel_id=1, source_target_pairs={{0,8},{2,10},{4,12},{6,14},{8,0},{10,2},{12,4},{14,6},{1,9},{3,11}... | collective-permute-start | bytes 61448 | tf_op jit(solution)/shard_map/ppermute | solution.py:18
  6.9 1.8 %collective-permute-done.1 = f32[40,128]{1,0:T(8,128)S(1)} collective-permute-done((f32[40,128]{1,0:T(8,128)S(1)}, f32[40,128]{1,0:T(8,128)S(1)}, u32[]{:S(2)}, u32[]{:S(2)}) %collective-permute-start.1) | collective-permute-done | bytes 20512 | tf_op jit(solution)/shard_map/ppermute | solution.py:18
  8.7 1.9 %collective-permute-start.3 = (f32[40,128]{1,0:T(8,128)S(1)}, f32[40,128]{1,0:T(8,128)S(1)}, u32[]{:S(2)}, u32[]{:S(2)}) collective-permute-start(f32[40,128]{1,0:T(8,128)S(1)} %add.3.a), channel_id=1, source_target_pairs={{0,4},{2,6},{4,0},{6,2},{8,12},{10,14},{12,8},{14,10},{1,5},{3,7},... | collective-permute-start | bytes 61448 | tf_op jit(solution)/shard_map/ppermute | solution.py:18
  10.6 1.4 %collective-permute-start.4 = (f32[40,128]{1,0:T(8,128)S(1)}, f32[40,128]{1,0:T(8,128)S(1)}, u32[]{:S(2)}, u32[]{:S(2)}) collective-permute-start(f32[40,128]{1,0:T(8,128)S(1)} %add.3.a), channel_id=1, source_target_pairs={{0,6},{2,4},{4,2},{6,0},{8,14},{10,12},{12,10},{14,8},{1,7},{3,5},... | collective-permute-start | bytes 61448 | tf_op jit(solution)/shard_map/ppermute | solution.py:18
  12.0 0.2 %collective-permute-start.2 = (f32[40,128]{1,0:T(8,128)S(1)}, f32[40,128]{1,0:T(8,128)S(1)}, u32[]{:S(2)}, u32[]{:S(2)}) collective-permute-start(f32[40,128]{1,0:T(8,128)S(1)} %add.3.a), channel_id=1, source_target_pairs={{0,2},{2,0},{4,6},{6,4},{8,10},{10,8},{12,14},{14,12},{1,3},{3,1},... | collective-permute-start | bytes 61448 | tf_op jit(solution)/shard_map/ppermute | solution.py:18
  12.2 0.3 %collective-permute-done.3.value = f32[40,128]{1,0:T(8,128)S(1)} collective-permute-done((f32[40,128]{1,0:T(8,128)S(1)}, f32[40,128]{1,0:T(8,128)S(1)}, u32[]{:S(2)}, u32[]{:S(2)}) %collective-permute-start.3) | collective-permute-done | bytes 20512 | tf_op jit(solution)/shard_map/ppermute | solution.py:18
  12.5 2.8 %collective-permute-done.4.d = f32[40,128]{1,0:T(8,128)S(1)} collective-permute-done((f32[40,128]{1,0:T(8,128)S(1)}, f32[40,128]{1,0:T(8,128)S(1)}, u32[]{:S(2)}, u32[]{:S(2)}) %collective-permute-start.4) | collective-permute-done | bytes 20512 | tf_op jit(solution)/shard_map/ppermute | solution.py:18
  15.3 0.5 %collective-permute-done.2.b = f32[40,128]{1,0:T(8,128)S(1)} collective-permute-done((f32[40,128]{1,0:T(8,128)S(1)}, f32[40,128]{1,0:T(8,128)S(1)}, u32[]{:S(2)}, u32[]{:S(2)}) %collective-permute-start.2) | collective-permute-done | bytes 20512 | tf_op jit(solution)/shard_map/ppermute | solution.py:18
  15.8 0.6 %backproject.1 = (f32[40,128]{1,0:T(8,128)S(1)}, bf16[64,128]{1,0:T(8,128)(2,1)S(1)}, f32[4,128]{1,0:T(4,128)S(1)}, f32[392,128]{1,0:T(8,128)S(1)}) custom-call(bf16[1,1,48,128,128]{4,3,2,1,0:T(8,128)(2,1)S(1)} %copy-done, f32[48,8]{1,0:T(8,128)S(1)} %get-tuple-element.11.pick, ...), custom_call_target="tpu_custom_call", output_to_operand_aliasing={{3}: (7, {})} | custom-call | tf_op jit(solution)/shard_map/backproject/pallas_call | solution.py:142
  16.4 0.0 collective-permute-start.5
  16.4 1.2 %collective-permute-done.5.there = bf16[64,128]{1,0:T(8,128)(2,1)S(1)} collective-permute-done((bf16[64,128]{1,0:T(8,128)(2,1)S(1)}, bf16[64,128]{1,0:T(8,128)(2,1)S(1)}, u32[]{:S(2)}, u32[]{:S(2)}) %collective-permute-start.5) | collective-permute-done | bytes 16416 | tf_op jit(solution)/shard_map/ppermute | solution.py:18
  17.6 0.6 %update.1 = (f32[8,4,128]{2,1,0:T(4,128)}, bf16[1,1,4,128]{3,2,1,0:T(4,128)(2,1)}) custom-call(f32[8,4,128]{2,1,0:T(4,128)S(1)} %copy-done.1, f32[40,128]{1,0:T(8,128)S(1)} %get-tuple-element.17.own, bf16[64,128]{1,0:T(8,128)(2,1)S(1)} %collective-permute-done.5.there, f32[4,128]{1,0:T(4,128)S(1)} %get-tuple-element.19.residual), custom_call_target="tpu_custom_call" | custom-call | tf_op jit(solution)/shard_map/update/pallas_call | solution.py:142
  (3 shorter events, 0.0 us)
Async XLA Ops:
  0.6 1.6 %copy-start.1 = (f32[8,4,128]{2,1,0:T(4,128)S(1)}, f32[8,4,128]{2,1,0:T(4,128)}, u32[]{:S(2)}) copy-start(f32[8,4,128]{2,1,0:T(4,128)} %volume.3) | copy-start | bytes 49156
  0.6 1.2 %copy-start.4 = (s32[1,1,48]{2,1,0:T(1,128)S(1)}, s32[1,1,48]{2,1,0:T(1,128)}, u32[]{:S(2)}) copy-start(s32[1,1,48]{2,1,0:T(1,128)} %cols.1) | copy-start | bytes 580
  0.7 1.2 %copy-start.3 = (s32[1,1,48]{2,1,0:T(1,128)S(1)}, s32[1,1,48]{2,1,0:T(1,128)}, u32[]{:S(2)}) copy-start(s32[1,1,48]{2,1,0:T(1,128)} %rows.2) | copy-start | bytes 580
  0.7 1.6 %copy-start = (bf16[1,1,48,128,128]{4,3,2,1,0:T(8,128)(2,1)S(1)}, bf16[1,1,48,128,128]{4,3,2,1,0:T(8,128)(2,1)}, u32[]{:S(2)}) copy-start(bf16[1,1,48,128,128]{4,3,2,1,0:T(8,128)(2,1)} %tiles.3) | copy-start | bytes 4718596
  0.7 1.6 %copy-start.2 = (f32[1,1,4,128]{3,2,1,0:T(4,128)S(1)}, f32[1,1,4,128]{3,2,1,0:T(4,128)}, u32[]{:S(2)}) copy-start(f32[1,1,4,128]{3,2,1,0:T(4,128)} %measured.1) | copy-start | bytes 6148
  0.7 1.6 %collective-permute-start = (f32[8,4,128]{2,1,0:T(4,128)}, f32[8,4,128]{2,1,0:T(4,128)S(1)}, u32[]{:S(2)}, u32[]{:S(2)}) collective-permute-start(f32[8,4,128]{2,1,0:T(4,128)} %volume.3), channel_id=1, source_target_pairs={{0,1},{1,0},{2,3},{3,2},{4,5},{5,4},{6,7},{7,6},{8,9},{9,8},{10,11... | collective-permute-start | bytes 49160 | tf_op jit(solution)/shard_map/ppermute | solution.py:18
  3.0 5.7 %collective-permute-start.1 = (f32[40,128]{1,0:T(8,128)S(1)}, f32[40,128]{1,0:T(8,128)S(1)}, u32[]{:S(2)}, u32[]{:S(2)}) collective-permute-start(f32[40,128]{1,0:T(8,128)S(1)} %get-tuple-element.15), channel_id=1, source_target_pairs={{0,8},{2,10},{4,12},{6,14},{8,0},{10,2},{12,4},{14,6},{1,9},{3,11}... | collective-permute-start | bytes 61448 | tf_op jit(solution)/shard_map/ppermute | solution.py:18
  8.7 3.8 %collective-permute-start.3 = (f32[40,128]{1,0:T(8,128)S(1)}, f32[40,128]{1,0:T(8,128)S(1)}, u32[]{:S(2)}, u32[]{:S(2)}) collective-permute-start(f32[40,128]{1,0:T(8,128)S(1)} %add.3.a), channel_id=1, source_target_pairs={{0,4},{2,6},{4,0},{6,2},{8,12},{10,14},{12,8},{14,10},{1,5},{3,7},... | collective-permute-start | bytes 61448 | tf_op jit(solution)/shard_map/ppermute | solution.py:18
  10.6 4.7 %collective-permute-start.4 = (f32[40,128]{1,0:T(8,128)S(1)}, f32[40,128]{1,0:T(8,128)S(1)}, u32[]{:S(2)}, u32[]{:S(2)}) collective-permute-start(f32[40,128]{1,0:T(8,128)S(1)} %add.3.a), channel_id=1, source_target_pairs={{0,6},{2,4},{4,2},{6,0},{8,14},{10,12},{12,10},{14,8},{1,7},{3,5},... | collective-permute-start | bytes 61448 | tf_op jit(solution)/shard_map/ppermute | solution.py:18
  12.0 3.8 %collective-permute-start.2 = (f32[40,128]{1,0:T(8,128)S(1)}, f32[40,128]{1,0:T(8,128)S(1)}, u32[]{:S(2)}, u32[]{:S(2)}) collective-permute-start(f32[40,128]{1,0:T(8,128)S(1)} %add.3.a), channel_id=1, source_target_pairs={{0,2},{2,0},{4,6},{6,4},{8,10},{10,8},{12,14},{14,12},{1,3},{3,1},... | collective-permute-start | bytes 61448 | tf_op jit(solution)/shard_map/ppermute | solution.py:18
  16.4 1.2 %collective-permute-start.5 = (bf16[64,128]{1,0:T(8,128)(2,1)S(1)}, bf16[64,128]{1,0:T(8,128)(2,1)S(1)}, u32[]{:S(2)}, u32[]{:S(2)}) collective-permute-start(bf16[64,128]{1,0:T(8,128)(2,1)S(1)} %get-tuple-element.18), channel_id=1, source_target_pairs={{0,1},{1,0},{2,3},{3,2},{4,5},{5,4},{6,7},{7,6},{8,9},{9,8},{10,11... | collective-permute-start | bytes 49160 | tf_op jit(solution)/shard_map/ppermute | solution.py:18

commit v27 on v25

--- a/solution.py
+++ b/solution.py
@@ -10,6 +10,7 @@
 SUB = 8
 ROWS_FLOPS = 20_000_000_000
 PARTS = 3
+UNROLL = 16
 VMEM_BYTES = 16 << 20
 
 
@@ -65,15 +66,21 @@
 
 def apply_tiles(picked, tiles, transposed, add, prods, kinds):
     slots, _, width = tiles.shape[2:]
-    for n in range(0, slots, 2):
-        pair = [tiles[0, 0, k] for k in (n, n + 1)]
-        if transposed:
-            pair = [tile.T for tile in pair]
-        pair = jnp.concatenate(pair, axis=1)
-        left = picked[n * SUB : (n + 2) * SUB, :].astype(jnp.bfloat16)
-        both = jnp.dot(left, pair, preferred_element_type=jnp.float32)
-        prods[pl.ds(n, SUB, stride=slots), :] = both[:SUB, :width]
-        prods[pl.ds(n + 1, SUB, stride=slots), :] = both[SUB:, width:]
+
+    def step(i, carry):
+        for k in range(0, UNROLL, 2):
+            n = i * UNROLL + k
+            pair = [tiles[0, 0, n], tiles[0, 0, n + 1]]
+            if transposed:
+                pair = [tile.T for tile in pair]
+            pair = jnp.concatenate(pair, axis=1)
+            rows = pl.ds(pl.multiple_of(n * SUB, 2 * SUB), 2 * SUB)
+            both = jnp.dot(picked[rows, :].astype(jnp.bfloat16), pair, preferred_element_type=jnp.float32)
+            prods[pl.ds(n, SUB, stride=slots), :] = both[:SUB, :width]
+            prods[pl.ds(n + 1, SUB, stride=slots), :] = both[SUB:, width:]
+        return carry
+
+    lax.fori_loop(0, slots // UNROLL, step, 0)
     left = jnp.concatenate([prods[c * slots : (c + 1) * slots, :] for c in range(kinds)], axis=1)
     parts = []
     for _ in range(PARTS):

time: 18.4 us -> 19.1 us (1.038)
  Pallas kernels: 2.12 us -> 2.86 us
    pallas_call x5, Pallas kernels: 2.12 us -> 2.86 us  [call(): pl.pallas_call(kernel, out_shape=[jax.ShapeDtypeStruct(shape, dtype) for...]
where the time goes in v27:
time: 19.1 us; the launch traced here: 19 us
  starting transfers between devices  7.99 us (42%)
  waiting for transfers between devices  6.76 us (35%)
  Pallas kernels  2.86 us (15%)
  between operations  1.36 us (7%)
    ppermute x6, starting transfers between devices, exchange(): return lax.ppermute(value, axis, [(i, i ^ mask) for i in range(size)])  7.99 us
    ppermute x6, waiting for transfers between devices, exchange(): return lax.ppermute(value, axis, [(i, i ^ mask) for i in range(size)])  6.76 us
    pallas_call x5, Pallas kernels, call(): pl.pallas_call(kernel, out_shape=[jax.ShapeDtypeStruct(shape, dtype) for...  2.86 us
  transfers between devices with their start and end apart: 6, of which 6 were waited for; matrix products, arithmetic and copies ran while one was open for 0% of the time, Pallas kernels for 1%

profile of v27, /device:TPU:0, one launch (start us, length us, event | category | flops | bytes accessed | tf_op | source)
XLA Modules:
  0.0 19.0 jit_solution(7406778594943589888)
XLA Ops:
  0.6 0.0 copy-start.1
  0.6 0.0 copy-start.4
  0.7 0.0 copy-start.3
  0.7 0.0 copy-start
  0.7 0.0 copy-start.2
  0.7 0.5 %collective-permute-start = (f32[8,4,128]{2,1,0:T(4,128)}, f32[8,4,128]{2,1,0:T(4,128)S(1)}, u32[]{:S(2)}, u32[]{:S(2)}) collective-permute-start(f32[8,4,128]{2,1,0:T(4,128)} %volume.3), channel_id=1, source_target_pairs={{0,1},{1,0},{2,3},{3,2},{4,5},{5,4},{6,7},{7,6},{8,9},{9,8},{10,11... | collective-permute-start | bytes 49160 | tf_op jit(solution)/shard_map/ppermute | solution.py:19
  1.9 0.0 copy-done.4
  1.9 0.0 copy-done.3
  1.9 0.1 prepare.1
  2.0 0.2 %collective-permute-done.other = f32[8,4,128]{2,1,0:T(4,128)S(1)} collective-permute-done((f32[8,4,128]{2,1,0:T(4,128)}, f32[8,4,128]{2,1,0:T(4,128)S(1)}, u32[]{:S(2)}, u32[]{:S(2)}) %collective-permute-start) | collective-permute-done | bytes 16416 | tf_op jit(solution)/shard_map/ppermute | solution.py:19
  2.2 0.0 copy-done.1
  2.3 0.0 copy-done
  2.3 0.0 copy-done.2
  2.3 1.2 %project.1 = (f32[40,128]{1,0:T(8,128)S(1)}, f32[392,128]{1,0:T(8,128)S(1)}) custom-call(bf16[1,1,48,128,128]{4,3,2,1,0:T(8,128)(2,1)S(1)} %copy-done, f32[48,16]{1,0:T(8,128)S(1)} %get-tuple-element.13.pick, f32[8,144]{1,0:T(8,128)S(1)} %get-tuple-element.14.add, f32[8,4,128]{2,1,0:T(4,128)S(1)} %copy-done.1, ...), custom_call_target="tpu_custom_call", output_to_operand_aliasing={{1}: (6, {})} | custom-call | tf_op jit(solution)/shard_map/project/pallas_call | solution.py:145
  3.5 3.9 %collective-permute-start.1 = (f32[40,128]{1,0:T(8,128)S(1)}, f32[40,128]{1,0:T(8,128)S(1)}, u32[]{:S(2)}, u32[]{:S(2)}) collective-permute-start(f32[40,128]{1,0:T(8,128)S(1)} %get-tuple-element.15), channel_id=1, source_target_pairs={{0,8},{2,10},{4,12},{6,14},{8,0},{10,2},{12,4},{14,6},{1,9},{3,11}... | collective-permute-start | bytes 61448 | tf_op jit(solution)/shard_map/ppermute | solution.py:19
  7.4 1.8 %collective-permute-done.1 = f32[40,128]{1,0:T(8,128)S(1)} collective-permute-done((f32[40,128]{1,0:T(8,128)S(1)}, f32[40,128]{1,0:T(8,128)S(1)}, u32[]{:S(2)}, u32[]{:S(2)}) %collective-permute-start.1) | collective-permute-done | bytes 20512 | tf_op jit(solution)/shard_map/ppermute | solution.py:19
  9.2 2.8 %collective-permute-start.4 = (f32[40,128]{1,0:T(8,128)S(1)}, f32[40,128]{1,0:T(8,128)S(1)}, u32[]{:S(2)}, u32[]{:S(2)}) collective-permute-start(f32[40,128]{1,0:T(8,128)S(1)} %add.3.a), channel_id=1, source_target_pairs={{0,6},{2,4},{4,2},{6,0},{8,14},{10,12},{12,10},{14,8},{1,7},{3,5},... | collective-permute-start | bytes 61448 | tf_op jit(solution)/shard_map/ppermute | solution.py:19
  12.0 0.5 %collective-permute-start.3 = (f32[40,128]{1,0:T(8,128)S(1)}, f32[40,128]{1,0:T(8,128)S(1)}, u32[]{:S(2)}, u32[]{:S(2)}) collective-permute-start(f32[40,128]{1,0:T(8,128)S(1)} %add.3.a), channel_id=1, source_target_pairs={{0,4},{2,6},{4,0},{6,2},{8,12},{10,14},{12,8},{14,10},{1,5},{3,7},... | collective-permute-start | bytes 61448 | tf_op jit(solution)/shard_map/ppermute | solution.py:19
  12.5 0.2 %collective-permute-start.2 = (f32[40,128]{1,0:T(8,128)S(1)}, f32[40,128]{1,0:T(8,128)S(1)}, u32[]{:S(2)}, u32[]{:S(2)}) collective-permute-start(f32[40,128]{1,0:T(8,128)S(1)} %add.3.a), channel_id=1, source_target_pairs={{0,2},{2,0},{4,6},{6,4},{8,10},{10,8},{12,14},{14,12},{1,3},{3,1},... | collective-permute-start | bytes 61448 | tf_op jit(solution)/shard_map/ppermute | solution.py:19
  12.7 1.3 %collective-permute-done.4.d = f32[40,128]{1,0:T(8,128)S(1)} collective-permute-done((f32[40,128]{1,0:T(8,128)S(1)}, f32[40,128]{1,0:T(8,128)S(1)}, u32[]{:S(2)}, u32[]{:S(2)}) %collective-permute-start.4) | collective-permute-done | bytes 20512 | tf_op jit(solution)/shard_map/ppermute | solution.py:19
  14.0 1.8 %collective-permute-done.3.c = f32[40,128]{1,0:T(8,128)S(1)} collective-permute-done((f32[40,128]{1,0:T(8,128)S(1)}, f32[40,128]{1,0:T(8,128)S(1)}, u32[]{:S(2)}, u32[]{:S(2)}) %collective-permute-start.3) | collective-permute-done | bytes 20512 | tf_op jit(solution)/shard_map/ppermute | solution.py:19
  15.8 0.5 %collective-permute-done.2.b = f32[40,128]{1,0:T(8,128)S(1)} collective-permute-done((f32[40,128]{1,0:T(8,128)S(1)}, f32[40,128]{1,0:T(8,128)S(1)}, u32[]{:S(2)}, u32[]{:S(2)}) %collective-permute-start.2) | collective-permute-done | bytes 20512 | tf_op jit(solution)/shard_map/ppermute | solution.py:19
  16.3 0.9 %backproject.1 = (f32[40,128]{1,0:T(8,128)S(1)}, bf16[64,128]{1,0:T(8,128)(2,1)S(1)}, f32[4,128]{1,0:T(4,128)S(1)}, f32[392,128]{1,0:T(8,128)S(1)}) custom-call(bf16[1,1,48,128,128]{4,3,2,1,0:T(8,128)(2,1)S(1)} %copy-done, f32[48,8]{1,0:T(8,128)S(1)} %get-tuple-element.11.pick, ...), custom_call_target="tpu_custom_call", output_to_operand_aliasing={{3}: (7, {})} | custom-call | tf_op jit(solution)/shard_map/backproject/pallas_call | solution.py:145
  17.1 0.0 collective-permute-start.5
  17.2 1.2 %collective-permute-done.5.there = bf16[64,128]{1,0:T(8,128)(2,1)S(1)} collective-permute-done((bf16[64,128]{1,0:T(8,128)(2,1)S(1)}, bf16[64,128]{1,0:T(8,128)(2,1)S(1)}, u32[]{:S(2)}, u32[]{:S(2)}) %collective-permute-start.5) | collective-permute-done | bytes 16416 | tf_op jit(solution)/shard_map/ppermute | solution.py:19
  18.4 0.6 %update.1 = (f32[8,4,128]{2,1,0:T(4,128)}, bf16[1,1,4,128]{3,2,1,0:T(4,128)(2,1)}) custom-call(f32[8,4,128]{2,1,0:T(4,128)S(1)} %copy-done.1, f32[40,128]{1,0:T(8,128)S(1)} %get-tuple-element.17.own, bf16[64,128]{1,0:T(8,128)(2,1)S(1)} %collective-permute-done.5.there, f32[4,128]{1,0:T(4,128)S(1)} %get-tuple-element.19.residual), custom_call_target="tpu_custom_call" | custom-call | tf_op jit(solution)/shard_map/update/pallas_call | solution.py:145
  (2 shorter events, 0.0 us)
Async XLA Ops:
  0.6 1.6 %copy-start.1 = (f32[8,4,128]{2,1,0:T(4,128)S(1)}, f32[8,4,128]{2,1,0:T(4,128)}, u32[]{:S(2)}) copy-start(f32[8,4,128]{2,1,0:T(4,128)} %volume.3) | copy-start | bytes 49156
  0.6 1.2 %copy-start.4 = (s32[1,1,48]{2,1,0:T(1,128)S(1)}, s32[1,1,48]{2,1,0:T(1,128)}, u32[]{:S(2)}) copy-start(s32[1,1,48]{2,1,0:T(1,128)} %cols.1) | copy-start | bytes 580
  0.7 1.2 %copy-start.3 = (s32[1,1,48]{2,1,0:T(1,128)S(1)}, s32[1,1,48]{2,1,0:T(1,128)}, u32[]{:S(2)}) copy-start(s32[1,1,48]{2,1,0:T(1,128)} %rows.2) | copy-start | bytes 580
  0.7 1.6 %copy-start = (bf16[1,1,48,128,128]{4,3,2,1,0:T(8,128)(2,1)S(1)}, bf16[1,1,48,128,128]{4,3,2,1,0:T(8,128)(2,1)}, u32[]{:S(2)}) copy-start(bf16[1,1,48,128,128]{4,3,2,1,0:T(8,128)(2,1)} %tiles.3) | copy-start | bytes 4718596
  0.7 1.6 %copy-start.2 = (f32[1,1,4,128]{3,2,1,0:T(4,128)S(1)}, f32[1,1,4,128]{3,2,1,0:T(4,128)}, u32[]{:S(2)}) copy-start(f32[1,1,4,128]{3,2,1,0:T(4,128)} %measured.1) | copy-start | bytes 6148
  0.7 1.6 %collective-permute-start = (f32[8,4,128]{2,1,0:T(4,128)}, f32[8,4,128]{2,1,0:T(4,128)S(1)}, u32[]{:S(2)}, u32[]{:S(2)}) collective-permute-start(f32[8,4,128]{2,1,0:T(4,128)} %volume.3), channel_id=1, source_target_pairs={{0,1},{1,0},{2,3},{3,2},{4,5},{5,4},{6,7},{7,6},{8,9},{9,8},{10,11... | collective-permute-start | bytes 49160 | tf_op jit(solution)/shard_map/ppermute | solution.py:19
  3.5 5.7 %collective-permute-start.1 = (f32[40,128]{1,0:T(8,128)S(1)}, f32[40,128]{1,0:T(8,128)S(1)}, u32[]{:S(2)}, u32[]{:S(2)}) collective-permute-start(f32[40,128]{1,0:T(8,128)S(1)} %get-tuple-element.15), channel_id=1, source_target_pairs={{0,8},{2,10},{4,12},{6,14},{8,0},{10,2},{12,4},{14,6},{1,9},{3,11}... | collective-permute-start | bytes 61448 | tf_op jit(solution)/shard_map/ppermute | solution.py:19
  9.2 4.8 %collective-permute-start.4 = (f32[40,128]{1,0:T(8,128)S(1)}, f32[40,128]{1,0:T(8,128)S(1)}, u32[]{:S(2)}, u32[]{:S(2)}) collective-permute-start(f32[40,128]{1,0:T(8,128)S(1)} %add.3.a), channel_id=1, source_target_pairs={{0,6},{2,4},{4,2},{6,0},{8,14},{10,12},{12,10},{14,8},{1,7},{3,5},... | collective-permute-start | bytes 61448 | tf_op jit(solution)/shard_map/ppermute | solution.py:19
  12.0 3.8 %collective-permute-start.3 = (f32[40,128]{1,0:T(8,128)S(1)}, f32[40,128]{1,0:T(8,128)S(1)}, u32[]{:S(2)}, u32[]{:S(2)}) collective-permute-start(f32[40,128]{1,0:T(8,128)S(1)} %add.3.a), channel_id=1, source_target_pairs={{0,4},{2,6},{4,0},{6,2},{8,12},{10,14},{12,8},{14,10},{1,5},{3,7},... | collective-permute-start | bytes 61448 | tf_op jit(solution)/shard_map/ppermute | solution.py:19
  12.5 3.8 %collective-permute-start.2 = (f32[40,128]{1,0:T(8,128)S(1)}, f32[40,128]{1,0:T(8,128)S(1)}, u32[]{:S(2)}, u32[]{:S(2)}) collective-permute-start(f32[40,128]{1,0:T(8,128)S(1)} %add.3.a), channel_id=1, source_target_pairs={{0,2},{2,0},{4,6},{6,4},{8,10},{10,8},{12,14},{14,12},{1,3},{3,1},... | collective-permute-start | bytes 61448 | tf_op jit(solution)/shard_map/ppermute | solution.py:19
  17.1 1.2 %collective-permute-start.5 = (bf16[64,128]{1,0:T(8,128)(2,1)S(1)}, bf16[64,128]{1,0:T(8,128)(2,1)S(1)}, u32[]{:S(2)}, u32[]{:S(2)}) collective-permute-start(bf16[64,128]{1,0:T(8,128)(2,1)S(1)} %get-tuple-element.18), channel_id=1, source_target_pairs={{0,1},{1,0},{2,3},{3,2},{4,5},{5,4},{6,7},{7,6},{8,9},{9,8},{10,11... | collective-permute-start | bytes 49160 | tf_op jit(solution)/shard_map/ppermute | solution.py:19

commit v28 on v25

v28 whole, which is shorter than its diff:
```python
import functools

import jax
import jax.numpy as jnp
from jax import lax
from jax.experimental import pallas as pl
from jax.experimental.pallas import tpu as pltpu
from jax.sharding import PartitionSpec as P

SUB = 8
ROWS_FLOPS = 20_000_000_000
PARTS = 3
FEW = 16
VMEM_BYTES = 16 << 20


def exchange(value, axis, mask):
    size = lax.axis_size(axis)
    return lax.ppermute(value, axis, [(i, i ^ mask) for i in range(size)])


def all_sum(value, axis):
    bits = (lax.axis_size(axis) - 1).bit_length()
    if bits % 2:
        bits -= 1
        value = value + exchange(value, axis, 1 << bits)
    while bits:
        bits -= 2
        stride = 1 << bits
        across = exchange(value, axis, stride)
        both = exchange(value, axis, 3 * stride)
        along = exchange(value, axis, 2 * stride)
        terms = (value, across, along, both)
        value = (value + across) + (along + both)
    return terms


def filler_kernel(inst, filler):
    filler[...] = (lax.broadcasted_iota(jnp.int32, filler.shape, 0) == inst).astype(jnp.float32)


def prepare_kernel(half, count, rows, cols, pick, add, row_key, place_key):
    blocks = add.shape[0]
    used = lax.broadcasted_iota(jnp.int32, rows.shape[1:], 1) < count[0, 0]
    place = cols[0] + lax.axis_index("ray") * half
    place = jnp.where(place < 2 * half, place, place - 2 * half)
    place = jnp.where(used, place, -1)
    row = jnp.where(used, rows[0], -1)
    for key, out in ((row, row_key), (place, place_key)):
        for n in range(key.shape[1]):
            out[n * SUB : (n + 1) * SUB, :] = jnp.broadcast_to(key[:, n : n + 1], (SUB, out.shape[1]))
    hit = (lax.broadcasted_iota(jnp.int32, (blocks, row.shape[1]), 0) == row).astype(jnp.float32)
    add[...] = jnp.concatenate([hit] * PARTS, axis=1)
    pick[...] = hit.T


def of_slot(ref, n):
    return ref[n * SUB : (n + 1) * SUB, :]


def take(key, blocks):
    bit = 1
    while len(blocks) > 1:
        odd = (key & bit) != 0
        blocks = [jnp.where(odd, blocks[i + 1], blocks[i]) for i in range(0, len(blocks), 2)]
        bit *= 2
    return blocks[0]


def products(tiles, transposed, rows_of):
    slots, _, width = tiles.shape[2:]
    for n in range(0, slots, 2):
        pair = [tiles[0, 0, k] for k in (n, n + 1)]
        if transposed:
            pair = [tile.T for tile in pair]
        left = jnp.concatenate([rows_of(n), rows_of(n + 1)], axis=0).astype(jnp.bfloat16)
        both = jnp.dot(left, jnp.concatenate(pair, axis=1), preferred_element_type=jnp.float32)
        yield n, both[:SUB, :width]
        yield n + 1, both[SUB:, width:]


def sums_by_key(prods, keys, blocks):
    sums = [jnp.zeros((SUB, keys.shape[1]), jnp.float32)] * blocks
    for n, prod in prods:
        key = of_slot(keys, n)
        sums = [total + jnp.where(key == b, prod, 0.0) for b, total in enumerate(sums)]
    return sums


def project_kernel(tiles, add, row_key, place_key, volume, other, measured, filler, part, store):
    half, inst, width = volume.shape
    slots = tiles.shape[2]
    blocks = add.shape[0]
    rest = filler[inst:, :]
    table = [jnp.concatenate([ref[b], rest], axis=0) for ref in (volume, other) for b in range(half)]
    prods = products(tiles, True, lambda n: take(of_slot(place_key, n), table))
    if blocks <= FEW:
        for b, total in enumerate(sums_by_key(prods, row_key, blocks)):
            store[pl.ds(b, SUB, stride=blocks), :] = total
        sums = [store[c * blocks : (c + 1) * blocks, :] for c in range(inst + 1)]
    else:
        for n, prod in prods:
            store[pl.ds(n, SUB, stride=slots), :] = prod
        left = jnp.concatenate([store[c * slots : (c + 1) * slots, :] for c in range(inst + 1)], axis=1)
        parts = []
        for _ in range(PARTS):
            parts.append(left.astype(jnp.bfloat16))
            left = left - parts[-1].astype(jnp.float32)
        sums = jnp.dot(
            add[...].astype(jnp.bfloat16), jnp.concatenate(parts, axis=0), preferred_element_type=jnp.float32
        )
        sums = [sums[:, c * width : (c + 1) * width] for c in range(inst + 1)]
    mine = lax.broadcasted_iota(jnp.int32, (blocks, width), 0) == lax.axis_index("vox")
    for c in range(inst):
        row = jnp.broadcast_to(measured[0, 0, c : c + 1, :], (blocks, width))
        part[c * blocks : (c + 1) * blocks, :] = jnp.where(mine, row, 0.0) - sums[c]
    part[inst * blocks : (inst + 1) * blocks, :] = sums[inst]


def backproject_kernel(tiles, pick, row_key, place_key, a, b, c, d, own, send, residual, store):
    inst, width = residual.shape
    slots, blocks = pick.shape
    half = own.shape[0] // SUB
    total = (a[...] + b[...]) + (c[...] + d[...])
    kinds = [total[k * blocks : (k + 1) * blocks] for k in range(inst + 1)]
    weight = kinds[inst] + 1.0
    table = [(kind / weight).astype(jnp.bfloat16).astype(jnp.float32) for kind in kinds[:inst]]
    mine = lax.broadcasted_iota(jnp.int32, weight.shape, 0) == lax.axis_index("vox")
    for k in range(inst):
        residual[k : k + 1, :] = jnp.sum(jnp.where(mine, table[k], 0.0), axis=0, keepdims=True)
    table += [jnp.ones_like(weight)] + [jnp.zeros_like(weight)] * (SUB - inst - 1)
    if blocks <= FEW:
        for k in range(SUB):
            store[pl.ds(k, blocks, stride=SUB), :] = table[k]
        by_block = [of_slot(store, block) for block in range(blocks)]
        rows_of = lambda n: take(of_slot(row_key, n), by_block)
    else:
        rows = jnp.dot(
            pick[...].astype(jnp.bfloat16),
            jnp.concatenate(table, axis=1).astype(jnp.bfloat16),
            preferred_element_type=jnp.float32,
        )
        for k in range(SUB):
            store[pl.ds(k, slots, stride=SUB), :] = rows[:, k * width : (k + 1) * width]
        rows_of = lambda n: of_slot(store, n)
    sums = sums_by_key(products(tiles, False, rows_of), place_key, 2 * half)
    own[...] = jnp.concatenate(sums[:half], axis=0)
    send[...] = jnp.concatenate(sums[half:], axis=0).astype(jnp.bfloat16)


def update_kernel(volume, own, there, residual, new_volume, own_residual):
    half, inst, _ = volume.shape
    both = own[...] + there[...].astype(jnp.float32)
    for b in range(half):
        block = both[b * SUB : (b + 1) * SUB]
        new_volume[b] = jnp.maximum(volume[b] + block[:inst] / (block[inst : inst + 1] + 1.0), 0.0)
    own_residual[0, 0] = residual[...].astype(jnp.bfloat16)


def on_device(volume, tiles, tile_row, tile_col, tile_count, measured):
    half, inst, width = volume.shape
    slots = tiles.shape[2]
    blocks = lax.axis_size("vox") * measured.shape[1]
    f32, bf16 = jnp.float32, jnp.bfloat16
    vmem = pl.BlockSpec(memory_space=pltpu.VMEM)
    smem = pl.BlockSpec(memory_space=pltpu.SMEM)
    params = pltpu.CompilerParams(vmem_limit_bytes=VMEM_BYTES)

    def call(kernel, name, outs, scratch, args, scalars=0, cost=None):
        return pl.pallas_call(
            kernel,
            out_shape=[jax.ShapeDtypeStruct(shape, dtype) for shape, dtype in outs],
            in_specs=[smem] * scalars + [vmem] * (len(args) - scalars),
            out_specs=[vmem] * len(outs),
            scratch_shapes=scratch,
            compiler_params=params,
            cost_estimate=cost,
            name=name,
        )(*args)

    other = exchange(volume, "ray", 1)
    keys = ((slots * SUB, width), jnp.int32)
    store = [pltpu.VMEM((max(slots, blocks) * (SUB + 1), width), f32)]
    (filler,) = call(
        functools.partial(filler_kernel, inst),
        "filler",
        [((SUB, width), f32)],
        [],
        [],
        cost=pl.CostEstimate(flops=ROWS_FLOPS, bytes_accessed=0, transcendentals=0),
    )
    pick, add, row_key, place_key = call(
        functools.partial(prepare_kernel, half),
        "prepare",
        [((slots, blocks), f32), ((blocks, PARTS * slots), f32), keys, keys],
        [],
        [tile_count, tile_row, tile_col],
        scalars=1,
    )
    (part,) = call(
        project_kernel,
        "project",
        [(((inst + 1) * blocks, width), f32)],
        store,
        [tiles, add, row_key, place_key, volume, other, measured, filler],
    )
    terms = all_sum(part, "vox")
    flat = (half * SUB, width)
    own, send, residual = call(
        backproject_kernel,
        "backproject",
        [(flat, f32), (flat, bf16), ((inst, width), f32)],
        store,
        [tiles, pick, row_key, place_key, *terms],
    )
    there = exchange(send, "ray", 1)
    new_volume, own_residual = call(
        update_kernel,
        "update",
        [(volume.shape, f32), ((1, 1, inst, width), bf16)],
        [],
        [volume, own, there, residual],
    )
    return new_volume, own_residual


def solution(mesh):
    in_specs = (
        P(("slab", "vox", "ray"), None, None),
        P(("slab", "vox"), "ray", None, None, None),
        P(("slab", "vox"), "ray", None),
        P(("slab", "vox"), "ray", None),
        P(("slab", "vox"), "ray"),
        P("ray", ("slab", "vox"), None, None),
    )
    out_specs = (P(("slab", "vox", "ray"), None, None), P("ray", ("slab", "vox"), None, None))
    return jax.shard_map(
        on_device, mesh=mesh, in_specs=in_specs, out_specs=out_specs, check_vma=False
    )
```

time: 18.4 us -> 18.2 us (0.989)
  no operation moved by 1% of the time
where the time goes in v28:
time: 18.2 us; the launch traced here: 18.1 us
  starting transfers between devices  8.08 us (44%)
  waiting for transfers between devices  6.65 us (37%)
  Pallas kernels  1.94 us (11%)
  between operations  1.38 us (8%)
    ppermute x6, starting transfers between devices, exchange(): return lax.ppermute(value, axis, [(i, i ^ mask) for i in range(size)])  8.08 us
    ppermute x6, waiting for transfers between devices, exchange(): return lax.ppermute(value, axis, [(i, i ^ mask) for i in range(size)])  6.65 us
    pallas_call x5, Pallas kernels, call(): pl.pallas_call(kernel, out_shape=[jax.ShapeDtypeStruct(shape, dtype) for...  1.94 us
  transfers between devices with their start and end apart: 6, of which 6 were waited for; matrix products, arithmetic and copies ran while one was open for 0% of the time, Pallas kernels for 1%

profile of v28, /device:TPU:0, one launch (start us, length us, event | category | flops | bytes accessed | tf_op | source)
XLA Modules:
  0.0 18.1 jit_solution(4103786055745290176)
XLA Ops:
  0.6 0.0 copy-start.1
  0.6 0.0 copy-start.4
  0.7 0.0 copy-start.3
  0.7 0.0 copy-start
  0.7 0.0 copy-start.2
  0.7 0.5 %collective-permute-start = (f32[8,4,128]{2,1,0:T(4,128)}, f32[8,4,128]{2,1,0:T(4,128)S(1)}, u32[]{:S(2)}, u32[]{:S(2)}) collective-permute-start(f32[8,4,128]{2,1,0:T(4,128)} %volume.3), channel_id=1, source_target_pairs={{0,1},{1,0},{2,3},{3,2},{4,5},{5,4},{6,7},{7,6},{8,9},{9,8},{10,11... | collective-permute-start | bytes 49160 | tf_op jit(solution)/shard_map/ppermute | solution.py:19
  1.9 0.0 copy-done.4
  1.9 0.0 copy-done.3
  1.9 0.2 %prepare.1 = (f32[48,8]{1,0:T(8,128)S(1)}, f32[8,144]{1,0:T(8,128)S(1)}, s32[384,128]{1,0:T(8,128)S(1)}, s32[384,128]{1,0:T(8,128)S(1)}) custom-call(s32[1,1]{1,0:T(1,128)S(6)} %copy.8.count, s32[1,1,48]{2,1,0:T(1,128)S(1)} %copy-done.3, s32[1,1,48]{2,1,0:T(1,128)S(1)} %copy-done.4), custom_call_target="tpu_custom_call" | custom-call | tf_op jit(solution)/shard_map/prepare/pallas_call | solution.py:170
  2.1 0.1 collective-permute-done.other
  2.2 0.0 copy-done.1
  2.3 0.0 copy-done
  2.3 0.0 copy-done.2
  2.3 0.6 %project.1 = f32[40,128]{1,0:T(8,128)S(1)} custom-call(bf16[1,1,48,128,128]{4,3,2,1,0:T(8,128)(2,1)S(1)} %copy-done, f32[8,144]{1,0:T(8,128)S(1)} %get-tuple-element.12.add, s32[384,128]{1,0:T(8,128)S(1)} %get-tuple-element.10.row_key, s32[384,128]{1,0:T(8,128)S(1)} %get-tuple-element.11.place_key, f32[8,4,128]{2,1,0:T(4,128)S(1)} %copy-done.1, ...), custom_call_target="tpu_custom_call" | custom-call | tf_op jit(solution)/shard_map/project/pallas_call | solution.py:170
  2.9 4.0 %collective-permute-start.1 = (f32[40,128]{1,0:T(8,128)S(1)}, f32[40,128]{1,0:T(8,128)S(1)}, u32[]{:S(2)}, u32[]{:S(2)}) collective-permute-start(f32[40,128]{1,0:T(8,128)S(1)} %project.1), channel_id=1, source_target_pairs={{0,8},{2,10},{4,12},{6,14},{8,0},{10,2},{12,4},{14,6},{1,9},{3,11}... | collective-permute-start | bytes 61448 | tf_op jit(solution)/shard_map/ppermute | solution.py:19
  6.9 1.8 %collective-permute-done.1 = f32[40,128]{1,0:T(8,128)S(1)} collective-permute-done((f32[40,128]{1,0:T(8,128)S(1)}, f32[40,128]{1,0:T(8,128)S(1)}, u32[]{:S(2)}, u32[]{:S(2)}) %collective-permute-start.1) | collective-permute-done | bytes 20512 | tf_op jit(solution)/shard_map/ppermute | solution.py:19
  8.6 2.8 %collective-permute-start.4 = (f32[40,128]{1,0:T(8,128)S(1)}, f32[40,128]{1,0:T(8,128)S(1)}, u32[]{:S(2)}, u32[]{:S(2)}) collective-permute-start(f32[40,128]{1,0:T(8,128)S(1)} %add.3.a), channel_id=1, source_target_pairs={{0,6},{2,4},{4,2},{6,0},{8,14},{10,12},{12,10},{14,8},{1,7},{3,5},... | collective-permute-start | bytes 61448 | tf_op jit(solution)/shard_map/ppermute | solution.py:19
  11.5 0.5 %collective-permute-start.3 = (f32[40,128]{1,0:T(8,128)S(1)}, f32[40,128]{1,0:T(8,128)S(1)}, u32[]{:S(2)}, u32[]{:S(2)}) collective-permute-start(f32[40,128]{1,0:T(8,128)S(1)} %add.3.a), channel_id=1, source_target_pairs={{0,4},{2,6},{4,0},{6,2},{8,12},{10,14},{12,8},{14,10},{1,5},{3,7},... | collective-permute-start | bytes 61448 | tf_op jit(solution)/shard_map/ppermute | solution.py:19
  11.9 0.2 %collective-permute-start.2 = (f32[40,128]{1,0:T(8,128)S(1)}, f32[40,128]{1,0:T(8,128)S(1)}, u32[]{:S(2)}, u32[]{:S(2)}) collective-permute-start(f32[40,128]{1,0:T(8,128)S(1)} %add.3.a), channel_id=1, source_target_pairs={{0,2},{2,0},{4,6},{6,4},{8,10},{10,8},{12,14},{14,12},{1,3},{3,1},... | collective-permute-start | bytes 61448 | tf_op jit(solution)/shard_map/ppermute | solution.py:19
  12.1 1.3 %collective-permute-done.4.d = f32[40,128]{1,0:T(8,128)S(1)} collective-permute-done((f32[40,128]{1,0:T(8,128)S(1)}, f32[40,128]{1,0:T(8,128)S(1)}, u32[]{:S(2)}, u32[]{:S(2)}) %collective-permute-start.4) | collective-permute-done | bytes 20512 | tf_op jit(solution)/shard_map/ppermute | solution.py:19
  13.4 1.8 %collective-permute-done.3.c = f32[40,128]{1,0:T(8,128)S(1)} collective-permute-done((f32[40,128]{1,0:T(8,128)S(1)}, f32[40,128]{1,0:T(8,128)S(1)}, u32[]{:S(2)}, u32[]{:S(2)}) %collective-permute-start.3) | collective-permute-done | bytes 20512 | tf_op jit(solution)/shard_map/ppermute | solution.py:19
  15.2 0.5 %collective-permute-done.2.b = f32[40,128]{1,0:T(8,128)S(1)} collective-permute-done((f32[40,128]{1,0:T(8,128)S(1)}, f32[40,128]{1,0:T(8,128)S(1)}, u32[]{:S(2)}, u32[]{:S(2)}) %collective-permute-start.2) | collective-permute-done | bytes 20512 | tf_op jit(solution)/shard_map/ppermute | solution.py:19
  15.7 0.5 %backproject.1 = (f32[64,128]{1,0:T(8,128)S(1)}, bf16[64,128]{1,0:T(8,128)(2,1)S(1)}, f32[4,128]{1,0:T(4,128)S(1)}) custom-call(bf16[1,1,48,128,128]{4,3,2,1,0:T(8,128)(2,1)S(1)} %copy-done, f32[48,8]{1,0:T(8,128)S(1)} %get-tuple-element.9.pick, s32[384,128]{1,0:T(8,128)S(1)} %get-tuple-element.10.row_key, s32[384,128]{1,0:T(8,128)S(1)} %get-tuple-element.11.place_key, ...), custom_call_target="tpu_custom_call" | custom-call | tf_op jit(solution)/shard_map/backproject/pallas_call | solution.py:170
  16.2 0.1 collective-permute-start.5
  16.3 1.2 %collective-permute-done.5.there = bf16[64,128]{1,0:T(8,128)(2,1)S(1)} collective-permute-done((bf16[64,128]{1,0:T(8,128)(2,1)S(1)}, bf16[64,128]{1,0:T(8,128)(2,1)S(1)}, u32[]{:S(2)}, u32[]{:S(2)}) %collective-permute-start.5) | collective-permute-done | bytes 16416 | tf_op jit(solution)/shard_map/ppermute | solution.py:19
  17.4 0.6 %update.1 = (f32[8,4,128]{2,1,0:T(4,128)}, bf16[1,1,4,128]{3,2,1,0:T(4,128)(2,1)}) custom-call(f32[8,4,128]{2,1,0:T(4,128)S(1)} %copy-done.1, f32[64,128]{1,0:T(8,128)S(1)} %get-tuple-element.13.own, bf16[64,128]{1,0:T(8,128)(2,1)S(1)} %collective-permute-done.5.there, f32[4,128]{1,0:T(4,128)S(1)} %get-tuple-element.15.residual), custom_call_target="tpu_custom_call" | custom-call | tf_op jit(solution)/shard_map/update/pallas_call | solution.py:170
  (2 shorter events, 0.0 us)
Async XLA Ops:
  0.6 1.6 %copy-start.1 = (f32[8,4,128]{2,1,0:T(4,128)S(1)}, f32[8,4,128]{2,1,0:T(4,128)}, u32[]{:S(2)}) copy-start(f32[8,4,128]{2,1,0:T(4,128)} %volume.3) | copy-start | bytes 49156
  0.6 1.2 %copy-start.4 = (s32[1,1,48]{2,1,0:T(1,128)S(1)}, s32[1,1,48]{2,1,0:T(1,128)}, u32[]{:S(2)}) copy-start(s32[1,1,48]{2,1,0:T(1,128)} %cols.1) | copy-start | bytes 580
  0.7 1.2 %copy-start.3 = (s32[1,1,48]{2,1,0:T(1,128)S(1)}, s32[1,1,48]{2,1,0:T(1,128)}, u32[]{:S(2)}) copy-start(s32[1,1,48]{2,1,0:T(1,128)} %rows.1) | copy-start | bytes 580
  0.7 1.6 %copy-start = (bf16[1,1,48,128,128]{4,3,2,1,0:T(8,128)(2,1)S(1)}, bf16[1,1,48,128,128]{4,3,2,1,0:T(8,128)(2,1)}, u32[]{:S(2)}) copy-start(bf16[1,1,48,128,128]{4,3,2,1,0:T(8,128)(2,1)} %tiles.3) | copy-start | bytes 4718596
  0.7 1.6 %copy-start.2 = (f32[1,1,4,128]{3,2,1,0:T(4,128)S(1)}, f32[1,1,4,128]{3,2,1,0:T(4,128)}, u32[]{:S(2)}) copy-start(f32[1,1,4,128]{3,2,1,0:T(4,128)} %measured.1) | copy-start | bytes 6148
  0.7 1.6 %collective-permute-start = (f32[8,4,128]{2,1,0:T(4,128)}, f32[8,4,128]{2,1,0:T(4,128)S(1)}, u32[]{:S(2)}, u32[]{:S(2)}) collective-permute-start(f32[8,4,128]{2,1,0:T(4,128)} %volume.3), channel_id=1, source_target_pairs={{0,1},{1,0},{2,3},{3,2},{4,5},{5,4},{6,7},{7,6},{8,9},{9,8},{10,11... | collective-permute-start | bytes 49160 | tf_op jit(solution)/shard_map/ppermute | solution.py:19
  2.9 5.8 %collective-permute-start.1 = (f32[40,128]{1,0:T(8,128)S(1)}, f32[40,128]{1,0:T(8,128)S(1)}, u32[]{:S(2)}, u32[]{:S(2)}) collective-permute-start(f32[40,128]{1,0:T(8,128)S(1)} %project.1), channel_id=1, source_target_pairs={{0,8},{2,10},{4,12},{6,14},{8,0},{10,2},{12,4},{14,6},{1,9},{3,11}... | collective-permute-start | bytes 61448 | tf_op jit(solution)/shard_map/ppermute | solution.py:19
  8.6 4.8 %collective-permute-start.4 = (f32[40,128]{1,0:T(8,128)S(1)}, f32[40,128]{1,0:T(8,128)S(1)}, u32[]{:S(2)}, u32[]{:S(2)}) collective-permute-start(f32[40,128]{1,0:T(8,128)S(1)} %add.3.a), channel_id=1, source_target_pairs={{0,6},{2,4},{4,2},{6,0},{8,14},{10,12},{12,10},{14,8},{1,7},{3,5},... | collective-permute-start | bytes 61448 | tf_op jit(solution)/shard_map/ppermute | solution.py:19
  11.5 3.8 %collective-permute-start.3 = (f32[40,128]{1,0:T(8,128)S(1)}, f32[40,128]{1,0:T(8,128)S(1)}, u32[]{:S(2)}, u32[]{:S(2)}) collective-permute-start(f32[40,128]{1,0:T(8,128)S(1)} %add.3.a), channel_id=1, source_target_pairs={{0,4},{2,6},{4,0},{6,2},{8,12},{10,14},{12,8},{14,10},{1,5},{3,7},... | collective-permute-start | bytes 61448 | tf_op jit(solution)/shard_map/ppermute | solution.py:19
  11.9 3.8 %collective-permute-start.2 = (f32[40,128]{1,0:T(8,128)S(1)}, f32[40,128]{1,0:T(8,128)S(1)}, u32[]{:S(2)}, u32[]{:S(2)}) collective-permute-start(f32[40,128]{1,0:T(8,128)S(1)} %add.3.a), channel_id=1, source_target_pairs={{0,2},{2,0},{4,6},{6,4},{8,10},{10,8},{12,14},{14,12},{1,3},{3,1},... | collective-permute-start | bytes 61448 | tf_op jit(solution)/shard_map/ppermute | solution.py:19
  16.2 1.2 %collective-permute-start.5 = (bf16[64,128]{1,0:T(8,128)(2,1)S(1)}, bf16[64,128]{1,0:T(8,128)(2,1)S(1)}, u32[]{:S(2)}, u32[]{:S(2)}) collective-permute-start(bf16[64,128]{1,0:T(8,128)(2,1)S(1)} %get-tuple-element.14), channel_id=1, source_target_pairs={{0,1},{1,0},{2,3},{3,2},{4,5},{5,4},{6,7},{7,6},{8,9},{9,8},{10,11... | collective-permute-start | bytes 49160 | tf_op jit(solution)/shard_map/ppermute | solution.py:19

commit v29 on v28

--- a/solution.py
+++ b/solution.py
@@ -71,10 +71,12 @@
     slots, _, width = tiles.shape[2:]
     for n in range(0, slots, 2):
         pair = [tiles[0, 0, k] for k in (n, n + 1)]
-        if transposed:
-            pair = [tile.T for tile in pair]
         left = jnp.concatenate([rows_of(n), rows_of(n + 1)], axis=0).astype(jnp.bfloat16)
-        both = jnp.dot(left, jnp.concatenate(pair, axis=1), preferred_element_type=jnp.float32)
+        if transposed and n % 4:
+            right, contract = jnp.concatenate(pair, axis=0), 1
+        else:
+            right, contract = jnp.concatenate([tile.T if transposed else tile for tile in pair], axis=1), 0
+        both = lax.dot_general(left, right, (((1,), (contract,)), ((), ())), preferred_element_type=jnp.float32)
         yield n, both[:SUB, :width]
         yield n + 1, both[SUB:, width:]
 

time: 18.2 us -> 18.2 us (level)
  no operation moved by 1% of the time
where the time goes in v29:
time: 18.2 us; the launch traced here: 18 us
  starting transfers between devices  8.08 us (44%)
  waiting for transfers between devices  6.65 us (37%)
  Pallas kernels  1.89 us (10%)
  between operations  1.38 us (8%)
    ppermute x6, starting transfers between devices, exchange(): return lax.ppermute(value, axis, [(i, i ^ mask) for i in range(size)])  8.08 us
    ppermute x6, waiting for transfers between devices, exchange(): return lax.ppermute(value, axis, [(i, i ^ mask) for i in range(size)])  6.65 us
    pallas_call x5, Pallas kernels, call(): pl.pallas_call(kernel, out_shape=[jax.ShapeDtypeStruct(shape, dtype) for...  1.89 us
  transfers between devices with their start and end apart: 6, of which 6 were waited for; matrix products, arithmetic and copies ran while one was open for 0% of the time, Pallas kernels for 1%

profile of v29, /device:TPU:0, one launch (start us, length us, event | category | flops | bytes accessed | tf_op | source)
XLA Modules:
  0.0 18.0 jit_solution(16751525701662950274)
XLA Ops:
  0.6 0.0 copy-start.1
  0.6 0.0 copy-start.4
  0.7 0.0 copy-start.3
  0.7 0.0 copy-start
  0.7 0.0 copy-start.2
  0.7 0.5 %collective-permute-start = (f32[8,4,128]{2,1,0:T(4,128)}, f32[8,4,128]{2,1,0:T(4,128)S(1)}, u32[]{:S(2)}, u32[]{:S(2)}) collective-permute-start(f32[8,4,128]{2,1,0:T(4,128)} %volume.3), channel_id=1, source_target_pairs={{0,1},{1,0},{2,3},{3,2},{4,5},{5,4},{6,7},{7,6},{8,9},{9,8},{10,11... | collective-permute-start | bytes 49160 | tf_op jit(solution)/shard_map/ppermute | solution.py:19
  1.9 0.0 copy-done.4
  1.9 0.0 copy-done.3
  1.9 0.2 %prepare.1 = (f32[48,8]{1,0:T(8,128)S(1)}, f32[8,144]{1,0:T(8,128)S(1)}, s32[384,128]{1,0:T(8,128)S(1)}, s32[384,128]{1,0:T(8,128)S(1)}) custom-call(s32[1,1]{1,0:T(1,128)S(6)} %copy.8.count, s32[1,1,48]{2,1,0:T(1,128)S(1)} %copy-done.3, s32[1,1,48]{2,1,0:T(1,128)S(1)} %copy-done.4), custom_call_target="tpu_custom_call" | custom-call | tf_op jit(solution)/shard_map/prepare/pallas_call | solution.py:172
  2.1 0.1 collective-permute-done.other
  2.2 0.0 copy-done.1
  2.3 0.0 copy-done
  2.3 0.0 copy-done.2
  2.3 0.5 %project.1 = f32[40,128]{1,0:T(8,128)S(1)} custom-call(bf16[1,1,48,128,128]{4,3,2,1,0:T(8,128)(2,1)S(1)} %copy-done, f32[8,144]{1,0:T(8,128)S(1)} %get-tuple-element.12.add, s32[384,128]{1,0:T(8,128)S(1)} %get-tuple-element.10.row_key, s32[384,128]{1,0:T(8,128)S(1)} %get-tuple-element.11.place_key, f32[8,4,128]{2,1,0:T(4,128)S(1)} %copy-done.1, ...), custom_call_target="tpu_custom_call" | custom-call | tf_op jit(solution)/shard_map/project/pallas_call | solution.py:172
  2.8 4.0 %collective-permute-start.1 = (f32[40,128]{1,0:T(8,128)S(1)}, f32[40,128]{1,0:T(8,128)S(1)}, u32[]{:S(2)}, u32[]{:S(2)}) collective-permute-start(f32[40,128]{1,0:T(8,128)S(1)} %project.1), channel_id=1, source_target_pairs={{0,8},{2,10},{4,12},{6,14},{8,0},{10,2},{12,4},{14,6},{1,9},{3,11}... | collective-permute-start | bytes 61448 | tf_op jit(solution)/shard_map/ppermute | solution.py:19
  6.8 1.8 %collective-permute-done.1 = f32[40,128]{1,0:T(8,128)S(1)} collective-permute-done((f32[40,128]{1,0:T(8,128)S(1)}, f32[40,128]{1,0:T(8,128)S(1)}, u32[]{:S(2)}, u32[]{:S(2)}) %collective-permute-start.1) | collective-permute-done | bytes 20512 | tf_op jit(solution)/shard_map/ppermute | solution.py:19
  8.6 2.8 %collective-permute-start.4 = (f32[40,128]{1,0:T(8,128)S(1)}, f32[40,128]{1,0:T(8,128)S(1)}, u32[]{:S(2)}, u32[]{:S(2)}) collective-permute-start(f32[40,128]{1,0:T(8,128)S(1)} %add.3.a), channel_id=1, source_target_pairs={{0,6},{2,4},{4,2},{6,0},{8,14},{10,12},{12,10},{14,8},{1,7},{3,5},... | collective-permute-start | bytes 61448 | tf_op jit(solution)/shard_map/ppermute | solution.py:19
  11.4 0.5 %collective-permute-start.3 = (f32[40,128]{1,0:T(8,128)S(1)}, f32[40,128]{1,0:T(8,128)S(1)}, u32[]{:S(2)}, u32[]{:S(2)}) collective-permute-start(f32[40,128]{1,0:T(8,128)S(1)} %add.3.a), channel_id=1, source_target_pairs={{0,4},{2,6},{4,0},{6,2},{8,12},{10,14},{12,8},{14,10},{1,5},{3,7},... | collective-permute-start | bytes 61448 | tf_op jit(solution)/shard_map/ppermute | solution.py:19
  11.9 0.2 %collective-permute-start.2 = (f32[40,128]{1,0:T(8,128)S(1)}, f32[40,128]{1,0:T(8,128)S(1)}, u32[]{:S(2)}, u32[]{:S(2)}) collective-permute-start(f32[40,128]{1,0:T(8,128)S(1)} %add.3.a), channel_id=1, source_target_pairs={{0,2},{2,0},{4,6},{6,4},{8,10},{10,8},{12,14},{14,12},{1,3},{3,1},... | collective-permute-start | bytes 61448 | tf_op jit(solution)/shard_map/ppermute | solution.py:19
  12.1 1.3 %collective-permute-done.4.d = f32[40,128]{1,0:T(8,128)S(1)} collective-permute-done((f32[40,128]{1,0:T(8,128)S(1)}, f32[40,128]{1,0:T(8,128)S(1)}, u32[]{:S(2)}, u32[]{:S(2)}) %collective-permute-start.4) | collective-permute-done | bytes 20512 | tf_op jit(solution)/shard_map/ppermute | solution.py:19
  13.3 1.8 %collective-permute-done.3.c = f32[40,128]{1,0:T(8,128)S(1)} collective-permute-done((f32[40,128]{1,0:T(8,128)S(1)}, f32[40,128]{1,0:T(8,128)S(1)}, u32[]{:S(2)}, u32[]{:S(2)}) %collective-permute-start.3) | collective-permute-done | bytes 20512 | tf_op jit(solution)/shard_map/ppermute | solution.py:19
  15.2 0.5 %collective-permute-done.2.b = f32[40,128]{1,0:T(8,128)S(1)} collective-permute-done((f32[40,128]{1,0:T(8,128)S(1)}, f32[40,128]{1,0:T(8,128)S(1)}, u32[]{:S(2)}, u32[]{:S(2)}) %collective-permute-start.2) | collective-permute-done | bytes 20512 | tf_op jit(solution)/shard_map/ppermute | solution.py:19
  15.6 0.5 %backproject.1 = (f32[64,128]{1,0:T(8,128)S(1)}, bf16[64,128]{1,0:T(8,128)(2,1)S(1)}, f32[4,128]{1,0:T(4,128)S(1)}) custom-call(bf16[1,1,48,128,128]{4,3,2,1,0:T(8,128)(2,1)S(1)} %copy-done, f32[48,8]{1,0:T(8,128)S(1)} %get-tuple-element.9.pick, s32[384,128]{1,0:T(8,128)S(1)} %get-tuple-element.10.row_key, s32[384,128]{1,0:T(8,128)S(1)} %get-tuple-element.11.place_key, ...), custom_call_target="tpu_custom_call" | custom-call | tf_op jit(solution)/shard_map/backproject/pallas_call | solution.py:172
  16.1 0.1 collective-permute-start.5
  16.2 1.2 %collective-permute-done.5.there = bf16[64,128]{1,0:T(8,128)(2,1)S(1)} collective-permute-done((bf16[64,128]{1,0:T(8,128)(2,1)S(1)}, bf16[64,128]{1,0:T(8,128)(2,1)S(1)}, u32[]{:S(2)}, u32[]{:S(2)}) %collective-permute-start.5) | collective-permute-done | bytes 16416 | tf_op jit(solution)/shard_map/ppermute | solution.py:19
  17.4 0.6 %update.1 = (f32[8,4,128]{2,1,0:T(4,128)}, bf16[1,1,4,128]{3,2,1,0:T(4,128)(2,1)}) custom-call(f32[8,4,128]{2,1,0:T(4,128)S(1)} %copy-done.1, f32[64,128]{1,0:T(8,128)S(1)} %get-tuple-element.13.own, bf16[64,128]{1,0:T(8,128)(2,1)S(1)} %collective-permute-done.5.there, f32[4,128]{1,0:T(4,128)S(1)} %get-tuple-element.15.residual), custom_call_target="tpu_custom_call" | custom-call | tf_op jit(solution)/shard_map/update/pallas_call | solution.py:172
  (2 shorter events, 0.0 us)
Async XLA Ops:
  0.6 1.6 %copy-start.1 = (f32[8,4,128]{2,1,0:T(4,128)S(1)}, f32[8,4,128]{2,1,0:T(4,128)}, u32[]{:S(2)}) copy-start(f32[8,4,128]{2,1,0:T(4,128)} %volume.3) | copy-start | bytes 49156
  0.6 1.2 %copy-start.4 = (s32[1,1,48]{2,1,0:T(1,128)S(1)}, s32[1,1,48]{2,1,0:T(1,128)}, u32[]{:S(2)}) copy-start(s32[1,1,48]{2,1,0:T(1,128)} %cols.1) | copy-start | bytes 580
  0.7 1.2 %copy-start.3 = (s32[1,1,48]{2,1,0:T(1,128)S(1)}, s32[1,1,48]{2,1,0:T(1,128)}, u32[]{:S(2)}) copy-start(s32[1,1,48]{2,1,0:T(1,128)} %rows.1) | copy-start | bytes 580
  0.7 1.6 %copy-start = (bf16[1,1,48,128,128]{4,3,2,1,0:T(8,128)(2,1)S(1)}, bf16[1,1,48,128,128]{4,3,2,1,0:T(8,128)(2,1)}, u32[]{:S(2)}) copy-start(bf16[1,1,48,128,128]{4,3,2,1,0:T(8,128)(2,1)} %tiles.3) | copy-start | bytes 4718596
  0.7 1.6 %copy-start.2 = (f32[1,1,4,128]{3,2,1,0:T(4,128)S(1)}, f32[1,1,4,128]{3,2,1,0:T(4,128)}, u32[]{:S(2)}) copy-start(f32[1,1,4,128]{3,2,1,0:T(4,128)} %measured.1) | copy-start | bytes 6148
  0.7 1.6 %collective-permute-start = (f32[8,4,128]{2,1,0:T(4,128)}, f32[8,4,128]{2,1,0:T(4,128)S(1)}, u32[]{:S(2)}, u32[]{:S(2)}) collective-permute-start(f32[8,4,128]{2,1,0:T(4,128)} %volume.3), channel_id=1, source_target_pairs={{0,1},{1,0},{2,3},{3,2},{4,5},{5,4},{6,7},{7,6},{8,9},{9,8},{10,11... | collective-permute-start | bytes 49160 | tf_op jit(solution)/shard_map/ppermute | solution.py:19
  2.8 5.8 %collective-permute-start.1 = (f32[40,128]{1,0:T(8,128)S(1)}, f32[40,128]{1,0:T(8,128)S(1)}, u32[]{:S(2)}, u32[]{:S(2)}) collective-permute-start(f32[40,128]{1,0:T(8,128)S(1)} %project.1), channel_id=1, source_target_pairs={{0,8},{2,10},{4,12},{6,14},{8,0},{10,2},{12,4},{14,6},{1,9},{3,11}... | collective-permute-start | bytes 61448 | tf_op jit(solution)/shard_map/ppermute | solution.py:19
  8.6 4.8 %collective-permute-start.4 = (f32[40,128]{1,0:T(8,128)S(1)}, f32[40,128]{1,0:T(8,128)S(1)}, u32[]{:S(2)}, u32[]{:S(2)}) collective-permute-start(f32[40,128]{1,0:T(8,128)S(1)} %add.3.a), channel_id=1, source_target_pairs={{0,6},{2,4},{4,2},{6,0},{8,14},{10,12},{12,10},{14,8},{1,7},{3,5},... | collective-permute-start | bytes 61448 | tf_op jit(solution)/shard_map/ppermute | solution.py:19
  11.4 3.8 %collective-permute-start.3 = (f32[40,128]{1,0:T(8,128)S(1)}, f32[40,128]{1,0:T(8,128)S(1)}, u32[]{:S(2)}, u32[]{:S(2)}) collective-permute-start(f32[40,128]{1,0:T(8,128)S(1)} %add.3.a), channel_id=1, source_target_pairs={{0,4},{2,6},{4,0},{6,2},{8,12},{10,14},{12,8},{14,10},{1,5},{3,7},... | collective-permute-start | bytes 61448 | tf_op jit(solution)/shard_map/ppermute | solution.py:19
  11.9 3.8 %collective-permute-start.2 = (f32[40,128]{1,0:T(8,128)S(1)}, f32[40,128]{1,0:T(8,128)S(1)}, u32[]{:S(2)}, u32[]{:S(2)}) collective-permute-start(f32[40,128]{1,0:T(8,128)S(1)} %add.3.a), channel_id=1, source_target_pairs={{0,2},{2,0},{4,6},{6,4},{8,10},{10,8},{12,14},{14,12},{1,3},{3,1},... | collective-permute-start | bytes 61448 | tf_op jit(solution)/shard_map/ppermute | solution.py:19
  16.1 1.2 %collective-permute-start.5 = (bf16[64,128]{1,0:T(8,128)(2,1)S(1)}, bf16[64,128]{1,0:T(8,128)(2,1)S(1)}, u32[]{:S(2)}, u32[]{:S(2)}) collective-permute-start(bf16[64,128]{1,0:T(8,128)(2,1)S(1)} %get-tuple-element.14), channel_id=1, source_target_pairs={{0,1},{1,0},{2,3},{3,2},{4,5},{5,4},{6,7},{7,6},{8,9},{9,8},{10,11... | collective-permute-start | bytes 49160 | tf_op jit(solution)/shard_map/ppermute | solution.py:19

commit v30 on v29

--- a/solution.py
+++ b/solution.py
@@ -72,7 +72,7 @@
     for n in range(0, slots, 2):
         pair = [tiles[0, 0, k] for k in (n, n + 1)]
         left = jnp.concatenate([rows_of(n), rows_of(n + 1)], axis=0).astype(jnp.bfloat16)
-        if transposed and n % 4:
+        if transposed and n % 6:
             right, contract = jnp.concatenate(pair, axis=0), 1
         else:
             right, contract = jnp.concatenate([tile.T if transposed else tile for tile in pair], axis=1), 0

time: 18.2 us -> 18.2 us (level)
  no operation moved by 1% of the time
where the time goes in v30:
time: 18.2 us; the launch traced here: 18 us
  starting transfers between devices  8.08 us (44%)
  waiting for transfers between devices  6.65 us (37%)
  Pallas kernels  1.9 us (10%)
  between operations  1.37 us (8%)
    ppermute x6, starting transfers between devices, exchange(): return lax.ppermute(value, axis, [(i, i ^ mask) for i in range(size)])  8.08 us
    ppermute x6, waiting for transfers between devices, exchange(): return lax.ppermute(value, axis, [(i, i ^ mask) for i in range(size)])  6.65 us
    pallas_call x5, Pallas kernels, call(): pl.pallas_call(kernel, out_shape=[jax.ShapeDtypeStruct(shape, dtype) for...  1.9 us
  transfers between devices with their start and end apart: 6, of which 6 were waited for; matrix products, arithmetic and copies ran while one was open for 0% of the time, Pallas kernels for 1%

profile of v30, /device:TPU:0, one launch (start us, length us, event | category | flops | bytes accessed | tf_op | source)
XLA Modules:
  0.0 18.0 jit_solution(366383853651822710)
XLA Ops:
  0.6 0.0 copy-start.1
  0.6 0.0 copy-start.4
  0.7 0.0 copy-start.3
  0.7 0.0 copy-start
  0.7 0.0 copy-start.2
  0.7 0.5 %collective-permute-start = (f32[8,4,128]{2,1,0:T(4,128)}, f32[8,4,128]{2,1,0:T(4,128)S(1)}, u32[]{:S(2)}, u32[]{:S(2)}) collective-permute-start(f32[8,4,128]{2,1,0:T(4,128)} %volume.3), channel_id=1, source_target_pairs={{0,1},{1,0},{2,3},{3,2},{4,5},{5,4},{6,7},{7,6},{8,9},{9,8},{10,11... | collective-permute-start | bytes 49160 | tf_op jit(solution)/shard_map/ppermute | solution.py:19
  1.9 0.0 copy-done.4
  1.9 0.0 copy-done.3
  1.9 0.2 %prepare.1 = (f32[48,8]{1,0:T(8,128)S(1)}, f32[8,144]{1,0:T(8,128)S(1)}, s32[384,128]{1,0:T(8,128)S(1)}, s32[384,128]{1,0:T(8,128)S(1)}) custom-call(s32[1,1]{1,0:T(1,128)S(6)} %copy.8.count, s32[1,1,48]{2,1,0:T(1,128)S(1)} %copy-done.3, s32[1,1,48]{2,1,0:T(1,128)S(1)} %copy-done.4), custom_call_target="tpu_custom_call" | custom-call | tf_op jit(solution)/shard_map/prepare/pallas_call | solution.py:172
  2.1 0.1 collective-permute-done.other
  2.2 0.0 copy-done.1
  2.3 0.0 copy-done
  2.3 0.0 copy-done.2
  2.3 0.5 %project.1 = f32[40,128]{1,0:T(8,128)S(1)} custom-call(bf16[1,1,48,128,128]{4,3,2,1,0:T(8,128)(2,1)S(1)} %copy-done, f32[8,144]{1,0:T(8,128)S(1)} %get-tuple-element.12.add, s32[384,128]{1,0:T(8,128)S(1)} %get-tuple-element.10.row_key, s32[384,128]{1,0:T(8,128)S(1)} %get-tuple-element.11.place_key, f32[8,4,128]{2,1,0:T(4,128)S(1)} %copy-done.1, ...), custom_call_target="tpu_custom_call" | custom-call | tf_op jit(solution)/shard_map/project/pallas_call | solution.py:172
  2.8 4.0 %collective-permute-start.1 = (f32[40,128]{1,0:T(8,128)S(1)}, f32[40,128]{1,0:T(8,128)S(1)}, u32[]{:S(2)}, u32[]{:S(2)}) collective-permute-start(f32[40,128]{1,0:T(8,128)S(1)} %project.1), channel_id=1, source_target_pairs={{0,8},{2,10},{4,12},{6,14},{8,0},{10,2},{12,4},{14,6},{1,9},{3,11}... | collective-permute-start | bytes 61448 | tf_op jit(solution)/shard_map/ppermute | solution.py:19
  6.8 1.8 %collective-permute-done.1 = f32[40,128]{1,0:T(8,128)S(1)} collective-permute-done((f32[40,128]{1,0:T(8,128)S(1)}, f32[40,128]{1,0:T(8,128)S(1)}, u32[]{:S(2)}, u32[]{:S(2)}) %collective-permute-start.1) | collective-permute-done | bytes 20512 | tf_op jit(solution)/shard_map/ppermute | solution.py:19
  8.6 2.8 %collective-permute-start.4 = (f32[40,128]{1,0:T(8,128)S(1)}, f32[40,128]{1,0:T(8,128)S(1)}, u32[]{:S(2)}, u32[]{:S(2)}) collective-permute-start(f32[40,128]{1,0:T(8,128)S(1)} %add.3.a), channel_id=1, source_target_pairs={{0,6},{2,4},{4,2},{6,0},{8,14},{10,12},{12,10},{14,8},{1,7},{3,5},... | collective-permute-start | bytes 61448 | tf_op jit(solution)/shard_map/ppermute | solution.py:19
  11.4 0.5 %collective-permute-start.3 = (f32[40,128]{1,0:T(8,128)S(1)}, f32[40,128]{1,0:T(8,128)S(1)}, u32[]{:S(2)}, u32[]{:S(2)}) collective-permute-start(f32[40,128]{1,0:T(8,128)S(1)} %add.3.a), channel_id=1, source_target_pairs={{0,4},{2,6},{4,0},{6,2},{8,12},{10,14},{12,8},{14,10},{1,5},{3,7},... | collective-permute-start | bytes 61448 | tf_op jit(solution)/shard_map/ppermute | solution.py:19
  11.9 0.2 %collective-permute-start.2 = (f32[40,128]{1,0:T(8,128)S(1)}, f32[40,128]{1,0:T(8,128)S(1)}, u32[]{:S(2)}, u32[]{:S(2)}) collective-permute-start(f32[40,128]{1,0:T(8,128)S(1)} %add.3.a), channel_id=1, source_target_pairs={{0,2},{2,0},{4,6},{6,4},{8,10},{10,8},{12,14},{14,12},{1,3},{3,1},... | collective-permute-start | bytes 61448 | tf_op jit(solution)/shard_map/ppermute | solution.py:19
  12.1 1.3 %collective-permute-done.4.d = f32[40,128]{1,0:T(8,128)S(1)} collective-permute-done((f32[40,128]{1,0:T(8,128)S(1)}, f32[40,128]{1,0:T(8,128)S(1)}, u32[]{:S(2)}, u32[]{:S(2)}) %collective-permute-start.4) | collective-permute-done | bytes 20512 | tf_op jit(solution)/shard_map/ppermute | solution.py:19
  13.3 1.8 %collective-permute-done.3.c = f32[40,128]{1,0:T(8,128)S(1)} collective-permute-done((f32[40,128]{1,0:T(8,128)S(1)}, f32[40,128]{1,0:T(8,128)S(1)}, u32[]{:S(2)}, u32[]{:S(2)}) %collective-permute-start.3) | collective-permute-done | bytes 20512 | tf_op jit(solution)/shard_map/ppermute | solution.py:19
  15.2 0.5 %collective-permute-done.2.b = f32[40,128]{1,0:T(8,128)S(1)} collective-permute-done((f32[40,128]{1,0:T(8,128)S(1)}, f32[40,128]{1,0:T(8,128)S(1)}, u32[]{:S(2)}, u32[]{:S(2)}) %collective-permute-start.2) | collective-permute-done | bytes 20512 | tf_op jit(solution)/shard_map/ppermute | solution.py:19
  15.6 0.5 %backproject.1 = (f32[64,128]{1,0:T(8,128)S(1)}, bf16[64,128]{1,0:T(8,128)(2,1)S(1)}, f32[4,128]{1,0:T(4,128)S(1)}) custom-call(bf16[1,1,48,128,128]{4,3,2,1,0:T(8,128)(2,1)S(1)} %copy-done, f32[48,8]{1,0:T(8,128)S(1)} %get-tuple-element.9.pick, s32[384,128]{1,0:T(8,128)S(1)} %get-tuple-element.10.row_key, s32[384,128]{1,0:T(8,128)S(1)} %get-tuple-element.11.place_key, ...), custom_call_target="tpu_custom_call" | custom-call | tf_op jit(solution)/shard_map/backproject/pallas_call | solution.py:172
  16.1 0.1 collective-permute-start.5
  16.2 1.2 %collective-permute-done.5.there = bf16[64,128]{1,0:T(8,128)(2,1)S(1)} collective-permute-done((bf16[64,128]{1,0:T(8,128)(2,1)S(1)}, bf16[64,128]{1,0:T(8,128)(2,1)S(1)}, u32[]{:S(2)}, u32[]{:S(2)}) %collective-permute-start.5) | collective-permute-done | bytes 16416 | tf_op jit(solution)/shard_map/ppermute | solution.py:19
  17.4 0.6 %update.1 = (f32[8,4,128]{2,1,0:T(4,128)}, bf16[1,1,4,128]{3,2,1,0:T(4,128)(2,1)}) custom-call(f32[8,4,128]{2,1,0:T(4,128)S(1)} %copy-done.1, f32[64,128]{1,0:T(8,128)S(1)} %get-tuple-element.13.own, bf16[64,128]{1,0:T(8,128)(2,1)S(1)} %collective-permute-done.5.there, f32[4,128]{1,0:T(4,128)S(1)} %get-tuple-element.15.residual), custom_call_target="tpu_custom_call" | custom-call | tf_op jit(solution)/shard_map/update/pallas_call | solution.py:172
  (2 shorter events, 0.0 us)
Async XLA Ops:
  0.6 1.6 %copy-start.1 = (f32[8,4,128]{2,1,0:T(4,128)S(1)}, f32[8,4,128]{2,1,0:T(4,128)}, u32[]{:S(2)}) copy-start(f32[8,4,128]{2,1,0:T(4,128)} %volume.3) | copy-start | bytes 49156
  0.6 1.2 %copy-start.4 = (s32[1,1,48]{2,1,0:T(1,128)S(1)}, s32[1,1,48]{2,1,0:T(1,128)}, u32[]{:S(2)}) copy-start(s32[1,1,48]{2,1,0:T(1,128)} %cols.1) | copy-start | bytes 580
  0.7 1.2 %copy-start.3 = (s32[1,1,48]{2,1,0:T(1,128)S(1)}, s32[1,1,48]{2,1,0:T(1,128)}, u32[]{:S(2)}) copy-start(s32[1,1,48]{2,1,0:T(1,128)} %rows.1) | copy-start | bytes 580
  0.7 1.6 %copy-start = (bf16[1,1,48,128,128]{4,3,2,1,0:T(8,128)(2,1)S(1)}, bf16[1,1,48,128,128]{4,3,2,1,0:T(8,128)(2,1)}, u32[]{:S(2)}) copy-start(bf16[1,1,48,128,128]{4,3,2,1,0:T(8,128)(2,1)} %tiles.3) | copy-start | bytes 4718596
  0.7 1.6 %copy-start.2 = (f32[1,1,4,128]{3,2,1,0:T(4,128)S(1)}, f32[1,1,4,128]{3,2,1,0:T(4,128)}, u32[]{:S(2)}) copy-start(f32[1,1,4,128]{3,2,1,0:T(4,128)} %measured.1) | copy-start | bytes 6148
  0.7 1.6 %collective-permute-start = (f32[8,4,128]{2,1,0:T(4,128)}, f32[8,4,128]{2,1,0:T(4,128)S(1)}, u32[]{:S(2)}, u32[]{:S(2)}) collective-permute-start(f32[8,4,128]{2,1,0:T(4,128)} %volume.3), channel_id=1, source_target_pairs={{0,1},{1,0},{2,3},{3,2},{4,5},{5,4},{6,7},{7,6},{8,9},{9,8},{10,11... | collective-permute-start | bytes 49160 | tf_op jit(solution)/shard_map/ppermute | solution.py:19
  2.8 5.8 %collective-permute-start.1 = (f32[40,128]{1,0:T(8,128)S(1)}, f32[40,128]{1,0:T(8,128)S(1)}, u32[]{:S(2)}, u32[]{:S(2)}) collective-permute-start(f32[40,128]{1,0:T(8,128)S(1)} %project.1), channel_id=1, source_target_pairs={{0,8},{2,10},{4,12},{6,14},{8,0},{10,2},{12,4},{14,6},{1,9},{3,11}... | collective-permute-start | bytes 61448 | tf_op jit(solution)/shard_map/ppermute | solution.py:19
  8.6 4.8 %collective-permute-start.4 = (f32[40,128]{1,0:T(8,128)S(1)}, f32[40,128]{1,0:T(8,128)S(1)}, u32[]{:S(2)}, u32[]{:S(2)}) collective-permute-start(f32[40,128]{1,0:T(8,128)S(1)} %add.3.a), channel_id=1, source_target_pairs={{0,6},{2,4},{4,2},{6,0},{8,14},{10,12},{12,10},{14,8},{1,7},{3,5},... | collective-permute-start | bytes 61448 | tf_op jit(solution)/shard_map/ppermute | solution.py:19
  11.4 3.8 %collective-permute-start.3 = (f32[40,128]{1,0:T(8,128)S(1)}, f32[40,128]{1,0:T(8,128)S(1)}, u32[]{:S(2)}, u32[]{:S(2)}) collective-permute-start(f32[40,128]{1,0:T(8,128)S(1)} %add.3.a), channel_id=1, source_target_pairs={{0,4},{2,6},{4,0},{6,2},{8,12},{10,14},{12,8},{14,10},{1,5},{3,7},... | collective-permute-start | bytes 61448 | tf_op jit(solution)/shard_map/ppermute | solution.py:19
  11.9 3.8 %collective-permute-start.2 = (f32[40,128]{1,0:T(8,128)S(1)}, f32[40,128]{1,0:T(8,128)S(1)}, u32[]{:S(2)}, u32[]{:S(2)}) collective-permute-start(f32[40,128]{1,0:T(8,128)S(1)} %add.3.a), channel_id=1, source_target_pairs={{0,2},{2,0},{4,6},{6,4},{8,10},{10,8},{12,14},{14,12},{1,3},{3,1},... | collective-permute-start | bytes 61448 | tf_op jit(solution)/shard_map/ppermute | solution.py:19
  16.1 1.2 %collective-permute-start.5 = (bf16[64,128]{1,0:T(8,128)(2,1)S(1)}, bf16[64,128]{1,0:T(8,128)(2,1)S(1)}, u32[]{:S(2)}, u32[]{:S(2)}) collective-permute-start(bf16[64,128]{1,0:T(8,128)(2,1)S(1)} %get-tuple-element.14), channel_id=1, source_target_pairs={{0,1},{1,0},{2,3},{3,2},{4,5},{5,4},{6,7},{7,6},{8,9},{9,8},{10,11... | collective-permute-start | bytes 49160 | tf_op jit(solution)/shard_map/ppermute | solution.py:19

commit v31 on v29

--- a/solution.py
+++ b/solution.py
@@ -19,7 +19,7 @@
     return lax.ppermute(value, axis, [(i, i ^ mask) for i in range(size)])
 
 
-def all_sum(value, axis):
+def all_sum(value, axis, add):
     bits = (lax.axis_size(axis) - 1).bit_length()
     if bits % 2:
         bits -= 1
@@ -30,25 +30,32 @@
         across = exchange(value, axis, stride)
         both = exchange(value, axis, 3 * stride)
         along = exchange(value, axis, 2 * stride)
-        terms = (value, across, along, both)
-        value = (value + across) + (along + both)
+        terms = (value, across, add(along, both))
+        value = (value + across) + terms[2]
     return terms
+
+
+def add_kernel(left, right, out):
+    out[...] = left[...] + right[...]
 
 
 def filler_kernel(inst, filler):
     filler[...] = (lax.broadcasted_iota(jnp.int32, filler.shape, 0) == inst).astype(jnp.float32)
 
 
-def prepare_kernel(half, count, rows, cols, pick, add, row_key, place_key):
+def prepare_kernel(half, count, rows, cols, pick, add, row_key, place_key, row_pair, place_pair):
     blocks = add.shape[0]
     used = lax.broadcasted_iota(jnp.int32, rows.shape[1:], 1) < count[0, 0]
     place = cols[0] + lax.axis_index("ray") * half
     place = jnp.where(place < 2 * half, place, place - 2 * half)
     place = jnp.where(used, place, -1)
     row = jnp.where(used, rows[0], -1)
-    for key, out in ((row, row_key), (place, place_key)):
-        for n in range(key.shape[1]):
-            out[n * SUB : (n + 1) * SUB, :] = jnp.broadcast_to(key[:, n : n + 1], (SUB, out.shape[1]))
+    for key, out, out_pair in ((row, row_key, row_pair), (place, place_key, place_pair)):
+        for n in range(0, key.shape[1], 2):
+            splats = [jnp.broadcast_to(key[:, k : k + 1], (SUB, out.shape[1])) for k in (n, n + 1)]
+            both = jnp.concatenate(splats, axis=0)
+            out[n * SUB : (n + 2) * SUB, :] = both
+            out_pair[n * SUB : (n + 2) * SUB, :] = both.astype(jnp.int16)
     hit = (lax.broadcasted_iota(jnp.int32, (blocks, row.shape[1]), 0) == row).astype(jnp.float32)
     add[...] = jnp.concatenate([hit] * PARTS, axis=1)
     pick[...] = hit.T
@@ -56,6 +63,14 @@
 
 def of_slot(ref, n):
     return ref[n * SUB : (n + 1) * SUB, :]
+
+
+def of_pair(ref, n):
+    return ref[n * SUB : (n + 2) * SUB, :]
+
+
+def twice(block):
+    return jnp.concatenate([block, block], axis=0).astype(jnp.bfloat16)
 
 
 def take(key, blocks):
@@ -67,11 +82,11 @@
     return blocks[0]
 
 
-def products(tiles, transposed, rows_of):
+def products(tiles, transposed, rows_of_pair):
     slots, _, width = tiles.shape[2:]
     for n in range(0, slots, 2):
         pair = [tiles[0, 0, k] for k in (n, n + 1)]
-        left = jnp.concatenate([rows_of(n), rows_of(n + 1)], axis=0).astype(jnp.bfloat16)
+        left = rows_of_pair(n)
         if transposed and n % 4:
             right, contract = jnp.concatenate(pair, axis=0), 1
         else:
@@ -89,13 +104,13 @@
     return sums
 
 
-def project_kernel(tiles, add, row_key, place_key, volume, other, measured, filler, part, store):
+def project_kernel(tiles, add, row_key, place_pair, volume, other, measured, filler, part, store):
     half, inst, width = volume.shape
     slots = tiles.shape[2]
     blocks = add.shape[0]
     rest = filler[inst:, :]
-    table = [jnp.concatenate([ref[b], rest], axis=0) for ref in (volume, other) for b in range(half)]
-    prods = products(tiles, True, lambda n: take(of_slot(place_key, n), table))
+    table = [twice(jnp.concatenate([ref[b], rest], axis=0)) for ref in (volume, other) for b in range(half)]
+    prods = products(tiles, True, lambda n: take(of_pair(place_pair, n), table))
     if blocks <= FEW:
         for b, total in enumerate(sums_by_key(prods, row_key, blocks)):
             store[pl.ds(b, SUB, stride=blocks), :] = total
@@ -119,11 +134,11 @@
     part[inst * blocks : (inst + 1) * blocks, :] = sums[inst]
 
 
-def backproject_kernel(tiles, pick, row_key, place_key, a, b, c, d, own, send, residual, store):
+def backproject_kernel(tiles, pick, row_pair, place_key, a, b, c, own, send, residual, store):
     inst, width = residual.shape
     slots, blocks = pick.shape
     half = own.shape[0] // SUB
-    total = (a[...] + b[...]) + (c[...] + d[...])
+    total = (a[...] + b[...]) + c[...]
     kinds = [total[k * blocks : (k + 1) * blocks] for k in range(inst + 1)]
     weight = kinds[inst] + 1.0
     table = [(kind / weight).astype(jnp.bfloat16).astype(jnp.float32) for kind in kinds[:inst]]
@@ -134,8 +149,8 @@
     if blocks <= FEW:
         for k in range(SUB):
             store[pl.ds(k, blocks, stride=SUB), :] = table[k]
-        by_block = [of_slot(store, block) for block in range(blocks)]
-        rows_of = lambda n: take(of_slot(row_key, n), by_block)
+        by_block = [twice(of_slot(store, block)) for block in range(blocks)]
+        rows_of_pair = lambda n: take(of_pair(row_pair, n), by_block)
     else:
         rows = jnp.dot(
             pick[...].astype(jnp.bfloat16),
@@ -144,8 +159,8 @@
         )
         for k in range(SUB):
             store[pl.ds(k, slots, stride=SUB), :] = rows[:, k * width : (k + 1) * width]
-        rows_of = lambda n: of_slot(store, n)
-    sums = sums_by_key(products(tiles, False, rows_of), place_key, 2 * half)
+        rows_of_pair = lambda n: of_pair(store, n).astype(jnp.bfloat16)
+    sums = sums_by_key(products(tiles, False, rows_of_pair), place_key, 2 * half)
     own[...] = jnp.concatenate(sums[:half], axis=0)
     send[...] = jnp.concatenate(sums[half:], axis=0).astype(jnp.bfloat16)
 
@@ -181,7 +196,7 @@
         )(*args)
 
     other = exchange(volume, "ray", 1)
-    keys = ((slots * SUB, width), jnp.int32)
+    keys, pair_keys = [((slots * SUB, width), dtype) for dtype in (jnp.int32, jnp.int16)]
     store = [pltpu.VMEM((max(slots, blocks) * (SUB + 1), width), f32)]
     (filler,) = call(
         functools.partial(filler_kernel, inst),
@@ -191,10 +206,10 @@
         [],
         cost=pl.CostEstimate(flops=ROWS_FLOPS, bytes_accessed=0, transcendentals=0),
     )
-    pick, add, row_key, place_key = call(
+    pick, add, row_key, place_key, row_pair, place_pair = call(
         functools.partial(prepare_kernel, half),
         "prepare",
-        [((slots, blocks), f32), ((blocks, PARTS * slots), f32), keys, keys],
+        [((slots, blocks), f32), ((blocks, PARTS * slots), f32), keys, keys, pair_keys, pair_keys],
         [],
         [tile_count, tile_row, tile_col],
         scalars=1,
@@ -204,16 +219,17 @@
         "project",
         [(((inst + 1) * blocks, width), f32)],
         store,
-        [tiles, add, row_key, place_key, volume, other, measured, filler],
-    )
-    terms = all_sum(part, "vox")
+        [tiles, add, row_key, place_pair, volume, other, measured, filler],
+    )
+    part_shape = (((inst + 1) * blocks, width), f32)
+    terms = all_sum(part, "vox", lambda *pair: call(add_kernel, "add", [part_shape], [], pair)[0])
     flat = (half * SUB, width)
     own, send, residual = call(
         backproject_kernel,
         "backproject",
         [(flat, f32), (flat, bf16), ((inst, width), f32)],
         store,
-        [tiles, pick, row_key, place_key, *terms],
+        [tiles, pick, row_pair, place_key, *terms],
     )
     there = exchange(send, "ray", 1)
     new_volume, own_residual = call(

time: 18.2 us -> 18.2 us (level)
    pallas_call x5 -> x6, Pallas kernels: 1.89 us -> 1.89 us  [call(): pl.pallas_call(kernel, out_shape=[jax.ShapeDtypeStruct(shape, dtype) for...]
where the time goes in v31:
time: 18.2 us; the launch traced here: 18 us
  starting transfers between devices  8.08 us (44%)
  waiting for transfers between devices  6.65 us (37%)
  Pallas kernels  1.89 us (10%)
  between operations  1.38 us (8%)
    ppermute x6, starting transfers between devices, exchange(): return lax.ppermute(value, axis, [(i, i ^ mask) for i in range(size)])  8.08 us
    ppermute x6, waiting for transfers between devices, exchange(): return lax.ppermute(value, axis, [(i, i ^ mask) for i in range(size)])  6.65 us
    pallas_call x6, Pallas kernels, call(): pl.pallas_call(kernel, out_shape=[jax.ShapeDtypeStruct(shape, dtype) for...  1.89 us
  transfers between devices with their start and end apart: 6, of which 6 were waited for; matrix products, arithmetic and copies ran while one was open for 0% of the time, Pallas kernels for 1%

profile of v31, /device:TPU:0, one launch (start us, length us, event | category | flops | bytes accessed | tf_op | source)
XLA Modules:
  0.0 18.0 jit_solution(4316341370764920153)
XLA Ops:
  0.6 0.0 copy-start.1
  0.6 0.0 copy-start.3
  0.7 0.0 copy-start.4
  0.7 0.0 copy-start
  0.7 0.0 copy-start.2
  0.7 0.5 %collective-permute-start = (f32[8,4,128]{2,1,0:T(4,128)}, f32[8,4,128]{2,1,0:T(4,128)S(1)}, u32[]{:S(2)}, u32[]{:S(2)}) collective-permute-start(f32[8,4,128]{2,1,0:T(4,128)} %volume.3), channel_id=1, source_target_pairs={{0,1},{1,0},{2,3},{3,2},{4,5},{5,4},{6,7},{7,6},{8,9},{9,8},{10,11... | collective-permute-start | bytes 49160 | tf_op jit(solution)/shard_map/ppermute | solution.py:19
  1.9 0.0 copy-done.3
  1.9 0.0 copy-done.4
  1.9 0.2 %prepare.1 = (f32[48,8]{1,0:T(8,128)S(1)}, f32[8,144]{1,0:T(8,128)S(1)}, s32[384,128]{1,0:T(8,128)S(1)}, s32[384,128]{1,0:T(8,128)S(1)}, s16[384,128]{1,0:T(8,128)(2,1)S(1)}, /*index=5*/s16[384,128]{1,0:T(8,128)(2,1)S(1)}) custom-call(s32[1,1]{1,0:T(1,128)S(6)} %copy.8.count, s32[1,1,48]{2,1,0:T(1,128)S(1)} %copy-done.3, s32[1,1,48]{2,1,0:T(1,128)S(1)} %copy-done.4), custom_call_target="tpu_custom_call" | custom-call | tf_op jit(solution)/shard_map/prepare/pallas_call | solution.py:187
  2.1 0.1 collective-permute-done.other
  2.2 0.0 copy-done.1
  2.3 0.0 copy-done
  2.3 0.0 copy-done.2
  2.3 0.5 %project.1 = f32[40,128]{1,0:T(8,128)S(1)} custom-call(bf16[1,1,48,128,128]{4,3,2,1,0:T(8,128)(2,1)S(1)} %copy-done, f32[8,144]{1,0:T(8,128)S(1)} %get-tuple-element.14.add, s32[384,128]{1,0:T(8,128)S(1)} %get-tuple-element.15.row_key, s16[384,128]{1,0:T(8,128)(2,1)S(1)} %get-tuple-element.16.place_pair, f32[8,4,128]{2,1,0:T(4,128)S(1)} %copy-done.1, ...), custom_call_target="tpu_custom_call" | custom-call | tf_op jit(solution)/shard_map/project/pallas_call | solution.py:187
  2.8 4.0 %collective-permute-start.1 = (f32[40,128]{1,0:T(8,128)S(1)}, f32[40,128]{1,0:T(8,128)S(1)}, u32[]{:S(2)}, u32[]{:S(2)}) collective-permute-start(f32[40,128]{1,0:T(8,128)S(1)} %project.1), channel_id=1, source_target_pairs={{0,8},{2,10},{4,12},{6,14},{8,0},{10,2},{12,4},{14,6},{1,9},{3,11}... | collective-permute-start | bytes 61448 | tf_op jit(solution)/shard_map/ppermute | solution.py:19
  6.8 1.8 %collective-permute-done.1 = f32[40,128]{1,0:T(8,128)S(1)} collective-permute-done((f32[40,128]{1,0:T(8,128)S(1)}, f32[40,128]{1,0:T(8,128)S(1)}, u32[]{:S(2)}, u32[]{:S(2)}) %collective-permute-start.1) | collective-permute-done | bytes 20512 | tf_op jit(solution)/shard_map/ppermute | solution.py:19
  8.6 1.9 %collective-permute-start.3 = (f32[40,128]{1,0:T(8,128)S(1)}, f32[40,128]{1,0:T(8,128)S(1)}, u32[]{:S(2)}, u32[]{:S(2)}) collective-permute-start(f32[40,128]{1,0:T(8,128)S(1)} %add.4.a), channel_id=1, source_target_pairs={{0,4},{2,6},{4,0},{6,2},{8,12},{10,14},{12,8},{14,10},{1,5},{3,7},... | collective-permute-start | bytes 61448 | tf_op jit(solution)/shard_map/ppermute | solution.py:19
  10.5 1.4 %collective-permute-start.4 = (f32[40,128]{1,0:T(8,128)S(1)}, f32[40,128]{1,0:T(8,128)S(1)}, u32[]{:S(2)}, u32[]{:S(2)}) collective-permute-start(f32[40,128]{1,0:T(8,128)S(1)} %add.4.a), channel_id=1, source_target_pairs={{0,6},{2,4},{4,2},{6,0},{8,14},{10,12},{12,10},{14,8},{1,7},{3,5},... | collective-permute-start | bytes 61448 | tf_op jit(solution)/shard_map/ppermute | solution.py:19
  11.9 0.2 %collective-permute-start.2 = (f32[40,128]{1,0:T(8,128)S(1)}, f32[40,128]{1,0:T(8,128)S(1)}, u32[]{:S(2)}, u32[]{:S(2)}) collective-permute-start(f32[40,128]{1,0:T(8,128)S(1)} %add.4.a), channel_id=1, source_target_pairs={{0,2},{2,0},{4,6},{6,4},{8,10},{10,8},{12,14},{14,12},{1,3},{3,1},... | collective-permute-start | bytes 61448 | tf_op jit(solution)/shard_map/ppermute | solution.py:19
  12.0 0.3 %collective-permute-done.3.left = f32[40,128]{1,0:T(8,128)S(1)} collective-permute-done((f32[40,128]{1,0:T(8,128)S(1)}, f32[40,128]{1,0:T(8,128)S(1)}, u32[]{:S(2)}, u32[]{:S(2)}) %collective-permute-start.3) | collective-permute-done | bytes 20512 | tf_op jit(solution)/shard_map/ppermute | solution.py:19
  12.3 2.8 %collective-permute-done.4.right = f32[40,128]{1,0:T(8,128)S(1)} collective-permute-done((f32[40,128]{1,0:T(8,128)S(1)}, f32[40,128]{1,0:T(8,128)S(1)}, u32[]{:S(2)}, u32[]{:S(2)}) %collective-permute-start.4) | collective-permute-done | bytes 20512 | tf_op jit(solution)/shard_map/ppermute | solution.py:19
  15.2 0.5 %collective-permute-done.2.b = f32[40,128]{1,0:T(8,128)S(1)} collective-permute-done((f32[40,128]{1,0:T(8,128)S(1)}, f32[40,128]{1,0:T(8,128)S(1)}, u32[]{:S(2)}, u32[]{:S(2)}) %collective-permute-start.2) | collective-permute-done | bytes 20512 | tf_op jit(solution)/shard_map/ppermute | solution.py:19
  15.6 0.5 %backproject.1 = (f32[64,128]{1,0:T(8,128)S(1)}, bf16[64,128]{1,0:T(8,128)(2,1)S(1)}, f32[4,128]{1,0:T(4,128)S(1)}) custom-call(bf16[1,1,48,128,128]{4,3,2,1,0:T(8,128)(2,1)S(1)} %copy-done, f32[48,8]{1,0:T(8,128)S(1)} %get-tuple-element.11.pick, s16[384,128]{1,0:T(8,128)(2,1)S(1)} %get-tuple-element.12.row_pair, ...), custom_call_target="tpu_custom_call" | custom-call | tf_op jit(solution)/shard_map/backproject/pallas_call | solution.py:187
  16.1 0.1 collective-permute-start.5
  16.2 1.2 %collective-permute-done.5.there = bf16[64,128]{1,0:T(8,128)(2,1)S(1)} collective-permute-done((bf16[64,128]{1,0:T(8,128)(2,1)S(1)}, bf16[64,128]{1,0:T(8,128)(2,1)S(1)}, u32[]{:S(2)}, u32[]{:S(2)}) %collective-permute-start.5) | collective-permute-done | bytes 16416 | tf_op jit(solution)/shard_map/ppermute | solution.py:19
  17.4 0.6 %update.1 = (f32[8,4,128]{2,1,0:T(4,128)}, bf16[1,1,4,128]{3,2,1,0:T(4,128)(2,1)}) custom-call(f32[8,4,128]{2,1,0:T(4,128)S(1)} %copy-done.1, f32[64,128]{1,0:T(8,128)S(1)} %get-tuple-element.17.own, bf16[64,128]{1,0:T(8,128)(2,1)S(1)} %collective-permute-done.5.there, f32[4,128]{1,0:T(4,128)S(1)} %get-tuple-element.19.residual), custom_call_target="tpu_custom_call" | custom-call | tf_op jit(solution)/shard_map/update/pallas_call | solution.py:187
  (3 shorter events, 0.0 us)
Async XLA Ops:
  0.6 1.6 %copy-start.1 = (f32[8,4,128]{2,1,0:T(4,128)S(1)}, f32[8,4,128]{2,1,0:T(4,128)}, u32[]{:S(2)}) copy-start(f32[8,4,128]{2,1,0:T(4,128)} %volume.3) | copy-start | bytes 49156
  0.6 1.2 %copy-start.3 = (s32[1,1,48]{2,1,0:T(1,128)S(1)}, s32[1,1,48]{2,1,0:T(1,128)}, u32[]{:S(2)}) copy-start(s32[1,1,48]{2,1,0:T(1,128)} %rows.1) | copy-start | bytes 580
  0.7 1.2 %copy-start.4 = (s32[1,1,48]{2,1,0:T(1,128)S(1)}, s32[1,1,48]{2,1,0:T(1,128)}, u32[]{:S(2)}) copy-start(s32[1,1,48]{2,1,0:T(1,128)} %cols.1) | copy-start | bytes 580
  0.7 1.6 %copy-start = (bf16[1,1,48,128,128]{4,3,2,1,0:T(8,128)(2,1)S(1)}, bf16[1,1,48,128,128]{4,3,2,1,0:T(8,128)(2,1)}, u32[]{:S(2)}) copy-start(bf16[1,1,48,128,128]{4,3,2,1,0:T(8,128)(2,1)} %tiles.3) | copy-start | bytes 4718596
  0.7 1.6 %copy-start.2 = (f32[1,1,4,128]{3,2,1,0:T(4,128)S(1)}, f32[1,1,4,128]{3,2,1,0:T(4,128)}, u32[]{:S(2)}) copy-start(f32[1,1,4,128]{3,2,1,0:T(4,128)} %measured.1) | copy-start | bytes 6148
  0.7 1.6 %collective-permute-start = (f32[8,4,128]{2,1,0:T(4,128)}, f32[8,4,128]{2,1,0:T(4,128)S(1)}, u32[]{:S(2)}, u32[]{:S(2)}) collective-permute-start(f32[8,4,128]{2,1,0:T(4,128)} %volume.3), channel_id=1, source_target_pairs={{0,1},{1,0},{2,3},{3,2},{4,5},{5,4},{6,7},{7,6},{8,9},{9,8},{10,11... | collective-permute-start | bytes 49160 | tf_op jit(solution)/shard_map/ppermute | solution.py:19
  2.8 5.8 %collective-permute-start.1 = (f32[40,128]{1,0:T(8,128)S(1)}, f32[40,128]{1,0:T(8,128)S(1)}, u32[]{:S(2)}, u32[]{:S(2)}) collective-permute-start(f32[40,128]{1,0:T(8,128)S(1)} %project.1), channel_id=1, source_target_pairs={{0,8},{2,10},{4,12},{6,14},{8,0},{10,2},{12,4},{14,6},{1,9},{3,11}... | collective-permute-start | bytes 61448 | tf_op jit(solution)/shard_map/ppermute | solution.py:19
  8.6 3.8 %collective-permute-start.3 = (f32[40,128]{1,0:T(8,128)S(1)}, f32[40,128]{1,0:T(8,128)S(1)}, u32[]{:S(2)}, u32[]{:S(2)}) collective-permute-start(f32[40,128]{1,0:T(8,128)S(1)} %add.4.a), channel_id=1, source_target_pairs={{0,4},{2,6},{4,0},{6,2},{8,12},{10,14},{12,8},{14,10},{1,5},{3,7},... | collective-permute-start | bytes 61448 | tf_op jit(solution)/shard_map/ppermute | solution.py:19
  10.5 4.7 %collective-permute-start.4 = (f32[40,128]{1,0:T(8,128)S(1)}, f32[40,128]{1,0:T(8,128)S(1)}, u32[]{:S(2)}, u32[]{:S(2)}) collective-permute-start(f32[40,128]{1,0:T(8,128)S(1)} %add.4.a), channel_id=1, source_target_pairs={{0,6},{2,4},{4,2},{6,0},{8,14},{10,12},{12,10},{14,8},{1,7},{3,5},... | collective-permute-start | bytes 61448 | tf_op jit(solution)/shard_map/ppermute | solution.py:19
  11.9 3.8 %collective-permute-start.2 = (f32[40,128]{1,0:T(8,128)S(1)}, f32[40,128]{1,0:T(8,128)S(1)}, u32[]{:S(2)}, u32[]{:S(2)}) collective-permute-start(f32[40,128]{1,0:T(8,128)S(1)} %add.4.a), channel_id=1, source_target_pairs={{0,2},{2,0},{4,6},{6,4},{8,10},{10,8},{12,14},{14,12},{1,3},{3,1},... | collective-permute-start | bytes 61448 | tf_op jit(solution)/shard_map/ppermute | solution.py:19
  16.1 1.2 %collective-permute-start.5 = (bf16[64,128]{1,0:T(8,128)(2,1)S(1)}, bf16[64,128]{1,0:T(8,128)(2,1)S(1)}, u32[]{:S(2)}, u32[]{:S(2)}) collective-permute-start(bf16[64,128]{1,0:T(8,128)(2,1)S(1)} %get-tuple-element.18), channel_id=1, source_target_pairs={{0,1},{1,0},{2,3},{3,2},{4,5},{5,4},{6,7},{7,6},{8,9},{9,8},{10,11... | collective-permute-start | bytes 49160 | tf_op jit(solution)/shard_map/ppermute | solution.py:19

commit v32 on v30

--- a/solution.py
+++ b/solution.py
@@ -72,7 +72,7 @@
     for n in range(0, slots, 2):
         pair = [tiles[0, 0, k] for k in (n, n + 1)]
         left = jnp.concatenate([rows_of(n), rows_of(n + 1)], axis=0).astype(jnp.bfloat16)
-        if transposed and n % 6:
+        if transposed and n % 4 == 0:
             right, contract = jnp.concatenate(pair, axis=0), 1
         else:
             right, contract = jnp.concatenate([tile.T if transposed else tile for tile in pair], axis=1), 0

time: 18.2 us -> 18.1 us (level)
  no operation moved by 1% of the time
where the time goes in v32:
time: 18.1 us; the launch traced here: 18 us
  starting transfers between devices  8.08 us (45%)
  waiting for transfers between devices  6.65 us (37%)
  Pallas kernels  1.88 us (10%)
  between operations  1.37 us (8%)
    ppermute x6, starting transfers between devices, exchange(): return lax.ppermute(value, axis, [(i, i ^ mask) for i in range(size)])  8.08 us
    ppermute x6, waiting for transfers between devices, exchange(): return lax.ppermute(value, axis, [(i, i ^ mask) for i in range(size)])  6.65 us
    pallas_call x5, Pallas kernels, call(): pl.pallas_call(kernel, out_shape=[jax.ShapeDtypeStruct(shape, dtype) for...  1.88 us
  transfers between devices with their start and end apart: 6, of which 6 were waited for; matrix products, arithmetic and copies ran while one was open for 0% of the time, Pallas kernels for 1%

profile of v32, /device:TPU:0, one launch (start us, length us, event | category | flops | bytes accessed | tf_op | source)
XLA Modules:
  0.0 18.0 jit_solution(2686801732861714803)
XLA Ops:
  0.6 0.0 copy-start.1
  0.6 0.0 copy-start.4
  0.7 0.0 copy-start.3
  0.7 0.0 copy-start
  0.7 0.0 copy-start.2
  0.7 0.5 %collective-permute-start = (f32[8,4,128]{2,1,0:T(4,128)}, f32[8,4,128]{2,1,0:T(4,128)S(1)}, u32[]{:S(2)}, u32[]{:S(2)}) collective-permute-start(f32[8,4,128]{2,1,0:T(4,128)} %volume.3), channel_id=1, source_target_pairs={{0,1},{1,0},{2,3},{3,2},{4,5},{5,4},{6,7},{7,6},{8,9},{9,8},{10,11... | collective-permute-start | bytes 49160 | tf_op jit(solution)/shard_map/ppermute | solution.py:19
  1.9 0.0 copy-done.4
  1.9 0.0 copy-done.3
  1.9 0.2 %prepare.1 = (f32[48,8]{1,0:T(8,128)S(1)}, f32[8,144]{1,0:T(8,128)S(1)}, s32[384,128]{1,0:T(8,128)S(1)}, s32[384,128]{1,0:T(8,128)S(1)}) custom-call(s32[1,1]{1,0:T(1,128)S(6)} %copy.8.count, s32[1,1,48]{2,1,0:T(1,128)S(1)} %copy-done.3, s32[1,1,48]{2,1,0:T(1,128)S(1)} %copy-done.4), custom_call_target="tpu_custom_call" | custom-call | tf_op jit(solution)/shard_map/prepare/pallas_call | solution.py:172
  2.1 0.1 collective-permute-done.other
  2.2 0.0 copy-done.1
  2.3 0.0 copy-done
  2.3 0.0 copy-done.2
  2.3 0.5 %project.1 = f32[40,128]{1,0:T(8,128)S(1)} custom-call(bf16[1,1,48,128,128]{4,3,2,1,0:T(8,128)(2,1)S(1)} %copy-done, f32[8,144]{1,0:T(8,128)S(1)} %get-tuple-element.12.add, s32[384,128]{1,0:T(8,128)S(1)} %get-tuple-element.10.row_key, s32[384,128]{1,0:T(8,128)S(1)} %get-tuple-element.11.place_key, f32[8,4,128]{2,1,0:T(4,128)S(1)} %copy-done.1, ...), custom_call_target="tpu_custom_call" | custom-call | tf_op jit(solution)/shard_map/project/pallas_call | solution.py:172
  2.8 4.0 %collective-permute-start.1 = (f32[40,128]{1,0:T(8,128)S(1)}, f32[40,128]{1,0:T(8,128)S(1)}, u32[]{:S(2)}, u32[]{:S(2)}) collective-permute-start(f32[40,128]{1,0:T(8,128)S(1)} %project.1), channel_id=1, source_target_pairs={{0,8},{2,10},{4,12},{6,14},{8,0},{10,2},{12,4},{14,6},{1,9},{3,11}... | collective-permute-start | bytes 61448 | tf_op jit(solution)/shard_map/ppermute | solution.py:19
  6.8 1.8 %collective-permute-done.1 = f32[40,128]{1,0:T(8,128)S(1)} collective-permute-done((f32[40,128]{1,0:T(8,128)S(1)}, f32[40,128]{1,0:T(8,128)S(1)}, u32[]{:S(2)}, u32[]{:S(2)}) %collective-permute-start.1) | collective-permute-done | bytes 20512 | tf_op jit(solution)/shard_map/ppermute | solution.py:19
  8.5 2.8 %collective-permute-start.4 = (f32[40,128]{1,0:T(8,128)S(1)}, f32[40,128]{1,0:T(8,128)S(1)}, u32[]{:S(2)}, u32[]{:S(2)}) collective-permute-start(f32[40,128]{1,0:T(8,128)S(1)} %add.3.a), channel_id=1, source_target_pairs={{0,6},{2,4},{4,2},{6,0},{8,14},{10,12},{12,10},{14,8},{1,7},{3,5},... | collective-permute-start | bytes 61448 | tf_op jit(solution)/shard_map/ppermute | solution.py:19
  11.4 0.5 %collective-permute-start.3 = (f32[40,128]{1,0:T(8,128)S(1)}, f32[40,128]{1,0:T(8,128)S(1)}, u32[]{:S(2)}, u32[]{:S(2)}) collective-permute-start(f32[40,128]{1,0:T(8,128)S(1)} %add.3.a), channel_id=1, source_target_pairs={{0,4},{2,6},{4,0},{6,2},{8,12},{10,14},{12,8},{14,10},{1,5},{3,7},... | collective-permute-start | bytes 61448 | tf_op jit(solution)/shard_map/ppermute | solution.py:19
  11.8 0.2 %collective-permute-start.2 = (f32[40,128]{1,0:T(8,128)S(1)}, f32[40,128]{1,0:T(8,128)S(1)}, u32[]{:S(2)}, u32[]{:S(2)}) collective-permute-start(f32[40,128]{1,0:T(8,128)S(1)} %add.3.a), channel_id=1, source_target_pairs={{0,2},{2,0},{4,6},{6,4},{8,10},{10,8},{12,14},{14,12},{1,3},{3,1},... | collective-permute-start | bytes 61448 | tf_op jit(solution)/shard_map/ppermute | solution.py:19
  12.0 1.3 %collective-permute-done.4.d = f32[40,128]{1,0:T(8,128)S(1)} collective-permute-done((f32[40,128]{1,0:T(8,128)S(1)}, f32[40,128]{1,0:T(8,128)S(1)}, u32[]{:S(2)}, u32[]{:S(2)}) %collective-permute-start.4) | collective-permute-done | bytes 20512 | tf_op jit(solution)/shard_map/ppermute | solution.py:19
  13.3 1.8 %collective-permute-done.3.c = f32[40,128]{1,0:T(8,128)S(1)} collective-permute-done((f32[40,128]{1,0:T(8,128)S(1)}, f32[40,128]{1,0:T(8,128)S(1)}, u32[]{:S(2)}, u32[]{:S(2)}) %collective-permute-start.3) | collective-permute-done | bytes 20512 | tf_op jit(solution)/shard_map/ppermute | solution.py:19
  15.2 0.5 %collective-permute-done.2.b = f32[40,128]{1,0:T(8,128)S(1)} collective-permute-done((f32[40,128]{1,0:T(8,128)S(1)}, f32[40,128]{1,0:T(8,128)S(1)}, u32[]{:S(2)}, u32[]{:S(2)}) %collective-permute-start.2) | collective-permute-done | bytes 20512 | tf_op jit(solution)/shard_map/ppermute | solution.py:19
  15.6 0.5 %backproject.1 = (f32[64,128]{1,0:T(8,128)S(1)}, bf16[64,128]{1,0:T(8,128)(2,1)S(1)}, f32[4,128]{1,0:T(4,128)S(1)}) custom-call(bf16[1,1,48,128,128]{4,3,2,1,0:T(8,128)(2,1)S(1)} %copy-done, f32[48,8]{1,0:T(8,128)S(1)} %get-tuple-element.9.pick, s32[384,128]{1,0:T(8,128)S(1)} %get-tuple-element.10.row_key, s32[384,128]{1,0:T(8,128)S(1)} %get-tuple-element.11.place_key, ...), custom_call_target="tpu_custom_call" | custom-call | tf_op jit(solution)/shard_map/backproject/pallas_call | solution.py:172
  16.1 0.1 collective-permute-start.5
  16.2 1.2 %collective-permute-done.5.there = bf16[64,128]{1,0:T(8,128)(2,1)S(1)} collective-permute-done((bf16[64,128]{1,0:T(8,128)(2,1)S(1)}, bf16[64,128]{1,0:T(8,128)(2,1)S(1)}, u32[]{:S(2)}, u32[]{:S(2)}) %collective-permute-start.5) | collective-permute-done | bytes 16416 | tf_op jit(solution)/shard_map/ppermute | solution.py:19
  17.4 0.6 %update.1 = (f32[8,4,128]{2,1,0:T(4,128)}, bf16[1,1,4,128]{3,2,1,0:T(4,128)(2,1)}) custom-call(f32[8,4,128]{2,1,0:T(4,128)S(1)} %copy-done.1, f32[64,128]{1,0:T(8,128)S(1)} %get-tuple-element.13.own, bf16[64,128]{1,0:T(8,128)(2,1)S(1)} %collective-permute-done.5.there, f32[4,128]{1,0:T(4,128)S(1)} %get-tuple-element.15.residual), custom_call_target="tpu_custom_call" | custom-call | tf_op jit(solution)/shard_map/update/pallas_call | solution.py:172
  (2 shorter events, 0.0 us)
Async XLA Ops:
  0.6 1.6 %copy-start.1 = (f32[8,4,128]{2,1,0:T(4,128)S(1)}, f32[8,4,128]{2,1,0:T(4,128)}, u32[]{:S(2)}) copy-start(f32[8,4,128]{2,1,0:T(4,128)} %volume.3) | copy-start | bytes 49156
  0.6 1.2 %copy-start.4 = (s32[1,1,48]{2,1,0:T(1,128)S(1)}, s32[1,1,48]{2,1,0:T(1,128)}, u32[]{:S(2)}) copy-start(s32[1,1,48]{2,1,0:T(1,128)} %cols.1) | copy-start | bytes 580
  0.7 1.2 %copy-start.3 = (s32[1,1,48]{2,1,0:T(1,128)S(1)}, s32[1,1,48]{2,1,0:T(1,128)}, u32[]{:S(2)}) copy-start(s32[1,1,48]{2,1,0:T(1,128)} %rows.1) | copy-start | bytes 580
  0.7 1.6 %copy-start = (bf16[1,1,48,128,128]{4,3,2,1,0:T(8,128)(2,1)S(1)}, bf16[1,1,48,128,128]{4,3,2,1,0:T(8,128)(2,1)}, u32[]{:S(2)}) copy-start(bf16[1,1,48,128,128]{4,3,2,1,0:T(8,128)(2,1)} %tiles.3) | copy-start | bytes 4718596
  0.7 1.6 %copy-start.2 = (f32[1,1,4,128]{3,2,1,0:T(4,128)S(1)}, f32[1,1,4,128]{3,2,1,0:T(4,128)}, u32[]{:S(2)}) copy-start(f32[1,1,4,128]{3,2,1,0:T(4,128)} %measured.1) | copy-start | bytes 6148
  0.7 1.6 %collective-permute-start = (f32[8,4,128]{2,1,0:T(4,128)}, f32[8,4,128]{2,1,0:T(4,128)S(1)}, u32[]{:S(2)}, u32[]{:S(2)}) collective-permute-start(f32[8,4,128]{2,1,0:T(4,128)} %volume.3), channel_id=1, source_target_pairs={{0,1},{1,0},{2,3},{3,2},{4,5},{5,4},{6,7},{7,6},{8,9},{9,8},{10,11... | collective-permute-start | bytes 49160 | tf_op jit(solution)/shard_map/ppermute | solution.py:19
  2.8 5.8 %collective-permute-start.1 = (f32[40,128]{1,0:T(8,128)S(1)}, f32[40,128]{1,0:T(8,128)S(1)}, u32[]{:S(2)}, u32[]{:S(2)}) collective-permute-start(f32[40,128]{1,0:T(8,128)S(1)} %project.1), channel_id=1, source_target_pairs={{0,8},{2,10},{4,12},{6,14},{8,0},{10,2},{12,4},{14,6},{1,9},{3,11}... | collective-permute-start | bytes 61448 | tf_op jit(solution)/shard_map/ppermute | solution.py:19
  8.5 4.8 %collective-permute-start.4 = (f32[40,128]{1,0:T(8,128)S(1)}, f32[40,128]{1,0:T(8,128)S(1)}, u32[]{:S(2)}, u32[]{:S(2)}) collective-permute-start(f32[40,128]{1,0:T(8,128)S(1)} %add.3.a), channel_id=1, source_target_pairs={{0,6},{2,4},{4,2},{6,0},{8,14},{10,12},{12,10},{14,8},{1,7},{3,5},... | collective-permute-start | bytes 61448 | tf_op jit(solution)/shard_map/ppermute | solution.py:19
  11.4 3.8 %collective-permute-start.3 = (f32[40,128]{1,0:T(8,128)S(1)}, f32[40,128]{1,0:T(8,128)S(1)}, u32[]{:S(2)}, u32[]{:S(2)}) collective-permute-start(f32[40,128]{1,0:T(8,128)S(1)} %add.3.a), channel_id=1, source_target_pairs={{0,4},{2,6},{4,0},{6,2},{8,12},{10,14},{12,8},{14,10},{1,5},{3,7},... | collective-permute-start | bytes 61448 | tf_op jit(solution)/shard_map/ppermute | solution.py:19
  11.8 3.8 %collective-permute-start.2 = (f32[40,128]{1,0:T(8,128)S(1)}, f32[40,128]{1,0:T(8,128)S(1)}, u32[]{:S(2)}, u32[]{:S(2)}) collective-permute-start(f32[40,128]{1,0:T(8,128)S(1)} %add.3.a), channel_id=1, source_target_pairs={{0,2},{2,0},{4,6},{6,4},{8,10},{10,8},{12,14},{14,12},{1,3},{3,1},... | collective-permute-start | bytes 61448 | tf_op jit(solution)/shard_map/ppermute | solution.py:19
  16.1 1.2 %collective-permute-start.5 = (bf16[64,128]{1,0:T(8,128)(2,1)S(1)}, bf16[64,128]{1,0:T(8,128)(2,1)S(1)}, u32[]{:S(2)}, u32[]{:S(2)}) collective-permute-start(bf16[64,128]{1,0:T(8,128)(2,1)S(1)} %get-tuple-element.14), channel_id=1, source_target_pairs={{0,1},{1,0},{2,3},{3,2},{4,5},{5,4},{6,7},{7,6},{8,9},{9,8},{10,11... | collective-permute-start | bytes 49160 | tf_op jit(solution)/shard_map/ppermute | solution.py:19

commit v33 on v32

--- a/solution.py
+++ b/solution.py
@@ -75,7 +75,8 @@
         if transposed and n % 4 == 0:
             right, contract = jnp.concatenate(pair, axis=0), 1
         else:
-            right, contract = jnp.concatenate([tile.T if transposed else tile for tile in pair], axis=1), 0
+            right = jnp.concatenate(pair, axis=0).T if transposed else jnp.concatenate(pair, axis=1)
+            contract = 0
         both = lax.dot_general(left, right, (((1,), (contract,)), ((), ())), preferred_element_type=jnp.float32)
         yield n, both[:SUB, :width]
         yield n + 1, both[SUB:, width:]

time: 18.1 us -> 18.2 us (level)
  no operation moved by 1% of the time
where the time goes in v33:
time: 18.2 us; the launch traced here: 18 us
  starting transfers between devices  8.08 us (44%)
  waiting for transfers between devices  6.65 us (37%)
  Pallas kernels  1.91 us (10%)
  between operations  1.37 us (8%)
    ppermute x6, starting transfers between devices, exchange(): return lax.ppermute(value, axis, [(i, i ^ mask) for i in range(size)])  8.08 us
    ppermute x6, waiting for transfers between devices, exchange(): return lax.ppermute(value, axis, [(i, i ^ mask) for i in range(size)])  6.65 us
    pallas_call x5, Pallas kernels, call(): pl.pallas_call(kernel, out_shape=[jax.ShapeDtypeStruct(shape, dtype) for...  1.91 us
  transfers between devices with their start and end apart: 6, of which 6 were waited for; matrix products, arithmetic and copies ran while one was open for 0% of the time, Pallas kernels for 1%

profile of v33, /device:TPU:0, one launch (start us, length us, event | category | flops | bytes accessed | tf_op | source)
XLA Modules:
  0.0 18.0 jit_solution(9337740255256859790)
XLA Ops:
  0.6 0.0 copy-start.1
  0.6 0.0 copy-start.4
  0.7 0.0 copy-start.3
  0.7 0.0 copy-start
  0.7 0.0 copy-start.2
  0.7 0.5 %collective-permute-start = (f32[8,4,128]{2,1,0:T(4,128)}, f32[8,4,128]{2,1,0:T(4,128)S(1)}, u32[]{:S(2)}, u32[]{:S(2)}) collective-permute-start(f32[8,4,128]{2,1,0:T(4,128)} %volume.3), channel_id=1, source_target_pairs={{0,1},{1,0},{2,3},{3,2},{4,5},{5,4},{6,7},{7,6},{8,9},{9,8},{10,11... | collective-permute-start | bytes 49160 | tf_op jit(solution)/shard_map/ppermute | solution.py:19
  1.9 0.0 copy-done.4
  1.9 0.0 copy-done.3
  1.9 0.2 %prepare.1 = (f32[48,8]{1,0:T(8,128)S(1)}, f32[8,144]{1,0:T(8,128)S(1)}, s32[384,128]{1,0:T(8,128)S(1)}, s32[384,128]{1,0:T(8,128)S(1)}) custom-call(s32[1,1]{1,0:T(1,128)S(6)} %copy.8.count, s32[1,1,48]{2,1,0:T(1,128)S(1)} %copy-done.3, s32[1,1,48]{2,1,0:T(1,128)S(1)} %copy-done.4), custom_call_target="tpu_custom_call" | custom-call | tf_op jit(solution)/shard_map/prepare/pallas_call | solution.py:173
  2.1 0.1 collective-permute-done.other
  2.2 0.0 copy-done.1
  2.3 0.0 copy-done
  2.3 0.0 copy-done.2
  2.3 0.6 %project.1 = f32[40,128]{1,0:T(8,128)S(1)} custom-call(bf16[1,1,48,128,128]{4,3,2,1,0:T(8,128)(2,1)S(1)} %copy-done, f32[8,144]{1,0:T(8,128)S(1)} %get-tuple-element.12.add, s32[384,128]{1,0:T(8,128)S(1)} %get-tuple-element.10.row_key, s32[384,128]{1,0:T(8,128)S(1)} %get-tuple-element.11.place_key, f32[8,4,128]{2,1,0:T(4,128)S(1)} %copy-done.1, ...), custom_call_target="tpu_custom_call" | custom-call | tf_op jit(solution)/shard_map/project/pallas_call | solution.py:173
  2.8 4.0 %collective-permute-start.1 = (f32[40,128]{1,0:T(8,128)S(1)}, f32[40,128]{1,0:T(8,128)S(1)}, u32[]{:S(2)}, u32[]{:S(2)}) collective-permute-start(f32[40,128]{1,0:T(8,128)S(1)} %project.1), channel_id=1, source_target_pairs={{0,8},{2,10},{4,12},{6,14},{8,0},{10,2},{12,4},{14,6},{1,9},{3,11}... | collective-permute-start | bytes 61448 | tf_op jit(solution)/shard_map/ppermute | solution.py:19
  6.8 1.8 %collective-permute-done.1 = f32[40,128]{1,0:T(8,128)S(1)} collective-permute-done((f32[40,128]{1,0:T(8,128)S(1)}, f32[40,128]{1,0:T(8,128)S(1)}, u32[]{:S(2)}, u32[]{:S(2)}) %collective-permute-start.1) | collective-permute-done | bytes 20512 | tf_op jit(solution)/shard_map/ppermute | solution.py:19
  8.6 2.8 %collective-permute-start.4 = (f32[40,128]{1,0:T(8,128)S(1)}, f32[40,128]{1,0:T(8,128)S(1)}, u32[]{:S(2)}, u32[]{:S(2)}) collective-permute-start(f32[40,128]{1,0:T(8,128)S(1)} %add.3.a), channel_id=1, source_target_pairs={{0,6},{2,4},{4,2},{6,0},{8,14},{10,12},{12,10},{14,8},{1,7},{3,5},... | collective-permute-start | bytes 61448 | tf_op jit(solution)/shard_map/ppermute | solution.py:19
  11.4 0.5 %collective-permute-start.3 = (f32[40,128]{1,0:T(8,128)S(1)}, f32[40,128]{1,0:T(8,128)S(1)}, u32[]{:S(2)}, u32[]{:S(2)}) collective-permute-start(f32[40,128]{1,0:T(8,128)S(1)} %add.3.a), channel_id=1, source_target_pairs={{0,4},{2,6},{4,0},{6,2},{8,12},{10,14},{12,8},{14,10},{1,5},{3,7},... | collective-permute-start | bytes 61448 | tf_op jit(solution)/shard_map/ppermute | solution.py:19
  11.9 0.2 %collective-permute-start.2 = (f32[40,128]{1,0:T(8,128)S(1)}, f32[40,128]{1,0:T(8,128)S(1)}, u32[]{:S(2)}, u32[]{:S(2)}) collective-permute-start(f32[40,128]{1,0:T(8,128)S(1)} %add.3.a), channel_id=1, source_target_pairs={{0,2},{2,0},{4,6},{6,4},{8,10},{10,8},{12,14},{14,12},{1,3},{3,1},... | collective-permute-start | bytes 61448 | tf_op jit(solution)/shard_map/ppermute | solution.py:19
  12.1 1.3 %collective-permute-done.4.d = f32[40,128]{1,0:T(8,128)S(1)} collective-permute-done((f32[40,128]{1,0:T(8,128)S(1)}, f32[40,128]{1,0:T(8,128)S(1)}, u32[]{:S(2)}, u32[]{:S(2)}) %collective-permute-start.4) | collective-permute-done | bytes 20512 | tf_op jit(solution)/shard_map/ppermute | solution.py:19
  13.4 1.8 %collective-permute-done.3.c = f32[40,128]{1,0:T(8,128)S(1)} collective-permute-done((f32[40,128]{1,0:T(8,128)S(1)}, f32[40,128]{1,0:T(8,128)S(1)}, u32[]{:S(2)}, u32[]{:S(2)}) %collective-permute-start.3) | collective-permute-done | bytes 20512 | tf_op jit(solution)/shard_map/ppermute | solution.py:19
  15.2 0.5 %collective-permute-done.2.b = f32[40,128]{1,0:T(8,128)S(1)} collective-permute-done((f32[40,128]{1,0:T(8,128)S(1)}, f32[40,128]{1,0:T(8,128)S(1)}, u32[]{:S(2)}, u32[]{:S(2)}) %collective-permute-start.2) | collective-permute-done | bytes 20512 | tf_op jit(solution)/shard_map/ppermute | solution.py:19
  15.7 0.5 %backproject.1 = (f32[64,128]{1,0:T(8,128)S(1)}, bf16[64,128]{1,0:T(8,128)(2,1)S(1)}, f32[4,128]{1,0:T(4,128)S(1)}) custom-call(bf16[1,1,48,128,128]{4,3,2,1,0:T(8,128)(2,1)S(1)} %copy-done, f32[48,8]{1,0:T(8,128)S(1)} %get-tuple-element.9.pick, s32[384,128]{1,0:T(8,128)S(1)} %get-tuple-element.10.row_key, s32[384,128]{1,0:T(8,128)S(1)} %get-tuple-element.11.place_key, ...), custom_call_target="tpu_custom_call" | custom-call | tf_op jit(solution)/shard_map/backproject/pallas_call | solution.py:173
  16.2 0.1 collective-permute-start.5
  16.2 1.2 %collective-permute-done.5.there = bf16[64,128]{1,0:T(8,128)(2,1)S(1)} collective-permute-done((bf16[64,128]{1,0:T(8,128)(2,1)S(1)}, bf16[64,128]{1,0:T(8,128)(2,1)S(1)}, u32[]{:S(2)}, u32[]{:S(2)}) %collective-permute-start.5) | collective-permute-done | bytes 16416 | tf_op jit(solution)/shard_map/ppermute | solution.py:19
  17.4 0.6 %update.1 = (f32[8,4,128]{2,1,0:T(4,128)}, bf16[1,1,4,128]{3,2,1,0:T(4,128)(2,1)}) custom-call(f32[8,4,128]{2,1,0:T(4,128)S(1)} %copy-done.1, f32[64,128]{1,0:T(8,128)S(1)} %get-tuple-element.13.own, bf16[64,128]{1,0:T(8,128)(2,1)S(1)} %collective-permute-done.5.there, f32[4,128]{1,0:T(4,128)S(1)} %get-tuple-element.15.residual), custom_call_target="tpu_custom_call" | custom-call | tf_op jit(solution)/shard_map/update/pallas_call | solution.py:173
  (2 shorter events, 0.0 us)
Async XLA Ops:
  0.6 1.6 %copy-start.1 = (f32[8,4,128]{2,1,0:T(4,128)S(1)}, f32[8,4,128]{2,1,0:T(4,128)}, u32[]{:S(2)}) copy-start(f32[8,4,128]{2,1,0:T(4,128)} %volume.3) | copy-start | bytes 49156
  0.6 1.2 %copy-start.4 = (s32[1,1,48]{2,1,0:T(1,128)S(1)}, s32[1,1,48]{2,1,0:T(1,128)}, u32[]{:S(2)}) copy-start(s32[1,1,48]{2,1,0:T(1,128)} %cols.1) | copy-start | bytes 580
  0.7 1.2 %copy-start.3 = (s32[1,1,48]{2,1,0:T(1,128)S(1)}, s32[1,1,48]{2,1,0:T(1,128)}, u32[]{:S(2)}) copy-start(s32[1,1,48]{2,1,0:T(1,128)} %rows.1) | copy-start | bytes 580
  0.7 1.6 %copy-start = (bf16[1,1,48,128,128]{4,3,2,1,0:T(8,128)(2,1)S(1)}, bf16[1,1,48,128,128]{4,3,2,1,0:T(8,128)(2,1)}, u32[]{:S(2)}) copy-start(bf16[1,1,48,128,128]{4,3,2,1,0:T(8,128)(2,1)} %tiles.3) | copy-start | bytes 4718596
  0.7 1.6 %copy-start.2 = (f32[1,1,4,128]{3,2,1,0:T(4,128)S(1)}, f32[1,1,4,128]{3,2,1,0:T(4,128)}, u32[]{:S(2)}) copy-start(f32[1,1,4,128]{3,2,1,0:T(4,128)} %measured.1) | copy-start | bytes 6148
  0.7 1.6 %collective-permute-start = (f32[8,4,128]{2,1,0:T(4,128)}, f32[8,4,128]{2,1,0:T(4,128)S(1)}, u32[]{:S(2)}, u32[]{:S(2)}) collective-permute-start(f32[8,4,128]{2,1,0:T(4,128)} %volume.3), channel_id=1, source_target_pairs={{0,1},{1,0},{2,3},{3,2},{4,5},{5,4},{6,7},{7,6},{8,9},{9,8},{10,11... | collective-permute-start | bytes 49160 | tf_op jit(solution)/shard_map/ppermute | solution.py:19
  2.8 5.8 %collective-permute-start.1 = (f32[40,128]{1,0:T(8,128)S(1)}, f32[40,128]{1,0:T(8,128)S(1)}, u32[]{:S(2)}, u32[]{:S(2)}) collective-permute-start(f32[40,128]{1,0:T(8,128)S(1)} %project.1), channel_id=1, source_target_pairs={{0,8},{2,10},{4,12},{6,14},{8,0},{10,2},{12,4},{14,6},{1,9},{3,11}... | collective-permute-start | bytes 61448 | tf_op jit(solution)/shard_map/ppermute | solution.py:19
  8.6 4.8 %collective-permute-start.4 = (f32[40,128]{1,0:T(8,128)S(1)}, f32[40,128]{1,0:T(8,128)S(1)}, u32[]{:S(2)}, u32[]{:S(2)}) collective-permute-start(f32[40,128]{1,0:T(8,128)S(1)} %add.3.a), channel_id=1, source_target_pairs={{0,6},{2,4},{4,2},{6,0},{8,14},{10,12},{12,10},{14,8},{1,7},{3,5},... | collective-permute-start | bytes 61448 | tf_op jit(solution)/shard_map/ppermute | solution.py:19
  11.4 3.8 %collective-permute-start.3 = (f32[40,128]{1,0:T(8,128)S(1)}, f32[40,128]{1,0:T(8,128)S(1)}, u32[]{:S(2)}, u32[]{:S(2)}) collective-permute-start(f32[40,128]{1,0:T(8,128)S(1)} %add.3.a), channel_id=1, source_target_pairs={{0,4},{2,6},{4,0},{6,2},{8,12},{10,14},{12,8},{14,10},{1,5},{3,7},... | collective-permute-start | bytes 61448 | tf_op jit(solution)/shard_map/ppermute | solution.py:19
  11.9 3.8 %collective-permute-start.2 = (f32[40,128]{1,0:T(8,128)S(1)}, f32[40,128]{1,0:T(8,128)S(1)}, u32[]{:S(2)}, u32[]{:S(2)}) collective-permute-start(f32[40,128]{1,0:T(8,128)S(1)} %add.3.a), channel_id=1, source_target_pairs={{0,2},{2,0},{4,6},{6,4},{8,10},{10,8},{12,14},{14,12},{1,3},{3,1},... | collective-permute-start | bytes 61448 | tf_op jit(solution)/shard_map/ppermute | solution.py:19
  16.2 1.2 %collective-permute-start.5 = (bf16[64,128]{1,0:T(8,128)(2,1)S(1)}, bf16[64,128]{1,0:T(8,128)(2,1)S(1)}, u32[]{:S(2)}, u32[]{:S(2)}) collective-permute-start(bf16[64,128]{1,0:T(8,128)(2,1)S(1)} %get-tuple-element.14), channel_id=1, source_target_pairs={{0,1},{1,0},{2,3},{3,2},{4,5},{5,4},{6,7},{7,6},{8,9},{9,8},{10,11... | collective-permute-start | bytes 49160 | tf_op jit(solution)/shard_map/ppermute | solution.py:19

commit v34 on v32

--- a/solution.py
+++ b/solution.py
@@ -82,10 +82,11 @@
 
 
 def sums_by_key(prods, keys, blocks):
-    sums = [jnp.zeros((SUB, keys.shape[1]), jnp.float32)] * blocks
+    sums = None
     for n, prod in prods:
         key = of_slot(keys, n)
-        sums = [total + jnp.where(key == b, prod, 0.0) for b, total in enumerate(sums)]
+        terms = [jnp.where(key == b, prod, 0.0) for b in range(blocks)]
+        sums = terms if sums is None else [total + term for total, term in zip(sums, terms)]
     return sums
 
 

time: 18.1 us -> 18.2 us (level)
  no operation moved by 1% of the time
where the time goes in v34:
time: 18.2 us; the launch traced here: 18 us
  starting transfers between devices  8.08 us (44%)
  waiting for transfers between devices  6.65 us (37%)
  Pallas kernels  1.88 us (10%)
  between operations  1.37 us (8%)
    ppermute x6, starting transfers between devices, exchange(): return lax.ppermute(value, axis, [(i, i ^ mask) for i in range(size)])  8.08 us
    ppermute x6, waiting for transfers between devices, exchange(): return lax.ppermute(value, axis, [(i, i ^ mask) for i in range(size)])  6.65 us
    pallas_call x5, Pallas kernels, call(): pl.pallas_call(kernel, out_shape=[jax.ShapeDtypeStruct(shape, dtype) for...  1.88 us
  transfers between devices with their start and end apart: 6, of which 6 were waited for; matrix products, arithmetic and copies ran while one was open for 0% of the time, Pallas kernels for 1%

profile of v34, /device:TPU:0, one launch (start us, length us, event | category | flops | bytes accessed | tf_op | source)
XLA Modules:
  0.0 18.0 jit_solution(14610288190625471741)
XLA Ops:
  0.6 0.0 copy-start.1
  0.6 0.0 copy-start.4
  0.7 0.0 copy-start.3
  0.7 0.0 copy-start
  0.7 0.0 copy-start.2
  0.7 0.5 %collective-permute-start = (f32[8,4,128]{2,1,0:T(4,128)}, f32[8,4,128]{2,1,0:T(4,128)S(1)}, u32[]{:S(2)}, u32[]{:S(2)}) collective-permute-start(f32[8,4,128]{2,1,0:T(4,128)} %volume.3), channel_id=1, source_target_pairs={{0,1},{1,0},{2,3},{3,2},{4,5},{5,4},{6,7},{7,6},{8,9},{9,8},{10,11... | collective-permute-start | bytes 49160 | tf_op jit(solution)/shard_map/ppermute | solution.py:19
  1.9 0.0 copy-done.4
  1.9 0.0 copy-done.3
  1.9 0.2 %prepare.1 = (f32[48,8]{1,0:T(8,128)S(1)}, f32[8,144]{1,0:T(8,128)S(1)}, s32[384,128]{1,0:T(8,128)S(1)}, s32[384,128]{1,0:T(8,128)S(1)}) custom-call(s32[1,1]{1,0:T(1,128)S(6)} %copy.8.count, s32[1,1,48]{2,1,0:T(1,128)S(1)} %copy-done.3, s32[1,1,48]{2,1,0:T(1,128)S(1)} %copy-done.4), custom_call_target="tpu_custom_call" | custom-call | tf_op jit(solution)/shard_map/prepare/pallas_call | solution.py:173
  2.1 0.1 collective-permute-done.other
  2.2 0.0 copy-done.1
  2.3 0.0 copy-done
  2.3 0.0 copy-done.2
  2.3 0.5 %project.1 = f32[40,128]{1,0:T(8,128)S(1)} custom-call(bf16[1,1,48,128,128]{4,3,2,1,0:T(8,128)(2,1)S(1)} %copy-done, f32[8,144]{1,0:T(8,128)S(1)} %get-tuple-element.12.add, s32[384,128]{1,0:T(8,128)S(1)} %get-tuple-element.10.row_key, s32[384,128]{1,0:T(8,128)S(1)} %get-tuple-element.11.place_key, f32[8,4,128]{2,1,0:T(4,128)S(1)} %copy-done.1, ...), custom_call_target="tpu_custom_call" | custom-call | tf_op jit(solution)/shard_map/project/pallas_call | solution.py:173
  2.8 4.0 %collective-permute-start.1 = (f32[40,128]{1,0:T(8,128)S(1)}, f32[40,128]{1,0:T(8,128)S(1)}, u32[]{:S(2)}, u32[]{:S(2)}) collective-permute-start(f32[40,128]{1,0:T(8,128)S(1)} %project.1), channel_id=1, source_target_pairs={{0,8},{2,10},{4,12},{6,14},{8,0},{10,2},{12,4},{14,6},{1,9},{3,11}... | collective-permute-start | bytes 61448 | tf_op jit(solution)/shard_map/ppermute | solution.py:19
  6.8 1.8 %collective-permute-done.1 = f32[40,128]{1,0:T(8,128)S(1)} collective-permute-done((f32[40,128]{1,0:T(8,128)S(1)}, f32[40,128]{1,0:T(8,128)S(1)}, u32[]{:S(2)}, u32[]{:S(2)}) %collective-permute-start.1) | collective-permute-done | bytes 20512 | tf_op jit(solution)/shard_map/ppermute | solution.py:19
  8.6 2.8 %collective-permute-start.4 = (f32[40,128]{1,0:T(8,128)S(1)}, f32[40,128]{1,0:T(8,128)S(1)}, u32[]{:S(2)}, u32[]{:S(2)}) collective-permute-start(f32[40,128]{1,0:T(8,128)S(1)} %add.3.a), channel_id=1, source_target_pairs={{0,6},{2,4},{4,2},{6,0},{8,14},{10,12},{12,10},{14,8},{1,7},{3,5},... | collective-permute-start | bytes 61448 | tf_op jit(solution)/shard_map/ppermute | solution.py:19
  11.4 0.5 %collective-permute-start.3 = (f32[40,128]{1,0:T(8,128)S(1)}, f32[40,128]{1,0:T(8,128)S(1)}, u32[]{:S(2)}, u32[]{:S(2)}) collective-permute-start(f32[40,128]{1,0:T(8,128)S(1)} %add.3.a), channel_id=1, source_target_pairs={{0,4},{2,6},{4,0},{6,2},{8,12},{10,14},{12,8},{14,10},{1,5},{3,7},... | collective-permute-start | bytes 61448 | tf_op jit(solution)/shard_map/ppermute | solution.py:19
  11.8 0.2 %collective-permute-start.2 = (f32[40,128]{1,0:T(8,128)S(1)}, f32[40,128]{1,0:T(8,128)S(1)}, u32[]{:S(2)}, u32[]{:S(2)}) collective-permute-start(f32[40,128]{1,0:T(8,128)S(1)} %add.3.a), channel_id=1, source_target_pairs={{0,2},{2,0},{4,6},{6,4},{8,10},{10,8},{12,14},{14,12},{1,3},{3,1},... | collective-permute-start | bytes 61448 | tf_op jit(solution)/shard_map/ppermute | solution.py:19
  12.0 1.3 %collective-permute-done.4.d = f32[40,128]{1,0:T(8,128)S(1)} collective-permute-done((f32[40,128]{1,0:T(8,128)S(1)}, f32[40,128]{1,0:T(8,128)S(1)}, u32[]{:S(2)}, u32[]{:S(2)}) %collective-permute-start.4) | collective-permute-done | bytes 20512 | tf_op jit(solution)/shard_map/ppermute | solution.py:19
  13.3 1.8 %collective-permute-done.3.c = f32[40,128]{1,0:T(8,128)S(1)} collective-permute-done((f32[40,128]{1,0:T(8,128)S(1)}, f32[40,128]{1,0:T(8,128)S(1)}, u32[]{:S(2)}, u32[]{:S(2)}) %collective-permute-start.3) | collective-permute-done | bytes 20512 | tf_op jit(solution)/shard_map/ppermute | solution.py:19
  15.2 0.5 %collective-permute-done.2.b = f32[40,128]{1,0:T(8,128)S(1)} collective-permute-done((f32[40,128]{1,0:T(8,128)S(1)}, f32[40,128]{1,0:T(8,128)S(1)}, u32[]{:S(2)}, u32[]{:S(2)}) %collective-permute-start.2) | collective-permute-done | bytes 20512 | tf_op jit(solution)/shard_map/ppermute | solution.py:19
  15.6 0.5 %backproject.1 = (f32[64,128]{1,0:T(8,128)S(1)}, bf16[64,128]{1,0:T(8,128)(2,1)S(1)}, f32[4,128]{1,0:T(4,128)S(1)}) custom-call(bf16[1,1,48,128,128]{4,3,2,1,0:T(8,128)(2,1)S(1)} %copy-done, f32[48,8]{1,0:T(8,128)S(1)} %get-tuple-element.9.pick, s32[384,128]{1,0:T(8,128)S(1)} %get-tuple-element.10.row_key, s32[384,128]{1,0:T(8,128)S(1)} %get-tuple-element.11.place_key, ...), custom_call_target="tpu_custom_call" | custom-call | tf_op jit(solution)/shard_map/backproject/pallas_call | solution.py:173
  16.1 0.1 collective-permute-start.5
  16.2 1.2 %collective-permute-done.5.there = bf16[64,128]{1,0:T(8,128)(2,1)S(1)} collective-permute-done((bf16[64,128]{1,0:T(8,128)(2,1)S(1)}, bf16[64,128]{1,0:T(8,128)(2,1)S(1)}, u32[]{:S(2)}, u32[]{:S(2)}) %collective-permute-start.5) | collective-permute-done | bytes 16416 | tf_op jit(solution)/shard_map/ppermute | solution.py:19
  17.4 0.6 %update.1 = (f32[8,4,128]{2,1,0:T(4,128)}, bf16[1,1,4,128]{3,2,1,0:T(4,128)(2,1)}) custom-call(f32[8,4,128]{2,1,0:T(4,128)S(1)} %copy-done.1, f32[64,128]{1,0:T(8,128)S(1)} %get-tuple-element.13.own, bf16[64,128]{1,0:T(8,128)(2,1)S(1)} %collective-permute-done.5.there, f32[4,128]{1,0:T(4,128)S(1)} %get-tuple-element.15.residual), custom_call_target="tpu_custom_call" | custom-call | tf_op jit(solution)/shard_map/update/pallas_call | solution.py:173
  (2 shorter events, 0.0 us)
Async XLA Ops:
  0.6 1.6 %copy-start.1 = (f32[8,4,128]{2,1,0:T(4,128)S(1)}, f32[8,4,128]{2,1,0:T(4,128)}, u32[]{:S(2)}) copy-start(f32[8,4,128]{2,1,0:T(4,128)} %volume.3) | copy-start | bytes 49156
  0.6 1.2 %copy-start.4 = (s32[1,1,48]{2,1,0:T(1,128)S(1)}, s32[1,1,48]{2,1,0:T(1,128)}, u32[]{:S(2)}) copy-start(s32[1,1,48]{2,1,0:T(1,128)} %cols.1) | copy-start | bytes 580
  0.7 1.2 %copy-start.3 = (s32[1,1,48]{2,1,0:T(1,128)S(1)}, s32[1,1,48]{2,1,0:T(1,128)}, u32[]{:S(2)}) copy-start(s32[1,1,48]{2,1,0:T(1,128)} %rows.1) | copy-start | bytes 580
  0.7 1.6 %copy-start = (bf16[1,1,48,128,128]{4,3,2,1,0:T(8,128)(2,1)S(1)}, bf16[1,1,48,128,128]{4,3,2,1,0:T(8,128)(2,1)}, u32[]{:S(2)}) copy-start(bf16[1,1,48,128,128]{4,3,2,1,0:T(8,128)(2,1)} %tiles.3) | copy-start | bytes 4718596
  0.7 1.6 %copy-start.2 = (f32[1,1,4,128]{3,2,1,0:T(4,128)S(1)}, f32[1,1,4,128]{3,2,1,0:T(4,128)}, u32[]{:S(2)}) copy-start(f32[1,1,4,128]{3,2,1,0:T(4,128)} %measured.1) | copy-start | bytes 6148
  0.7 1.6 %collective-permute-start = (f32[8,4,128]{2,1,0:T(4,128)}, f32[8,4,128]{2,1,0:T(4,128)S(1)}, u32[]{:S(2)}, u32[]{:S(2)}) collective-permute-start(f32[8,4,128]{2,1,0:T(4,128)} %volume.3), channel_id=1, source_target_pairs={{0,1},{1,0},{2,3},{3,2},{4,5},{5,4},{6,7},{7,6},{8,9},{9,8},{10,11... | collective-permute-start | bytes 49160 | tf_op jit(solution)/shard_map/ppermute | solution.py:19
  2.8 5.8 %collective-permute-start.1 = (f32[40,128]{1,0:T(8,128)S(1)}, f32[40,128]{1,0:T(8,128)S(1)}, u32[]{:S(2)}, u32[]{:S(2)}) collective-permute-start(f32[40,128]{1,0:T(8,128)S(1)} %project.1), channel_id=1, source_target_pairs={{0,8},{2,10},{4,12},{6,14},{8,0},{10,2},{12,4},{14,6},{1,9},{3,11}... | collective-permute-start | bytes 61448 | tf_op jit(solution)/shard_map/ppermute | solution.py:19
  8.6 4.8 %collective-permute-start.4 = (f32[40,128]{1,0:T(8,128)S(1)}, f32[40,128]{1,0:T(8,128)S(1)}, u32[]{:S(2)}, u32[]{:S(2)}) collective-permute-start(f32[40,128]{1,0:T(8,128)S(1)} %add.3.a), channel_id=1, source_target_pairs={{0,6},{2,4},{4,2},{6,0},{8,14},{10,12},{12,10},{14,8},{1,7},{3,5},... | collective-permute-start | bytes 61448 | tf_op jit(solution)/shard_map/ppermute | solution.py:19
  11.4 3.8 %collective-permute-start.3 = (f32[40,128]{1,0:T(8,128)S(1)}, f32[40,128]{1,0:T(8,128)S(1)}, u32[]{:S(2)}, u32[]{:S(2)}) collective-permute-start(f32[40,128]{1,0:T(8,128)S(1)} %add.3.a), channel_id=1, source_target_pairs={{0,4},{2,6},{4,0},{6,2},{8,12},{10,14},{12,8},{14,10},{1,5},{3,7},... | collective-permute-start | bytes 61448 | tf_op jit(solution)/shard_map/ppermute | solution.py:19
  11.8 3.8 %collective-permute-start.2 = (f32[40,128]{1,0:T(8,128)S(1)}, f32[40,128]{1,0:T(8,128)S(1)}, u32[]{:S(2)}, u32[]{:S(2)}) collective-permute-start(f32[40,128]{1,0:T(8,128)S(1)} %add.3.a), channel_id=1, source_target_pairs={{0,2},{2,0},{4,6},{6,4},{8,10},{10,8},{12,14},{14,12},{1,3},{3,1},... | collective-permute-start | bytes 61448 | tf_op jit(solution)/shard_map/ppermute | solution.py:19
  16.1 1.2 %collective-permute-start.5 = (bf16[64,128]{1,0:T(8,128)(2,1)S(1)}, bf16[64,128]{1,0:T(8,128)(2,1)S(1)}, u32[]{:S(2)}, u32[]{:S(2)}) collective-permute-start(bf16[64,128]{1,0:T(8,128)(2,1)S(1)} %get-tuple-element.14), channel_id=1, source_target_pairs={{0,1},{1,0},{2,3},{3,2},{4,5},{5,4},{6,7},{7,6},{8,9},{9,8},{10,11... | collective-permute-start | bytes 49160 | tf_op jit(solution)/shard_map/ppermute | solution.py:19
